TPU v7x, 32 devices: a whole 2x2x4 slice. The times are simulated.
32 devices in a mesh: seed: 4 (over y, x), fsdp: 2 (over core), seq: 4 (over z).
Axes of the slice: x: 2, y: 2, z: 4, core: 2. Of those that a mesh axis runs over, the one named last changes fastest.
Arguments:
- mel_frames: bfloat16 [2, 16384, 80], P('fsdp', 'seq'), may hold values from -6 to 6
- lengths: int32 [2], P('fsdp'), may hold values from 1 to 4096, 5120 in all
- targets: int32 [2, 4096], P('fsdp', 'seq'), may hold values from 0 to 511
- frame_mask: int32 [2, 4096], P('fsdp', 'seq'), may hold values 0 or 1
- stem_weight: bfloat16 [4, 640, 1536], P('seed'), may hold values from -0.25 to 0.25
- conv_in_weight: bfloat16 [4, 1536, 1536], P('seed', ('fsdp', 'seq')), may hold values from -0.15625 to 0.15625
- conv_out_weight: bfloat16 [4, 768, 1536], P('seed', ('fsdp', 'seq')), may hold values from -0.21875 to 0.21875
- depth_weight: bfloat16 [4, 31, 768], P('seed'), may hold values from -1 to 1
- head_weight: bfloat16 [4, 1536, 512], P('seed', ('fsdp', 'seq')), may hold values from -80 to 80
- norm_gain: float32 [4, 2, 1536], P('seed'), may hold values from 0.5 to 1.5
Outputs:
- frame_error: float32 [2, 4096], P('fsdp', 'seq')
- utt_score: float32 [2], P('fsdp')
Inputs may be any that keep to these rules, and one draw needn't show every extreme that they name: `lengths`: some utterance has exactly 4096 valid frames.
All inputs are finite; a program needn't handle non-finite values. No bound on the sum of `lengths` or of `frame_mask` on one device may be relied on, other than what follows from the above.
Results may differ from a plain program's by a relative error of at most 0.0022.
Values may be sent and summed in bfloat16 or wider, within the bound.
No kernel may reach another device: no remote copies, remote signals or barrier semaphores. Data moves between devices by JAX's collectives and lax.ppermute only.
A program may use at most 64 MiB of HBM per device.

v0:
```python
import jax
import jax.numpy as jnp
from jax import lax
from jax.sharding import PartitionSpec as P


def from_behind(x, axis, by):
    count = lax.axis_size(axis)
    pairs = [(i, i + by) for i in range(count) if 0 <= i + by < count]
    return lax.ppermute(x, axis, pairs)


def extended(x, sides, width):
    for axis, dim in sides:
        count, length = (lax.axis_size(axis), x.shape[dim])
        up = [(i, (i + 1) % count) for i in range(count - 1)]
        down = [(j, i) for i, j in up]
        last = lax.slice_in_dim(x, length - width, length, axis=dim)
        first = lax.slice_in_dim(x, 0, width, axis=dim)
        before = lax.ppermute(last, axis, up)
        after = lax.ppermute(first, axis, down)
        x = jnp.concatenate([before, x, after], axis=dim)
    return x


def layer_norm(values, gain_row):
    row_mean = jnp.mean(values, axis=-1, keepdims=True)
    centred = values - row_mean
    row_var = jnp.mean(centred * centred, axis=-1, keepdims=True)
    return (centred * lax.rsqrt(row_var + 1e-05) * gain_row).astype(jnp.bfloat16)


def block_product(left_rows, right_matrix):
    return jnp.dot(left_rows, right_matrix, preferred_element_type=jnp.float32)


def row_product(activations, shard_piece):
    return block_product(activations, shard_piece[0])


def body(
    mel_frames,
    lengths,
    targets,
    frame_mask,
    stem_weight,
    conv_in_weight,
    conv_out_weight,
    depth_weight,
    head_weight,
    norm_gain,
):
    frame_rows = targets.shape[1]
    blocks = mel_frames[0].reshape(frame_rows, -1)
    next_block = from_behind(blocks[:1], "seq", -1)
    following = jnp.concatenate([blocks[1:], next_block], 0)
    half_width = blocks.shape[1]
    stem_matrix = stem_weight[0]
    stem_out = (
        jnp.dot(blocks, stem_matrix[:half_width], preferred_element_type=jnp.float32)
        + jnp.dot(following, stem_matrix[half_width:], preferred_element_type=jnp.float32)
    ).astype(jnp.bfloat16)
    offset = lax.axis_index("seq") * frame_rows
    length = lengths[0]
    positions = offset + jnp.arange(frame_rows, dtype=jnp.int32)
    frame_live = positions < length
    gain_rows = norm_gain[0]
    normed_one = layer_norm(stem_out.astype(jnp.float32), gain_rows[0])
    tap_count = depth_weight.shape[1]
    channels = depth_weight.shape[2]
    halo_width = tap_count // 2
    conv_input = extended(normed_one, (("seq", 0),), halo_width)
    mixed_rows = row_product(
        conv_input, lax.all_gather(conv_in_weight, ("fsdp", "seq"), axis=1, tiled=True)
    )
    input_positions = offset - halo_width + jnp.arange(conv_input.shape[0], dtype=jnp.int32)
    input_live = jnp.logical_and(input_positions >= 0, input_positions < length)
    gated_rows = (
        mixed_rows[:, :channels]
        * jax.nn.sigmoid(mixed_rows[:, channels:])
        * input_live[:, None].astype(jnp.float32)
    ).astype(jnp.bfloat16)
    depthwise = jnp.zeros((frame_rows, channels), jnp.float32)
    for tap_index in range(tap_count):
        depthwise = depthwise + gated_rows[tap_index : tap_index + frame_rows].astype(
            jnp.float32
        ) * depth_weight[0, tap_index].astype(jnp.float32)
    swished = jax.nn.silu(depthwise).astype(jnp.bfloat16)
    conv_proj = row_product(
        swished, lax.all_gather(conv_out_weight, ("fsdp", "seq"), axis=1, tiled=True)
    )
    after_conv = stem_out.astype(jnp.float32) + conv_proj
    normed_two = layer_norm(after_conv, gain_rows[1])
    logits = row_product(
        normed_two, lax.all_gather(head_weight, ("fsdp", "seq"), axis=1, tiled=True)
    )
    posterior = jax.nn.softmax(logits, axis=-1)
    vocab_size = logits.shape[1]
    onehot = (jnp.arange(vocab_size, dtype=jnp.int32)[None, :] == targets[0][:, None]).astype(
        jnp.float32
    )
    differ = posterior - onehot
    frame_err = (
        jnp.sqrt(jnp.sum(differ * differ, axis=-1))
        * frame_live.astype(jnp.float32)
        * frame_mask[0].astype(jnp.float32)
    )
    seed_count = lax.axis_size("seed")
    frame_error = lax.psum(frame_err, "seed") / jnp.float32(seed_count)
    numerator = lax.psum(jnp.sum(frame_error), "seq")
    utt_score = numerator / length.astype(jnp.float32)
    return (frame_error[None, :], utt_score.reshape(1))


def solution(mesh):
    in_specs = (
        P("fsdp", "seq", None),
        P("fsdp"),
        P("fsdp", "seq"),
        P("fsdp", "seq"),
        P("seed", None, None),
        P("seed", ("fsdp", "seq"), None),
        P("seed", ("fsdp", "seq"), None),
        P("seed", None, None),
        P("seed", ("fsdp", "seq"), None),
        P("seed", None, None),
    )
    out_specs = (P("fsdp", "seq"), P("fsdp"))
    return jax.shard_map(body, mesh=mesh, in_specs=in_specs, out_specs=out_specs, check_vma=False)
```

profile of v0, /device:TPU:0, one launch (start us, length us, event | category | flops | bytes accessed | tf_op | source)
XLA Modules:
  0.0 178.0 jit_solution(8987852436973627269)
XLA Ops:
  7.2 0.0 copy-start.3
  7.2 0.0 all-gather.4.cloned.1.call-start
  7.2 0.7 all-gather.4.cloned.1.call-update
  7.9 0.0 all-gather.6.cloned.1.call-start
  8.0 0.7 all-gather.6.cloned.1.call-update
  8.7 0.0 all-gather.8.cloned.1.call-start
  8.7 0.7 slice.234
  9.4 0.1 copy.14
  9.5 0.1 slice.235
  9.6 1.3 collective-permute-start
  10.9 0.0 all-gather.8.cloned.1.call-update
  10.9 1.6 copy.12
  12.5 1.3 convert_reduce_fusion.31
  13.8 1.1 convert_reduce_fusion.30
  14.9 0.7 reshape_squeeze.3
  15.6 0.0 copy-done.3
  15.7 0.0 copy-start.2
  15.7 5.8 %fusion.21 = f32[1024,1536]{1,0:T(8,128)} fusion(bf16[1024,320]{1,0:T(8,128)(2,1)S(1)} %reshape_squeeze.3, bf16[1,640,1536]{2,1,0:T(8,128)(2,1)} %param.14), kind=kOutput, calls=%fused_computation.32 | convolution fusion | flops 1006632960 | bytes 7929856 | tf_op jit(solution)/shard_map/dot_general | solution.py:60
  21.4 0.0 copy-done.2
  21.4 0.2 slice.232
  21.7 0.6 copy.13
  22.3 1.6 slice.233
  24.6 0.0 collective-permute-done
  24.6 5.3 %convert_reduce_fusion = (f32[1024]{0:T(1024)S(1)}, bf16[1024,1536]{1,0:T(8,128)(2,1)S(1)}) fusion(f32[1024,1536]{1,0:T(8,128)} %fusion.21, bf16[1,640,1536]{2,1,0:T(8,128)(2,1)} %param.14, bf16[1,320]{1,0:T(2,128)(2,1)S(1)} %collective-permute-done, bf16[1023,320]{1,0:T(8,128)(2,1)} %slice.233), kind=kOutput, calls=%fused_computation.2 | convolution fusion | flops 1014234112 | bytes 11211392 | tf_op jit(solution)/shard_map/dot_general | solution.py:61
  29.9 1.0 fusion.2
  30.8 0.0 copy-start.5
  30.9 1.0 fusion.4
  31.9 0.0 copy-start
  31.9 1.7 copy-done
  33.6 5.5 %collective-permute-start.1 = (bf16[15,1536]{1,0:T(8,128)(2,1)S(1)}, bf16[15,1536]{1,0:T(8,128)(2,1)S(1)}, u32[]{:S(2)}, u32[]{:S(2)}) collective-permute-start(bf16[15,1536]{1,0:T(8,128)(2,1)S(1)} %get-tuple-element.36), channel_id=1, source_target_pairs={{0,1},{1,2},{2,3},{4,5},{5,6},{6,7},{8,9},{9,10},{10,11},{12,13},{... | collective-permute-start | bytes 138248 | tf_op jit(solution)/shard_map/ppermute | solution.py:20
  39.2 1.5 collective-permute-start.2
  40.7 0.0 copy-done.5
  40.7 1.2 collective-permute-done.1
  41.9 5.7 %collective-permute-done.2 = bf16[15,1536]{1,0:T(8,128)(2,1)S(1)} collective-permute-done((bf16[15,1536]{1,0:T(8,128)(2,1)S(1)}, bf16[15,1536]{1,0:T(8,128)(2,1)S(1)}, u32[]{:S(2)}, u32[]{:S(2)}) %collective-permute-start.2) | collective-permute-done | bytes 46112 | tf_op jit(solution)/shard_map/ppermute | solution.py:21
  47.6 18.7 %concatenate.7 = bf16[1054,1536]{1,0:T(8,128)(2,1)} concatenate(bf16[15,1536]{1,0:T(8,128)(2,1)S(1)} %collective-permute-done.1, bf16[1024,1536]{1,0:T(8,128)(2,1)} %copy-done, bf16[15,1536]{1,0:T(8,128)(2,1)S(1)} %collective-permute-done.2), dimensions={0} | concatenate | bytes 6475776 | tf_op jit(solution)/shard_map/concatenate | solution.py:22
  66.3 0.0 all-gather.4.cloned.1.call-done
  66.3 8.1 %fusion.5 = f32[1054,1536]{1,0:T(8,128)S(1)} fusion(bf16[1054,1536]{1,0:T(8,128)(2,1)} %concatenate.7, bf16[1,1536,1536]{2,1,0:T(8,128)(2,1)} %all-gather.4.cloned.1.call-done), kind=kOutput, calls=%fused_computation.11 | convolution fusion | flops 4973395968 | bytes 14432256 | tf_op jit(solution)/shard_map/dot_general | solution.py:34
  74.3 2.0 %fusion.12 = bf16[1054,768]{1,0:T(8,128)(2,1)} fusion(f32[1054,1536]{1,0:T(8,128)S(1)} %fusion.5, f32[1054]{0:T(1024)S(1)} %fusion.31), kind=kLoop, calls=%fused_computation.19 | loop fusion | flops 4856832 | bytes 8098936 | tf_op jit(solution)/shard_map/convert_element_type | solution.py:82
  76.4 20.7 %all-gather.6.cloned.1.call-done = bf16[1,768,1536]{2,1,0:T(8,128)(2,1)} async-done(((bf16[1,96,1536]{2,1,0:T(8,128)(2,1)}), bf16[1,768,1536]{2,1,0:T(8,128)(2,1)}) %all-gather.6.cloned.1.call-update) | async-done | bytes 2359312 | tf_op jit(solution)/shard_map/all_gather | solution.py:90
  97.1 42.4 %fusion.36 = (f32[1024]{0:T(1024)S(1)}, f32[1024,1536]{1,0:T(8,128)S(1)}) fusion(bf16[1,768,1536]{2,1,0:T(8,128)(2,1)} %all-gather.6.cloned.1.call-done, bf16[1054,768]{1,0:T(8,128)(2,1)} %fusion.12, f32[768]{0:T(1024)S(1)} %get-tuple-element.31, f32[768]{0:T(1024)S(1)} %get-tuple-element.32, f32[768]{0:T(1024)S(1)} %get-tuple-element.3, ...), kind=kOutput, calls=%fused_computation.88 | convolution fusion | flops 2496920576 | bytes 60654592 | tf_op jit(solution)/shard_map/dot_general | solution.py:34
  139.5 0.0 copy-start.1
  139.5 0.8 multiply_reduce_fusion
  140.3 1.8 %copy-done.1 = f32[1024,1536]{1,0:T(8,128)} copy-done((f32[1024,1536]{1,0:T(8,128)}, f32[1024,1536]{1,0:T(8,128)S(1)}, u32[]{:S(2)}) %copy-start.1) | copy-done | bytes 6291480
  142.1 0.0 all-gather.8.cloned.1.call-done
  142.1 0.0 copy-start.4
  142.1 5.0 %fusion.37 = (f32[1024]{0:T(1024)S(1)}, f32[1024,512]{0,1:T(8,128)S(1)}) fusion(bf16[1,1536,512]{2,1,0:T(8,128)(2,1)} %all-gather.8.cloned.1.call-done, f32[1024,1536]{1,0:T(8,128)} %copy-done.1, f32[1536]{0:T(1024)S(1)} %get-tuple-element.33, f32[1024]{0:T(1024)S(1)} %add_rsqrt_fusion, f32[1024]{0:T(1024)S(1)} %broadcast_multiply_fusion.1), kind=kOutput, calls=%fused_computation.89 | convolution fusion | flops 1617427456 | bytes 9979904 | tf_op jit(solution)/shard_map/dot_general | solution.py:34
  147.1 0.3 fusion.18
  147.5 0.0 copy-done.4
  147.5 0.7 multiply_reduce_fusion.1
  148.2 9.8 %psum.14 = f32[1024]{0:T(1024)S(1)} all-reduce(f32[1024]{0:T(1024)S(1)} %select_multiply_fusion), channel_id=1, replica_groups=mesh['seed'=4,'fsdp'=2,'seq'=4] {'seed'}, use_global_device_ids=true, to_apply=%region_7.8 | all-reduce | flops 1024 | bytes 8192 | tf_op jit(solution)/shard_map/psum | solution.py:109
  158.0 1.2 fusion.34
  159.2 10.5 %psum.15 = f32[]{:T(128)} all-reduce(f32[]{:T(128)} %get-tuple-element.37), channel_id=1, replica_groups=mesh['seed'=4,'fsdp'=2,'seq'=4] {'seq'}, use_global_device_ids=true, to_apply=%region_9.10 | all-reduce | flops 1 | bytes 8 | tf_op jit(solution)/shard_map/psum | solution.py:110
  (9 shorter events, 0.1 us)
Async XLA Ops:
  7.2 8.4 %copy-start.3 = (f32[1,2,1536]{2,1,0:T(2,128)S(1)}, f32[1,2,1536]{2,1,0:T(2,128)}, u32[]{:S(2)}) copy-start(f32[1,2,1536]{2,1,0:T(2,128)} %param.19) | copy-start | bytes 36868
  7.2 59.1 %all-gather.4.cloned.1.call-start = ((), (), s32[]{:S(2)}) async-start(), calls=%async_computation | async-start | bytes 5308416 | tf_op jit(solution)/shard_map/all_gather | solution.py:74
  7.9 89.2 %all-gather.6.cloned.1.call-start = ((), (), s32[]{:S(2)}) async-start(), calls=%async_computation.1 | async-start | bytes 2654208 | tf_op jit(solution)/shard_map/all_gather | solution.py:90
  8.7 133.5 %all-gather.8.cloned.1.call-start = ((), (), s32[]{:S(2)}) async-start(), calls=%async_computation.2 | async-start | bytes 1769472 | tf_op jit(solution)/shard_map/all_gather | solution.py:95
  9.6 15.0 %collective-permute-start = (bf16[1,320]{1,0:T(2,128)(2,1)S(1)}, bf16[1,320]{1,0:T(2,128)(2,1)S(1)}, u32[]{:S(2)}, u32[]{:S(2)}) collective-permute-start(bf16[1,320]{1,0:T(2,128)(2,1)S(1)} %slice.235), channel_id=1, source_target_pairs={{1,0},{2,1},{3,2},{5,4},{6,5},{7,6},{9,8},{10,9},{11,10},{13,12},{... | collective-permute-start | bytes 1928 | tf_op jit(solution)/shard_map/ppermute | solution.py:10
  15.7 5.8 %copy-start.2 = (bf16[1,4096,80]{1,2,0:T(8,128)(2,1)S(1)}, bf16[1,4096,80]{1,2,0:T(8,128)(2,1)}, u32[]{:S(2)}) copy-start(bf16[1,4096,80]{1,2,0:T(8,128)(2,1)} %param.10) | copy-start | bytes 1966084
  30.8 9.8 %copy-start.5 = (s32[1,1024]{1,0:T(1,128)S(1)}, s32[1,1024]{1,0:T(1,128)}, u32[]{:S(2)}) copy-start(s32[1,1024]{1,0:T(1,128)} %param.13) | copy-start | bytes 12292
  31.9 1.7 copy-start
  33.6 8.3 %collective-permute-start.1 = (bf16[15,1536]{1,0:T(8,128)(2,1)S(1)}, bf16[15,1536]{1,0:T(8,128)(2,1)S(1)}, u32[]{:S(2)}, u32[]{:S(2)}) collective-permute-start(bf16[15,1536]{1,0:T(8,128)(2,1)S(1)} %get-tuple-element.36), channel_id=1, source_target_pairs={{0,1},{1,2},{2,3},{4,5},{5,6},{6,7},{8,9},{9,10},{10,11},{12,13},{... | collective-permute-start | bytes 138248 | tf_op jit(solution)/shard_map/ppermute | solution.py:20
  39.2 8.5 %collective-permute-start.2 = (bf16[15,1536]{1,0:T(8,128)(2,1)S(1)}, bf16[15,1536]{1,0:T(8,128)(2,1)S(1)}, u32[]{:S(2)}, u32[]{:S(2)}) collective-permute-start(bf16[15,1536]{1,0:T(8,128)(2,1)S(1)} %get-tuple-element.35), channel_id=1, source_target_pairs={{1,0},{2,1},{3,2},{5,4},{6,5},{7,6},{9,8},{10,9},{11,10},{13,12},{... | collective-permute-start | bytes 138248 | tf_op jit(solution)/shard_map/ppermute | solution.py:21
  139.5 2.6 %copy-start.1 = (f32[1024,1536]{1,0:T(8,128)}, f32[1024,1536]{1,0:T(8,128)S(1)}, u32[]{:S(2)}) copy-start(f32[1024,1536]{1,0:T(8,128)S(1)} %get-tuple-element.42) | copy-start | bytes 18874372
  142.1 5.4 %copy-start.4 = (s32[1,1024]{1,0:T(1,128)S(1)}, s32[1,1024]{1,0:T(1,128)}, u32[]{:S(2)}) copy-start(s32[1,1024]{1,0:T(1,128)} %param.12) | copy-start | bytes 12292
Sparse Core Ops, SparseCore 0:
  9.6 55.4 all-gather.3
  66.7 30.4 all-gather.5
  98.7 24.1 all-gather.7
where the time goes:
time: 179 us; the launch traced here: 178 us
  matrix products  66.5 us (37%)
  waiting for transfers between devices  29.1 us (16%)
  local copies, waits for them, and re-layouts  27.9 us (16%)
  blocking collectives  20.3 us (11%)
  between operations  16.4 us (9%)
  other arithmetic  9.41 us (5%)
  starting transfers between devices  8.4 us (5%)
    dot_general x3, matrix products, block_product(): return jnp.dot(left_rows, right_matrix, preferred_element_type=jnp.float32)  55.4 us
    all_gather x1, waiting for transfers between devices, body(): lax.all_gather(conv_out_weight, ('fsdp', 'seq'), axis=1, tiled=True)  20.7 us
    concatenate x1, local copies, waits for them, and re-layouts, extended(): x = jnp.concatenate([before, x, after], axis=dim)  18.7 us
    psum x1, blocking collectives, body(): numerator = lax.psum(jnp.sum(frame_error), 'seq')  10.5 us
    psum x1, blocking collectives, body(): frame_error = lax.psum(frame_err, 'seed') / jnp.float32(seed_count)  9.85 us
    dot_general x1, matrix products, body(): jnp.dot(blocks, stem_matrix[:half_width], preferred_element_type=jnp.floa...  5.77 us
    ppermute x1, waiting for transfers between devices, extended(): after = lax.ppermute(first, axis, down)  5.71 us
    ppermute x1, starting transfers between devices, extended(): before = lax.ppermute(last, axis, up)  5.52 us
  transfers between devices with their start and end apart: 6, of which 3 were waited for; matrix products, arithmetic and copies ran while one was open for 52% of the time, Pallas kernels for 0%

commit v1 on v0

--- a/solution.py
+++ b/solution.py
@@ -1,7 +1,429 @@
 import jax
 import jax.numpy as jnp
 from jax import lax
+from jax.experimental import pallas as pl
+from jax.experimental.pallas import tpu as pltpu
 from jax.sharding import PartitionSpec as P
+
+LANES = 128
+EDGE = 16
+VMEM_BYTES = 56 * 1024 * 1024
+
+
+def norm_rows(values, gain_row):
+    row_mean = jnp.mean(values, axis=-1, keepdims=True)
+    centred = values - row_mean
+    row_var = jnp.mean(centred * centred, axis=-1, keepdims=True)
+    return (centred * lax.rsqrt(row_var + 1e-05) * gain_row).astype(jnp.bfloat16)
+
+
+def stem_kernel(meta, pairs_ref, stem_ref, gain_ref, stem_out_ref, normed_ref):
+    slot = pl.program_id(0)
+    rows = pairs_ref.shape[1]
+    part = rows // 2
+
+    @pl.when(meta[8 + slot] > 0)
+    def _():
+        for at in (0, part):
+            here = slice(at, at + part)
+            stem_out = jnp.dot(
+                pairs_ref[0, here, :], stem_ref[...], preferred_element_type=jnp.float32
+            ).astype(jnp.bfloat16)
+            stem_out_ref[0, here, :] = stem_out
+            normed_ref[0, here, :] = norm_rows(stem_out.astype(jnp.float32), gain_ref[0:1, :])
+
+
+def conv_kernel(
+    meta,
+    normed_ref,
+    taps_ref,
+    own_ref,
+    near_ref,
+    hub_ref,
+    far_ref,
+    mate_own_ref,
+    mate_rest_ref,
+    swished_ref,
+    weight,
+    gated_a,
+    gated_b,
+    convolved,
+    sems,
+):
+    slot = pl.program_id(0)
+    rows = normed_ref.shape[1]
+    frames = swished_ref.shape[1]
+    channels = swished_ref.shape[2]
+    tap_count = taps_ref.shape[0]
+    piece = own_ref.shape[0]
+    side = meta[16]
+
+    @pl.when(jnp.logical_and(slot == 0, meta[17] > 0))
+    def _():
+        copies = []
+        for i, (ref, first, other) in enumerate(
+            (
+                (own_ref, 0, 0),
+                (near_ref, 0, 0),
+                (hub_ref, 0, 0),
+                (far_ref, 0, 0),
+                (mate_own_ref, 0, 1),
+                (mate_rest_ref, 0, 1),
+                (mate_rest_ref, piece, 1),
+                (mate_rest_ref, 2 * piece, 1),
+            )
+        ):
+            core = 1 - side if other else side
+            block = core * 4 + meta[12 + i % 4]
+            copies.append(
+                pltpu.make_async_copy(
+                    ref.at[pl.ds(first, piece)],
+                    weight.at[pl.ds(pl.multiple_of(block * piece, 16), piece)],
+                    sems.at[i],
+                )
+            )
+        for copy in copies:
+            copy.start()
+        for copy in copies:
+            copy.wait()
+
+    @pl.when(meta[8 + slot] > 0)
+    def _():
+        at = meta[slot] - EDGE + lax.broadcasted_iota(jnp.int32, (rows, 1), 0)
+        live = jnp.logical_and(at >= 0, at < meta[4 + slot]).astype(jnp.float32)
+        stride = frames // 8
+        run = 16
+        buffers = (gated_a, gated_b)
+
+        def gate(block, into):
+            low = block * LANES
+            right = jnp.concatenate(
+                [weight[:, low : low + LANES], weight[:, channels + low : channels + low + LANES]], axis=1
+            )
+            mixed = jnp.dot(normed_ref[0], right, preferred_element_type=jnp.float32)
+            gated = mixed[:, :LANES] * jax.nn.sigmoid(mixed[:, LANES:]) * live
+            into[...] = gated.astype(jnp.bfloat16).astype(jnp.float32)
+
+        def convolve(block, source):
+            low = block * LANES
+            for start in range(0, stride, run):
+                sums = [None] * run
+                for row in range(start, start + run + tap_count - 1):
+                    value = source[pl.ds(row + EDGE - tap_count // 2, 8, stride=stride), :]
+                    for m in range(max(start, row - tap_count + 1), min(start + run, row + 1)):
+                        term = value * taps_ref[row - m, :, low : low + LANES]
+                        k = m - start
+                        sums[k] = term if sums[k] is None else sums[k] + term
+                for k in range(run):
+                    total = sums[k]
+                    convolved[pl.ds(start + k, 8, stride=stride), :] = total * jax.nn.sigmoid(total)
+            swished_ref[0, :, low : low + LANES] = convolved[...].astype(jnp.bfloat16)
+
+        blocks = channels // LANES
+        gate(0, buffers[0])
+        for block in range(blocks):
+            if block + 1 < blocks:
+                gate(block + 1, buffers[(block + 1) % 2])
+            convolve(block, buffers[block % 2])
+
+
+def head_kernel(
+    meta,
+    swished_ref,
+    stem_out_ref,
+    code_ref,
+    gain_ref,
+    own_ref,
+    near_ref,
+    hub_ref,
+    far_ref,
+    mate_own_ref,
+    mate_rest_ref,
+    error_ref,
+    back,
+    head,
+    sems,
+):
+    slot = pl.program_id(0)
+    frames = swished_ref.shape[1]
+    vocab = head.shape[1]
+    groups = back.shape[1] // vocab
+    piece = own_ref.shape[0]
+    back_rows = back.shape[0] // 8
+    head_rows = head.shape[0] // 8
+    group_rows = head_rows // groups
+    side = meta[16]
+
+    @pl.when(jnp.logical_and(slot == 0, meta[17] > 0))
+    def _():
+        copies = []
+        for i, (ref, first, other) in enumerate(
+            (
+                (own_ref, 0, 0),
+                (near_ref, 0, 0),
+                (hub_ref, 0, 0),
+                (far_ref, 0, 0),
+                (mate_own_ref, 0, 1),
+                (mate_rest_ref, 0, 1),
+                (mate_rest_ref, piece, 1),
+                (mate_rest_ref, 2 * piece, 1),
+            )
+        ):
+            core = 1 - side if other else side
+            block = core * 4 + meta[12 + i % 4]
+            copies.append(
+                pltpu.make_async_copy(
+                    ref.at[pl.ds(first, back_rows)],
+                    back.at[pl.ds(pl.multiple_of(block * back_rows, 16), back_rows)],
+                    sems.at[i, 0],
+                )
+            )
+            for g in range(groups):
+                copies.append(
+                    pltpu.make_async_copy(
+                        ref.at[pl.ds(first + back_rows, group_rows), pl.ds(g * vocab, vocab)],
+                        head.at[pl.ds(pl.multiple_of(block * head_rows + g * group_rows, 16), group_rows)],
+                        sems.at[i, 1 + g],
+                    )
+                )
+        for copy in copies:
+            copy.start()
+        for copy in copies:
+            copy.wait()
+
+    @pl.when(meta[8 + slot] <= 0)
+    def _():
+        error_ref[...] = jnp.zeros_like(error_ref)
+
+    @pl.when(meta[8 + slot] > 0)
+    def _():
+        part = 256
+        diagonal = lax.broadcasted_iota(jnp.int32, (LANES, LANES), 0) == lax.broadcasted_iota(
+            jnp.int32, (LANES, LANES), 1
+        )
+        for at in range(0, frames, part):
+            here = slice(at, at + part)
+            after = jnp.dot(swished_ref[0, here, :], back[...], preferred_element_type=jnp.float32)
+            after = after + stem_out_ref[0, EDGE + at : EDGE + at + part, :].astype(jnp.float32)
+            normed = norm_rows(after, gain_ref[1:2, :])
+            logits = jnp.dot(normed, head[...], preferred_element_type=jnp.float32)
+            top = jnp.max(logits, axis=-1, keepdims=True)
+            grown = jnp.exp(logits - top)
+            posterior = grown / jnp.sum(grown, axis=-1, keepdims=True)
+            code = code_ref[0, here, :]
+            onehot = (lax.broadcasted_iota(jnp.int32, (part, vocab), 1) == code).astype(jnp.float32)
+            differ = posterior - onehot
+            error = jnp.sqrt(jnp.sum(differ * differ, axis=-1, keepdims=True))
+            error = jnp.where(code >= 0, error, 0.0)
+            for row in range(0, part, LANES):
+                column = error[row : row + LANES, :]
+                error_ref[0, :, at + row : at + row + LANES] = jnp.sum(
+                    jnp.where(diagonal, column, 0.0), axis=0, keepdims=True
+                )
+
+
+def call(kernel, grid, in_specs, out_specs, out_shape, scratch, flops, moved, operands):
+    return pl.pallas_call(
+        kernel,
+        grid_spec=pltpu.PrefetchScalarGridSpec(
+            num_scalar_prefetch=1,
+            grid=grid,
+            in_specs=in_specs,
+            out_specs=out_specs,
+            scratch_shapes=scratch,
+        ),
+        out_shape=out_shape,
+        compiler_params=pltpu.CompilerParams(
+            dimension_semantics=("arbitrary",), vmem_limit_bytes=VMEM_BYTES
+        ),
+        cost_estimate=pl.CostEstimate(flops=flops, bytes_accessed=moved, transcendentals=0),
+    )(*operands)
+
+
+def whole(shape):
+    return pl.BlockSpec(shape, lambda i, meta: (0,) * len(shape))
+
+
+def by_slot(shape):
+    return pl.BlockSpec((1,) + shape, lambda i, meta: (i,) + (0,) * len(shape))
+
+
+OUTWARD = [(0, 1), (3, 2)]
+ACROSS = [(1, 2), (2, 1)]
+BEYOND = [(0, 2), (3, 1)]
+SWAP = [(0, 1), (1, 0)]
+
+
+def to_hub(x, pairs):
+    return lax.ppermute(x, "seq", pairs)
+
+
+def to_mate(x):
+    pairs = [(a * 4 + z, b * 4 + z) for a, b in SWAP for z in (1, 2)]
+    return lax.ppermute(x, ("fsdp", "seq"), pairs)
+
+
+def hub_body(
+    mel_frames,
+    lengths,
+    targets,
+    frame_mask,
+    stem_weight,
+    conv_in_weight,
+    conv_out_weight,
+    depth_weight,
+    head_weight,
+    norm_gain,
+):
+    chip = lax.axis_index("seq")
+    side = lax.axis_index("fsdp")
+    seed = lax.axis_index("seed")
+    seeds = lax.axis_size("seed")
+    rows = targets.shape[1]
+    width = stem_weight.shape[2]
+    channels = depth_weight.shape[2]
+    vocab = head_weight.shape[2]
+    tile = rows // 2
+    low = chip == 1
+    is_hub = jnp.logical_or(low, chip == 2)
+
+    first = conv_in_weight[0]
+    groups = width // vocab
+    head_rows = head_weight.shape[1]
+    second = jnp.concatenate(
+        [
+            conv_out_weight[0],
+            jnp.concatenate(jnp.split(head_weight[0], groups, axis=0), axis=1),
+        ],
+        axis=0,
+    )
+    first_in = [to_hub(first, pairs) for pairs in (OUTWARD, ACROSS, BEYOND)]
+    first_mate = to_mate(first)
+    second_mate = to_mate(second)
+
+    blocks = mel_frames[0].reshape(rows, -1)
+    share = rows // seeds
+    quarter = lax.dynamic_slice_in_dim(blocks, seed * share, share, 0)
+    outer = lax.all_gather(to_hub(quarter, OUTWARD), "seed", axis=0, tiled=True)
+    edge = to_hub(jnp.where(low, blocks[-EDGE:], blocks[:EDGE]), ACROSS)
+    none = jnp.zeros_like(edge)
+    frames = jnp.concatenate(
+        [
+            jnp.where(low, none, edge),
+            jnp.where(low, outer, blocks),
+            jnp.where(low, blocks, outer),
+            jnp.where(low, edge, none),
+            none,
+        ],
+        axis=0,
+    )
+    reach = tile + 3 * EDGE
+    tiles = [frames[k * tile : k * tile + reach] for k in range(4)]
+    mine = jnp.stack([tiles[0], tiles[2]])
+    lent = to_mate(jnp.stack([tiles[1], tiles[3]]))
+    held = jnp.concatenate([mine, lent], axis=0)
+    deep = tile + 2 * EDGE
+    pairs = jnp.concatenate([held[:, :deep], held[:, 1 : deep + 1]], axis=2)
+
+    length = lengths[0]
+    positions = chip * rows + jnp.arange(rows, dtype=jnp.int32)
+    counted = jnp.logical_and(frame_mask[0] > 0, positions < length)
+    code = jnp.where(counted, targets[0], -1)
+    outer_code = to_hub(code, OUTWARD)
+    codes = jnp.concatenate(
+        [jnp.where(low, outer_code, code), jnp.where(low, code, outer_code)]
+    ).reshape(4, tile)
+    lent_ints = to_mate(jnp.concatenate([codes[1], codes[3], lengths]))
+    code_slots = jnp.stack([codes[0], codes[2], lent_ints[:tile], lent_ints[tile : 2 * tile]])
+    mate_length = lent_ints[2 * tile]
+
+    base = (chip - 1) * 2 * rows
+    starts = base + tile * jnp.array([0, 2, 1, 3], jnp.int32)
+    spans = jnp.stack([length, length, mate_length, mate_length])
+    alive = jnp.logical_and(is_hub, starts < spans).astype(jnp.int32)
+    hub = jnp.clip(chip, 1, 2)
+    meta = jnp.concatenate(
+        [
+            starts,
+            spans,
+            alive,
+            jnp.stack([hub, 3 * (hub - 1), 3 - hub, 3 * (2 - hub)]),
+            jnp.stack([side, jnp.max(alive)]),
+        ]
+    ).astype(jnp.int32)
+
+    slots = 4
+    gains = norm_gain[0]
+    stem_out, normed = call(
+        stem_kernel,
+        (slots,),
+        [by_slot((deep, pairs.shape[2])), whole(stem_weight.shape[1:]), whole(gains.shape)],
+        [by_slot((deep, width))] * 2,
+        [jax.ShapeDtypeStruct((slots, deep, width), jnp.bfloat16)] * 2,
+        [],
+        2 * slots * deep * pairs.shape[2] * width,
+        slots * deep * (pairs.shape[2] + 2 * width) * 2,
+        (meta, pairs, stem_weight[0], gains),
+    )
+
+    first_rest = to_mate(jnp.concatenate(first_in, axis=0))
+    second_held, _ = lax.optimization_barrier((second, first_in))
+    second_in = [to_hub(second_held, pairs_) for pairs_ in (OUTWARD, ACROSS, BEYOND)]
+
+    taps = jnp.broadcast_to(
+        depth_weight[0].astype(jnp.float32)[:, None, :], (depth_weight.shape[1], 8, channels)
+    )
+    apart = pl.BlockSpec(memory_space=pl.ANY)
+    swished = call(
+        conv_kernel,
+        (slots,),
+        [by_slot((deep, width)), whole(taps.shape)] + [apart] * 6,
+        by_slot((tile, channels)),
+        jax.ShapeDtypeStruct((slots, tile, channels), jnp.bfloat16),
+        [
+            pltpu.VMEM((8 * first.shape[0], first.shape[1]), jnp.bfloat16),
+            pltpu.VMEM((deep, LANES), jnp.float32),
+            pltpu.VMEM((deep, LANES), jnp.float32),
+            pltpu.VMEM((tile, LANES), jnp.float32),
+            pltpu.SemaphoreType.DMA((8,)),
+        ],
+        2 * slots * deep * width * 2 * channels,
+        slots * deep * width * 2 + 8 * first.size * 2,
+        (meta, normed, taps, first, *first_in, first_mate, first_rest),
+    )
+
+    second_rest = to_mate(jnp.concatenate(second_in, axis=0))
+    errors = call(
+        head_kernel,
+        (slots,),
+        [by_slot((tile, channels)), by_slot((deep, width)), by_slot((tile, 1)), whole(gains.shape)] + [apart] * 6,
+        by_slot((1, tile)),
+        jax.ShapeDtypeStruct((slots, 1, tile), jnp.float32),
+        [
+            pltpu.VMEM((8 * conv_out_weight.shape[1], width), jnp.bfloat16),
+            pltpu.VMEM((8 * head_rows, vocab), jnp.bfloat16),
+            pltpu.SemaphoreType.DMA((8, 1 + groups)),
+        ],
+        2 * slots * tile * (channels + vocab) * width,
+        slots * tile * (channels + width) * 2,
+        (meta, swished, stem_out, code_slots[:, :, None], gains, second, *second_in, second_mate, second_rest),
+    )
+
+    errors = errors.reshape(2, 2, tile)
+    zero = jnp.zeros_like(errors[0])
+    own_part = jnp.stack([errors[0], zero], axis=1)
+    lent_part = jnp.stack([zero, errors[1]], axis=1)
+    by_utt = jnp.stack(
+        [jnp.where(side == 0, own_part, lent_part), jnp.where(side == 0, lent_part, own_part)]
+    )
+    by_hub = jnp.stack(
+        [jnp.where(low, by_utt, 0.0), jnp.where(chip == 2, by_utt, 0.0)], axis=1
+    ).reshape(2, 4 * rows)
+    total = lax.psum(by_hub, ("seed", "fsdp", "seq")) / jnp.float32(seeds)
+    mine_total = lax.dynamic_index_in_dim(total, side, 0, keepdims=True)
+    frame_error = lax.dynamic_slice_in_dim(mine_total, chip * rows, rows, 1)
+    utt_score = jnp.sum(mine_total) / length.astype(jnp.float32)
+    return (frame_error, utt_score.reshape(1))
 
 
 def from_behind(x, axis, by):
@@ -126,4 +548,7 @@
         P("seed", None, None),
     )
     out_specs = (P("fsdp", "seq"), P("fsdp"))
-    return jax.shard_map(body, mesh=mesh, in_specs=in_specs, out_specs=out_specs, check_vma=False)
+    hubs = mesh.shape["seq"] == 4 and mesh.shape["fsdp"] == 2
+    return jax.shard_map(
+        hub_body if hubs else body, mesh=mesh, in_specs=in_specs, out_specs=out_specs, check_vma=False
+    )

time: 179 us -> 221 us (1.23)
  blocking collectives: 20.3 us -> 102 us
  matrix products: 66.5 us -> 0 us
  starting transfers between devices: 8.4 us -> 41.6 us
  Pallas kernels: 0 us -> 20.3 us
  local copies, waits for them, and re-layouts: 27.9 us -> 14.7 us
  between operations: 16.4 us -> 3.46 us
  waiting for transfers between devices: 29.1 us -> 25.6 us
  other arithmetic: 9.41 us -> 12.2 us
    psum x2 -> x1, blocking collectives: 20.3 us -> 90.1 us  [hub_body(): total = lax.psum(by_hub, ('seed', 'fsdp', 'seq')) / jnp.float32(seeds)]
    dot_general x5 -> x0, matrix products: 66.5 us -> none  [the longest x3 55.4 us: block_product(): return jnp.dot(left_rows, right_matrix, preferred_element_type=jnp.float32)]
    ppermute x3 -> x15, starting transfers between devices: 8.29 us -> 41.6 us  [the longest x9 35.1 us: to_hub(): return lax.ppermute(x, 'seq', pairs)]
    all_gather x3 -> x0, waiting for transfers between devices: 20.7 us -> none  [the longest x1 20.7 us: body(): lax.all_gather(conv_out_weight, ('fsdp', 'seq'), axis=1, tiled=True)]
    pallas_call x0 -> x3, Pallas kernels: none -> 20.3 us  [call(): pl.pallas_call(kernel, grid_spec=pltpu.PrefetchScalarGridSpec(num_scalar_...]
    ppermute x3 -> x15, waiting for transfers between devices: 6.94 us -> 25.6 us  [the longest x9 25.6 us: to_hub(): return lax.ppermute(x, 'seq', pairs)]
    concatenate x1, local copies, waits for them, and re-layouts: 18.7 us -> 2.53 us  [hub_body(): jnp.concatenate([starts, spans, alive, jnp.stack([hub, 3 * (hub - 1), 3 -...]
    all_gather x0 -> x1, blocking collectives: none -> 12.1 us  [hub_body(): outer = lax.all_gather(to_hub(quarter, OUTWARD), 'seed', axis=0, tiled=True)]
  transfers between devices with their start and end apart: 6 -> 15, of which waited for: 3 -> 4; matrix products, arithmetic and copies ran while one was open for 52% -> 10% of each run, Pallas kernels for 0% -> 6%
where the time goes in v1:
time: 221 us; the launch traced here: 220 us
  blocking collectives  102 us (46%)
  starting transfers between devices  41.6 us (19%)
  waiting for transfers between devices  25.6 us (12%)
  Pallas kernels  20.3 us (9%)
  local copies, waits for them, and re-layouts  14.7 us (7%)
  other arithmetic  12.2 us (6%)
  between operations  3.46 us (2%)
    psum x1, blocking collectives, hub_body(): total = lax.psum(by_hub, ('seed', 'fsdp', 'seq')) / jnp.float32(seeds)  90.1 us
    ppermute x9, starting transfers between devices, to_hub(): return lax.ppermute(x, 'seq', pairs)  35.1 us
    ppermute x9, waiting for transfers between devices, to_hub(): return lax.ppermute(x, 'seq', pairs)  25.6 us
    pallas_call x3, Pallas kernels, call(): pl.pallas_call(kernel, grid_spec=pltpu.PrefetchScalarGridSpec(num_scalar_...  20.3 us
    all_gather x1, blocking collectives, hub_body(): outer = lax.all_gather(to_hub(quarter, OUTWARD), 'seed', axis=0, tiled=True)  12.1 us
    ppermute x6, starting transfers between devices, to_mate(): return lax.ppermute(x, ('fsdp', 'seq'), pairs)  6.51 us
  transfers between devices with their start and end apart: 15, of which 4 were waited for; matrix products, arithmetic and copies ran while one was open for 10% of the time, Pallas kernels for 6%

profile of v1, /device:TPU:0, one launch (start us, length us, event | category | flops | bytes accessed | tf_op | source)
XLA Modules:
  0.0 220.1 jit_solution(15539211128513993711)
XLA Ops:
  0.6 5.7 %collective-permute-start.5 = (bf16[192,1536]{1,0:T(8,128)(2,1)}, bf16[192,1536]{1,0:T(8,128)(2,1)}, u32[]{:S(2)}, u32[]{:S(2)}) collective-permute-start(bf16[192,1536]{1,0:T(8,128)(2,1)} %bitcast.49), channel_id=1, source_target_pairs={{0,1},{3,2},{4,5},{7,6},{8,9},{11,10},{12,13},{15,14},{16,17},{19,... | collective-permute-start | bytes 1769480 | tf_op jit(solution)/shard_map/ppermute | solution.py:258
  6.4 1.5 collective-permute-start.6
  7.8 3.2 %collective-permute-start.7 = (bf16[192,1536]{1,0:T(8,128)(2,1)}, bf16[192,1536]{1,0:T(8,128)(2,1)}, u32[]{:S(2)}, u32[]{:S(2)}) collective-permute-start(bf16[192,1536]{1,0:T(8,128)(2,1)} %bitcast.51), channel_id=1, source_target_pairs={{0,2},{3,1},{4,6},{7,5},{8,10},{11,9},{12,14},{15,13},{16,18},{19,... | collective-permute-start | bytes 1769480 | tf_op jit(solution)/shard_map/ppermute | solution.py:258
  11.1 1.5 collective-permute-start.8
  13.2 0.7 compare_reduce_fusion
  14.0 0.7 fusion.6
  14.6 1.3 collective-permute-start
  15.9 0.0 copy-start.5
  16.0 0.0 copy-start.4
  16.0 0.0 copy-start.3
  16.0 1.6 copy.19
  17.6 0.7 reshape_squeeze.3
  18.3 0.8 slice_select_fusion
  19.1 0.6 bitcast_convert_fusion
  19.8 0.8 maximum_maximum_fusion.own_ref
  20.7 0.1 copy.18
  20.8 0.1 select_n.112
  20.8 10.3 %collective-permute-done = s32[1024]{0:T(1024)S(1)} collective-permute-done((s32[1024]{0:T(1024)S(1)}, s32[1024]{0:T(1024)S(1)}, u32[]{:S(2)}, u32[]{:S(2)}) %collective-permute-start) | collective-permute-done | bytes 4128 | tf_op jit(solution)/shard_map/ppermute | solution.py:258
  31.2 0.7 collective-permute-start.2
  31.9 0.0 collective-permute-done.2
  31.9 9.2 %collective-permute-start.3 = (bf16[256,320]{1,0:T(8,128)(2,1)S(1)}, bf16[256,320]{1,0:T(8,128)(2,1)S(1)}, u32[]{:S(2)}, u32[]{:S(2)}) collective-permute-start(bf16[256,320]{1,0:T(8,128)(2,1)S(1)} %constant_dynamic-slice_fusion), channel_id=1, source_target_pairs={{0,1},{3,2},{4,5},{7,6},{8,9},{11,10},{12,13},{15,14},{16,17},{19,... | collective-permute-start | bytes 491528 | tf_op jit(solution)/shard_map/ppermute | solution.py:258
  41.1 3.1 %collective-permute-done.3 = bf16[256,320]{1,0:T(8,128)(2,1)S(1)} collective-permute-done((bf16[256,320]{1,0:T(8,128)(2,1)S(1)}, bf16[256,320]{1,0:T(8,128)(2,1)S(1)}, u32[]{:S(2)}, u32[]{:S(2)}) %collective-permute-start.3) | collective-permute-done | bytes 163872 | tf_op jit(solution)/shard_map/ppermute | solution.py:258
  44.3 0.6 collective-permute-start.1
  44.9 12.1 %all_gather.3 = bf16[1024,320]{1,0:T(8,128)(2,1)S(1)} all-gather(bf16[256,320]{1,0:T(8,128)(2,1)S(1)} %collective-permute-done.3), channel_id=1, replica_groups=mesh['seed'=4,'fsdp'=2,'seq'=4] {'seed'}, dimensions={0}, use_global_device_ids=true | all-gather | bytes 819200 | tf_op jit(solution)/shard_map/all_gather | solution.py:307
  57.0 0.1 broadcast_select_fusion.1
  57.2 0.2 maximum_bitcast_fusion
  57.4 0.2 pad_maximum_fusion.4
  57.6 1.3 copy.20
  58.8 0.8 collective-permute-start.4
  59.7 0.0 collective-permute-done.6.hub_ref
  59.7 1.5 pad_maximum_fusion.1
  61.2 1.9 collective-permute-start.9
  63.1 0.0 collective-permute-done.1
  63.2 1.4 copy.22.code_ref
  64.5 0.5 slice.93
  65.0 1.3 fusion.7
  66.4 2.5 %concatenate.52.meta = s32[18]{0:T(128)} concatenate(s32[4]{0:T(128)S(1)} %get-tuple-element.37, s32[1]{0:T(128)} %copy.23, s32[1]{0:T(128)} %copy.23, s32[1]{0:T(128)} %slice.93, s32[1]{0:T(128)} %slice.93, s32[4]{0:T(128)S(1)} %get-tuple-element.9, s32[1]{0:T(128)} %bitcast.2, s32[1]{0:T(128)} %bitcast.3, s32[1]{0:T(128)} %bitcast.4, s32[1]{0:T(128)} %bitcast.5, s32[1]{0:T(128)} %bitcast.6, ...), dimensions={0} | concatenate | bytes 144 | tf_op jit(solution)/shard_map/concatenate | solution.py:345
  68.9 8.9 %collective-permute-start.10 = (bf16[160,1536]{1,0:T(8,128)(2,1)}, bf16[160,1536]{1,0:T(8,128)(2,1)}, u32[]{:S(2)}, u32[]{:S(2)}) collective-permute-start(bf16[160,1536]{1,0:T(8,128)(2,1)} %maximum_maximum_fusion.own_ref), channel_id=1, source_target_pairs={{0,1},{3,2},{4,5},{7,6},{8,9},{11,10},{12,13},{15,14},{16,17},{19,... | collective-permute-start | bytes 1474568 | tf_op jit(solution)/shard_map/ppermute | solution.py:258
  77.8 1.4 collective-permute-start.11
  79.2 0.0 collective-permute-done.4
  79.2 0.9 copy-done
  80.1 3.2 %collective-permute-start.12 = (bf16[160,1536]{1,0:T(8,128)(2,1)}, bf16[160,1536]{1,0:T(8,128)(2,1)}, u32[]{:S(2)}, u32[]{:S(2)}) collective-permute-start(bf16[160,1536]{1,0:T(8,128)(2,1)} %maximum_maximum_fusion.own_ref), channel_id=1, source_target_pairs={{0,2},{3,1},{4,6},{7,5},{8,10},{11,9},{12,14},{15,13},{16,18},{19,... | collective-permute-start | bytes 1474568 | tf_op jit(solution)/shard_map/ppermute | solution.py:258
  83.3 1.5 copy.21
  84.8 0.3 pad_maximum_fusion.2
  85.2 0.5 fusion.8
  85.7 3.1 %collective-permute-done.10.near_ref = bf16[160,1536]{1,0:T(8,128)(2,1)} collective-permute-done((bf16[160,1536]{1,0:T(8,128)(2,1)}, bf16[160,1536]{1,0:T(8,128)(2,1)}, u32[]{:S(2)}, u32[]{:S(2)}) %collective-permute-start.10) | collective-permute-done | bytes 491552 | tf_op jit(solution)/shard_map/ppermute | solution.py:258
  88.9 0.7 collective-permute-start.13
  89.6 0.0 collective-permute-done.11.hub_ref
  89.6 8.9 %collective-permute-done.12.far_ref = bf16[160,1536]{1,0:T(8,128)(2,1)} collective-permute-done((bf16[160,1536]{1,0:T(8,128)(2,1)}, bf16[160,1536]{1,0:T(8,128)(2,1)}, u32[]{:S(2)}, u32[]{:S(2)}) %collective-permute-start.12) | collective-permute-done | bytes 491552 | tf_op jit(solution)/shard_map/ppermute | solution.py:258
  98.5 1.4 pad_maximum_fusion.3
  99.9 0.9 collective-permute-start.14
  100.9 2.6 %pad_maximum_fusion.pairs_ref = bf16[4,544,640]{2,1,0:T(8,128)(2,1)} fusion(bf16[4,544,320]{2,1,0:T(8,128)(2,1)S(1)} %get-tuple-element.11, bf16[4,544,320]{2,1,0:T(8,128)(2,1)S(1)} %get-tuple-element.10), kind=kLoop, calls=%fused_computation | loop fusion | flops 5570560 | bytes 5570560 | tf_op jit(solution)/shard_map/concatenate | solution.py:326
  103.5 7.7 %shard_map.122 = (bf16[4,544,1536]{2,1,0:T(8,128)(2,1)}, bf16[4,544,1536]{2,1,0:T(8,128)(2,1)}) custom-call(s32[18]{0:T(128)} %concatenate.52.meta, bf16[4,544,640]{2,1,0:T(8,128)(2,1)} %pad_maximum_fusion.pairs_ref, bf16[640,1536]{1,0:T(8,128)(2,1)} %bitcast.48, f32[2,1536]{1,0:T(2,128)} %bitcast.54), custom_call_target="tpu_custom_call" | custom-call | flops 4278190080 | bytes 16154624 | tf_op jit(solution)/shard_map/pallas_call | solution.py:226
  111.2 0.9 broadcast_in_dim.23.taps_ref
  112.2 5.8 %shard_map.123.swished_ref = bf16[4,512,768]{2,1,0:T(8,128)(2,1)} custom-call(s32[18]{0:T(128)} %concatenate.52.meta, bf16[4,544,1536]{2,1,0:T(8,128)(2,1)} %get-tuple-element.5.normed_ref, f32[31,8,768]{2,1,0:T(8,128)} %broadcast_in_dim.23.taps_ref, bf16[192,1536]{1,0:T(8,128)(2,1)} %bitcast.53, bf16[192,1536]{1,0:T(8,128)(2,1)} %collective-permute-done.5.near_ref, ...), custom_call_target="tpu_custom_call" | custom-call | flops 10267656192 | bytes 11403264 | tf_op jit(solution)/shard_map/pallas_call | solution.py:226
  118.0 0.0 collective-permute-done.13.mate_own_ref
  118.0 0.0 collective-permute-done.14.mate_rest_ref
  118.0 0.8 copy-done.8
  118.8 0.5 copy-done.7
  119.3 6.7 %shard_map.124 = f32[4,1,512]{2,1,0:T(1,128)} custom-call(s32[18]{0:T(128)} %concatenate.52.meta, bf16[4,512,768]{2,1,0:T(8,128)(2,1)} %shard_map.123.swished_ref, bf16[4,544,1536]{2,1,0:T(8,128)(2,1)} %get-tuple-element.6.stem_out_ref, s32[4,512,1]{2,1,0:T(8,128)} %copy.22.code_ref, f32[2,1536]{1,0:T(2,128)} %bitcast.55, ...), custom_call_target="tpu_custom_call" | custom-call | flops 8053063680 | bytes 9437184 | tf_op jit(solution)/shard_map/pallas_call | solution.py:226
  126.0 0.7 fusion.9
  126.8 90.1 %psum.7 = f32[2,4096]{1,0:T(2,128)S(1)} all-reduce(f32[2,4096]{1,0:T(2,128)S(1)} %reshape.100), channel_id=1, replica_groups=mesh['seed'=4,'fsdp'=2,'seq'=4] {'seed','fsdp','seq'}, use_global_device_ids=true, to_apply=%region_1.2 | all-reduce | flops 8192 | bytes 65536 | tf_op jit(solution)/shard_map/psum | solution.py:422
  217.0 0.6 dynamic-slice_reduce_fusion
  218.3 0.7 dynamic_slice.11
  (30 shorter events, 0.2 us)
Async XLA Ops:
  0.6 58.2 %collective-permute-start.5 = (bf16[192,1536]{1,0:T(8,128)(2,1)}, bf16[192,1536]{1,0:T(8,128)(2,1)}, u32[]{:S(2)}, u32[]{:S(2)}) collective-permute-start(bf16[192,1536]{1,0:T(8,128)(2,1)} %bitcast.49), channel_id=1, source_target_pairs={{0,1},{3,2},{4,5},{7,6},{8,9},{11,10},{12,13},{15,14},{16,17},{19,... | collective-permute-start | bytes 1769480 | tf_op jit(solution)/shard_map/ppermute | solution.py:258
  6.4 53.3 %collective-permute-start.6 = (bf16[192,1536]{1,0:T(8,128)(2,1)}, bf16[192,1536]{1,0:T(8,128)(2,1)}, u32[]{:S(2)}, u32[]{:S(2)}) collective-permute-start(bf16[192,1536]{1,0:T(8,128)(2,1)} %bitcast.50), channel_id=1, source_target_pairs={{1,2},{2,1},{5,6},{6,5},{9,10},{10,9},{13,14},{14,13},{17,18},{18,... | collective-permute-start | bytes 1769480 | tf_op jit(solution)/shard_map/ppermute | solution.py:258
  7.8 51.8 %collective-permute-start.7 = (bf16[192,1536]{1,0:T(8,128)(2,1)}, bf16[192,1536]{1,0:T(8,128)(2,1)}, u32[]{:S(2)}, u32[]{:S(2)}) collective-permute-start(bf16[192,1536]{1,0:T(8,128)(2,1)} %bitcast.51), channel_id=1, source_target_pairs={{0,2},{3,1},{4,6},{7,5},{8,10},{11,9},{12,14},{15,13},{16,18},{19,... | collective-permute-start | bytes 1769480 | tf_op jit(solution)/shard_map/ppermute | solution.py:258
  11.1 100.2 %collective-permute-start.8 = (bf16[192,1536]{1,0:T(8,128)(2,1)}, bf16[192,1536]{1,0:T(8,128)(2,1)}, u32[]{:S(2)}, u32[]{:S(2)}) collective-permute-start(bf16[192,1536]{1,0:T(8,128)(2,1)} %bitcast.52), channel_id=1, source_target_pairs={{1,5},{2,6},{5,1},{6,2},{9,13},{10,14},{13,9},{14,10},{17,21},{18,... | collective-permute-start | bytes 1769480 | tf_op jit(solution)/shard_map/ppermute | solution.py:263
  14.6 16.5 %collective-permute-start = (s32[1024]{0:T(1024)S(1)}, s32[1024]{0:T(1024)S(1)}, u32[]{:S(2)}, u32[]{:S(2)}) collective-permute-start(s32[1024]{0:T(1024)S(1)} %fusion.6), channel_id=1, source_target_pairs={{0,1},{3,2},{4,5},{7,6},{8,9},{11,10},{12,13},{15,14},{16,17},{19,... | collective-permute-start | bytes 12296 | tf_op jit(solution)/shard_map/ppermute | solution.py:258
  15.9 3.2 %copy-start.5 = (bf16[1,31,768]{2,1,0:T(8,128)(2,1)S(1)}, bf16[1,31,768]{2,1,0:T(8,128)(2,1)}, u32[]{:S(2)}) copy-start(bf16[1,31,768]{2,1,0:T(8,128)(2,1)} %param.18) | copy-start | bytes 142852
  16.0 3.8 %copy-start.4 = (bf16[1,192,512]{2,1,0:T(8,128)(2,1)S(1)}, bf16[1,192,512]{2,1,0:T(8,128)(2,1)}, u32[]{:S(2)}) copy-start(bf16[1,192,512]{2,1,0:T(8,128)(2,1)} %param.19) | copy-start | bytes 589828
  16.0 3.8 %copy-start.3 = (bf16[1,96,1536]{2,1,0:T(8,128)(2,1)S(1)}, bf16[1,96,1536]{2,1,0:T(8,128)(2,1)}, u32[]{:S(2)}) copy-start(bf16[1,96,1536]{2,1,0:T(8,128)(2,1)} %param.17) | copy-start | bytes 884740
  31.2 0.7 collective-permute-start.2
  31.9 12.4 %collective-permute-start.3 = (bf16[256,320]{1,0:T(8,128)(2,1)S(1)}, bf16[256,320]{1,0:T(8,128)(2,1)S(1)}, u32[]{:S(2)}, u32[]{:S(2)}) collective-permute-start(bf16[256,320]{1,0:T(8,128)(2,1)S(1)} %constant_dynamic-slice_fusion), channel_id=1, source_target_pairs={{0,1},{3,2},{4,5},{7,6},{8,9},{11,10},{12,13},{15,14},{16,17},{19,... | collective-permute-start | bytes 491528 | tf_op jit(solution)/shard_map/ppermute | solution.py:258
  44.3 18.9 %collective-permute-start.1 = (s32[1025]{0:T(1024)S(1)}, s32[1025]{0:T(1024)S(1)}, u32[]{:S(2)}, u32[]{:S(2)}) collective-permute-start(s32[1025]{0:T(1024)S(1)} %pad_add_fusion), channel_id=1, source_target_pairs={{1,5},{2,6},{5,1},{6,2},{9,13},{10,14},{13,9},{14,10},{17,21},{18,... | collective-permute-start | bytes 12308 | tf_op jit(solution)/shard_map/ppermute | solution.py:263
  58.8 6.2 %copy-start.6 = (s32[4]{0:T(128)S(1)}, s32[4]{0:T(128)}, u32[]{:S(2)}) copy-start(s32[4]{0:T(128)} %constant.77) | copy-start | bytes 52
  58.8 20.4 %collective-permute-start.4 = (bf16[2,560,320]{1,2,0:T(8,128)(2,1)}, bf16[2,560,320]{1,2,0:T(8,128)(2,1)S(1)}, u32[]{:S(2)}, u32[]{:S(2)}) collective-permute-start(bf16[2,560,320]{1,2,0:T(8,128)(2,1)} %copy.20), channel_id=1, source_target_pairs={{1,5},{2,6},{5,1},{6,2},{9,13},{10,14},{13,9},{14,10},{17,21},{18,... | collective-permute-start | bytes 2150408 | tf_op jit(solution)/shard_map/ppermute | solution.py:263
  61.2 50.0 %collective-permute-start.9 = (bf16[576,1536]{1,0:T(8,128)(2,1)S(1)}, bf16[576,1536]{1,0:T(8,128)(2,1)}, u32[]{:S(2)}, u32[]{:S(2)}) collective-permute-start(bf16[576,1536]{1,0:T(8,128)(2,1)S(1)} %pad_maximum_fusion.1), channel_id=1, source_target_pairs={{1,5},{2,6},{5,1},{6,2},{9,13},{10,14},{13,9},{14,10},{17,21},{18,... | collective-permute-start | bytes 5308424 | tf_op jit(solution)/shard_map/ppermute | solution.py:263
  68.9 20.0 %collective-permute-start.10 = (bf16[160,1536]{1,0:T(8,128)(2,1)}, bf16[160,1536]{1,0:T(8,128)(2,1)}, u32[]{:S(2)}, u32[]{:S(2)}) collective-permute-start(bf16[160,1536]{1,0:T(8,128)(2,1)} %maximum_maximum_fusion.own_ref), channel_id=1, source_target_pairs={{0,1},{3,2},{4,5},{7,6},{8,9},{11,10},{12,13},{15,14},{16,17},{19,... | collective-permute-start | bytes 1474568 | tf_op jit(solution)/shard_map/ppermute | solution.py:258
  77.8 11.8 %collective-permute-start.11 = (bf16[160,1536]{1,0:T(8,128)(2,1)}, bf16[160,1536]{1,0:T(8,128)(2,1)}, u32[]{:S(2)}, u32[]{:S(2)}) collective-permute-start(bf16[160,1536]{1,0:T(8,128)(2,1)} %maximum_maximum_fusion.own_ref), channel_id=1, source_target_pairs={{1,2},{2,1},{5,6},{6,5},{9,10},{10,9},{13,14},{14,13},{17,18},{18,... | collective-permute-start | bytes 1474568 | tf_op jit(solution)/shard_map/ppermute | solution.py:258
  79.2 0.9 copy-start
  80.1 18.4 %collective-permute-start.12 = (bf16[160,1536]{1,0:T(8,128)(2,1)}, bf16[160,1536]{1,0:T(8,128)(2,1)}, u32[]{:S(2)}, u32[]{:S(2)}) collective-permute-start(bf16[160,1536]{1,0:T(8,128)(2,1)} %maximum_maximum_fusion.own_ref), channel_id=1, source_target_pairs={{0,2},{3,1},{4,6},{7,5},{8,10},{11,9},{12,14},{15,13},{16,18},{19,... | collective-permute-start | bytes 1474568 | tf_op jit(solution)/shard_map/ppermute | solution.py:258
  85.2 3.7 %copy-start.1 = (bf16[160,1536]{1,0:T(8,128)(2,1)S(1)}, bf16[160,1536]{1,0:T(8,128)(2,1)}, u32[]{:S(2)}) copy-start(bf16[160,1536]{1,0:T(8,128)(2,1)} %maximum_maximum_fusion.own_ref) | copy-start | bytes 1474564
  88.9 29.1 %collective-permute-start.13 = (bf16[160,1536]{1,0:T(8,128)(2,1)S(1)}, bf16[160,1536]{1,0:T(8,128)(2,1)S(1)}, u32[]{:S(2)}, u32[]{:S(2)}) collective-permute-start(bf16[160,1536]{1,0:T(8,128)(2,1)S(1)} %copy-done.1), channel_id=1, source_target_pairs={{1,5},{2,6},{5,1},{6,2},{9,13},{10,14},{13,9},{14,10},{17,21},{18,... | collective-permute-start | bytes 1474568 | tf_op jit(solution)/shard_map/ppermute | solution.py:263
  99.9 18.1 %collective-permute-start.14 = (bf16[480,1536]{1,0:T(8,128)(2,1)S(1)}, bf16[480,1536]{1,0:T(8,128)(2,1)S(1)}, u32[]{:S(2)}, u32[]{:S(2)}) collective-permute-start(bf16[480,1536]{1,0:T(8,128)(2,1)S(1)} %pad_maximum_fusion.3), channel_id=1, source_target_pairs={{1,5},{2,6},{5,1},{6,2},{9,13},{10,14},{13,9},{14,10},{17,21},{18,... | collective-permute-start | bytes 4423688 | tf_op jit(solution)/shard_map/ppermute | solution.py:263
  103.5 7.7 %copy-start.2 = (f32[31,768]{1,0:T(8,128)S(1)}, f32[31,768]{1,0:T(8,128)}, u32[]{:S(2)}) copy-start(f32[31,768]{1,0:T(8,128)} %bitcast_convert_fusion) | copy-start | bytes 285700
  118.0 0.8 copy-start.8
  118.0 1.3 copy-start.7

commit v2 on v0

--- a/solution.py
+++ b/solution.py
@@ -1,7 +1,423 @@
+import functools
+
 import jax
 import jax.numpy as jnp
 from jax import lax
+from jax.experimental import pallas as pl
+from jax.experimental.pallas import tpu as pltpu
 from jax.sharding import PartitionSpec as P
+
+LANES = 128
+CHUNKS = 8
+EDGE = 16
+VMEM_BYTES = 56 * 1024 * 1024
+
+
+def norm_rows(values, gain_row):
+    row_mean = jnp.mean(values, axis=-1, keepdims=True)
+    centred = values - row_mean
+    row_var = jnp.mean(centred * centred, axis=-1, keepdims=True)
+    return (centred * lax.rsqrt(row_var + 1e-05) * gain_row).astype(jnp.bfloat16)
+
+
+def sigmoid(x):
+    return 0.5 * jnp.tanh(0.5 * x) + 0.5
+
+
+def stem_kernel(meta, pairs_ref, stem_ref, gain_ref, stem_out_ref, normed_ref):
+    slot = pl.program_id(0)
+    rows = pairs_ref.shape[1]
+    part = rows // 2
+
+    @pl.when(meta[5 + slot] > 0)
+    def _():
+        parts = (slice(0, part), slice(part, rows))
+        made = [
+            jnp.dot(pairs_ref[0, here, :], stem_ref[...], preferred_element_type=jnp.float32).astype(jnp.bfloat16)
+            for here in parts
+        ]
+        for here, stem_out in zip(parts, made):
+            stem_out_ref[0, here, :] = stem_out
+            normed_ref[0, here, :] = norm_rows(stem_out.astype(jnp.float32), gain_ref[0:1, :])
+
+
+def shards(meta, pieces):
+    side = meta[13]
+    length = pieces[0].shape[0]
+    mine = [(pieces[i], 0, side * 4 + meta[9 + i]) for i in range(4)]
+    return mine + [(pieces[4], i * length, (1 - side) * 4 + meta[9 + i]) for i in range(4)]
+
+
+def conv_kernel(first_slot, meta, normed_ref, taps_ref, *rest):
+    pieces = rest[:5]
+    swished_ref, weight, gated_a, gated_b, margin, mask, sems = rest[-7:]
+    slot = pl.program_id(0) + first_slot
+    rows = normed_ref.shape[1]
+    frames = swished_ref.shape[1]
+    channels = swished_ref.shape[2]
+    tap_count = taps_ref.shape[0]
+    reach = tap_count // 2
+    piece = pieces[0].shape[0]
+    run_length = frames // CHUNKS
+
+    @pl.when(jnp.logical_and(pl.program_id(0) == 0, meta[14] > 0))
+    def _():
+        copies = [
+            pltpu.make_async_copy(
+                ref.at[pl.ds(at, piece)], weight.at[pl.ds(pl.multiple_of(block * piece, 16), piece)], sems.at[i]
+            )
+            for i, (ref, at, block) in enumerate(shards(meta, pieces))
+        ]
+        for copy in copies:
+            copy.start()
+        for copy in copies:
+            copy.wait()
+
+    @pl.when(meta[5 + slot] > 0)
+    def _():
+        row = lax.broadcasted_iota(jnp.int32, (rows, LANES), 0)
+        inner = (row % CHUNKS) * run_length + row // CHUNKS
+        outer = jnp.where(row < frames + EDGE, row - frames - EDGE, row - EDGE)
+        at = meta[slot] + jnp.where(row < frames, inner, outer)
+        mask[...] = jnp.logical_and(at >= 0, at < meta[4]).astype(jnp.float32)
+        sublane = lax.broadcasted_iota(jnp.int32, (CHUNKS, LANES), 0)
+        buffers = (gated_a, gated_b)
+
+        def gate(block, into):
+            low = block * LANES
+            right = jnp.concatenate(
+                [weight[:, low : low + LANES], weight[:, channels + low : channels + low + LANES]], axis=1
+            )
+            mixed = jnp.dot(normed_ref[0], right, preferred_element_type=jnp.float32)
+            gated = mixed[:, :LANES] * sigmoid(mixed[:, LANES:]) * mask[...]
+            gated = gated.astype(jnp.bfloat16).astype(jnp.float32)
+            into[reach : reach + run_length] = gated[:frames].reshape(run_length, CHUNKS, LANES)
+            margin[...] = gated[frames:]
+            for i in range(reach):
+                before = pltpu.roll(into[run_length + i], 1, 0)
+                edge = margin[EDGE - reach + i : EDGE - reach + i + 1, :]
+                into[i] = jnp.where(sublane == 0, edge, before)
+                after = pltpu.roll(into[reach + i], CHUNKS - 1, 0)
+                edge = margin[EDGE + i : EDGE + i + 1, :]
+                into[reach + run_length + i] = jnp.where(sublane == CHUNKS - 1, edge, after)
+
+        def convolve(block, source):
+            low = block * LANES
+            run = 16
+            for start in range(0, run_length, run):
+                sums = [None] * run
+                for at in range(start, start + run + tap_count - 1):
+                    value = source[at]
+                    for m in range(max(start, at - tap_count + 1), min(start + run, at + 1)):
+                        term = value * taps_ref[at - m, :, low : low + LANES]
+                        k = m - start
+                        sums[k] = term if sums[k] is None else sums[k] + term
+                for k in range(0, run, 2):
+                    total = jnp.concatenate(sums[k : k + 2], axis=0)
+                    first = (start + k) * CHUNKS
+                    swished_ref[0, first : first + 2 * CHUNKS, low : low + LANES] = (
+                        total * sigmoid(total)
+                    ).astype(jnp.bfloat16)
+
+        blocks = channels // LANES
+        gate(0, buffers[0])
+        for block in range(blocks):
+            if block + 1 < blocks:
+                gate(block + 1, buffers[(block + 1) % 2])
+            convolve(block, buffers[block % 2])
+
+
+def head_kernel(meta, swished_ref, stem_out_ref, code_ref, gain_ref, *rest):
+    pieces = rest[:5]
+    error_ref, back, head, sems = rest[5:]
+    slot = pl.program_id(0)
+    frames = swished_ref.shape[1]
+    vocab = head.shape[1]
+    groups = back.shape[1] // vocab
+    back_rows = back.shape[0] // 8
+    head_rows = head.shape[0] // 8
+    group_rows = head_rows // groups
+
+    @pl.when(jnp.logical_and(pl.program_id(0) == 0, meta[14] > 0))
+    def _():
+        copies = []
+        for i, (ref, at, block) in enumerate(shards(meta, pieces)):
+            copies.append(
+                pltpu.make_async_copy(
+                    ref.at[pl.ds(at, back_rows)],
+                    back.at[pl.ds(pl.multiple_of(block * back_rows, 16), back_rows)],
+                    sems.at[i, 0],
+                )
+            )
+            for g in range(groups):
+                copies.append(
+                    pltpu.make_async_copy(
+                        ref.at[pl.ds(at + back_rows, group_rows), pl.ds(g * vocab, vocab)],
+                        head.at[pl.ds(pl.multiple_of(block * head_rows + g * group_rows, 16), group_rows)],
+                        sems.at[i, 1 + g],
+                    )
+                )
+        for copy in copies:
+            copy.start()
+        for copy in copies:
+            copy.wait()
+
+    @pl.when(meta[5 + slot] <= 0)
+    def _():
+        error_ref[...] = jnp.zeros_like(error_ref)
+
+    @pl.when(meta[5 + slot] > 0)
+    def _():
+        part = 256
+        lane = lax.broadcasted_iota(jnp.int32, (CHUNKS, LANES), 1)
+        starts = range(0, frames, part)
+        after = [
+            jnp.dot(swished_ref[0, at : at + part, :], back[...], preferred_element_type=jnp.float32)
+            for at in starts
+        ]
+        logits = []
+        for at, values in zip(starts, after):
+            values = values + stem_out_ref[0, at : at + part, :].astype(jnp.float32)
+            normed = norm_rows(values, gain_ref[1:2, :])
+            logits.append(jnp.dot(normed, head[...], preferred_element_type=jnp.float32))
+        row = jnp.zeros((CHUNKS, LANES), jnp.float32)
+        for at, scores in zip(starts, logits):
+            top = jnp.max(scores, axis=-1, keepdims=True)
+            grown = jnp.exp(scores - top)
+            posterior = grown * (1.0 / jnp.sum(grown, axis=-1, keepdims=True))
+            code = code_ref[0, at : at + part, :]
+            onehot = (lax.broadcasted_iota(jnp.int32, (part, vocab), 1) == code).astype(jnp.float32)
+            differ = posterior - onehot
+            error = jnp.sqrt(jnp.sum(differ * differ, axis=-1, keepdims=True))
+            error = jnp.where(code >= 0, error, 0.0)
+            for m in range(part // CHUNKS):
+                step = error[m * CHUNKS : (m + 1) * CHUNKS, :]
+                row = row + jnp.where(lane == at // CHUNKS + m, step, 0.0)
+        error_ref[0] = row
+
+
+def call(kernel, grid, in_specs, out_specs, out_shape, scratch, flops, moved, operands, aliases={}):
+    return pl.pallas_call(
+        kernel,
+        grid_spec=pltpu.PrefetchScalarGridSpec(
+            num_scalar_prefetch=1,
+            grid=grid,
+            in_specs=in_specs,
+            out_specs=out_specs,
+            scratch_shapes=scratch,
+        ),
+        out_shape=out_shape,
+        input_output_aliases=aliases,
+        compiler_params=pltpu.CompilerParams(
+            dimension_semantics=("arbitrary",), vmem_limit_bytes=VMEM_BYTES
+        ),
+        cost_estimate=pl.CostEstimate(flops=flops // 16, bytes_accessed=moved // 16, transcendentals=0),
+    )(*operands)
+
+
+def whole(shape):
+    return pl.BlockSpec(shape, lambda i, meta: (0,) * len(shape))
+
+
+def by_slot(shape, first=0):
+    return pl.BlockSpec((1,) + shape, lambda i, meta: (i + first,) + (0,) * len(shape))
+
+
+INWARD = [(0, 1), (3, 2)]
+ACROSS = [(1, 2), (2, 1)]
+BEYOND = [(0, 2), (3, 1)]
+OUTWARD = [(1, 0), (2, 3)]
+OUT_BEYOND = [(2, 0), (1, 3)]
+
+
+def along(x, pairs):
+    return lax.ppermute(x, "seq", pairs)
+
+
+def to_mate(x):
+    pairs = [(a * 4 + z, (1 - a) * 4 + z) for a in (0, 1) for z in (1, 2)]
+    return lax.ppermute(x, ("fsdp", "seq"), pairs)
+
+
+def seed_swap(x, bit):
+    return lax.ppermute(x, "seed", [(i, i ^ bit) for i in range(4)])
+
+
+def hub_body(
+    mel_frames,
+    lengths,
+    targets,
+    frame_mask,
+    stem_weight,
+    conv_in_weight,
+    conv_out_weight,
+    depth_weight,
+    head_weight,
+    norm_gain,
+):
+    chip = lax.axis_index("seq")
+    side = lax.axis_index("fsdp")
+    seed = lax.axis_index("seed")
+    seeds = lax.axis_size("seed")
+    rows = targets.shape[1]
+    width = stem_weight.shape[2]
+    channels = depth_weight.shape[2]
+    vocab = head_weight.shape[2]
+    step = mel_frames.shape[1] // rows
+    tile = rows // 2
+    low = chip == 1
+    is_hub = jnp.logical_or(low, chip == 2)
+
+    first = conv_in_weight[0]
+    hub_first = along(first, ACROSS)
+    share = rows // seeds
+    quarter = lax.dynamic_slice_in_dim(mel_frames[0], seed * share * step, share * step, 0).reshape(share, -1)
+    quarter_in = along(quarter, INWARD)
+    margin = step * EDGE
+    edge = along(jnp.where(low, mel_frames[0, -margin:], mel_frames[0, :margin]).reshape(EDGE, -1), ACROSS)
+    first_held, _ = lax.optimization_barrier((first, quarter_in))
+    near_first = along(first_held, INWARD)
+    far_first = along(first_held, BEYOND)
+
+    pair = seed_swap(quarter_in, 1)
+    odd = seed % 2 == 1
+    half = jnp.concatenate([jnp.where(odd, pair, quarter_in), jnp.where(odd, quarter_in, pair)], axis=0)
+    other = seed_swap(half, 2)
+    upper = seed // 2 == 1
+
+    groups = width // vocab
+    head_rows = head_weight.shape[1]
+    second = jnp.concatenate(
+        [
+            conv_out_weight[0],
+            jnp.concatenate(jnp.split(head_weight[0], groups, axis=0), axis=1),
+        ],
+        axis=0,
+    )
+    second_held, other, edge, hub_first = lax.optimization_barrier((second, other, edge, hub_first))
+    near_second = along(second_held, INWARD)
+    far_second = along(second_held, BEYOND)
+    hub_second = along(second_held, ACROSS)
+    outer = jnp.concatenate([jnp.where(upper, other, half), jnp.where(upper, half, other)], axis=0)
+
+    blocks = mel_frames[0].reshape(rows, -1)
+    none = jnp.zeros_like(edge)
+    frames = jnp.concatenate(
+        [
+            jnp.where(low, none, edge),
+            jnp.where(low, outer, blocks),
+            jnp.where(low, blocks, outer),
+            jnp.where(low, edge, none),
+            none,
+        ],
+        axis=0,
+    )
+    slots = 4
+    deep = tile + 2 * EDGE
+    pairs = jnp.concatenate([frames[:-1], frames[1:]], axis=1)
+    inner = pairs[EDGE : EDGE + slots * tile].reshape(slots, CHUNKS, tile // CHUNKS, -1)
+    inner = inner.transpose(0, 2, 1, 3).reshape(slots, tile, -1)
+    before = jnp.stack([pairs[k * tile : k * tile + EDGE] for k in range(slots)])
+    after = jnp.stack([pairs[(k + 1) * tile + EDGE : (k + 1) * tile + 2 * EDGE] for k in range(slots)])
+    pairs = jnp.concatenate([inner, before, after], axis=1)
+
+    length = lengths[0]
+    positions = chip * rows + jnp.arange(rows, dtype=jnp.int32)
+    counted = jnp.logical_and(frame_mask[0] > 0, positions < length)
+    code = jnp.where(counted, targets[0], -1)
+    starts = (chip - 1) * 2 * rows + tile * jnp.arange(slots, dtype=jnp.int32)
+    alive = jnp.logical_and(is_hub, starts < length).astype(jnp.int32)
+    hub = jnp.clip(chip, 1, 2)
+    meta = jnp.concatenate(
+        [
+            starts,
+            lengths,
+            alive,
+            jnp.stack([hub, 3 * (hub - 1), 3 - hub, 3 * (2 - hub), side, jnp.max(alive)]),
+        ]
+    ).astype(jnp.int32)
+
+    gains = norm_gain[0]
+    stem_out, normed = call(
+        stem_kernel,
+        (slots,),
+        [by_slot((deep, pairs.shape[2])), whole(stem_weight.shape[1:]), whole(gains.shape)],
+        [by_slot((deep, width))] * 2,
+        [jax.ShapeDtypeStruct((slots, deep, width), jnp.bfloat16)] * 2,
+        [],
+        2 * slots * deep * pairs.shape[2] * width,
+        slots * deep * (pairs.shape[2] + 2 * width) * 2,
+        (meta, pairs, stem_weight[0], gains),
+    )
+
+    near_first, far_first, normed = lax.optimization_barrier((near_first, far_first, normed))
+    mine = [first, near_first, hub_first, far_first]
+    first_pieces = (*mine, to_mate(jnp.concatenate(mine, axis=0)))
+    code_held, _ = lax.optimization_barrier((code, first_pieces[-1]))
+    outer_code = along(code_held, INWARD)
+    codes = jnp.concatenate([jnp.where(low, outer_code, code), jnp.where(low, code, outer_code)])
+    codes = codes.reshape(slots, CHUNKS, tile // CHUNKS).transpose(0, 2, 1).reshape(slots, tile, 1)
+
+    taps = jnp.broadcast_to(
+        depth_weight[0].astype(jnp.float32)[:, None, :], (depth_weight.shape[1], CHUNKS, channels)
+    )
+    apart = pl.BlockSpec(memory_space=pl.ANY)
+    extent = tile // CHUNKS + depth_weight.shape[1] - 1
+    def convolve(part, normed, pieces, *made):
+        return call(
+            functools.partial(conv_kernel, 2 * part),
+            (2,),
+            [by_slot((deep, width), 2 * part), whole(taps.shape)] + [apart] * (5 + len(made)),
+            by_slot((tile, channels), 2 * part),
+            jax.ShapeDtypeStruct((slots, tile, channels), jnp.bfloat16),
+            [
+                pltpu.VMEM((8 * first.shape[0], first.shape[1]), jnp.bfloat16),
+                pltpu.VMEM((extent, CHUNKS, LANES), jnp.float32),
+                pltpu.VMEM((extent, CHUNKS, LANES), jnp.float32),
+                pltpu.VMEM((2 * EDGE, LANES), jnp.float32),
+                pltpu.VMEM((deep, LANES), jnp.float32),
+                pltpu.SemaphoreType.DMA((8,)),
+            ],
+            slots * deep * width * 2 * channels,
+            slots * deep * width + 8 * first.size * 2,
+            (meta, normed, taps, *pieces, *made),
+            {8: 0} if made else {},
+        )
+
+    swished = convolve(0, normed, first_pieces)
+    near_second, hub_second, far_second, swished = lax.optimization_barrier(
+        (near_second, hub_second, far_second, swished)
+    )
+    mine = [second, near_second, hub_second, far_second]
+    second_pieces = (*mine, to_mate(jnp.concatenate(mine, axis=0)))
+    swished = convolve(1, normed, first_pieces, swished)
+    errors = call(
+        head_kernel,
+        (slots,),
+        [by_slot((tile, channels)), by_slot((deep, width)), by_slot((tile, 1)), whole(gains.shape)] + [apart] * 5,
+        by_slot((CHUNKS, LANES)),
+        jax.ShapeDtypeStruct((slots, CHUNKS, LANES), jnp.float32),
+        [
+            pltpu.VMEM((8 * conv_out_weight.shape[1], width), jnp.bfloat16),
+            pltpu.VMEM((8 * head_rows, vocab), jnp.bfloat16),
+            pltpu.SemaphoreType.DMA((8, 1 + groups)),
+        ],
+        2 * slots * tile * (channels + vocab) * width,
+        slots * tile * (channels + width) * 2,
+        (meta, swished, stem_out, codes, gains, *second_pieces),
+    )
+
+    one, two, three = [seed_swap(errors, bit) for bit in (1, 2, 3)]
+    total = ((errors + one) + (two + three)) / jnp.float32(seeds)
+    total = total[:, :, : tile // CHUNKS].reshape(2, rows)
+    part = jnp.sum(total).reshape(1)
+    outer_half = jnp.where(low, total[0], total[1])
+    own_half = jnp.where(low, total[1], total[0])
+    from_hub = along(jnp.concatenate([outer_half, part]), OUTWARD)
+    parts = [part[0], along(part, ACROSS)[0], along(part, OUT_BEYOND)[0], from_hub[rows]]
+    frame_error = jnp.where(is_hub, own_half, from_hub[:rows])
+    utt_score = ((parts[0] + parts[3]) + (parts[1] + parts[2])) / length.astype(jnp.float32)
+    return (frame_error[None, :], utt_score.reshape(1))
 
 
 def from_behind(x, axis, by):
@@ -126,4 +542,7 @@
         P("seed", None, None),
     )
     out_specs = (P("fsdp", "seq"), P("fsdp"))
-    return jax.shard_map(body, mesh=mesh, in_specs=in_specs, out_specs=out_specs, check_vma=False)
+    hubs = mesh.shape["seq"] == 4 and mesh.shape["fsdp"] == 2
+    return jax.shard_map(
+        hub_body if hubs else body, mesh=mesh, in_specs=in_specs, out_specs=out_specs, check_vma=False
+    )

time: 179 us -> 154 us (0.86)
  matrix products: 66.5 us -> 0 us
  starting transfers between devices: 8.4 us -> 43.9 us
  Pallas kernels: 0 us -> 21.8 us
  waiting for transfers between devices: 29.1 us -> 50 us
  blocking collectives: 20.3 us -> 0 us
  between operations: 16.4 us -> 5.67 us
  local copies, waits for them, and re-layouts: 27.9 us -> 17.7 us
  other arithmetic: 9.41 us -> 14.3 us
    dot_general x5 -> x0, matrix products: 66.5 us -> none  [the longest x3 55.4 us: block_product(): return jnp.dot(left_rows, right_matrix, preferred_element_type=jnp.float32)]
    ppermute x3 -> x19, waiting for transfers between devices: 6.94 us -> 50 us  [the longest x12 44.5 us: along(): return lax.ppermute(x, 'seq', pairs)]
    ppermute x3 -> x19, starting transfers between devices: 8.29 us -> 43.9 us  [the longest x12 35.6 us: along(): return lax.ppermute(x, 'seq', pairs)]
    pallas_call x0 -> x4, Pallas kernels: none -> 21.8 us  [call(): pl.pallas_call(kernel, grid_spec=pltpu.PrefetchScalarGridSpec(num_scalar_...]
    all_gather x3 -> x0, waiting for transfers between devices: 20.7 us -> none  [the longest x1 20.7 us: body(): lax.all_gather(conv_out_weight, ('fsdp', 'seq'), axis=1, tiled=True)]
    psum x2 -> x0, blocking collectives: 20.3 us -> none  [the longest x1 10.5 us: body(): numerator = lax.psum(jnp.sum(frame_error), 'seq')]
    concatenate x1 -> x5, local copies, waits for them, and re-layouts: 18.7 us -> 2.78 us  [the longest x1 1.82 us: hub_body(): jnp.concatenate([starts, lengths, alive, jnp.stack([hub, 3 * (hub - 1), 3...]
    concatenate x0 -> x6, other arithmetic: none -> 7.63 us  [the longest x1 4.24 us: hub_body(): pairs = jnp.concatenate([inner, before, after], axis=1)]
  transfers between devices with their start and end apart: 6 -> 19, of which waited for: 3 -> 8; matrix products, arithmetic and copies ran while one was open for 52% -> 15% of each run, Pallas kernels for 0% -> 10%
where the time goes in v2:
time: 154 us; the launch traced here: 153 us
  waiting for transfers between devices  50 us (32%)
  starting transfers between devices  43.9 us (29%)
  Pallas kernels  21.8 us (14%)
  local copies, waits for them, and re-layouts  17.7 us (11%)
  other arithmetic  14.3 us (9%)
  between operations  5.67 us (4%)
    ppermute x12, waiting for transfers between devices, along(): return lax.ppermute(x, 'seq', pairs)  44.5 us
    ppermute x12, starting transfers between devices, along(): return lax.ppermute(x, 'seq', pairs)  35.6 us
    pallas_call x4, Pallas kernels, call(): pl.pallas_call(kernel, grid_spec=pltpu.PrefetchScalarGridSpec(num_scalar_...  21.8 us
    ppermute x5, starting transfers between devices, seed_swap(): return lax.ppermute(x, 'seed', [(i, i ^ bit) for i in range(4)])  6.56 us
    unnamed x46, local copies, waits for them, and re-layouts  6.08 us
    ppermute x5, waiting for transfers between devices, seed_swap(): return lax.ppermute(x, 'seed', [(i, i ^ bit) for i in range(4)])  5.53 us
    concatenate x1, other arithmetic, hub_body(): pairs = jnp.concatenate([inner, before, after], axis=1)  4.24 us
  transfers between devices with their start and end apart: 19, of which 8 were waited for; matrix products, arithmetic and copies ran while one was open for 15% of the time, Pallas kernels for 10%

profile of v2, /device:TPU:0, one launch (start us, length us, event | category | flops | bytes accessed | tf_op | source)
XLA Modules:
  0.0 153.3 jit_solution(15159593651596526659)
XLA Ops:
  0.6 1.0 constant_dynamic-slice_fusion
  1.8 0.2 reshape.54
  2.0 4.9 %collective-permute-start = (bf16[256,320]{1,0:T(8,128)(2,1)S(1)}, bf16[256,320]{1,0:T(8,128)(2,1)S(1)}, u32[]{:S(2)}, u32[]{:S(2)}) collective-permute-start(bf16[256,320]{1,0:T(8,128)(2,1)S(1)} %reshape.54), channel_id=1, source_target_pairs={{0,1},{3,2},{4,5},{7,6},{8,9},{11,10},{12,13},{15,14},{16,17},{19,... | collective-permute-start | bytes 491528 | tf_op jit(solution)/shard_map/ppermute | solution.py:234
  7.0 0.8 slice_select_fusion
  7.9 0.7 select_n.124
  8.6 0.7 collective-permute-start.5
  9.2 0.7 collective-permute-start.6
  9.9 1.1 collective-permute-done
  11.1 1.5 collective-permute-start.3
  12.6 0.9 slice_bitcast_fusion.2
  14.2 0.5 multiply_add_fusion
  14.7 2.1 %collective-permute-done.3 = bf16[256,320]{1,0:T(8,128)(2,1)S(1)} collective-permute-done((bf16[256,320]{1,0:T(8,128)(2,1)S(1)}, bf16[256,320]{1,0:T(8,128)(2,1)S(1)}, u32[]{:S(2)}, u32[]{:S(2)}) %collective-permute-start.3) | collective-permute-done | bytes 163872 | tf_op jit(solution)/shard_map/ppermute | solution.py:243
  16.9 0.8 pad_maximum_fusion.2
  17.7 1.5 collective-permute-start.4
  19.2 0.8 maximum_maximum_fusion.1.rest_0_
  20.0 0.6 fusion.18
  20.7 1.5 %copy.19 = bf16[1,4096,80]{2,1,0:T(8,128)(2,1)S(1)} copy(bf16[1,4096,80]{1,2,0:T(8,128)(2,1)} %param.10) | data formatting | bytes 1310720 | tf_op args[0]
  22.3 0.7 reshape_squeeze.3
  23.0 1.8 %concatenate.42.meta = s32[15]{0:T(128)} concatenate(s32[4]{0:T(128)} %multiply_add_fusion, s32[1]{0:T(128)} %copy.34, s32[4]{0:T(128)S(1)} %get-tuple-element.33, s32[1]{0:T(128)} %bitcast.1, s32[1]{0:T(128)} %bitcast.2, s32[1]{0:T(128)} %bitcast.3, s32[1]{0:T(128)} %bitcast.4, s32[1]{0:T(128)} %bitcast.5, s32[1]{0:T(128)} %bitcast.6), dimensions={0} | concatenate | bytes 120 | tf_op jit(solution)/shard_map/concatenate | solution.py:331
  24.8 5.0 %collective-permute-start.1 = (bf16[192,1536]{1,0:T(8,128)(2,1)S(1)}, bf16[192,1536]{1,0:T(8,128)(2,1)S(1)}, u32[]{:S(2)}, u32[]{:S(2)}) collective-permute-start(bf16[192,1536]{1,0:T(8,128)(2,1)S(1)} %bitcast.59), channel_id=1, source_target_pairs={{0,1},{3,2},{4,5},{7,6},{8,9},{11,10},{12,13},{15,14},{16,17},{19,... | collective-permute-start | bytes 1769480 | tf_op jit(solution)/shard_map/ppermute | solution.py:234
  29.9 2.3 %collective-permute-start.2 = (bf16[192,1536]{1,0:T(8,128)(2,1)S(1)}, bf16[192,1536]{1,0:T(8,128)(2,1)S(1)}, u32[]{:S(2)}, u32[]{:S(2)}) collective-permute-start(bf16[192,1536]{1,0:T(8,128)(2,1)S(1)} %bitcast.60), channel_id=1, source_target_pairs={{0,2},{3,1},{4,6},{7,5},{8,10},{11,9},{12,14},{15,13},{16,18},{19,... | collective-permute-start | bytes 1769480 | tf_op jit(solution)/shard_map/ppermute | solution.py:234
  32.2 1.3 broadcast_select_fusion.1
  33.6 0.3 select_dynamic-update-slice_fusion.1
  33.8 0.3 select_dynamic-update-slice_fusion
  34.1 0.5 fusion.19
  34.8 1.0 fusion
  35.8 1.5 copy.24
  37.3 4.2 %maximum_maximum_fusion.pairs_ref = bf16[4,544,640]{2,1,0:T(8,128)(2,1)} fusion(bf16[1,16,640]{2,1,0:T(8,128)(2,1)S(1)} %get-tuple-element.40, bf16[1,16,640]{2,1,0:T(8,128)(2,1)S(1)} %get-tuple-element.41, bf16[1,16,640]{2,1,0:T(8,128)(2,1)S(1)} %get-tuple-element.39, bf16[1,16,640]{2,1,0:T(8,128)(2,1)S(1)} %get-tuple-element.38, ...), kind=kLoop, calls=%fused_computation.16 | loop fusion | flops 25067520 | bytes 5570560 | tf_op jit(solution)/shard_map/concatenate | solution.py:322
  41.5 7.7 %shard_map.113 = (bf16[4,544,1536]{2,1,0:T(8,128)(2,1)}, bf16[4,544,1536]{2,1,0:T(8,128)(2,1)}) custom-call(s32[15]{0:T(128)} %concatenate.42.meta, bf16[4,544,640]{2,1,0:T(8,128)(2,1)} %maximum_maximum_fusion.pairs_ref, bf16[640,1536]{1,0:T(8,128)(2,1)} %bitcast.62, f32[2,1536]{1,0:T(2,128)} %bitcast.64), custom_call_target="tpu_custom_call" | custom-call | flops 267386880 | bytes 1009664 | tf_op jit(solution)/shard_map/pallas_call | solution.py:200
  49.2 4.0 %collective-permute-done.2.rest_3_ = bf16[192,1536]{1,0:T(8,128)(2,1)S(1)} collective-permute-done((bf16[192,1536]{1,0:T(8,128)(2,1)S(1)}, bf16[192,1536]{1,0:T(8,128)(2,1)S(1)}, u32[]{:S(2)}, u32[]{:S(2)}) %collective-permute-start.2) | collective-permute-done | bytes 589856 | tf_op jit(solution)/shard_map/ppermute | solution.py:234
  53.5 0.9 collective-permute-start.7
  54.4 6.5 %collective-permute-start.8 = (bf16[160,1536]{1,0:T(8,128)(2,1)S(1)}, bf16[160,1536]{1,0:T(8,128)(2,1)S(1)}, u32[]{:S(2)}, u32[]{:S(2)}) collective-permute-start(bf16[160,1536]{1,0:T(8,128)(2,1)S(1)} %copy-done.6), channel_id=1, source_target_pairs={{0,1},{3,2},{4,5},{7,6},{8,9},{11,10},{12,13},{15,14},{16,17},{19,... | collective-permute-start | bytes 1474568 | tf_op jit(solution)/shard_map/ppermute | solution.py:234
  61.0 0.7 collective-permute-start.9
  61.7 4.2 %collective-permute-start.10 = (bf16[160,1536]{1,0:T(8,128)(2,1)S(1)}, bf16[160,1536]{1,0:T(8,128)(2,1)S(1)}, u32[]{:S(2)}, u32[]{:S(2)}) collective-permute-start(bf16[160,1536]{1,0:T(8,128)(2,1)S(1)} %copy-done.6), channel_id=1, source_target_pairs={{0,2},{3,1},{4,6},{7,5},{8,10},{11,9},{12,14},{15,13},{16,18},{19,... | collective-permute-start | bytes 1474568 | tf_op jit(solution)/shard_map/ppermute | solution.py:234
  65.8 0.7 constant_dynamic-update-slice_fusion.6
  66.6 0.7 maximum_dynamic-update-slice_fusion
  67.3 1.0 broadcast_in_dim.17.taps_ref
  68.3 0.7 copy-done
  69.0 3.8 %shard_map.114.rest_5_ = bf16[4,512,768]{2,1,0:T(8,128)(2,1)} custom-call(s32[15]{0:T(128)} %concatenate.42.meta, bf16[4,544,1536]{2,1,0:T(8,128)(2,1)} %get-tuple-element.21.normed_ref, f32[31,8,768]{2,1,0:T(8,128)} %broadcast_in_dim.17.taps_ref, bf16[192,1536]{1,0:T(8,128)(2,1)} %bitcast.57, bf16[192,1536]{1,0:T(8,128)(2,1)} %copy-done.3, ...), custom_call_target="tpu_custom_call" | custom-call | flops 320864256 | bytes 503808 | tf_op jit(solution)/shard_map/pallas_call | solution.py:200
  72.9 9.8 %collective-permute-done.10.rest_3_ = bf16[160,1536]{1,0:T(8,128)(2,1)S(1)} collective-permute-done((bf16[160,1536]{1,0:T(8,128)(2,1)S(1)}, bf16[160,1536]{1,0:T(8,128)(2,1)S(1)}, u32[]{:S(2)}, u32[]{:S(2)}) %collective-permute-start.10) | collective-permute-done | bytes 491552 | tf_op jit(solution)/shard_map/ppermute | solution.py:234
  82.6 0.9 constant_dynamic-update-slice_fusion.5
  83.5 0.8 constant_dynamic-update-slice_fusion.4
  84.3 0.8 constant_dynamic-update-slice_fusion.3
  85.1 0.8 collective-permute-start.12
  86.0 6.8 %collective-permute-start.11 = (s32[1024]{0:T(1024)S(1)}, s32[1024]{0:T(1024)S(1)}, u32[]{:S(2)}, u32[]{:S(2)}) collective-permute-start(s32[1024]{0:T(1024)S(1)} %fusion.17), channel_id=1, source_target_pairs={{0,1},{3,2},{4,5},{7,6},{8,9},{11,10},{12,13},{15,14},{16,17},{19,... | collective-permute-start | bytes 12296 | tf_op jit(solution)/shard_map/ppermute | solution.py:234
  92.8 3.8 %shard_map.115.swished_ref = bf16[4,512,768]{2,1,0:T(8,128)(2,1)} custom-call(s32[15]{0:T(128)} %concatenate.42.meta, bf16[4,544,1536]{2,1,0:T(8,128)(2,1)} %get-tuple-element.21.normed_ref, f32[31,8,768]{2,1,0:T(8,128)} %broadcast_in_dim.17.taps_ref, bf16[192,1536]{1,0:T(8,128)(2,1)} %bitcast.58, ...), custom_call_target="tpu_custom_call", output_to_operand_aliasing={{}: (8, {})} | custom-call | flops 320864256 | bytes 503808 | tf_op jit(solution)/shard_map/pallas_call | solution.py:200
  96.9 1.3 reshape.61.code_ref
  98.2 1.3 copy-done.5
  99.6 6.4 %shard_map.116 = f32[4,8,128]{2,1,0:T(8,128)} custom-call(s32[15]{0:T(128)} %concatenate.42.meta, bf16[4,512,768]{2,1,0:T(8,128)(2,1)} %shard_map.115.swished_ref, bf16[4,544,1536]{2,1,0:T(8,128)(2,1)} %get-tuple-element.27.stem_out_ref, s32[4,512,1]{2,1,0:T(8,128)} %reshape.61.code_ref, f32[2,1536]{1,0:T(2,128)} %bitcast.65, ...), custom_call_target="tpu_custom_call" | custom-call | flops 503316480 | bytes 589824 | tf_op jit(solution)/shard_map/pallas_call | solution.py:200
  106.0 0.6 collective-permute-start.14
  106.6 2.4 %collective-permute-start.15 = (f32[4,8,128]{2,1,0:T(8,128)}, f32[4,8,128]{2,1,0:T(8,128)S(1)}, u32[]{:S(2)}, u32[]{:S(2)}) collective-permute-start(f32[4,8,128]{2,1,0:T(8,128)} %shard_map.116), channel_id=1, source_target_pairs={{0,24},{8,16},{16,8},{24,0},{1,25},{9,17},{17,9},{25,1},{2,26},{10... | collective-permute-start | bytes 49160 | tf_op jit(solution)/shard_map/ppermute | solution.py:243
  109.0 0.5 collective-permute-start.13
  109.6 0.5 collective-permute-done.14
  110.0 1.4 collective-permute-done.15
  111.4 1.5 %collective-permute-done.13 = f32[4,8,128]{2,1,0:T(8,128)S(1)} collective-permute-done((f32[4,8,128]{2,1,0:T(8,128)}, f32[4,8,128]{2,1,0:T(8,128)S(1)}, u32[]{:S(2)}, u32[]{:S(2)}) %collective-permute-start.13) | collective-permute-done | bytes 16416 | tf_op jit(solution)/shard_map/ppermute | solution.py:243
  113.0 0.7 add_multiply_fusion
  113.7 0.6 slice_reduce_fusion
  114.4 0.6 pad_maximum_fusion.4
  115.0 1.3 collective-permute-start.16
  116.3 1.2 collective-permute-start.17
  117.6 1.3 collective-permute-start.18
  118.9 29.5 %collective-permute-done.18 = f32[1]{0:T(128)} collective-permute-done((f32[1]{0:T(128)}, f32[1]{0:T(128)}, u32[]{:S(2)}, u32[]{:S(2)}) %collective-permute-start.18) | collective-permute-done | bytes 36 | tf_op jit(solution)/shard_map/ppermute | solution.py:234
  149.7 0.5 slice.103
  151.6 0.6 slice_select_fusion.3
  (70 shorter events, 1.1 us)
Async XLA Ops:
  0.6 18.6 %copy-start.10 = (bf16[1,96,1536]{2,1,0:T(8,128)(2,1)S(1)}, bf16[1,96,1536]{2,1,0:T(8,128)(2,1)}, u32[]{:S(2)}) copy-start(bf16[1,96,1536]{2,1,0:T(8,128)(2,1)} %param.16) | copy-start | bytes 884740
  2.0 9.1 %collective-permute-start = (bf16[256,320]{1,0:T(8,128)(2,1)S(1)}, bf16[256,320]{1,0:T(8,128)(2,1)S(1)}, u32[]{:S(2)}, u32[]{:S(2)}) collective-permute-start(bf16[256,320]{1,0:T(8,128)(2,1)S(1)} %reshape.54), channel_id=1, source_target_pairs={{0,1},{3,2},{4,5},{7,6},{8,9},{11,10},{12,13},{15,14},{16,17},{19,... | collective-permute-start | bytes 491528 | tf_op jit(solution)/shard_map/ppermute | solution.py:234
  8.6 23.6 %collective-permute-start.5 = (bf16[16,320]{1,0:T(8,128)(2,1)}, bf16[16,320]{1,0:T(8,128)(2,1)S(1)}, u32[]{:S(2)}, u32[]{:S(2)}) collective-permute-start(bf16[16,320]{1,0:T(8,128)(2,1)} %select_n.124), channel_id=1, source_target_pairs={{1,2},{2,1},{5,6},{6,5},{9,10},{10,9},{13,14},{14,13},{17,18},{18,... | collective-permute-start | bytes 30728 | tf_op jit(solution)/shard_map/ppermute | solution.py:234
  9.2 22.9 %collective-permute-start.6 = (bf16[192,1536]{1,0:T(8,128)(2,1)}, bf16[192,1536]{1,0:T(8,128)(2,1)S(1)}, u32[]{:S(2)}, u32[]{:S(2)}) collective-permute-start(bf16[192,1536]{1,0:T(8,128)(2,1)} %bitcast.56), channel_id=1, source_target_pairs={{1,2},{2,1},{5,6},{6,5},{9,10},{10,9},{13,14},{14,13},{17,18},{18,... | collective-permute-start | bytes 1769480 | tf_op jit(solution)/shard_map/ppermute | solution.py:234
  11.1 5.8 %collective-permute-start.3 = (bf16[256,320]{1,0:T(8,128)(2,1)S(1)}, bf16[256,320]{1,0:T(8,128)(2,1)S(1)}, u32[]{:S(2)}, u32[]{:S(2)}) collective-permute-start(bf16[256,320]{1,0:T(8,128)(2,1)S(1)} %collective-permute-done), channel_id=1, source_target_pairs={{0,8},{8,0},{16,24},{24,16},{1,9},{9,1},{17,25},{25,17},{2,10},{10... | collective-permute-start | bytes 491528 | tf_op jit(solution)/shard_map/ppermute | solution.py:243
  13.5 8.8 %copy-start.16 = (bf16[64,512]{1,0:T(8,128)(2,1)}, bf16[64,512]{1,0:T(8,128)(2,1)S(1)}, u32[]{:S(2)}) copy-start(bf16[64,512]{1,0:T(8,128)(2,1)S(1)} %get-tuple-element.50) | copy-start | bytes 196612
  13.5 9.4 %copy-start.12 = (bf16[64,512]{1,0:T(8,128)(2,1)}, bf16[64,512]{1,0:T(8,128)(2,1)S(1)}, u32[]{:S(2)}) copy-start(bf16[64,512]{1,0:T(8,128)(2,1)S(1)} %get-tuple-element.48) | copy-start | bytes 196612
  13.5 9.4 %copy-start.14 = (bf16[64,512]{1,0:T(8,128)(2,1)}, bf16[64,512]{1,0:T(8,128)(2,1)S(1)}, u32[]{:S(2)}) copy-start(bf16[64,512]{1,0:T(8,128)(2,1)S(1)} %get-tuple-element.49) | copy-start | bytes 196612
  16.9 7.9 %copy-start.1 = (bf16[1,192,1536]{2,1,0:T(8,128)(2,1)S(1)}, bf16[1,192,1536]{2,1,0:T(8,128)(2,1)}, u32[]{:S(2)}) copy-start(bf16[1,192,1536]{2,1,0:T(8,128)(2,1)} %param.15) | copy-start | bytes 1769476
  17.7 14.5 %collective-permute-start.4 = (bf16[512,320]{1,0:T(8,128)(2,1)}, bf16[512,320]{1,0:T(8,128)(2,1)}, u32[]{:S(2)}, u32[]{:S(2)}) collective-permute-start(bf16[512,320]{1,0:T(8,128)(2,1)} %pad_maximum_fusion.2), channel_id=1, source_target_pairs={{0,16},{8,24},{16,0},{24,8},{1,17},{9,25},{17,1},{25,9},{2,18},{10... | collective-permute-start | bytes 983048 | tf_op jit(solution)/shard_map/ppermute | solution.py:243
  24.8 24.4 %collective-permute-start.1 = (bf16[192,1536]{1,0:T(8,128)(2,1)S(1)}, bf16[192,1536]{1,0:T(8,128)(2,1)S(1)}, u32[]{:S(2)}, u32[]{:S(2)}) collective-permute-start(bf16[192,1536]{1,0:T(8,128)(2,1)S(1)} %bitcast.59), channel_id=1, source_target_pairs={{0,1},{3,2},{4,5},{7,6},{8,9},{11,10},{12,13},{15,14},{16,17},{19,... | collective-permute-start | bytes 1769480 | tf_op jit(solution)/shard_map/ppermute | solution.py:234
  29.9 23.4 %collective-permute-start.2 = (bf16[192,1536]{1,0:T(8,128)(2,1)S(1)}, bf16[192,1536]{1,0:T(8,128)(2,1)S(1)}, u32[]{:S(2)}, u32[]{:S(2)}) collective-permute-start(bf16[192,1536]{1,0:T(8,128)(2,1)S(1)} %bitcast.60), channel_id=1, source_target_pairs={{0,2},{3,1},{4,6},{7,5},{8,10},{11,9},{12,14},{15,13},{16,18},{19,... | collective-permute-start | bytes 1769480 | tf_op jit(solution)/shard_map/ppermute | solution.py:234
  32.2 21.1 %copy-start.2 = (bf16[192,1536]{1,0:T(8,128)(2,1)}, bf16[192,1536]{1,0:T(8,128)(2,1)S(1)}, u32[]{:S(2)}) copy-start(bf16[192,1536]{1,0:T(8,128)(2,1)S(1)} %collective-permute-done.6.rest_2_) | copy-start | bytes 1769476
  49.2 5.2 %copy-start.6 = (bf16[160,1536]{1,0:T(8,128)(2,1)S(1)}, bf16[160,1536]{1,0:T(8,128)(2,1)}, u32[]{:S(2)}) copy-start(bf16[160,1536]{1,0:T(8,128)(2,1)} %maximum_maximum_fusion.1.rest_0_) | copy-start | bytes 1474564
  49.2 16.6 %copy-start.11 = (bf16[1,96,1536]{2,1,0:T(8,128)(2,1)S(1)}, bf16[1,96,1536]{2,1,0:T(8,128)(2,1)}, u32[]{:S(2)}) copy-start(bf16[1,96,1536]{2,1,0:T(8,128)(2,1)} %param.16) | copy-start | bytes 884740
  49.2 17.4 %copy-start.3 = (bf16[192,1536]{1,0:T(8,128)(2,1)}, bf16[192,1536]{1,0:T(8,128)(2,1)S(1)}, u32[]{:S(2)}) copy-start(bf16[192,1536]{1,0:T(8,128)(2,1)S(1)} %collective-permute-done.1.rest_1_) | copy-start | bytes 1769476
  53.3 13.3 %copy-start.4 = (bf16[192,1536]{1,0:T(8,128)(2,1)}, bf16[192,1536]{1,0:T(8,128)(2,1)S(1)}, u32[]{:S(2)}) copy-start(bf16[192,1536]{1,0:T(8,128)(2,1)S(1)} %collective-permute-done.2.rest_3_) | copy-start | bytes 1769476
  53.3 13.3 %copy-start.18 = (bf16[1,31,768]{2,1,0:T(8,128)(2,1)S(1)}, bf16[1,31,768]{2,1,0:T(8,128)(2,1)}, u32[]{:S(2)}) copy-start(bf16[1,31,768]{2,1,0:T(8,128)(2,1)} %param.17) | copy-start | bytes 142852
  53.3 13.3 %copy-start.13 = (bf16[64,512]{1,0:T(8,128)(2,1)S(1)}, bf16[64,512]{1,0:T(8,128)(2,1)}, u32[]{:S(2)}) copy-start(bf16[64,512]{1,0:T(8,128)(2,1)} %copy-done.12) | copy-start | bytes 196612
  53.3 13.3 %copy-start.15 = (bf16[64,512]{1,0:T(8,128)(2,1)S(1)}, bf16[64,512]{1,0:T(8,128)(2,1)}, u32[]{:S(2)}) copy-start(bf16[64,512]{1,0:T(8,128)(2,1)} %copy-done.14) | copy-start | bytes 196612
  53.3 13.3 %copy-start.17 = (bf16[64,512]{1,0:T(8,128)(2,1)S(1)}, bf16[64,512]{1,0:T(8,128)(2,1)}, u32[]{:S(2)}) copy-start(bf16[64,512]{1,0:T(8,128)(2,1)} %copy-done.16) | copy-start | bytes 196612
  53.5 13.9 %collective-permute-start.7 = (bf16[768,1536]{1,0:T(8,128)(2,1)S(1)}, bf16[768,1536]{1,0:T(8,128)(2,1)S(1)}, u32[]{:S(2)}, u32[]{:S(2)}) collective-permute-start(bf16[768,1536]{1,0:T(8,128)(2,1)S(1)} %pad_maximum_fusion), channel_id=1, source_target_pairs={{1,5},{2,6},{5,1},{6,2},{9,13},{10,14},{13,9},{14,10},{17,21},{18,... | collective-permute-start | bytes 7077896 | tf_op jit(solution)/shard_map/ppermute | solution.py:239
  54.4 18.4 %collective-permute-start.8 = (bf16[160,1536]{1,0:T(8,128)(2,1)S(1)}, bf16[160,1536]{1,0:T(8,128)(2,1)S(1)}, u32[]{:S(2)}, u32[]{:S(2)}) collective-permute-start(bf16[160,1536]{1,0:T(8,128)(2,1)S(1)} %copy-done.6), channel_id=1, source_target_pairs={{0,1},{3,2},{4,5},{7,6},{8,9},{11,10},{12,13},{15,14},{16,17},{19,... | collective-permute-start | bytes 1474568 | tf_op jit(solution)/shard_map/ppermute | solution.py:234
  61.0 11.9 %collective-permute-start.9 = (bf16[160,1536]{1,0:T(8,128)(2,1)S(1)}, bf16[160,1536]{1,0:T(8,128)(2,1)S(1)}, u32[]{:S(2)}, u32[]{:S(2)}) collective-permute-start(bf16[160,1536]{1,0:T(8,128)(2,1)S(1)} %copy-done.6), channel_id=1, source_target_pairs={{1,2},{2,1},{5,6},{6,5},{9,10},{10,9},{13,14},{14,13},{17,18},{18,... | collective-permute-start | bytes 1474568 | tf_op jit(solution)/shard_map/ppermute | solution.py:234
  61.7 21.0 %collective-permute-start.10 = (bf16[160,1536]{1,0:T(8,128)(2,1)S(1)}, bf16[160,1536]{1,0:T(8,128)(2,1)S(1)}, u32[]{:S(2)}, u32[]{:S(2)}) collective-permute-start(bf16[160,1536]{1,0:T(8,128)(2,1)S(1)} %copy-done.6), channel_id=1, source_target_pairs={{0,2},{3,1},{4,6},{7,5},{8,10},{11,9},{12,14},{15,13},{16,18},{19,... | collective-permute-start | bytes 1474568 | tf_op jit(solution)/shard_map/ppermute | solution.py:234
  67.3 1.7 %copy-start = (bf16[768,1536]{1,0:T(8,128)(2,1)}, bf16[768,1536]{1,0:T(8,128)(2,1)S(1)}, u32[]{:S(2)}) copy-start(bf16[768,1536]{1,0:T(8,128)(2,1)S(1)} %collective-permute-done.7.rest_4_) | copy-start | bytes 7077892
  72.8 13.1 %copy-start.19 = (s32[1,1024]{1,0:T(1,128)S(1)}, s32[1,1024]{1,0:T(1,128)}, u32[]{:S(2)}) copy-start(s32[1,1024]{1,0:T(1,128)} %param.13) | copy-start | bytes 12292
  72.8 13.1 %copy-start.20 = (s32[1,1024]{1,0:T(1,128)S(1)}, s32[1,1024]{1,0:T(1,128)}, u32[]{:S(2)}) copy-start(s32[1,1024]{1,0:T(1,128)} %param.12) | copy-start | bytes 12292
  72.8 23.8 %copy-start.7 = (bf16[160,1536]{1,0:T(8,128)(2,1)}, bf16[160,1536]{1,0:T(8,128)(2,1)S(1)}, u32[]{:S(2)}) copy-start(bf16[160,1536]{1,0:T(8,128)(2,1)S(1)} %collective-permute-done.8.rest_1_) | copy-start | bytes 1474564
  72.9 23.7 %copy-start.8 = (bf16[160,1536]{1,0:T(8,128)(2,1)}, bf16[160,1536]{1,0:T(8,128)(2,1)S(1)}, u32[]{:S(2)}) copy-start(bf16[160,1536]{1,0:T(8,128)(2,1)S(1)} %collective-permute-done.9.rest_2_) | copy-start | bytes 1474564
  82.6 1.7 %copy-start.9 = (bf16[160,1536]{1,0:T(8,128)(2,1)}, bf16[160,1536]{1,0:T(8,128)(2,1)S(1)}, u32[]{:S(2)}) copy-start(bf16[160,1536]{1,0:T(8,128)(2,1)S(1)} %collective-permute-done.10.rest_3_) | copy-start | bytes 1474564
  85.1 13.1 %collective-permute-start.12 = (bf16[640,1536]{1,0:T(8,128)(2,1)}, bf16[640,1536]{1,0:T(8,128)(2,1)S(1)}, u32[]{:S(2)}, u32[]{:S(2)}) collective-permute-start(bf16[640,1536]{1,0:T(8,128)(2,1)} %constant_dynamic-update-slice_fusion.3), channel_id=1, source_target_pairs={{1,5},{2,6},{5,1},{6,2},{9,13},{10,14},{13,9},{14,10},{17,21},{18,... | collective-permute-start | bytes 5898248 | tf_op jit(solution)/shard_map/ppermute | solution.py:239
  86.0 10.6 %collective-permute-start.11 = (s32[1024]{0:T(1024)S(1)}, s32[1024]{0:T(1024)S(1)}, u32[]{:S(2)}, u32[]{:S(2)}) collective-permute-start(s32[1024]{0:T(1024)S(1)} %fusion.17), channel_id=1, source_target_pairs={{0,1},{3,2},{4,5},{7,6},{8,9},{11,10},{12,13},{15,14},{16,17},{19,... | collective-permute-start | bytes 12296 | tf_op jit(solution)/shard_map/ppermute | solution.py:234
  98.2 1.3 copy-start.5
  106.0 4.0 %collective-permute-start.14 = (f32[4,8,128]{2,1,0:T(8,128)}, f32[4,8,128]{2,1,0:T(8,128)S(1)}, u32[]{:S(2)}, u32[]{:S(2)}) collective-permute-start(f32[4,8,128]{2,1,0:T(8,128)} %shard_map.116), channel_id=1, source_target_pairs={{0,16},{8,24},{16,0},{24,8},{1,17},{9,25},{17,1},{25,9},{2,18},{10... | collective-permute-start | bytes 49160 | tf_op jit(solution)/shard_map/ppermute | solution.py:243
  106.6 4.8 %collective-permute-start.15 = (f32[4,8,128]{2,1,0:T(8,128)}, f32[4,8,128]{2,1,0:T(8,128)S(1)}, u32[]{:S(2)}, u32[]{:S(2)}) collective-permute-start(f32[4,8,128]{2,1,0:T(8,128)} %shard_map.116), channel_id=1, source_target_pairs={{0,24},{8,16},{16,8},{24,0},{1,25},{9,17},{17,9},{25,1},{2,26},{10... | collective-permute-start | bytes 49160 | tf_op jit(solution)/shard_map/ppermute | solution.py:243
  109.0 3.9 %collective-permute-start.13 = (f32[4,8,128]{2,1,0:T(8,128)}, f32[4,8,128]{2,1,0:T(8,128)S(1)}, u32[]{:S(2)}, u32[]{:S(2)}) collective-permute-start(f32[4,8,128]{2,1,0:T(8,128)} %shard_map.116), channel_id=1, source_target_pairs={{0,8},{8,0},{16,24},{24,16},{1,9},{9,1},{17,25},{25,17},{2,10},{10... | collective-permute-start | bytes 49160 | tf_op jit(solution)/shard_map/ppermute | solution.py:243
  115.0 34.6 %collective-permute-start.16 = (f32[1025]{0:T(1024)S(1)}, f32[1025]{0:T(1024)S(1)}, u32[]{:S(2)}, u32[]{:S(2)}) collective-permute-start(f32[1025]{0:T(1024)S(1)} %pad_maximum_fusion.4), channel_id=1, source_target_pairs={{1,0},{2,3},{5,4},{6,7},{9,8},{10,11},{13,12},{14,15},{17,16},{18,... | collective-permute-start | bytes 12308 | tf_op jit(solution)/shard_map/ppermute | solution.py:234
  116.3 2.6 %collective-permute-start.17 = (f32[1]{0:T(128)}, f32[1]{0:T(128)}, u32[]{:S(2)}, u32[]{:S(2)}) collective-permute-start(f32[1]{0:T(128)} %bitcast.28), channel_id=1, source_target_pairs={{1,2},{2,1},{5,6},{6,5},{9,10},{10,9},{13,14},{14,13},{17,18},{18,... | collective-permute-start | bytes 20 | tf_op jit(solution)/shard_map/ppermute | solution.py:234
  117.6 30.9 %collective-permute-start.18 = (f32[1]{0:T(128)}, f32[1]{0:T(128)}, u32[]{:S(2)}, u32[]{:S(2)}) collective-permute-start(f32[1]{0:T(128)} %bitcast.28), channel_id=1, source_target_pairs={{2,0},{1,3},{6,4},{5,7},{10,8},{9,11},{14,12},{13,15},{18,16},{17,... | collective-permute-start | bytes 20 | tf_op jit(solution)/shard_map/ppermute | solution.py:234

commit v3 on v2

--- a/solution.py
+++ b/solution.py
@@ -10,7 +10,7 @@
 LANES = 128
 CHUNKS = 8
 EDGE = 16
-VMEM_BYTES = 56 * 1024 * 1024
+VMEM_BYTES = 24 * 1024 * 1024
 
 
 def norm_rows(values, gain_row):
@@ -24,21 +24,28 @@
     return 0.5 * jnp.tanh(0.5 * x) + 0.5
 
 
-def stem_kernel(meta, pairs_ref, stem_ref, gain_ref, stem_out_ref, normed_ref):
-    slot = pl.program_id(0)
-    rows = pairs_ref.shape[1]
-    part = rows // 2
+def stem_kernel(first_slot, meta, main_ref, margin_ref, stem_ref, gain_ref, *rest):
+    stem_out_ref, normed_ref, acc_a, acc_b, acc_c = rest[-5:]
+    slot = pl.program_id(0) + first_slot
+    frames = main_ref.shape[1]
+    part = acc_a.shape[0]
+    group = 16
+
+    def norm(acc, at, keep):
+        for row in range(0, acc.shape[0], group):
+            stem_out = acc[row : row + group, :].astype(jnp.bfloat16)
+            if keep:
+                stem_out_ref[0, at + row : at + row + group, :] = stem_out
+            normed_ref[0, at + row : at + row + group, :] = norm_rows(stem_out.astype(jnp.float32), gain_ref[0:1, :])
 
     @pl.when(meta[5 + slot] > 0)
     def _():
-        parts = (slice(0, part), slice(part, rows))
-        made = [
-            jnp.dot(pairs_ref[0, here, :], stem_ref[...], preferred_element_type=jnp.float32).astype(jnp.bfloat16)
-            for here in parts
-        ]
-        for here, stem_out in zip(parts, made):
-            stem_out_ref[0, here, :] = stem_out
-            normed_ref[0, here, :] = norm_rows(stem_out.astype(jnp.float32), gain_ref[0:1, :])
+        for acc, at in ((acc_a, 0), (acc_b, part)):
+            acc[...] = jnp.dot(main_ref[0, at : at + part, :], stem_ref[...], preferred_element_type=jnp.float32)
+        norm(acc_a, 0, True)
+        acc_c[...] = jnp.dot(margin_ref[0], stem_ref[...], preferred_element_type=jnp.float32)
+        norm(acc_b, part, True)
+        norm(acc_c, frames, False)
 
 
 def shards(meta, pieces):
@@ -50,7 +57,7 @@
 
 def conv_kernel(first_slot, meta, normed_ref, taps_ref, *rest):
     pieces = rest[:5]
-    swished_ref, weight, gated_a, gated_b, margin, mask, sems = rest[-7:]
+    swished_ref, weight, mixed_a, mixed_b, gated, margin, mask, sems = rest[-8:]
     slot = pl.program_id(0) + first_slot
     rows = normed_ref.shape[1]
     frames = swished_ref.shape[1]
@@ -81,33 +88,42 @@
         at = meta[slot] + jnp.where(row < frames, inner, outer)
         mask[...] = jnp.logical_and(at >= 0, at < meta[4]).astype(jnp.float32)
         sublane = lax.broadcasted_iota(jnp.int32, (CHUNKS, LANES), 0)
-        buffers = (gated_a, gated_b)
-
-        def gate(block, into):
+        buffers = (mixed_a, mixed_b)
+
+        def mix(block):
             low = block * LANES
             right = jnp.concatenate(
                 [weight[:, low : low + LANES], weight[:, channels + low : channels + low + LANES]], axis=1
             )
-            mixed = jnp.dot(normed_ref[0], right, preferred_element_type=jnp.float32)
-            gated = mixed[:, :LANES] * sigmoid(mixed[:, LANES:]) * mask[...]
-            gated = gated.astype(jnp.bfloat16).astype(jnp.float32)
-            into[reach : reach + run_length] = gated[:frames].reshape(run_length, CHUNKS, LANES)
-            margin[...] = gated[frames:]
+            buffers[block % 2][...] = jnp.dot(normed_ref[0], right, preferred_element_type=jnp.float32)
+
+        def gate(block):
+            mixed = buffers[block % 2]
+            group = 32
+            for at in range(0, rows, group):
+                here = slice(at, at + group)
+                made = mixed[here, :LANES] * sigmoid(mixed[here, LANES:]) * mask[here, :]
+                made = made.astype(jnp.bfloat16).astype(jnp.float32)
+                if at < frames:
+                    first = reach + at // CHUNKS
+                    gated[first : first + group // CHUNKS] = made.reshape(group // CHUNKS, CHUNKS, LANES)
+                else:
+                    margin[...] = made
             for i in range(reach):
-                before = pltpu.roll(into[run_length + i], 1, 0)
+                before = pltpu.roll(gated[run_length + i], 1, 0)
                 edge = margin[EDGE - reach + i : EDGE - reach + i + 1, :]
-                into[i] = jnp.where(sublane == 0, edge, before)
-                after = pltpu.roll(into[reach + i], CHUNKS - 1, 0)
+                gated[i] = jnp.where(sublane == 0, edge, before)
+                after = pltpu.roll(gated[reach + i], CHUNKS - 1, 0)
                 edge = margin[EDGE + i : EDGE + i + 1, :]
-                into[reach + run_length + i] = jnp.where(sublane == CHUNKS - 1, edge, after)
-
-        def convolve(block, source):
+                gated[reach + run_length + i] = jnp.where(sublane == CHUNKS - 1, edge, after)
+
+        def convolve(block):
             low = block * LANES
             run = 16
             for start in range(0, run_length, run):
                 sums = [None] * run
                 for at in range(start, start + run + tap_count - 1):
-                    value = source[at]
+                    value = gated[at]
                     for m in range(max(start, at - tap_count + 1), min(start + run, at + 1)):
                         term = value * taps_ref[at - m, :, low : low + LANES]
                         k = m - start
@@ -120,16 +136,17 @@
                     ).astype(jnp.bfloat16)
 
         blocks = channels // LANES
-        gate(0, buffers[0])
+        mix(0)
         for block in range(blocks):
             if block + 1 < blocks:
-                gate(block + 1, buffers[(block + 1) % 2])
-            convolve(block, buffers[block % 2])
+                mix(block + 1)
+            gate(block)
+            convolve(block)
 
 
 def head_kernel(meta, swished_ref, stem_out_ref, code_ref, gain_ref, *rest):
     pieces = rest[:5]
-    error_ref, back, head, sems = rest[5:]
+    error_ref, back, head, acc_a, acc_b, norm_a, norm_b, logit_a, logit_b, sems = rest[5:]
     slot = pl.program_id(0)
     frames = swished_ref.shape[1]
     vocab = head.shape[1]
@@ -168,32 +185,39 @@
 
     @pl.when(meta[5 + slot] > 0)
     def _():
-        part = 256
+        part = acc_a.shape[0]
         lane = lax.broadcasted_iota(jnp.int32, (CHUNKS, LANES), 1)
-        starts = range(0, frames, part)
-        after = [
-            jnp.dot(swished_ref[0, at : at + part, :], back[...], preferred_element_type=jnp.float32)
-            for at in starts
-        ]
-        logits = []
-        for at, values in zip(starts, after):
-            values = values + stem_out_ref[0, at : at + part, :].astype(jnp.float32)
-            normed = norm_rows(values, gain_ref[1:2, :])
-            logits.append(jnp.dot(normed, head[...], preferred_element_type=jnp.float32))
-        row = jnp.zeros((CHUNKS, LANES), jnp.float32)
-        for at, scores in zip(starts, logits):
-            top = jnp.max(scores, axis=-1, keepdims=True)
-            grown = jnp.exp(scores - top)
-            posterior = grown * (1.0 / jnp.sum(grown, axis=-1, keepdims=True))
-            code = code_ref[0, at : at + part, :]
-            onehot = (lax.broadcasted_iota(jnp.int32, (part, vocab), 1) == code).astype(jnp.float32)
-            differ = posterior - onehot
-            error = jnp.sqrt(jnp.sum(differ * differ, axis=-1, keepdims=True))
-            error = jnp.where(code >= 0, error, 0.0)
-            for m in range(part // CHUNKS):
-                step = error[m * CHUNKS : (m + 1) * CHUNKS, :]
-                row = row + jnp.where(lane == at // CHUNKS + m, step, 0.0)
-        error_ref[0] = row
+        halves = ((0, acc_a, norm_a, logit_a), (part, acc_b, norm_b, logit_b))
+
+        def norm(at, acc, normed):
+            group = 16
+            for row in range(0, part, group):
+                values = acc[row : row + group, :] + stem_out_ref[0, at + row : at + row + group, :].astype(jnp.float32)
+                normed[row : row + group, :] = norm_rows(values, gain_ref[1:2, :])
+
+        def errors(at, logits):
+            group = 32
+            token = lax.broadcasted_iota(jnp.int32, (group, vocab), 1)
+            row = jnp.zeros((CHUNKS, LANES), jnp.float32)
+            for first in range(0, part, group):
+                scores = logits[first : first + group, :]
+                grown = jnp.exp(scores - jnp.max(scores, axis=-1, keepdims=True))
+                posterior = grown * (1.0 / jnp.sum(grown, axis=-1, keepdims=True))
+                code = code_ref[0, at + first : at + first + group, :]
+                differ = posterior - (token == code).astype(jnp.float32)
+                error = jnp.sqrt(jnp.sum(differ * differ, axis=-1, keepdims=True))
+                error = jnp.where(code >= 0, error, 0.0)
+                for m in range(group // CHUNKS):
+                    step = error[m * CHUNKS : (m + 1) * CHUNKS, :]
+                    row = row + jnp.where(lane == (at + first) // CHUNKS + m, step, 0.0)
+            return row
+
+        for at, acc, _, _ in halves:
+            acc[...] = jnp.dot(swished_ref[0, at : at + part, :], back[...], preferred_element_type=jnp.float32)
+        for at, acc, normed, logits in halves:
+            norm(at, acc, normed)
+            logits[...] = jnp.dot(normed[...], head[...], preferred_element_type=jnp.float32)
+        error_ref[0] = errors(0, logit_a) + errors(part, logit_b)
 
 
 def call(kernel, grid, in_specs, out_specs, out_shape, scratch, flops, moved, operands, aliases={}):
@@ -227,6 +251,8 @@
 ACROSS = [(1, 2), (2, 1)]
 BEYOND = [(0, 2), (3, 1)]
 OUTWARD = [(1, 0), (2, 3)]
+FORWARD = [(0, 1), (1, 2), (2, 3)]
+BACKWARD = [(1, 0), (2, 1), (3, 2)]
 OUT_BEYOND = [(2, 0), (1, 3)]
 
 
@@ -257,7 +283,6 @@
 ):
     chip = lax.axis_index("seq")
     side = lax.axis_index("fsdp")
-    seed = lax.axis_index("seed")
     seeds = lax.axis_size("seed")
     rows = targets.shape[1]
     width = stem_weight.shape[2]
@@ -269,21 +294,14 @@
     is_hub = jnp.logical_or(low, chip == 2)
 
     first = conv_in_weight[0]
+    near_first = along(first, INWARD)
     hub_first = along(first, ACROSS)
-    share = rows // seeds
-    quarter = lax.dynamic_slice_in_dim(mel_frames[0], seed * share * step, share * step, 0).reshape(share, -1)
-    quarter_in = along(quarter, INWARD)
     margin = step * EDGE
-    edge = along(jnp.where(low, mel_frames[0, -margin:], mel_frames[0, :margin]).reshape(EDGE, -1), ACROSS)
-    first_held, _ = lax.optimization_barrier((first, quarter_in))
-    near_first = along(first_held, INWARD)
-    far_first = along(first_held, BEYOND)
-
-    pair = seed_swap(quarter_in, 1)
-    odd = seed % 2 == 1
-    half = jnp.concatenate([jnp.where(odd, pair, quarter_in), jnp.where(odd, quarter_in, pair)], axis=0)
-    other = seed_swap(half, 2)
-    upper = seed // 2 == 1
+    before = along(mel_frames[0, -margin:].reshape(EDGE, -1), FORWARD)
+    after = along(mel_frames[0, :margin].reshape(EDGE, -1), BACKWARD)
+    blocks = mel_frames[0].reshape(rows, -1)
+    outer = along(blocks, INWARD)
+    far_first = along(near_first, ACROSS)
 
     groups = width // vocab
     head_rows = head_weight.shape[1]
@@ -294,38 +312,30 @@
         ],
         axis=0,
     )
-    second_held, other, edge, hub_first = lax.optimization_barrier((second, other, edge, hub_first))
+    second_held, before, after, hub_first = lax.optimization_barrier((second, before, after, hub_first))
     near_second = along(second_held, INWARD)
     far_second = along(second_held, BEYOND)
-    hub_second = along(second_held, ACROSS)
-    outer = jnp.concatenate([jnp.where(upper, other, half), jnp.where(upper, half, other)], axis=0)
-
-    blocks = mel_frames[0].reshape(rows, -1)
-    none = jnp.zeros_like(edge)
-    frames = jnp.concatenate(
-        [
-            jnp.where(low, none, edge),
-            jnp.where(low, outer, blocks),
-            jnp.where(low, blocks, outer),
-            jnp.where(low, edge, none),
-            none,
-        ],
-        axis=0,
-    )
+
     slots = 4
     deep = tile + 2 * EDGE
-    pairs = jnp.concatenate([frames[:-1], frames[1:]], axis=1)
-    inner = pairs[EDGE : EDGE + slots * tile].reshape(slots, CHUNKS, tile // CHUNKS, -1)
-    inner = inner.transpose(0, 2, 1, 3).reshape(slots, tile, -1)
-    before = jnp.stack([pairs[k * tile : k * tile + EDGE] for k in range(slots)])
-    after = jnp.stack([pairs[(k + 1) * tile + EDGE : (k + 1) * tile + 2 * EDGE] for k in range(slots)])
-    pairs = jnp.concatenate([inner, before, after], axis=1)
+
+    def paired(before, block, after):
+        frames = jnp.concatenate([before, block, after, after[:1]], axis=0)
+        pairs = jnp.concatenate([frames[:-1], frames[1:]], axis=1)
+        main = pairs[EDGE : EDGE + 2 * tile].reshape(2, CHUNKS, tile // CHUNKS, -1)
+        main = main.transpose(0, 2, 1, 3).reshape(2, tile, -1)
+        sides = [
+            jnp.concatenate([pairs[k * tile : k * tile + EDGE], pairs[(k + 1) * tile + EDGE : (k + 1) * tile + 2 * EDGE]])
+            for k in range(2)
+        ]
+        return main, jnp.stack(sides)
 
     length = lengths[0]
     positions = chip * rows + jnp.arange(rows, dtype=jnp.int32)
     counted = jnp.logical_and(frame_mask[0] > 0, positions < length)
     code = jnp.where(counted, targets[0], -1)
-    starts = (chip - 1) * 2 * rows + tile * jnp.arange(slots, dtype=jnp.int32)
+    lone = jnp.where(low, 0, 3)
+    starts = jnp.stack([chip * rows, chip * rows + tile, lone * rows, lone * rows + tile]).astype(jnp.int32)
     alive = jnp.logical_and(is_hub, starts < length).astype(jnp.int32)
     hub = jnp.clip(chip, 1, 2)
     meta = jnp.concatenate(
@@ -338,41 +348,63 @@
     ).astype(jnp.int32)
 
     gains = norm_gain[0]
-    stem_out, normed = call(
-        stem_kernel,
-        (slots,),
-        [by_slot((deep, pairs.shape[2])), whole(stem_weight.shape[1:]), whole(gains.shape)],
-        [by_slot((deep, width))] * 2,
-        [jax.ShapeDtypeStruct((slots, deep, width), jnp.bfloat16)] * 2,
-        [],
-        2 * slots * deep * pairs.shape[2] * width,
-        slots * deep * (pairs.shape[2] + 2 * width) * 2,
-        (meta, pairs, stem_weight[0], gains),
-    )
-
-    near_first, far_first, normed = lax.optimization_barrier((near_first, far_first, normed))
+    def stems(part, main, sides, *made):
+        half = tile // 2
+        return call(
+            functools.partial(stem_kernel, 2 * part),
+            (2,),
+            [by_slot(main.shape[1:]), by_slot(sides.shape[1:]), whole(stem_weight.shape[1:]), whole(gains.shape)]
+            + [apart] * len(made),
+            [by_slot((tile, width), 2 * part), by_slot((deep, width))],
+            [
+                jax.ShapeDtypeStruct((slots, tile, width), jnp.bfloat16),
+                jax.ShapeDtypeStruct((2, deep, width), jnp.bfloat16),
+            ],
+            [
+                pltpu.VMEM((half, width), jnp.float32),
+                pltpu.VMEM((half, width), jnp.float32),
+                pltpu.VMEM((2 * EDGE, width), jnp.float32),
+            ],
+            slots * deep * main.shape[2] * width,
+            slots * deep * (main.shape[2] + 2 * width),
+            (meta, main, sides, stem_weight[0], gains, *made),
+            {5: 0} if made else {},
+        )
+
+    apart = pl.BlockSpec(memory_space=pl.ANY)
+    stem_out, own_normed = stems(0, *paired(before, blocks, after))
+
+    near_first, far_first, outer, own_normed = lax.optimization_barrier((near_first, far_first, outer, own_normed))
     mine = [first, near_first, hub_first, far_first]
     first_pieces = (*mine, to_mate(jnp.concatenate(mine, axis=0)))
+    second_late, _ = lax.optimization_barrier((second, outer))
+    hub_second = along(second_late, ACROSS)
+
+    none = jnp.zeros_like(before)
+    outer_before = jnp.where(low, none, blocks[-EDGE:])
+    outer_after = jnp.where(low, blocks[:EDGE], none)
+    stem_out, outer_normed = stems(1, *paired(outer_before, outer, outer_after), stem_out)
+
     code_held, _ = lax.optimization_barrier((code, first_pieces[-1]))
     outer_code = along(code_held, INWARD)
-    codes = jnp.concatenate([jnp.where(low, outer_code, code), jnp.where(low, code, outer_code)])
+    codes = jnp.concatenate([code, outer_code])
     codes = codes.reshape(slots, CHUNKS, tile // CHUNKS).transpose(0, 2, 1).reshape(slots, tile, 1)
 
     taps = jnp.broadcast_to(
         depth_weight[0].astype(jnp.float32)[:, None, :], (depth_weight.shape[1], CHUNKS, channels)
     )
-    apart = pl.BlockSpec(memory_space=pl.ANY)
     extent = tile // CHUNKS + depth_weight.shape[1] - 1
     def convolve(part, normed, pieces, *made):
         return call(
             functools.partial(conv_kernel, 2 * part),
             (2,),
-            [by_slot((deep, width), 2 * part), whole(taps.shape)] + [apart] * (5 + len(made)),
+            [by_slot((deep, width)), whole(taps.shape)] + [apart] * (5 + len(made)),
             by_slot((tile, channels), 2 * part),
             jax.ShapeDtypeStruct((slots, tile, channels), jnp.bfloat16),
             [
                 pltpu.VMEM((8 * first.shape[0], first.shape[1]), jnp.bfloat16),
-                pltpu.VMEM((extent, CHUNKS, LANES), jnp.float32),
+                pltpu.VMEM((deep, 2 * LANES), jnp.float32),
+                pltpu.VMEM((deep, 2 * LANES), jnp.float32),
                 pltpu.VMEM((extent, CHUNKS, LANES), jnp.float32),
                 pltpu.VMEM((2 * EDGE, LANES), jnp.float32),
                 pltpu.VMEM((deep, LANES), jnp.float32),
@@ -384,22 +416,28 @@
             {8: 0} if made else {},
         )
 
-    swished = convolve(0, normed, first_pieces)
-    near_second, hub_second, far_second, swished = lax.optimization_barrier(
-        (near_second, hub_second, far_second, swished)
+    swished = convolve(0, own_normed, first_pieces)
+    near_second, hub_second, far_second, swished, outer_normed = lax.optimization_barrier(
+        (near_second, hub_second, far_second, swished, outer_normed)
     )
     mine = [second, near_second, hub_second, far_second]
     second_pieces = (*mine, to_mate(jnp.concatenate(mine, axis=0)))
-    swished = convolve(1, normed, first_pieces, swished)
+    swished = convolve(1, outer_normed, first_pieces, swished)
     errors = call(
         head_kernel,
         (slots,),
-        [by_slot((tile, channels)), by_slot((deep, width)), by_slot((tile, 1)), whole(gains.shape)] + [apart] * 5,
+        [by_slot((tile, channels)), by_slot((tile, width)), by_slot((tile, 1)), whole(gains.shape)] + [apart] * 5,
         by_slot((CHUNKS, LANES)),
         jax.ShapeDtypeStruct((slots, CHUNKS, LANES), jnp.float32),
         [
             pltpu.VMEM((8 * conv_out_weight.shape[1], width), jnp.bfloat16),
             pltpu.VMEM((8 * head_rows, vocab), jnp.bfloat16),
+            pltpu.VMEM((tile // 2, width), jnp.float32),
+            pltpu.VMEM((tile // 2, width), jnp.float32),
+            pltpu.VMEM((tile // 2, width), jnp.bfloat16),
+            pltpu.VMEM((tile // 2, width), jnp.bfloat16),
+            pltpu.VMEM((tile // 2, vocab), jnp.float32),
+            pltpu.VMEM((tile // 2, vocab), jnp.float32),
             pltpu.SemaphoreType.DMA((8, 1 + groups)),
         ],
         2 * slots * tile * (channels + vocab) * width,
@@ -411,8 +449,7 @@
     total = ((errors + one) + (two + three)) / jnp.float32(seeds)
     total = total[:, :, : tile // CHUNKS].reshape(2, rows)
     part = jnp.sum(total).reshape(1)
-    outer_half = jnp.where(low, total[0], total[1])
-    own_half = jnp.where(low, total[1], total[0])
+    own_half, outer_half = total
     from_hub = along(jnp.concatenate([outer_half, part]), OUTWARD)
     parts = [part[0], along(part, ACROSS)[0], along(part, OUT_BEYOND)[0], from_hub[rows]]
     frame_error = jnp.where(is_hub, own_half, from_hub[:rows])

time: 154 us -> 154 us (level)
  local copies, waits for them, and re-layouts: 17.7 us -> 40.4 us
  Pallas kernels: 21.8 us -> 3.61 us
  starting transfers between devices: 43.9 us -> 50.1 us
  waiting for transfers between devices: 50 us -> 44.2 us
  other arithmetic: 14.3 us -> 8.95 us
    unnamed x46 -> x77, local copies, waits for them, and re-layouts: 6.08 us -> 29.3 us
    pallas_call x4 -> x5, Pallas kernels: 21.8 us -> 3.61 us  [call(): pl.pallas_call(kernel, grid_spec=pltpu.PrefetchScalarGridSpec(num_scalar_...]
    ppermute x12 -> x13, starting transfers between devices: 35.6 us -> 42.6 us  [along(): return lax.ppermute(x, 'seq', pairs)]
    concatenate x3 -> x2, other arithmetic: 6.01 us -> 1.16 us  [paired(): pairs = jnp.concatenate([frames[:-1], frames[1:]], axis=1)]
    ppermute x12 -> x13, waiting for transfers between devices: 44.5 us -> 40 us  [along(): return lax.ppermute(x, 'seq', pairs)]
    ppermute x5 -> x3, starting transfers between devices: 6.56 us -> 3.55 us  [seed_swap(): return lax.ppermute(x, 'seed', [(i, i ^ bit) for i in range(4)])]
    ppermute x2, starting transfers between devices: 1.72 us -> 3.97 us  [to_mate(): return lax.ppermute(x, ('fsdp', 'seq'), pairs)]
    select_n x5 -> x2, other arithmetic: 2.23 us -> 0.02 us  [the longest x1 0.01 us: hub_body(): outer_after = jnp.where(low, blocks[:EDGE], none)]
  transfers between devices with their start and end apart: 19 -> 18, of which waited for: 8 -> 6; matrix products, arithmetic and copies ran while one was open for 15% -> 13% of each run, Pallas kernels for 10% -> 2%
where the time goes in v3:
time: 154 us; the launch traced here: 153 us
  starting transfers between devices  50.1 us (33%)
  waiting for transfers between devices  44.2 us (29%)
  local copies, waits for them, and re-layouts  40.4 us (26%)
  other arithmetic  8.95 us (6%)
  between operations  5.55 us (4%)
  Pallas kernels  3.61 us (2%)
    ppermute x13, starting transfers between devices, along(): return lax.ppermute(x, 'seq', pairs)  42.6 us
    ppermute x13, waiting for transfers between devices, along(): return lax.ppermute(x, 'seq', pairs)  40 us
    unnamed x77, local copies, waits for them, and re-layouts  29.3 us
    ppermute x3, waiting for transfers between devices, seed_swap(): return lax.ppermute(x, 'seed', [(i, i ^ bit) for i in range(4)])  4.16 us
    ppermute x2, starting transfers between devices, to_mate(): return lax.ppermute(x, ('fsdp', 'seq'), pairs)  3.97 us
    pallas_call x5, Pallas kernels, call(): pl.pallas_call(kernel, grid_spec=pltpu.PrefetchScalarGridSpec(num_scalar_...  3.61 us
    ppermute x3, starting transfers between devices, seed_swap(): return lax.ppermute(x, 'seed', [(i, i ^ bit) for i in range(4)])  3.55 us
  transfers between devices with their start and end apart: 18, of which 6 were waited for; matrix products, arithmetic and copies ran while one was open for 13% of the time, Pallas kernels for 2%

profile of v3, /device:TPU:0, one launch (start us, length us, event | category | flops | bytes accessed | tf_op | source)
XLA Modules:
  0.0 152.8 jit_solution(5115491731637226191)
XLA Ops:
  0.6 0.7 collective-permute-start.2
  1.3 7.8 %collective-permute-start.4 = (bf16[192,1536]{1,0:T(8,128)(2,1)}, bf16[192,1536]{1,0:T(8,128)(2,1)S(1)}, u32[]{:S(2)}, u32[]{:S(2)}) collective-permute-start(bf16[192,1536]{1,0:T(8,128)(2,1)} %bitcast.62), channel_id=1, source_target_pairs={{0,1},{3,2},{4,5},{7,6},{8,9},{11,10},{12,13},{15,14},{16,17},{19,... | collective-permute-start | bytes 1769480 | tf_op jit(solution)/shard_map/ppermute | solution.py:260
  9.1 0.8 fusion.93
  10.1 1.3 collective-permute-start
  11.6 1.3 collective-permute-start.1
  12.9 1.6 %copy.30 = bf16[1,4096,80]{2,1,0:T(8,128)(2,1)S(1)} copy(bf16[1,4096,80]{1,2,0:T(8,128)(2,1)} %param.10) | data formatting | bytes 1310720 | tf_op args[0]
  14.5 0.7 reshape_squeeze.11
  15.1 1.1 copy.31
  16.3 4.7 %collective-permute-start.6 = (bf16[1024,320]{0,1:T(8,128)(2,1)}, bf16[1024,320]{0,1:T(8,128)(2,1)S(1)}, u32[]{:S(2)}, u32[]{:S(2)}) collective-permute-start(bf16[1024,320]{0,1:T(8,128)(2,1)} %copy.31), channel_id=1, source_target_pairs={{0,1},{3,2},{4,5},{7,6},{8,9},{11,10},{12,13},{15,14},{16,17},{19,... | collective-permute-start | bytes 1966088 | tf_op jit(solution)/shard_map/ppermute | solution.py:260
  21.0 2.0 %fusion.92 = (bf16[1024,640]{1,0:T(8,128)(2,1)}, bf16[1024,640]{1,0:T(8,128)(2,1)}) fusion(bf16[1024,320]{1,0:T(8,128)(2,1)S(1)} %reshape_squeeze.11), kind=kLoop, calls=%fused_computation.136 | loop fusion | bytes 3276800
  23.6 0.8 maximum_maximum_fusion.rest_0_
  24.5 0.8 fusion.90
  25.3 0.8 concatenate.56.meta
  26.1 0.7 collective-permute-start.5
  26.8 0.6 fusion.1
  27.6 0.7 copy.41
  28.3 0.9 fusion.48
  29.3 0.6 shard_map.113
  30.0 2.7 %copy-done = bf16[4,512,1536]{2,1,0:T(8,128)(2,1)} copy-done((bf16[4,512,1536]{2,1,0:T(8,128)(2,1)}, bf16[4,512,1536]{2,1,0:T(8,128)(2,1)S(1)}, u32[]{:S(2)}) %copy-start) | copy-done | bytes 6291480
  32.6 3.3 %collective-permute-done.6 = bf16[1024,320]{0,1:T(8,128)(2,1)S(1)} collective-permute-done((bf16[1024,320]{0,1:T(8,128)(2,1)}, bf16[1024,320]{0,1:T(8,128)(2,1)S(1)}, u32[]{:S(2)}, u32[]{:S(2)}) %collective-permute-start.6) | collective-permute-done | bytes 655392 | tf_op jit(solution)/shard_map/ppermute | solution.py:260
  36.0 1.7 %pad_maximum_fusion = bf16[768,1536]{1,0:T(8,128)(2,1)} fusion(bf16[192,1536]{1,0:T(8,128)(2,1)S(1)} %collective-permute-done.5.rest_3_, bf16[192,1536]{1,0:T(8,128)(2,1)S(1)} %collective-permute-done.2.rest_2_, bf16[192,1536]{1,0:T(8,128)(2,1)S(1)} %collective-permute-done.4.rest_1_, bf16[192,1536]{1,0:T(8,128)(2,1)S(1)} %bitcast.63), kind=kLoop, calls=%fused_computation | loop fusion | flops 9437184 | bytes 4718592 | tf_op jit(solution)/shard_map/concatenate | solution.py:379
  37.7 2.1 %collective-permute-start.9 = (bf16[768,1536]{1,0:T(8,128)(2,1)}, bf16[768,1536]{1,0:T(8,128)(2,1)}, u32[]{:S(2)}, u32[]{:S(2)}) collective-permute-start(bf16[768,1536]{1,0:T(8,128)(2,1)} %pad_maximum_fusion), channel_id=1, source_target_pairs={{1,5},{2,6},{5,1},{6,2},{9,13},{10,14},{13,9},{14,10},{17,21},{18,... | collective-permute-start | bytes 7077896 | tf_op jit(solution)/shard_map/ppermute | solution.py:265
  39.8 0.7 constant_dynamic-update-slice_fusion.3
  40.6 0.7 maximum_dynamic-update-slice_fusion
  41.3 8.2 %collective-permute-start.3 = (bf16[160,1536]{1,0:T(8,128)(2,1)}, bf16[160,1536]{1,0:T(8,128)(2,1)}, u32[]{:S(2)}, u32[]{:S(2)}) collective-permute-start(bf16[160,1536]{1,0:T(8,128)(2,1)} %maximum_maximum_fusion.rest_0_), channel_id=1, source_target_pairs={{0,1},{3,2},{4,5},{7,6},{8,9},{11,10},{12,13},{15,14},{16,17},{19,... | collective-permute-start | bytes 1474568 | tf_op jit(solution)/shard_map/ppermute | solution.py:260
  49.5 2.1 %collective-permute-start.8 = (bf16[160,1536]{1,0:T(8,128)(2,1)}, bf16[160,1536]{1,0:T(8,128)(2,1)}, u32[]{:S(2)}, u32[]{:S(2)}) collective-permute-start(bf16[160,1536]{1,0:T(8,128)(2,1)} %maximum_maximum_fusion.rest_0_), channel_id=1, source_target_pairs={{0,2},{3,1},{4,6},{7,5},{8,10},{11,9},{12,14},{15,13},{16,18},{19,... | collective-permute-start | bytes 1474568 | tf_op jit(solution)/shard_map/ppermute | solution.py:260
  51.5 1.4 copy.33
  53.0 0.9 collective-permute-start.7
  55.2 0.7 copy.40
  56.5 0.8 copy-done.4
  57.4 0.6 shard_map.115
  58.0 3.2 %copy-done.1 = bf16[4,512,1536]{2,1,0:T(8,128)(2,1)} copy-done((bf16[4,512,1536]{2,1,0:T(8,128)(2,1)}, bf16[4,512,1536]{2,1,0:T(8,128)(2,1)S(1)}, u32[]{:S(2)}) %copy-start.1) | copy-done | bytes 6291480
  61.3 1.3 copy-done.21
  62.6 0.7 shard_map.114.rest_5_
  63.5 7.2 %collective-permute-done.8.rest_3_ = bf16[160,1536]{1,0:T(8,128)(2,1)} collective-permute-done((bf16[160,1536]{1,0:T(8,128)(2,1)}, bf16[160,1536]{1,0:T(8,128)(2,1)}, u32[]{:S(2)}, u32[]{:S(2)}) %collective-permute-start.8) | collective-permute-done | bytes 491552 | tf_op jit(solution)/shard_map/ppermute | solution.py:260
  70.7 2.0 %constant_dynamic-update-slice_fusion.2 = bf16[640,1536]{1,0:T(8,128)(2,1)} fusion(bf16[640,1536]{1,0:T(8,128)(2,1)} %maximum_dynamic-update-slice_fusion, bf16[160,1536]{1,0:T(8,128)(2,1)} %collective-permute-done.3.rest_1_), kind=kLoop, calls=%fused_computation.123 | loop fusion | bytes 983040
  72.7 0.8 constant_dynamic-update-slice_fusion.1
  73.5 1.8 %constant_dynamic-update-slice_fusion = bf16[640,1536]{1,0:T(8,128)(2,1)} fusion(bf16[640,1536]{1,0:T(8,128)(2,1)} %constant_dynamic-update-slice_fusion.1, bf16[160,1536]{1,0:T(8,128)(2,1)} %collective-permute-done.8.rest_3_), kind=kLoop, calls=%fused_computation.121 | loop fusion | bytes 983040 | tf_op jit(solution)/shard_map/concatenate | solution.py:424
  75.4 1.9 %collective-permute-start.11 = (bf16[640,1536]{1,0:T(8,128)(2,1)}, bf16[640,1536]{1,0:T(8,128)(2,1)}, u32[]{:S(2)}, u32[]{:S(2)}) collective-permute-start(bf16[640,1536]{1,0:T(8,128)(2,1)} %constant_dynamic-update-slice_fusion), channel_id=1, source_target_pairs={{1,5},{2,6},{5,1},{6,2},{9,13},{10,14},{13,9},{14,10},{17,21},{18,... | collective-permute-start | bytes 5898248 | tf_op jit(solution)/shard_map/ppermute | solution.py:265
  77.9 0.7 reduce.7
  78.7 11.3 %collective-permute-start.10 = (s32[1024]{0:T(1024)S(1)}, s32[1024]{0:T(1024)S(1)}, u32[]{:S(2)}, u32[]{:S(2)}) collective-permute-start(s32[1024]{0:T(1024)S(1)} %fusion.89), channel_id=1, source_target_pairs={{0,1},{3,2},{4,5},{7,6},{8,9},{11,10},{12,13},{15,14},{16,17},{19,... | collective-permute-start | bytes 12296 | tf_op jit(solution)/shard_map/ppermute | solution.py:260
  90.0 1.1 copy-done.6
  91.1 1.1 copy-done.9
  92.2 1.1 copy-done.12
  93.2 1.1 copy-done.15
  94.3 1.1 copy-done.18
  95.4 1.9 %copy-done.23 = bf16[2,544,1536]{2,1,0:T(8,128)(2,1)S(1)} copy-done((bf16[2,544,1536]{2,1,0:T(8,128)(2,1)S(1)}, bf16[2,544,1536]{2,1,0:T(8,128)(2,1)}, u32[]{:S(2)}) %copy-start.23) | copy-done | bytes 3342360
  97.3 0.7 shard_map.116.swished_ref
  98.2 1.3 reshape.61.code_ref
  99.5 2.8 %copy-done.2 = bf16[4,512,1536]{2,1,0:T(8,128)(2,1)S(1)} copy-done((bf16[4,512,1536]{2,1,0:T(8,128)(2,1)S(1)}, bf16[4,512,1536]{2,1,0:T(8,128)(2,1)}, u32[]{:S(2)}) %copy-start.2) | copy-done | bytes 6291480
  102.3 1.2 copy-done.19
  103.5 1.0 copy-done.25
  104.6 1.0 shard_map.117
  105.6 1.6 %collective-permute-start.12 = (f32[4,8,128]{2,1,0:T(8,128)S(1)}, f32[4,8,128]{2,1,0:T(8,128)S(1)}, u32[]{:S(2)}, u32[]{:S(2)}) collective-permute-start(f32[4,8,128]{2,1,0:T(8,128)S(1)} %shard_map.117), channel_id=1, source_target_pairs={{0,8},{8,0},{16,24},{24,16},{1,9},{9,1},{17,25},{25,17},{2,10},{10... | collective-permute-start | bytes 49160 | tf_op jit(solution)/shard_map/ppermute | solution.py:269
  107.1 1.5 collective-permute-start.13
  109.4 1.5 collective-permute-done.13
  110.9 2.4 %collective-permute-done.14 = f32[4,8,128]{2,1,0:T(8,128)S(1)} collective-permute-done((f32[4,8,128]{2,1,0:T(8,128)S(1)}, f32[4,8,128]{2,1,0:T(8,128)S(1)}, u32[]{:S(2)}, u32[]{:S(2)}) %collective-permute-start.14) | collective-permute-done | bytes 16416 | tf_op jit(solution)/shard_map/ppermute | solution.py:269
  113.3 0.6 slice_reduce_fusion
  114.0 0.6 pad_maximum_fusion.19
  114.6 1.3 collective-permute-start.15
  115.9 1.2 collective-permute-start.16
  117.1 1.3 collective-permute-start.17
  118.5 29.5 %collective-permute-done.17 = f32[1]{0:T(128)} collective-permute-done((f32[1]{0:T(128)}, f32[1]{0:T(128)}, u32[]{:S(2)}, u32[]{:S(2)}) %collective-permute-start.17) | collective-permute-done | bytes 36 | tf_op jit(solution)/shard_map/ppermute | solution.py:260
  151.1 0.6 slice_select_fusion
  (106 shorter events, 5.2 us)
Async XLA Ops:
  0.6 25.5 %collective-permute-start.2 = (bf16[192,1536]{1,0:T(8,128)(2,1)}, bf16[192,1536]{1,0:T(8,128)(2,1)S(1)}, u32[]{:S(2)}, u32[]{:S(2)}) collective-permute-start(bf16[192,1536]{1,0:T(8,128)(2,1)} %bitcast.61), channel_id=1, source_target_pairs={{1,2},{2,1},{5,6},{6,5},{9,10},{10,9},{13,14},{14,13},{17,18},{18,... | collective-permute-start | bytes 1769480 | tf_op jit(solution)/shard_map/ppermute | solution.py:260
  1.3 24.8 %collective-permute-start.4 = (bf16[192,1536]{1,0:T(8,128)(2,1)}, bf16[192,1536]{1,0:T(8,128)(2,1)S(1)}, u32[]{:S(2)}, u32[]{:S(2)}) collective-permute-start(bf16[192,1536]{1,0:T(8,128)(2,1)} %bitcast.62), channel_id=1, source_target_pairs={{0,1},{3,2},{4,5},{7,6},{8,9},{11,10},{12,13},{15,14},{16,17},{19,... | collective-permute-start | bytes 1769480 | tf_op jit(solution)/shard_map/ppermute | solution.py:260
  10.1 16.0 %collective-permute-start = (bf16[16,320]{1,0:T(8,128)(2,1)S(1)}, bf16[16,320]{1,0:T(8,128)(2,1)S(1)}, u32[]{:S(2)}, u32[]{:S(2)}) collective-permute-start(bf16[16,320]{1,0:T(8,128)(2,1)S(1)} %reshape_squeeze.9), channel_id=1, source_target_pairs={{0,1},{1,2},{2,3},{4,5},{5,6},{6,7},{8,9},{9,10},{10,11},{12,13},{... | collective-permute-start | bytes 30728 | tf_op jit(solution)/shard_map/ppermute | solution.py:260
  11.6 14.5 %collective-permute-start.1 = (bf16[16,320]{1,0:T(8,128)(2,1)S(1)}, bf16[16,320]{1,0:T(8,128)(2,1)S(1)}, u32[]{:S(2)}, u32[]{:S(2)}) collective-permute-start(bf16[16,320]{1,0:T(8,128)(2,1)S(1)} %reshape_squeeze.10), channel_id=1, source_target_pairs={{1,0},{2,1},{3,2},{5,4},{6,5},{7,6},{9,8},{10,9},{11,10},{13,12},{... | collective-permute-start | bytes 30728 | tf_op jit(solution)/shard_map/ppermute | solution.py:260
  16.3 7.4 %copy-start.29 = (bf16[1,192,512]{2,1,0:T(8,128)(2,1)S(1)}, bf16[1,192,512]{2,1,0:T(8,128)(2,1)}, u32[]{:S(2)}) copy-start(bf16[1,192,512]{2,1,0:T(8,128)(2,1)} %param.18) | copy-start | bytes 589828
  16.3 7.4 %copy-start.27 = (bf16[1,96,1536]{2,1,0:T(8,128)(2,1)S(1)}, bf16[1,96,1536]{2,1,0:T(8,128)(2,1)}, u32[]{:S(2)}) copy-start(bf16[1,96,1536]{2,1,0:T(8,128)(2,1)} %param.16) | copy-start | bytes 884740
  16.3 19.7 %collective-permute-start.6 = (bf16[1024,320]{0,1:T(8,128)(2,1)}, bf16[1024,320]{0,1:T(8,128)(2,1)S(1)}, u32[]{:S(2)}, u32[]{:S(2)}) collective-permute-start(bf16[1024,320]{0,1:T(8,128)(2,1)} %copy.31), channel_id=1, source_target_pairs={{0,1},{3,2},{4,5},{7,6},{8,9},{11,10},{12,13},{15,14},{16,17},{19,... | collective-permute-start | bytes 1966088 | tf_op jit(solution)/shard_map/ppermute | solution.py:260
  26.1 9.9 %copy-start.10 = (bf16[192,1536]{1,0:T(8,128)(2,1)}, bf16[192,1536]{1,0:T(8,128)(2,1)S(1)}, u32[]{:S(2)}) copy-start(bf16[192,1536]{1,0:T(8,128)(2,1)S(1)} %collective-permute-done.2.rest_2_) | copy-start | bytes 1769476
  26.1 9.9 %copy-start.13 = (bf16[192,1536]{1,0:T(8,128)(2,1)}, bf16[192,1536]{1,0:T(8,128)(2,1)S(1)}, u32[]{:S(2)}) copy-start(bf16[192,1536]{1,0:T(8,128)(2,1)S(1)} %collective-permute-done.4.rest_1_) | copy-start | bytes 1769476
  26.1 9.8 %collective-permute-start.5 = (bf16[192,1536]{1,0:T(8,128)(2,1)S(1)}, bf16[192,1536]{1,0:T(8,128)(2,1)S(1)}, u32[]{:S(2)}, u32[]{:S(2)}) collective-permute-start(bf16[192,1536]{1,0:T(8,128)(2,1)S(1)} %collective-permute-done.4.rest_1_), channel_id=1, source_target_pairs={{1,2},{2,1},{5,6},{6,5},{9,10},{10,9},{13,14},{14,13},{17,18},{18,... | collective-permute-start | bytes 1769480 | tf_op jit(solution)/shard_map/ppermute | solution.py:260
  27.5 1.8 %copy-start.3 = (bf16[1,640,1536]{2,1,0:T(8,128)(2,1)S(1)}, bf16[1,640,1536]{2,1,0:T(8,128)(2,1)}, u32[]{:S(2)}) copy-start(bf16[1,640,1536]{2,1,0:T(8,128)(2,1)} %param.14) | copy-start | bytes 5898244
  27.6 1.8 %copy-start.26 = (f32[1,2,1536]{2,1,0:T(2,128)S(1)}, f32[1,2,1536]{2,1,0:T(2,128)}, u32[]{:S(2)}) copy-start(f32[1,2,1536]{2,1,0:T(2,128)} %param.19) | copy-start | bytes 36868
  29.3 6.7 %copy-start.7 = (bf16[1,192,1536]{2,1,0:T(8,128)(2,1)S(1)}, bf16[1,192,1536]{2,1,0:T(8,128)(2,1)}, u32[]{:S(2)}) copy-start(bf16[1,192,1536]{2,1,0:T(8,128)(2,1)} %param.15) | copy-start | bytes 1769476
  30.0 2.7 %copy-start = (bf16[4,512,1536]{2,1,0:T(8,128)(2,1)}, bf16[4,512,1536]{2,1,0:T(8,128)(2,1)S(1)}, u32[]{:S(2)}) copy-start(bf16[4,512,1536]{2,1,0:T(8,128)(2,1)S(1)} %get-tuple-element.31.rest_0_) | copy-start | bytes 18874372
  32.6 5.1 %copy-start.20 = (bf16[2,544,1536]{2,1,0:T(8,128)(2,1)}, bf16[2,544,1536]{2,1,0:T(8,128)(2,1)S(1)}, u32[]{:S(2)}) copy-start(bf16[2,544,1536]{2,1,0:T(8,128)(2,1)S(1)} %get-tuple-element.27.normed_ref) | copy-start | bytes 10027012
  36.0 13.5 %copy-start.28 = (bf16[1024,320]{0,1:T(8,128)(2,1)}, bf16[1024,320]{0,1:T(8,128)(2,1)S(1)}, u32[]{:S(2)}) copy-start(bf16[1024,320]{0,1:T(8,128)(2,1)S(1)} %collective-permute-done.6) | copy-start | bytes 1966084
  36.0 1.7 %copy-start.16 = (bf16[192,1536]{1,0:T(8,128)(2,1)}, bf16[192,1536]{1,0:T(8,128)(2,1)S(1)}, u32[]{:S(2)}) copy-start(bf16[192,1536]{1,0:T(8,128)(2,1)S(1)} %collective-permute-done.5.rest_3_) | copy-start | bytes 1769476
  36.0 3.8 %copy-start.30 = (bf16[1,31,768]{2,1,0:T(8,128)(2,1)S(1)}, bf16[1,31,768]{2,1,0:T(8,128)(2,1)}, u32[]{:S(2)}) copy-start(bf16[1,31,768]{2,1,0:T(8,128)(2,1)} %param.17) | copy-start | bytes 142852
  37.7 23.5 %collective-permute-start.9 = (bf16[768,1536]{1,0:T(8,128)(2,1)}, bf16[768,1536]{1,0:T(8,128)(2,1)}, u32[]{:S(2)}, u32[]{:S(2)}) collective-permute-start(bf16[768,1536]{1,0:T(8,128)(2,1)} %pad_maximum_fusion), channel_id=1, source_target_pairs={{1,5},{2,6},{5,1},{6,2},{9,13},{10,14},{13,9},{14,10},{17,21},{18,... | collective-permute-start | bytes 7077896 | tf_op jit(solution)/shard_map/ppermute | solution.py:265
  40.6 15.4 %slice-start = ((s8[6291456]{0:T(1024)(128)(4,1)}), s8[2097152]{0:T(1024)(128)(4,1)S(1)}, s32[]{:S(2)}) async-start(s8[6291456]{0:T(1024)(128)(4,1)} %bitcast.57), calls=%async_computation | async-start | bytes 4194304
  41.3 22.2 %collective-permute-start.3 = (bf16[160,1536]{1,0:T(8,128)(2,1)}, bf16[160,1536]{1,0:T(8,128)(2,1)}, u32[]{:S(2)}, u32[]{:S(2)}) collective-permute-start(bf16[160,1536]{1,0:T(8,128)(2,1)} %maximum_maximum_fusion.rest_0_), channel_id=1, source_target_pairs={{0,1},{3,2},{4,5},{7,6},{8,9},{11,10},{12,13},{15,14},{16,17},{19,... | collective-permute-start | bytes 1474568 | tf_op jit(solution)/shard_map/ppermute | solution.py:260
  49.5 21.2 %collective-permute-start.8 = (bf16[160,1536]{1,0:T(8,128)(2,1)}, bf16[160,1536]{1,0:T(8,128)(2,1)}, u32[]{:S(2)}, u32[]{:S(2)}) collective-permute-start(bf16[160,1536]{1,0:T(8,128)(2,1)} %maximum_maximum_fusion.rest_0_), channel_id=1, source_target_pairs={{0,2},{3,1},{4,6},{7,5},{8,10},{11,9},{12,14},{15,13},{16,18},{19,... | collective-permute-start | bytes 1474568 | tf_op jit(solution)/shard_map/ppermute | solution.py:260
  53.0 17.7 %collective-permute-start.7 = (bf16[160,1536]{1,0:T(8,128)(2,1)}, bf16[160,1536]{1,0:T(8,128)(2,1)S(1)}, u32[]{:S(2)}, u32[]{:S(2)}) collective-permute-start(bf16[160,1536]{1,0:T(8,128)(2,1)} %maximum_maximum_fusion.rest_0_), channel_id=1, source_target_pairs={{1,2},{2,1},{5,6},{6,5},{9,10},{10,9},{13,14},{14,13},{17,18},{18,... | collective-permute-start | bytes 1474568 | tf_op jit(solution)/shard_map/ppermute | solution.py:260
  54.4 2.2 %slice-start.1 = ((s8[6291456]{0:T(1024)(128)(4,1)}), s8[4194304]{0:T(1024)(128)(4,1)S(1)}, s32[]{:S(2)}) async-start(s8[6291456]{0:T(1024)(128)(4,1)} %bitcast.57), calls=%async_computation.1 | async-start | bytes 8388608
  55.1 2.2 %copy-start.4 = (bf16[1,640,1536]{2,1,0:T(8,128)(2,1)S(1)}, bf16[1,640,1536]{2,1,0:T(8,128)(2,1)}, u32[]{:S(2)}) copy-start(bf16[1,640,1536]{2,1,0:T(8,128)(2,1)} %param.14) | copy-start | bytes 5898244
  57.4 3.9 %copy-start.8 = (bf16[1,192,1536]{2,1,0:T(8,128)(2,1)S(1)}, bf16[1,192,1536]{2,1,0:T(8,128)(2,1)}, u32[]{:S(2)}) copy-start(bf16[1,192,1536]{2,1,0:T(8,128)(2,1)} %param.15) | copy-start | bytes 1769476
  57.4 3.9 %copy-start.11 = (bf16[192,1536]{1,0:T(8,128)(2,1)S(1)}, bf16[192,1536]{1,0:T(8,128)(2,1)}, u32[]{:S(2)}) copy-start(bf16[192,1536]{1,0:T(8,128)(2,1)} %copy-done.10) | copy-start | bytes 1769476
  57.4 3.9 %copy-start.14 = (bf16[192,1536]{1,0:T(8,128)(2,1)S(1)}, bf16[192,1536]{1,0:T(8,128)(2,1)}, u32[]{:S(2)}) copy-start(bf16[192,1536]{1,0:T(8,128)(2,1)} %copy-done.13) | copy-start | bytes 1769476
  57.4 3.9 %copy-start.17 = (bf16[192,1536]{1,0:T(8,128)(2,1)S(1)}, bf16[192,1536]{1,0:T(8,128)(2,1)}, u32[]{:S(2)}) copy-start(bf16[192,1536]{1,0:T(8,128)(2,1)} %copy-done.16) | copy-start | bytes 1769476
  57.4 5.2 %copy-start.21 = (bf16[2,544,1536]{2,1,0:T(8,128)(2,1)S(1)}, bf16[2,544,1536]{2,1,0:T(8,128)(2,1)}, u32[]{:S(2)}) copy-start(bf16[2,544,1536]{2,1,0:T(8,128)(2,1)} %copy-done.20) | copy-start | bytes 10027012
  58.0 3.2 %copy-start.1 = (bf16[4,512,1536]{2,1,0:T(8,128)(2,1)}, bf16[4,512,1536]{2,1,0:T(8,128)(2,1)S(1)}, u32[]{:S(2)}) copy-start(bf16[4,512,1536]{2,1,0:T(8,128)(2,1)S(1)} %get-tuple-element.35.stem_out_ref) | copy-start | bytes 18874372
  61.2 2.1 %copy-start.22 = (bf16[2,544,1536]{2,1,0:T(8,128)(2,1)}, bf16[2,544,1536]{2,1,0:T(8,128)(2,1)S(1)}, u32[]{:S(2)}) copy-start(bf16[2,544,1536]{2,1,0:T(8,128)(2,1)S(1)} %get-tuple-element.33.normed_ref) | copy-start | bytes 10027012
  62.6 0.9 copy-start.5
  63.5 13.8 %copy-start.32 = (s32[1,1024]{1,0:T(1,128)S(1)}, s32[1,1024]{1,0:T(1,128)}, u32[]{:S(2)}) copy-start(s32[1,1024]{1,0:T(1,128)} %param.13) | copy-start | bytes 12292
  63.5 14.4 %copy-start.31 = (s32[1,1024]{1,0:T(1,128)S(1)}, s32[1,1024]{1,0:T(1,128)}, u32[]{:S(2)}) copy-start(s32[1,1024]{1,0:T(1,128)} %param.12) | copy-start | bytes 12292
  70.7 2.0 %copy-start.24 = (bf16[160,1536]{1,0:T(8,128)(2,1)}, bf16[160,1536]{1,0:T(8,128)(2,1)S(1)}, u32[]{:S(2)}) copy-start(bf16[160,1536]{1,0:T(8,128)(2,1)S(1)} %collective-permute-done.7.rest_2_) | copy-start | bytes 1474564
  75.4 24.1 %collective-permute-start.11 = (bf16[640,1536]{1,0:T(8,128)(2,1)}, bf16[640,1536]{1,0:T(8,128)(2,1)}, u32[]{:S(2)}, u32[]{:S(2)}) collective-permute-start(bf16[640,1536]{1,0:T(8,128)(2,1)} %constant_dynamic-update-slice_fusion), channel_id=1, source_target_pairs={{1,5},{2,6},{5,1},{6,2},{9,13},{10,14},{13,9},{14,10},{17,21},{18,... | collective-permute-start | bytes 5898248 | tf_op jit(solution)/shard_map/ppermute | solution.py:265
  78.7 19.3 %collective-permute-start.10 = (s32[1024]{0:T(1024)S(1)}, s32[1024]{0:T(1024)S(1)}, u32[]{:S(2)}, u32[]{:S(2)}) collective-permute-start(s32[1024]{0:T(1024)S(1)} %fusion.89), channel_id=1, source_target_pairs={{0,1},{3,2},{4,5},{7,6},{8,9},{11,10},{12,13},{15,14},{16,17},{19,... | collective-permute-start | bytes 12296 | tf_op jit(solution)/shard_map/ppermute | solution.py:260
  90.0 1.1 copy-start.6
  91.1 1.1 copy-start.9
  92.2 1.1 copy-start.12
  93.2 1.1 copy-start.15
  94.3 1.1 copy-start.18
  95.4 1.9 %copy-start.23 = (bf16[2,544,1536]{2,1,0:T(8,128)(2,1)S(1)}, bf16[2,544,1536]{2,1,0:T(8,128)(2,1)}, u32[]{:S(2)}) copy-start(bf16[2,544,1536]{2,1,0:T(8,128)(2,1)} %copy-done.22) | copy-start | bytes 10027012
  99.5 2.8 %copy-start.2 = (bf16[4,512,1536]{2,1,0:T(8,128)(2,1)S(1)}, bf16[4,512,1536]{2,1,0:T(8,128)(2,1)}, u32[]{:S(2)}) copy-start(bf16[4,512,1536]{2,1,0:T(8,128)(2,1)} %copy-done.1) | copy-start | bytes 18874372
  102.3 1.2 copy-start.19
  103.5 1.0 copy-start.25
  105.6 3.8 %collective-permute-start.12 = (f32[4,8,128]{2,1,0:T(8,128)S(1)}, f32[4,8,128]{2,1,0:T(8,128)S(1)}, u32[]{:S(2)}, u32[]{:S(2)}) collective-permute-start(f32[4,8,128]{2,1,0:T(8,128)S(1)} %shard_map.117), channel_id=1, source_target_pairs={{0,8},{8,0},{16,24},{24,16},{1,9},{9,1},{17,25},{25,17},{2,10},{10... | collective-permute-start | bytes 49160 | tf_op jit(solution)/shard_map/ppermute | solution.py:269
  107.1 3.7 %collective-permute-start.13 = (f32[4,8,128]{2,1,0:T(8,128)S(1)}, f32[4,8,128]{2,1,0:T(8,128)S(1)}, u32[]{:S(2)}, u32[]{:S(2)}) collective-permute-start(f32[4,8,128]{2,1,0:T(8,128)S(1)} %shard_map.117), channel_id=1, source_target_pairs={{0,16},{8,24},{16,0},{24,8},{1,17},{9,25},{17,1},{25,9},{2,18},{10... | collective-permute-start | bytes 49160 | tf_op jit(solution)/shard_map/ppermute | solution.py:269
  108.7 4.6 %collective-permute-start.14 = (f32[4,8,128]{2,1,0:T(8,128)S(1)}, f32[4,8,128]{2,1,0:T(8,128)S(1)}, u32[]{:S(2)}, u32[]{:S(2)}) collective-permute-start(f32[4,8,128]{2,1,0:T(8,128)S(1)} %shard_map.117), channel_id=1, source_target_pairs={{0,24},{8,16},{16,8},{24,0},{1,25},{9,17},{17,9},{25,1},{2,26},{10... | collective-permute-start | bytes 49160 | tf_op jit(solution)/shard_map/ppermute | solution.py:269
  114.6 34.6 %collective-permute-start.15 = (f32[1025]{0:T(1024)S(1)}, f32[1025]{0:T(1024)S(1)}, u32[]{:S(2)}, u32[]{:S(2)}) collective-permute-start(f32[1025]{0:T(1024)S(1)} %pad_maximum_fusion.19), channel_id=1, source_target_pairs={{1,0},{2,3},{5,4},{6,7},{9,8},{10,11},{13,12},{14,15},{17,16},{18,... | collective-permute-start | bytes 12308 | tf_op jit(solution)/shard_map/ppermute | solution.py:260
  115.9 2.5 %collective-permute-start.16 = (f32[1]{0:T(128)}, f32[1]{0:T(128)}, u32[]{:S(2)}, u32[]{:S(2)}) collective-permute-start(f32[1]{0:T(128)} %bitcast.31), channel_id=1, source_target_pairs={{1,2},{2,1},{5,6},{6,5},{9,10},{10,9},{13,14},{14,13},{17,18},{18,... | collective-permute-start | bytes 20 | tf_op jit(solution)/shard_map/ppermute | solution.py:260
  117.1 30.9 %collective-permute-start.17 = (f32[1]{0:T(128)}, f32[1]{0:T(128)}, u32[]{:S(2)}, u32[]{:S(2)}) collective-permute-start(f32[1]{0:T(128)} %bitcast.31), channel_id=1, source_target_pairs={{2,0},{1,3},{6,4},{5,7},{10,8},{9,11},{14,12},{13,15},{18,16},{17,... | collective-permute-start | bytes 20 | tf_op jit(solution)/shard_map/ppermute | solution.py:260

commit v4 on v3

--- a/solution.py
+++ b/solution.py
@@ -24,6 +24,19 @@
     return 0.5 * jnp.tanh(0.5 * x) + 0.5
 
 
+def weave(*tracks):
+    steps = [((i + 0.5) / len(track), k, step) for k, track in enumerate(tracks) for i, step in enumerate(track)]
+    for _, _, step in sorted(steps, key=lambda entry: entry[:2]):
+        step()
+
+
+def column_steps(left, right, into, block):
+    def step(at):
+        into[:, at : at + block] = jnp.dot(left(), right[:, at : at + block], preferred_element_type=jnp.float32)
+
+    return [functools.partial(step, at) for at in range(0, right.shape[1], block)]
+
+
 def stem_kernel(first_slot, meta, main_ref, margin_ref, stem_ref, gain_ref, *rest):
     stem_out_ref, normed_ref, acc_a, acc_b, acc_c = rest[-5:]
     slot = pl.program_id(0) + first_slot
@@ -31,32 +44,31 @@
     part = acc_a.shape[0]
     group = 16
 
+    def norm_step(acc, at, keep, row):
+        stem_out = acc[row : row + group, :].astype(jnp.bfloat16)
+        if keep:
+            stem_out_ref[0, at + row : at + row + group, :] = stem_out
+        normed_ref[0, at + row : at + row + group, :] = norm_rows(stem_out.astype(jnp.float32), gain_ref[0:1, :])
+
     def norm(acc, at, keep):
-        for row in range(0, acc.shape[0], group):
-            stem_out = acc[row : row + group, :].astype(jnp.bfloat16)
-            if keep:
-                stem_out_ref[0, at + row : at + row + group, :] = stem_out
-            normed_ref[0, at + row : at + row + group, :] = norm_rows(stem_out.astype(jnp.float32), gain_ref[0:1, :])
+        return [functools.partial(norm_step, acc, at, keep, row) for row in range(0, acc.shape[0], group)]
 
     @pl.when(meta[5 + slot] > 0)
     def _():
-        for acc, at in ((acc_a, 0), (acc_b, part)):
-            acc[...] = jnp.dot(main_ref[0, at : at + part, :], stem_ref[...], preferred_element_type=jnp.float32)
-        norm(acc_a, 0, True)
-        acc_c[...] = jnp.dot(margin_ref[0], stem_ref[...], preferred_element_type=jnp.float32)
-        norm(acc_b, part, True)
-        norm(acc_c, frames, False)
+        block = 2 * LANES
+        weave(column_steps(lambda: main_ref[0, :part, :], stem_ref, acc_a, block))
+        weave(column_steps(lambda: main_ref[0, part:, :], stem_ref, acc_b, block), norm(acc_a, 0, True))
+        weave(column_steps(lambda: margin_ref[0], stem_ref, acc_c, block), norm(acc_b, part, True))
+        weave(norm(acc_c, frames, False))
 
 
 def shards(meta, pieces):
     side = meta[13]
-    length = pieces[0].shape[0]
-    mine = [(pieces[i], 0, side * 4 + meta[9 + i]) for i in range(4)]
-    return mine + [(pieces[4], i * length, (1 - side) * 4 + meta[9 + i]) for i in range(4)]
+    return [(pieces[i], (side if i < 4 else 1 - side) * 4 + meta[9 + i % 4]) for i in range(8)]
 
 
 def conv_kernel(first_slot, meta, normed_ref, taps_ref, *rest):
-    pieces = rest[:5]
+    pieces = rest[:8]
     swished_ref, weight, mixed_a, mixed_b, gated, margin, mask, sems = rest[-8:]
     slot = pl.program_id(0) + first_slot
     rows = normed_ref.shape[1]
@@ -71,9 +83,9 @@
     def _():
         copies = [
             pltpu.make_async_copy(
-                ref.at[pl.ds(at, piece)], weight.at[pl.ds(pl.multiple_of(block * piece, 16), piece)], sems.at[i]
+                ref, weight.at[pl.ds(pl.multiple_of(block * piece, 16), piece)], sems.at[i]
             )
-            for i, (ref, at, block) in enumerate(shards(meta, pieces))
+            for i, (ref, block) in enumerate(shards(meta, pieces))
         ]
         for copy in copies:
             copy.start()
@@ -92,15 +104,23 @@
 
         def mix(block):
             low = block * LANES
-            right = jnp.concatenate(
-                [weight[:, low : low + LANES], weight[:, channels + low : channels + low + LANES]], axis=1
-            )
-            buffers[block % 2][...] = jnp.dot(normed_ref[0], right, preferred_element_type=jnp.float32)
+            half = rows // 2
+
+            def step(at):
+                right = jnp.concatenate(
+                    [weight[:, low : low + LANES], weight[:, channels + low : channels + low + LANES]], axis=1
+                )
+                buffers[block % 2][at : at + half, :] = jnp.dot(
+                    normed_ref[0, at : at + half, :], right, preferred_element_type=jnp.float32
+                )
+
+            return [functools.partial(step, at) for at in (0, half)]
 
         def gate(block):
             mixed = buffers[block % 2]
             group = 32
-            for at in range(0, rows, group):
+
+            def step(at):
                 here = slice(at, at + group)
                 made = mixed[here, :LANES] * sigmoid(mixed[here, LANES:]) * mask[here, :]
                 made = made.astype(jnp.bfloat16).astype(jnp.float32)
@@ -109,7 +129,8 @@
                     gated[first : first + group // CHUNKS] = made.reshape(group // CHUNKS, CHUNKS, LANES)
                 else:
                     margin[...] = made
-            for i in range(reach):
+
+            def sides(i):
                 before = pltpu.roll(gated[run_length + i], 1, 0)
                 edge = margin[EDGE - reach + i : EDGE - reach + i + 1, :]
                 gated[i] = jnp.where(sublane == 0, edge, before)
@@ -117,10 +138,15 @@
                 edge = margin[EDGE + i : EDGE + i + 1, :]
                 gated[reach + run_length + i] = jnp.where(sublane == CHUNKS - 1, edge, after)
 
+            return [functools.partial(step, at) for at in range(0, rows, group)] + [
+                functools.partial(sides, i) for i in range(reach)
+            ]
+
         def convolve(block):
             low = block * LANES
             run = 16
-            for start in range(0, run_length, run):
+
+            def step(start):
                 sums = [None] * run
                 for at in range(start, start + run + tap_count - 1):
                     value = gated[at]
@@ -135,18 +161,17 @@
                         total * sigmoid(total)
                     ).astype(jnp.bfloat16)
 
+            return [functools.partial(step, start) for start in range(0, run_length, run)]
+
         blocks = channels // LANES
-        mix(0)
+        weave(mix(0))
         for block in range(blocks):
-            if block + 1 < blocks:
-                mix(block + 1)
-            gate(block)
-            convolve(block)
+            weave(gate(block) + convolve(block), mix(block + 1) if block + 1 < blocks else [])
 
 
 def head_kernel(meta, swished_ref, stem_out_ref, code_ref, gain_ref, *rest):
-    pieces = rest[:5]
-    error_ref, back, head, acc_a, acc_b, norm_a, norm_b, logit_a, logit_b, sems = rest[5:]
+    pieces = rest[:8]
+    error_ref, back, head, acc_a, acc_b, norm_a, norm_b, logit_a, logit_b, sems = rest[8:]
     slot = pl.program_id(0)
     frames = swished_ref.shape[1]
     vocab = head.shape[1]
@@ -158,10 +183,10 @@
     @pl.when(jnp.logical_and(pl.program_id(0) == 0, meta[14] > 0))
     def _():
         copies = []
-        for i, (ref, at, block) in enumerate(shards(meta, pieces)):
+        for i, (ref, block) in enumerate(shards(meta, pieces)):
             copies.append(
                 pltpu.make_async_copy(
-                    ref.at[pl.ds(at, back_rows)],
+                    ref.at[pl.ds(0, back_rows)],
                     back.at[pl.ds(pl.multiple_of(block * back_rows, 16), back_rows)],
                     sems.at[i, 0],
                 )
@@ -169,7 +194,7 @@
             for g in range(groups):
                 copies.append(
                     pltpu.make_async_copy(
-                        ref.at[pl.ds(at + back_rows, group_rows), pl.ds(g * vocab, vocab)],
+                        ref.at[pl.ds(back_rows, group_rows), pl.ds(g * vocab, vocab)],
                         head.at[pl.ds(pl.multiple_of(block * head_rows + g * group_rows, 16), group_rows)],
                         sems.at[i, 1 + g],
                     )
@@ -187,37 +212,43 @@
     def _():
         part = acc_a.shape[0]
         lane = lax.broadcasted_iota(jnp.int32, (CHUNKS, LANES), 1)
-        halves = ((0, acc_a, norm_a, logit_a), (part, acc_b, norm_b, logit_b))
+        error_ref[...] = jnp.zeros_like(error_ref)
 
         def norm(at, acc, normed):
             group = 16
-            for row in range(0, part, group):
+
+            def step(row):
                 values = acc[row : row + group, :] + stem_out_ref[0, at + row : at + row + group, :].astype(jnp.float32)
                 normed[row : row + group, :] = norm_rows(values, gain_ref[1:2, :])
+
+            return [functools.partial(step, row) for row in range(0, part, group)]
 
         def errors(at, logits):
             group = 32
             token = lax.broadcasted_iota(jnp.int32, (group, vocab), 1)
-            row = jnp.zeros((CHUNKS, LANES), jnp.float32)
-            for first in range(0, part, group):
+
+            def step(first):
                 scores = logits[first : first + group, :]
                 grown = jnp.exp(scores - jnp.max(scores, axis=-1, keepdims=True))
                 posterior = grown * (1.0 / jnp.sum(grown, axis=-1, keepdims=True))
-                code = code_ref[0, at + first : at + first + group, :]
+                steps = range((at + first) // CHUNKS, (at + first + group) // CHUNKS)
+                code = jnp.concatenate([code_ref[0, :, m : m + 1] for m in steps], axis=0)
                 differ = posterior - (token == code).astype(jnp.float32)
                 error = jnp.sqrt(jnp.sum(differ * differ, axis=-1, keepdims=True))
                 error = jnp.where(code >= 0, error, 0.0)
-                for m in range(group // CHUNKS):
-                    step = error[m * CHUNKS : (m + 1) * CHUNKS, :]
-                    row = row + jnp.where(lane == (at + first) // CHUNKS + m, step, 0.0)
-            return row
-
-        for at, acc, _, _ in halves:
-            acc[...] = jnp.dot(swished_ref[0, at : at + part, :], back[...], preferred_element_type=jnp.float32)
-        for at, acc, normed, logits in halves:
-            norm(at, acc, normed)
-            logits[...] = jnp.dot(normed[...], head[...], preferred_element_type=jnp.float32)
-        error_ref[0] = errors(0, logit_a) + errors(part, logit_b)
+                row = error_ref[0]
+                for k, m in enumerate(steps):
+                    row = jnp.where(lane == m, error[k * CHUNKS : (k + 1) * CHUNKS, :], row)
+                error_ref[0] = row
+
+            return [functools.partial(step, first) for first in range(0, part, group)]
+
+        block = 2 * LANES
+        weave(column_steps(lambda: swished_ref[0, :part, :], back, acc_a, block))
+        weave(column_steps(lambda: swished_ref[0, part:, :], back, acc_b, block), norm(0, acc_a, norm_a))
+        weave(column_steps(lambda: norm_a[...], head, logit_a, block), norm(part, acc_b, norm_b))
+        weave(column_steps(lambda: norm_b[...], head, logit_b, block), errors(0, logit_a))
+        weave(errors(part, logit_b))
 
 
 def call(kernel, grid, in_specs, out_specs, out_shape, scratch, flops, moved, operands, aliases={}):
@@ -312,9 +343,7 @@
         ],
         axis=0,
     )
-    second_held, before, after, hub_first = lax.optimization_barrier((second, before, after, hub_first))
-    near_second = along(second_held, INWARD)
-    far_second = along(second_held, BEYOND)
+    mates = [to_mate(x) for x in (first, near_first, hub_first)]
 
     slots = 4
     deep = tile + 2 * EDGE
@@ -372,23 +401,23 @@
         )
 
     apart = pl.BlockSpec(memory_space=pl.ANY)
-    stem_out, own_normed = stems(0, *paired(before, blocks, after))
-
-    near_first, far_first, outer, own_normed = lax.optimization_barrier((near_first, far_first, outer, own_normed))
-    mine = [first, near_first, hub_first, far_first]
-    first_pieces = (*mine, to_mate(jnp.concatenate(mine, axis=0)))
-    second_late, _ = lax.optimization_barrier((second, outer))
-    hub_second = along(second_late, ACROSS)
-
+    pinned = pl.BlockSpec(memory_space=pltpu.HBM)
+    own_pairs, mates = lax.optimization_barrier((paired(before, blocks, after), mates))
+    stem_out, own_normed = stems(0, *own_pairs)
+
+    far_first, outer, own_normed = lax.optimization_barrier((far_first, outer, own_normed))
+    first_pieces = (first, near_first, hub_first, far_first, *mates, to_mate(far_first))
     none = jnp.zeros_like(before)
     outer_before = jnp.where(low, none, blocks[-EDGE:])
     outer_after = jnp.where(low, blocks[:EDGE], none)
-    stem_out, outer_normed = stems(1, *paired(outer_before, outer, outer_after), stem_out)
+    outer_pairs = paired(outer_before, outer, outer_after)
+    second_held, outer_pairs = lax.optimization_barrier((second, outer_pairs))
+    near_second, hub_second, far_second = [along(second_held, pairs) for pairs in (INWARD, ACROSS, BEYOND)]
+    second_mate = to_mate(second_held)
+    stem_out, outer_normed = stems(1, *outer_pairs, stem_out)
 
     code_held, _ = lax.optimization_barrier((code, first_pieces[-1]))
-    outer_code = along(code_held, INWARD)
-    codes = jnp.concatenate([code, outer_code])
-    codes = codes.reshape(slots, CHUNKS, tile // CHUNKS).transpose(0, 2, 1).reshape(slots, tile, 1)
+    codes = jnp.concatenate([code, along(code_held, INWARD)]).reshape(slots, CHUNKS, tile // CHUNKS)
 
     taps = jnp.broadcast_to(
         depth_weight[0].astype(jnp.float32)[:, None, :], (depth_weight.shape[1], CHUNKS, channels)
@@ -398,7 +427,7 @@
         return call(
             functools.partial(conv_kernel, 2 * part),
             (2,),
-            [by_slot((deep, width)), whole(taps.shape)] + [apart] * (5 + len(made)),
+            [by_slot((deep, width)), whole(taps.shape)] + [pinned] * 8 + [apart] * len(made),
             by_slot((tile, channels), 2 * part),
             jax.ShapeDtypeStruct((slots, tile, channels), jnp.bfloat16),
             [
@@ -413,20 +442,20 @@
             slots * deep * width * 2 * channels,
             slots * deep * width + 8 * first.size * 2,
             (meta, normed, taps, *pieces, *made),
-            {8: 0} if made else {},
+            {11: 0} if made else {},
         )
 
     swished = convolve(0, own_normed, first_pieces)
     near_second, hub_second, far_second, swished, outer_normed = lax.optimization_barrier(
         (near_second, hub_second, far_second, swished, outer_normed)
     )
-    mine = [second, near_second, hub_second, far_second]
-    second_pieces = (*mine, to_mate(jnp.concatenate(mine, axis=0)))
+    second_rest = [near_second, hub_second, far_second]
+    second_pieces = (second, *second_rest, second_mate, *[to_mate(x) for x in second_rest])
     swished = convolve(1, outer_normed, first_pieces, swished)
     errors = call(
         head_kernel,
         (slots,),
-        [by_slot((tile, channels)), by_slot((tile, width)), by_slot((tile, 1)), whole(gains.shape)] + [apart] * 5,
+        [by_slot((tile, channels)), by_slot((tile, width)), by_slot(codes.shape[1:]), whole(gains.shape)] + [pinned] * 8,
         by_slot((CHUNKS, LANES)),
         jax.ShapeDtypeStruct((slots, CHUNKS, LANES), jnp.float32),
         [

time: 154 us -> 154 us (level)
  starting transfers between devices: 50.1 us -> 62.7 us
  local copies, waits for them, and re-layouts: 40.4 us -> 28.1 us
  waiting for transfers between devices: 44.2 us -> 47.1 us
  other arithmetic: 8.95 us -> 6.66 us
    unnamed x77 -> x52, local copies, waits for them, and re-layouts: 29.3 us -> 20.3 us
    ppermute x13, starting transfers between devices: 42.6 us -> 48.9 us  [along(): return lax.ppermute(x, 'seq', pairs)]
    ppermute x2 -> x8, starting transfers between devices: 3.97 us -> 10.3 us  [to_mate(): return lax.ppermute(x, ('fsdp', 'seq'), pairs)]
    ppermute x13, waiting for transfers between devices: 40 us -> 43 us  [along(): return lax.ppermute(x, 'seq', pairs)]
    concatenate x2 -> x1, local copies, waits for them, and re-layouts: 1.91 us -> 0.07 us  [hub_body(): jnp.concatenate([code, along(code_held, INWARD)])]
    concatenate x1, other arithmetic: 1.69 us -> 0.01 us  [hub_body(): jnp.concatenate([code, along(code_held, INWARD)])]
  transfers between devices with their start and end apart: 18 -> 24, of which waited for: 6 -> 7; matrix products, arithmetic and copies ran while one was open for 13% -> 10% of each run, Pallas kernels for 2% -> 2%
where the time goes in v4:
time: 154 us
  starting transfers between devices  62.7 us (41%)
  waiting for transfers between devices  47.1 us (31%)
  local copies, waits for them, and re-layouts  28.1 us (18%)
  other arithmetic  6.66 us (4%)
  between operations  5.48 us (4%)
  Pallas kernels  3.64 us (2%)
    ppermute x13, starting transfers between devices, along(): return lax.ppermute(x, 'seq', pairs)  48.9 us
    ppermute x13, waiting for transfers between devices, along(): return lax.ppermute(x, 'seq', pairs)  43 us
    unnamed x52, local copies, waits for them, and re-layouts  20.3 us
    ppermute x8, starting transfers between devices, to_mate(): return lax.ppermute(x, ('fsdp', 'seq'), pairs)  10.3 us
    ppermute x3, waiting for transfers between devices, seed_swap(): return lax.ppermute(x, 'seed', [(i, i ^ bit) for i in range(4)])  4.15 us
    pallas_call x5, Pallas kernels, call(): pl.pallas_call(kernel, grid_spec=pltpu.PrefetchScalarGridSpec(num_scalar_...  3.64 us
    ppermute x3, starting transfers between devices, seed_swap(): return lax.ppermute(x, 'seed', [(i, i ^ bit) for i in range(4)])  3.55 us
  transfers between devices with their start and end apart: 24, of which 7 were waited for; matrix products, arithmetic and copies ran while one was open for 10% of the time, Pallas kernels for 2%

profile of v4, /device:TPU:0, one launch (start us, length us, event | category | flops | bytes accessed | tf_op | source)
XLA Modules:
  0.0 153.7 jit_solution(14213489282346317201)
XLA Ops:
  0.6 5.0 %collective-permute-start = (bf16[192,1536]{1,0:T(8,128)(2,1)}, bf16[192,1536]{1,0:T(8,128)(2,1)S(1)}, u32[]{:S(2)}, u32[]{:S(2)}) collective-permute-start(bf16[192,1536]{1,0:T(8,128)(2,1)} %bitcast.58), channel_id=1, source_target_pairs={{0,1},{3,2},{4,5},{7,6},{8,9},{11,10},{12,13},{15,14},{16,17},{19,... | collective-permute-start | bytes 1769480 | tf_op jit(solution)/shard_map/ppermute | solution.py:291
  5.6 0.7 collective-permute-start.7
  6.3 1.5 collective-permute-start.5
  7.8 0.8 fusion.93
  8.8 1.3 collective-permute-start.4
  10.3 5.1 %collective-permute-start.3 = (bf16[16,320]{1,0:T(8,128)(2,1)S(1)}, bf16[16,320]{1,0:T(8,128)(2,1)S(1)}, u32[]{:S(2)}, u32[]{:S(2)}) collective-permute-start(bf16[16,320]{1,0:T(8,128)(2,1)S(1)} %slice.75), channel_id=1, source_target_pairs={{0,1},{1,2},{2,3},{4,5},{5,6},{6,7},{8,9},{9,10},{10,11},{12,13},{... | collective-permute-start | bytes 30728 | tf_op jit(solution)/shard_map/ppermute | solution.py:291
  15.4 1.6 %copy.25 = bf16[1,4096,80]{2,1,0:T(8,128)(2,1)S(1)} copy(bf16[1,4096,80]{1,2,0:T(8,128)(2,1)} %param.10) | data formatting | bytes 1310720 | tf_op args[0]
  17.0 0.7 reshape_squeeze.7
  17.7 2.0 %fusion.92 = (bf16[1024,640]{1,0:T(8,128)(2,1)}, bf16[1024,640]{1,0:T(8,128)(2,1)}) fusion(bf16[1024,320]{1,0:T(8,128)(2,1)S(1)} %reshape_squeeze.7), kind=kLoop, calls=%fused_computation.130 | loop fusion | bytes 3276800
  20.4 0.8 maximum_maximum_fusion.rest_0_
  21.3 0.7 fusion.90
  22.0 1.1 copy.26
  23.1 0.7 concatenate.49.meta
  23.9 4.8 %collective-permute-start.2 = (bf16[1024,320]{0,1:T(8,128)(2,1)}, bf16[1024,320]{0,1:T(8,128)(2,1)}, u32[]{:S(2)}, u32[]{:S(2)}) collective-permute-start(bf16[1024,320]{0,1:T(8,128)(2,1)} %copy.26), channel_id=1, source_target_pairs={{0,1},{3,2},{4,5},{7,6},{8,9},{11,10},{12,13},{15,14},{16,17},{19,... | collective-permute-start | bytes 1966088 | tf_op jit(solution)/shard_map/ppermute | solution.py:291
  28.7 0.7 collective-permute-start.6
  29.4 1.5 collective-permute-start.1
  30.9 0.7 collective-permute-start.8
  31.6 0.6 fusion.1
  32.3 0.7 copy.35
  33.1 0.3 copy-done.18
  33.4 1.1 fusion.48
  34.6 0.8 copy-done.12
  35.5 0.6 shard_map.113
  36.3 2.7 %copy-done = bf16[4,512,1536]{2,1,0:T(8,128)(2,1)} copy-done((bf16[4,512,1536]{2,1,0:T(8,128)(2,1)}, bf16[4,512,1536]{2,1,0:T(8,128)(2,1)S(1)}, u32[]{:S(2)}) %copy-start) | copy-done | bytes 6291480
  39.0 1.8 %copy-done.5 = bf16[2,544,1536]{2,1,0:T(8,128)(2,1)} copy-done((bf16[2,544,1536]{2,1,0:T(8,128)(2,1)}, bf16[2,544,1536]{2,1,0:T(8,128)(2,1)S(1)}, u32[]{:S(2)}) %copy-start.5) | copy-done | bytes 3342360
  40.7 1.4 collective-permute-done.2
  42.2 1.4 copy.29
  43.6 0.5 fusion.91
  44.1 1.5 collective-permute-start.12
  45.6 0.6 fusion
  46.5 0.7 copy.34
  47.3 1.5 collective-permute-start.10
  48.8 10.3 %collective-permute-start.11 = (bf16[160,1536]{1,0:T(8,128)(2,1)}, bf16[160,1536]{1,0:T(8,128)(2,1)}, u32[]{:S(2)}, u32[]{:S(2)}) collective-permute-start(bf16[160,1536]{1,0:T(8,128)(2,1)} %maximum_maximum_fusion.rest_0_), channel_id=1, source_target_pairs={{0,2},{3,1},{4,6},{7,5},{8,10},{11,9},{12,14},{15,13},{16,18},{19,... | collective-permute-start | bytes 1474568 | tf_op jit(solution)/shard_map/ppermute | solution.py:291
  59.1 2.1 %collective-permute-start.9 = (bf16[160,1536]{1,0:T(8,128)(2,1)}, bf16[160,1536]{1,0:T(8,128)(2,1)}, u32[]{:S(2)}, u32[]{:S(2)}) collective-permute-start(bf16[160,1536]{1,0:T(8,128)(2,1)} %maximum_maximum_fusion.rest_0_), channel_id=1, source_target_pairs={{0,1},{3,2},{4,5},{7,6},{8,9},{11,10},{12,13},{15,14},{16,17},{19,... | collective-permute-start | bytes 1474568 | tf_op jit(solution)/shard_map/ppermute | solution.py:291
  61.3 0.5 broadcast.101
  61.8 0.7 reduce.7
  62.6 1.5 collective-permute-start.14
  64.0 2.8 %copy-done.1 = bf16[4,512,1536]{2,1,0:T(8,128)(2,1)S(1)} copy-done((bf16[4,512,1536]{2,1,0:T(8,128)(2,1)S(1)}, bf16[4,512,1536]{2,1,0:T(8,128)(2,1)}, u32[]{:S(2)}) %copy-start.1) | copy-done | bytes 6291480
  66.9 0.6 shard_map.115
  67.5 3.2 %copy-done.2 = bf16[4,512,1536]{2,1,0:T(8,128)(2,1)} copy-done((bf16[4,512,1536]{2,1,0:T(8,128)(2,1)}, bf16[4,512,1536]{2,1,0:T(8,128)(2,1)S(1)}, u32[]{:S(2)}) %copy-start.2) | copy-done | bytes 6291480
  70.8 0.6 copy-done.11
  71.9 0.7 shard_map.114.rest_8_
  72.6 7.2 %collective-permute-done.9.rest_1_ = bf16[160,1536]{1,0:T(8,128)(2,1)} collective-permute-done((bf16[160,1536]{1,0:T(8,128)(2,1)}, bf16[160,1536]{1,0:T(8,128)(2,1)}, u32[]{:S(2)}, u32[]{:S(2)}) %collective-permute-start.9) | collective-permute-done | bytes 491552 | tf_op jit(solution)/shard_map/ppermute | solution.py:291
  79.8 1.5 collective-permute-start.15
  81.3 1.5 collective-permute-start.16
  82.7 1.5 collective-permute-start.17
  84.2 13.0 %collective-permute-start.13 = (s32[1024]{0:T(1024)S(1)}, s32[1024]{0:T(1024)S(1)}, u32[]{:S(2)}, u32[]{:S(2)}) collective-permute-start(s32[1024]{0:T(1024)S(1)} %fusion.89), channel_id=1, source_target_pairs={{0,1},{3,2},{4,5},{7,6},{8,9},{11,10},{12,13},{15,14},{16,17},{19,... | collective-permute-start | bytes 12296 | tf_op jit(solution)/shard_map/ppermute | solution.py:291
  97.2 0.7 shard_map.116.swished_ref
  97.9 0.4 collective-permute-done.13
  98.4 2.8 %copy-done.3 = bf16[4,512,1536]{2,1,0:T(8,128)(2,1)S(1)} copy-done((bf16[4,512,1536]{2,1,0:T(8,128)(2,1)S(1)}, bf16[4,512,1536]{2,1,0:T(8,128)(2,1)}, u32[]{:S(2)}) %copy-start.3) | copy-done | bytes 6291480
  101.1 1.0 shard_map.117
  102.2 1.5 %collective-permute-start.18 = (f32[4,8,128]{2,1,0:T(8,128)S(1)}, f32[4,8,128]{2,1,0:T(8,128)S(1)}, u32[]{:S(2)}, u32[]{:S(2)}) collective-permute-start(f32[4,8,128]{2,1,0:T(8,128)S(1)} %shard_map.117), channel_id=1, source_target_pairs={{0,8},{8,0},{16,24},{24,16},{1,9},{9,1},{17,25},{25,17},{2,10},{10... | collective-permute-start | bytes 49160 | tf_op jit(solution)/shard_map/ppermute | solution.py:300
  103.7 1.5 collective-permute-start.19
  105.2 0.5 collective-permute-start.20
  106.0 1.5 collective-permute-done.19
  107.5 2.4 %collective-permute-done.20 = f32[4,8,128]{2,1,0:T(8,128)S(1)} collective-permute-done((f32[4,8,128]{2,1,0:T(8,128)S(1)}, f32[4,8,128]{2,1,0:T(8,128)S(1)}, u32[]{:S(2)}, u32[]{:S(2)}) %collective-permute-start.20) | collective-permute-done | bytes 16416 | tf_op jit(solution)/shard_map/ppermute | solution.py:300
  109.9 0.6 slice_reduce_fusion
  110.6 0.6 pad_maximum_fusion.18
  111.2 1.3 collective-permute-start.21
  112.5 1.1 collective-permute-start.22
  113.7 1.3 collective-permute-start.23
  115.0 33.9 %collective-permute-done.23 = f32[1]{0:T(128)} collective-permute-done((f32[1]{0:T(128)}, f32[1]{0:T(128)}, u32[]{:S(2)}, u32[]{:S(2)}) %collective-permute-start.23) | collective-permute-done | bytes 36 | tf_op jit(solution)/shard_map/ppermute | solution.py:291
  150.1 0.5 slice.100
  152.0 0.6 slice_select_fusion
  (87 shorter events, 2.5 us)
Async XLA Ops:
  0.6 28.0 %collective-permute-start = (bf16[192,1536]{1,0:T(8,128)(2,1)}, bf16[192,1536]{1,0:T(8,128)(2,1)S(1)}, u32[]{:S(2)}, u32[]{:S(2)}) collective-permute-start(bf16[192,1536]{1,0:T(8,128)(2,1)} %bitcast.58), channel_id=1, source_target_pairs={{0,1},{3,2},{4,5},{7,6},{8,9},{11,10},{12,13},{15,14},{16,17},{19,... | collective-permute-start | bytes 1769480 | tf_op jit(solution)/shard_map/ppermute | solution.py:291
  5.6 25.3 %collective-permute-start.7 = (bf16[192,1536]{1,0:T(8,128)(2,1)}, bf16[192,1536]{1,0:T(8,128)(2,1)S(1)}, u32[]{:S(2)}, u32[]{:S(2)}) collective-permute-start(bf16[192,1536]{1,0:T(8,128)(2,1)} %bitcast.59), channel_id=1, source_target_pairs={{1,2},{2,1},{5,6},{6,5},{9,10},{10,9},{13,14},{14,13},{17,18},{18,... | collective-permute-start | bytes 1769480 | tf_op jit(solution)/shard_map/ppermute | solution.py:291
  6.3 28.3 %collective-permute-start.5 = (bf16[192,1536]{1,0:T(8,128)(2,1)}, bf16[192,1536]{1,0:T(8,128)(2,1)}, u32[]{:S(2)}, u32[]{:S(2)}) collective-permute-start(bf16[192,1536]{1,0:T(8,128)(2,1)} %bitcast.60), channel_id=1, source_target_pairs={{1,5},{2,6},{5,1},{6,2},{9,13},{10,14},{13,9},{14,10},{17,21},{18,... | collective-permute-start | bytes 1769480 | tf_op jit(solution)/shard_map/ppermute | solution.py:296
  8.8 15.0 %collective-permute-start.4 = (bf16[16,320]{1,0:T(8,128)(2,1)S(1)}, bf16[16,320]{1,0:T(8,128)(2,1)S(1)}, u32[]{:S(2)}, u32[]{:S(2)}) collective-permute-start(bf16[16,320]{1,0:T(8,128)(2,1)S(1)} %reshape_squeeze.8), channel_id=1, source_target_pairs={{1,0},{2,1},{3,2},{5,4},{6,5},{7,6},{9,8},{10,9},{11,10},{13,12},{... | collective-permute-start | bytes 30728 | tf_op jit(solution)/shard_map/ppermute | solution.py:291
  10.3 19.1 %collective-permute-start.3 = (bf16[16,320]{1,0:T(8,128)(2,1)S(1)}, bf16[16,320]{1,0:T(8,128)(2,1)S(1)}, u32[]{:S(2)}, u32[]{:S(2)}) collective-permute-start(bf16[16,320]{1,0:T(8,128)(2,1)S(1)} %slice.75), channel_id=1, source_target_pairs={{0,1},{1,2},{2,3},{4,5},{5,6},{6,7},{8,9},{9,10},{10,11},{12,13},{... | collective-permute-start | bytes 30728 | tf_op jit(solution)/shard_map/ppermute | solution.py:291
  17.7 13.9 %copy-start.17 = (bf16[1024,320]{1,0:T(8,128)(2,1)}, bf16[1024,320]{1,0:T(8,128)(2,1)S(1)}, u32[]{:S(2)}) copy-start(bf16[1024,320]{1,0:T(8,128)(2,1)S(1)} %reshape_squeeze.7) | copy-start | bytes 1966084
  17.7 2.7 %copy-start.20 = (bf16[1,192,512]{2,1,0:T(8,128)(2,1)S(1)}, bf16[1,192,512]{2,1,0:T(8,128)(2,1)}, u32[]{:S(2)}) copy-start(bf16[1,192,512]{2,1,0:T(8,128)(2,1)} %param.18) | copy-start | bytes 589828
  17.7 2.7 %copy-start.19 = (bf16[1,96,1536]{2,1,0:T(8,128)(2,1)S(1)}, bf16[1,96,1536]{2,1,0:T(8,128)(2,1)}, u32[]{:S(2)}) copy-start(bf16[1,96,1536]{2,1,0:T(8,128)(2,1)} %param.16) | copy-start | bytes 884740
  23.9 18.3 %collective-permute-start.2 = (bf16[1024,320]{0,1:T(8,128)(2,1)}, bf16[1024,320]{0,1:T(8,128)(2,1)}, u32[]{:S(2)}, u32[]{:S(2)}) collective-permute-start(bf16[1024,320]{0,1:T(8,128)(2,1)} %copy.26), channel_id=1, source_target_pairs={{0,1},{3,2},{4,5},{7,6},{8,9},{11,10},{12,13},{15,14},{16,17},{19,... | collective-permute-start | bytes 1966088 | tf_op jit(solution)/shard_map/ppermute | solution.py:291
  28.7 3.6 %copy-start.8 = (bf16[192,1536]{1,0:T(8,128)(2,1)}, bf16[192,1536]{1,0:T(8,128)(2,1)S(1)}, u32[]{:S(2)}) copy-start(bf16[192,1536]{1,0:T(8,128)(2,1)S(1)} %collective-permute-done.rest_1_) | copy-start | bytes 1769476
  28.7 6.0 %collective-permute-start.6 = (bf16[192,1536]{1,0:T(8,128)(2,1)S(1)}, bf16[192,1536]{1,0:T(8,128)(2,1)S(1)}, u32[]{:S(2)}, u32[]{:S(2)}) collective-permute-start(bf16[192,1536]{1,0:T(8,128)(2,1)S(1)} %collective-permute-done.rest_1_), channel_id=1, source_target_pairs={{1,5},{2,6},{5,1},{6,2},{9,13},{10,14},{13,9},{14,10},{17,21},{18,... | collective-permute-start | bytes 1769480 | tf_op jit(solution)/shard_map/ppermute | solution.py:296
  29.4 12.8 %collective-permute-start.1 = (bf16[192,1536]{1,0:T(8,128)(2,1)S(1)}, bf16[192,1536]{1,0:T(8,128)(2,1)}, u32[]{:S(2)}, u32[]{:S(2)}) collective-permute-start(bf16[192,1536]{1,0:T(8,128)(2,1)S(1)} %collective-permute-done.rest_1_), channel_id=1, source_target_pairs={{1,2},{2,1},{5,6},{6,5},{9,10},{10,9},{13,14},{14,13},{17,18},{18,... | collective-permute-start | bytes 1769480 | tf_op jit(solution)/shard_map/ppermute | solution.py:291
  30.9 1.4 copy-start.10
  30.9 4.6 %collective-permute-start.8 = (bf16[192,1536]{1,0:T(8,128)(2,1)S(1)}, bf16[192,1536]{1,0:T(8,128)(2,1)S(1)}, u32[]{:S(2)}, u32[]{:S(2)}) collective-permute-start(bf16[192,1536]{1,0:T(8,128)(2,1)S(1)} %collective-permute-done.7.rest_2_), channel_id=1, source_target_pairs={{1,5},{2,6},{5,1},{6,2},{9,13},{10,14},{13,9},{14,10},{17,21},{18,... | collective-permute-start | bytes 1769480 | tf_op jit(solution)/shard_map/ppermute | solution.py:296
  32.3 1.1 copy-start.18
  33.1 2.4 %copy-start.4 = (bf16[1,640,1536]{2,1,0:T(8,128)(2,1)S(1)}, bf16[1,640,1536]{2,1,0:T(8,128)(2,1)}, u32[]{:S(2)}) copy-start(bf16[1,640,1536]{2,1,0:T(8,128)(2,1)} %param.14) | copy-start | bytes 5898244
  33.1 2.4 %copy-start.16 = (f32[1,2,1536]{2,1,0:T(2,128)S(1)}, f32[1,2,1536]{2,1,0:T(2,128)}, u32[]{:S(2)}) copy-start(f32[1,2,1536]{2,1,0:T(2,128)} %param.19) | copy-start | bytes 36868
  34.6 0.8 copy-start.12
  35.4 0.8 copy-start.14
  36.3 2.7 %copy-start = (bf16[4,512,1536]{2,1,0:T(8,128)(2,1)}, bf16[4,512,1536]{2,1,0:T(8,128)(2,1)S(1)}, u32[]{:S(2)}) copy-start(bf16[4,512,1536]{2,1,0:T(8,128)(2,1)S(1)} %get-tuple-element.35.rest_0_) | copy-start | bytes 18874372
  39.0 1.8 %copy-start.5 = (bf16[2,544,1536]{2,1,0:T(8,128)(2,1)}, bf16[2,544,1536]{2,1,0:T(8,128)(2,1)S(1)}, u32[]{:S(2)}) copy-start(bf16[2,544,1536]{2,1,0:T(8,128)(2,1)S(1)} %get-tuple-element.28.normed_ref) | copy-start | bytes 10027012
  44.1 26.5 %collective-permute-start.12 = (bf16[192,1536]{1,0:T(8,128)(2,1)}, bf16[192,1536]{1,0:T(8,128)(2,1)}, u32[]{:S(2)}, u32[]{:S(2)}) collective-permute-start(bf16[192,1536]{1,0:T(8,128)(2,1)} %collective-permute-done.1.rest_3_), channel_id=1, source_target_pairs={{1,5},{2,6},{5,1},{6,2},{9,13},{10,14},{13,9},{14,10},{17,21},{18,... | collective-permute-start | bytes 1769480 | tf_op jit(solution)/shard_map/ppermute | solution.py:296
  46.5 14.7 %copy-start.23 = (s32[1,1024]{1,0:T(1,128)S(1)}, s32[1,1024]{1,0:T(1,128)}, u32[]{:S(2)}) copy-start(s32[1,1024]{1,0:T(1,128)} %param.13) | copy-start | bytes 12292
  46.5 15.3 %copy-start.22 = (s32[1,1024]{1,0:T(1,128)S(1)}, s32[1,1024]{1,0:T(1,128)}, u32[]{:S(2)}) copy-start(s32[1,1024]{1,0:T(1,128)} %param.12) | copy-start | bytes 12292
  46.5 16.0 %copy-start.21 = (bf16[1,31,768]{2,1,0:T(8,128)(2,1)S(1)}, bf16[1,31,768]{2,1,0:T(8,128)(2,1)}, u32[]{:S(2)}) copy-start(bf16[1,31,768]{2,1,0:T(8,128)(2,1)} %param.17) | copy-start | bytes 142852
  47.3 25.3 %collective-permute-start.10 = (bf16[160,1536]{1,0:T(8,128)(2,1)}, bf16[160,1536]{1,0:T(8,128)(2,1)}, u32[]{:S(2)}, u32[]{:S(2)}) collective-permute-start(bf16[160,1536]{1,0:T(8,128)(2,1)} %maximum_maximum_fusion.rest_0_), channel_id=1, source_target_pairs={{1,2},{2,1},{5,6},{6,5},{9,10},{10,9},{13,14},{14,13},{17,18},{18,... | collective-permute-start | bytes 1474568 | tf_op jit(solution)/shard_map/ppermute | solution.py:291
  48.8 23.8 %collective-permute-start.11 = (bf16[160,1536]{1,0:T(8,128)(2,1)}, bf16[160,1536]{1,0:T(8,128)(2,1)}, u32[]{:S(2)}, u32[]{:S(2)}) collective-permute-start(bf16[160,1536]{1,0:T(8,128)(2,1)} %maximum_maximum_fusion.rest_0_), channel_id=1, source_target_pairs={{0,2},{3,1},{4,6},{7,5},{8,10},{11,9},{12,14},{15,13},{16,18},{19,... | collective-permute-start | bytes 1474568 | tf_op jit(solution)/shard_map/ppermute | solution.py:291
  59.1 20.7 %collective-permute-start.9 = (bf16[160,1536]{1,0:T(8,128)(2,1)}, bf16[160,1536]{1,0:T(8,128)(2,1)}, u32[]{:S(2)}, u32[]{:S(2)}) collective-permute-start(bf16[160,1536]{1,0:T(8,128)(2,1)} %maximum_maximum_fusion.rest_0_), channel_id=1, source_target_pairs={{0,1},{3,2},{4,5},{7,6},{8,9},{11,10},{12,13},{15,14},{16,17},{19,... | collective-permute-start | bytes 1474568 | tf_op jit(solution)/shard_map/ppermute | solution.py:291
  62.6 35.8 %collective-permute-start.14 = (bf16[160,1536]{1,0:T(8,128)(2,1)}, bf16[160,1536]{1,0:T(8,128)(2,1)}, u32[]{:S(2)}, u32[]{:S(2)}) collective-permute-start(bf16[160,1536]{1,0:T(8,128)(2,1)} %maximum_maximum_fusion.rest_0_), channel_id=1, source_target_pairs={{1,5},{2,6},{5,1},{6,2},{9,13},{10,14},{13,9},{14,10},{17,21},{18,... | collective-permute-start | bytes 1474568 | tf_op jit(solution)/shard_map/ppermute | solution.py:296
  64.0 2.8 %copy-start.1 = (bf16[4,512,1536]{2,1,0:T(8,128)(2,1)S(1)}, bf16[4,512,1536]{2,1,0:T(8,128)(2,1)}, u32[]{:S(2)}) copy-start(bf16[4,512,1536]{2,1,0:T(8,128)(2,1)} %copy-done) | copy-start | bytes 18874372
  66.8 3.9 %copy-start.6 = (bf16[2,544,1536]{2,1,0:T(8,128)(2,1)S(1)}, bf16[2,544,1536]{2,1,0:T(8,128)(2,1)}, u32[]{:S(2)}) copy-start(bf16[2,544,1536]{2,1,0:T(8,128)(2,1)} %copy-done.5) | copy-start | bytes 10027012
  66.8 3.9 %copy-start.7 = (bf16[1,192,1536]{2,1,0:T(8,128)(2,1)S(1)}, bf16[1,192,1536]{2,1,0:T(8,128)(2,1)}, u32[]{:S(2)}) copy-start(bf16[1,192,1536]{2,1,0:T(8,128)(2,1)} %param.15) | copy-start | bytes 1769476
  66.8 4.0 %copy-start.9 = (bf16[192,1536]{1,0:T(8,128)(2,1)S(1)}, bf16[192,1536]{1,0:T(8,128)(2,1)}, u32[]{:S(2)}) copy-start(bf16[192,1536]{1,0:T(8,128)(2,1)} %copy-done.8) | copy-start | bytes 1769476
  66.8 4.6 %copy-start.11 = (bf16[192,1536]{1,0:T(8,128)(2,1)S(1)}, bf16[192,1536]{1,0:T(8,128)(2,1)}, u32[]{:S(2)}) copy-start(bf16[192,1536]{1,0:T(8,128)(2,1)} %copy-done.10) | copy-start | bytes 1769476
  66.8 4.9 %copy-start.13 = (bf16[192,1536]{1,0:T(8,128)(2,1)S(1)}, bf16[192,1536]{1,0:T(8,128)(2,1)}, u32[]{:S(2)}) copy-start(bf16[192,1536]{1,0:T(8,128)(2,1)} %copy-done.12) | copy-start | bytes 1769476
  66.8 5.0 %copy-start.15 = (bf16[192,1536]{1,0:T(8,128)(2,1)S(1)}, bf16[192,1536]{1,0:T(8,128)(2,1)}, u32[]{:S(2)}) copy-start(bf16[192,1536]{1,0:T(8,128)(2,1)} %copy-done.14) | copy-start | bytes 1769476
  67.5 3.2 %copy-start.2 = (bf16[4,512,1536]{2,1,0:T(8,128)(2,1)}, bf16[4,512,1536]{2,1,0:T(8,128)(2,1)S(1)}, u32[]{:S(2)}) copy-start(bf16[4,512,1536]{2,1,0:T(8,128)(2,1)S(1)} %get-tuple-element.39.stem_out_ref) | copy-start | bytes 18874372
  79.8 18.6 %collective-permute-start.15 = (bf16[160,1536]{1,0:T(8,128)(2,1)}, bf16[160,1536]{1,0:T(8,128)(2,1)}, u32[]{:S(2)}, u32[]{:S(2)}) collective-permute-start(bf16[160,1536]{1,0:T(8,128)(2,1)} %collective-permute-done.9.rest_1_), channel_id=1, source_target_pairs={{1,5},{2,6},{5,1},{6,2},{9,13},{10,14},{13,9},{14,10},{17,21},{18,... | collective-permute-start | bytes 1474568 | tf_op jit(solution)/shard_map/ppermute | solution.py:296
  81.3 17.1 %collective-permute-start.16 = (bf16[160,1536]{1,0:T(8,128)(2,1)}, bf16[160,1536]{1,0:T(8,128)(2,1)}, u32[]{:S(2)}, u32[]{:S(2)}) collective-permute-start(bf16[160,1536]{1,0:T(8,128)(2,1)} %collective-permute-done.10.rest_2_), channel_id=1, source_target_pairs={{1,5},{2,6},{5,1},{6,2},{9,13},{10,14},{13,9},{14,10},{17,21},{18,... | collective-permute-start | bytes 1474568 | tf_op jit(solution)/shard_map/ppermute | solution.py:296
  82.7 15.6 %collective-permute-start.17 = (bf16[160,1536]{1,0:T(8,128)(2,1)}, bf16[160,1536]{1,0:T(8,128)(2,1)}, u32[]{:S(2)}, u32[]{:S(2)}) collective-permute-start(bf16[160,1536]{1,0:T(8,128)(2,1)} %collective-permute-done.11.rest_3_), channel_id=1, source_target_pairs={{1,5},{2,6},{5,1},{6,2},{9,13},{10,14},{13,9},{14,10},{17,21},{18,... | collective-permute-start | bytes 1474568 | tf_op jit(solution)/shard_map/ppermute | solution.py:296
  84.2 14.1 %collective-permute-start.13 = (s32[1024]{0:T(1024)S(1)}, s32[1024]{0:T(1024)S(1)}, u32[]{:S(2)}, u32[]{:S(2)}) collective-permute-start(s32[1024]{0:T(1024)S(1)} %fusion.89), channel_id=1, source_target_pairs={{0,1},{3,2},{4,5},{7,6},{8,9},{11,10},{12,13},{15,14},{16,17},{19,... | collective-permute-start | bytes 12296 | tf_op jit(solution)/shard_map/ppermute | solution.py:291
  98.4 2.8 %copy-start.3 = (bf16[4,512,1536]{2,1,0:T(8,128)(2,1)S(1)}, bf16[4,512,1536]{2,1,0:T(8,128)(2,1)}, u32[]{:S(2)}) copy-start(bf16[4,512,1536]{2,1,0:T(8,128)(2,1)} %copy-done.2) | copy-start | bytes 18874372
  102.2 3.8 %collective-permute-start.18 = (f32[4,8,128]{2,1,0:T(8,128)S(1)}, f32[4,8,128]{2,1,0:T(8,128)S(1)}, u32[]{:S(2)}, u32[]{:S(2)}) collective-permute-start(f32[4,8,128]{2,1,0:T(8,128)S(1)} %shard_map.117), channel_id=1, source_target_pairs={{0,8},{8,0},{16,24},{24,16},{1,9},{9,1},{17,25},{25,17},{2,10},{10... | collective-permute-start | bytes 49160 | tf_op jit(solution)/shard_map/ppermute | solution.py:300
  103.7 3.7 %collective-permute-start.19 = (f32[4,8,128]{2,1,0:T(8,128)S(1)}, f32[4,8,128]{2,1,0:T(8,128)S(1)}, u32[]{:S(2)}, u32[]{:S(2)}) collective-permute-start(f32[4,8,128]{2,1,0:T(8,128)S(1)} %shard_map.117), channel_id=1, source_target_pairs={{0,16},{8,24},{16,0},{24,8},{1,17},{9,25},{17,1},{25,9},{2,18},{10... | collective-permute-start | bytes 49160 | tf_op jit(solution)/shard_map/ppermute | solution.py:300
  105.2 4.6 %collective-permute-start.20 = (f32[4,8,128]{2,1,0:T(8,128)S(1)}, f32[4,8,128]{2,1,0:T(8,128)S(1)}, u32[]{:S(2)}, u32[]{:S(2)}) collective-permute-start(f32[4,8,128]{2,1,0:T(8,128)S(1)} %shard_map.117), channel_id=1, source_target_pairs={{0,24},{8,16},{16,8},{24,0},{1,25},{9,17},{17,9},{25,1},{2,26},{10... | collective-permute-start | bytes 49160 | tf_op jit(solution)/shard_map/ppermute | solution.py:300
  111.2 38.9 %collective-permute-start.21 = (f32[1025]{0:T(1024)S(1)}, f32[1025]{0:T(1024)S(1)}, u32[]{:S(2)}, u32[]{:S(2)}) collective-permute-start(f32[1025]{0:T(1024)S(1)} %pad_maximum_fusion.18), channel_id=1, source_target_pairs={{1,0},{2,3},{5,4},{6,7},{9,8},{10,11},{13,12},{14,15},{17,16},{18,... | collective-permute-start | bytes 12308 | tf_op jit(solution)/shard_map/ppermute | solution.py:291
  112.5 2.5 %collective-permute-start.22 = (f32[1]{0:T(128)}, f32[1]{0:T(128)}, u32[]{:S(2)}, u32[]{:S(2)}) collective-permute-start(f32[1]{0:T(128)} %bitcast.30), channel_id=1, source_target_pairs={{1,2},{2,1},{5,6},{6,5},{9,10},{10,9},{13,14},{14,13},{17,18},{18,... | collective-permute-start | bytes 20 | tf_op jit(solution)/shard_map/ppermute | solution.py:291
  113.7 35.3 %collective-permute-start.23 = (f32[1]{0:T(128)}, f32[1]{0:T(128)}, u32[]{:S(2)}, u32[]{:S(2)}) collective-permute-start(f32[1]{0:T(128)} %bitcast.30), channel_id=1, source_target_pairs={{2,0},{1,3},{6,4},{5,7},{10,8},{9,11},{14,12},{13,15},{18,16},{17,... | collective-permute-start | bytes 20 | tf_op jit(solution)/shard_map/ppermute | solution.py:291

commit v5 on v3

v5 whole, which is shorter than its diff:
```python
import jax
import jax.numpy as jnp
from jax import lax
from jax.experimental import pallas as pl
from jax.experimental.pallas import tpu as pltpu
from jax.sharding import PartitionSpec as P

LANES = 128
CHUNKS = 8
EDGE = 16
VMEM_BYTES = 56 * 1024 * 1024


def norm_rows(values, gain_row):
    row_mean = jnp.mean(values, axis=-1, keepdims=True)
    centred = values - row_mean
    row_var = jnp.mean(centred * centred, axis=-1, keepdims=True)
    return (centred * lax.rsqrt(row_var + 1e-05) * gain_row).astype(jnp.bfloat16)


def sigmoid(x):
    return 0.5 * jnp.tanh(0.5 * x) + 0.5


def stem_kernel(
    meta, main_ref, margin_ref, stem_ref, gain_ref, stem_out_ref, normed_ref, acc_a, acc_b, acc_c
):
    slot = pl.program_id(0)
    frames = main_ref.shape[1]
    part = acc_a.shape[0]
    group = 16

    def norm(acc, at, keep):
        for row in range(0, acc.shape[0], group):
            stem_out = acc[row : row + group, :].astype(jnp.bfloat16)
            if keep:
                stem_out_ref[0, at + row : at + row + group, :] = stem_out
            normed_ref[0, at + row : at + row + group, :] = norm_rows(stem_out.astype(jnp.float32), gain_ref[0:1, :])

    @pl.when(meta[5 + slot] > 0)
    def _():
        for acc, left in ((acc_a, main_ref[0, :part, :]), (acc_b, main_ref[0, part:, :]), (acc_c, margin_ref[0])):
            acc[...] = jnp.dot(left, stem_ref[...], preferred_element_type=jnp.float32)
        norm(acc_a, 0, True)
        norm(acc_b, part, True)
        norm(acc_c, frames, False)


def shards(meta, pieces):
    side = meta[13]
    return [(pieces[i], (side if i < 4 else 1 - side) * 4 + meta[9 + i % 4]) for i in range(8)]


def conv_kernel(meta, normed_ref, taps_ref, *rest):
    pieces = rest[:8]
    swished_ref, weight, mixed, gated_a, gated_b, margin, mask, sems = rest[8:]
    slot = pl.program_id(0)
    rows = normed_ref.shape[1]
    frames = swished_ref.shape[1]
    channels = swished_ref.shape[2]
    tap_count = taps_ref.shape[0]
    reach = tap_count // 2
    piece = weight.shape[0] // 8
    run_length = frames // CHUNKS

    @pl.when(jnp.logical_and(pl.program_id(0) == 0, meta[14] > 0))
    def _():
        copies = [
            pltpu.make_async_copy(
                ref.at[pl.ds(0, piece)], weight.at[pl.ds(pl.multiple_of(block * piece, 16), piece)], sems.at[i]
            )
            for i, (ref, block) in enumerate(shards(meta, pieces))
        ]
        for copy in copies:
            copy.start()
        for copy in copies:
            copy.wait()

    @pl.when(meta[5 + slot] > 0)
    def _():
        row = lax.broadcasted_iota(jnp.int32, (rows, LANES), 0)
        inner = (row % CHUNKS) * run_length + row // CHUNKS
        outer = jnp.where(row < frames + EDGE, row - frames - EDGE, row - EDGE)
        at = meta[slot] + jnp.where(row < frames, inner, outer)
        mask[...] = jnp.logical_and(at >= 0, at < meta[4]).astype(jnp.float32)
        sublane = lax.broadcasted_iota(jnp.int32, (CHUNKS, LANES), 0)
        half = rows // 2
        for first in (0, half):
            mixed[first : first + half, :] = jnp.dot(
                normed_ref[0, first : first + half, :], weight[...], preferred_element_type=jnp.float32
            )

        def gate(block):
            low = block * LANES
            gated = (gated_a, gated_b)[block % 2]
            group = 32
            for at in range(0, rows, group):
                here = slice(at, at + group)
                made = mixed[here, low : low + LANES] * mask[here, :]
                made = made * sigmoid(mixed[here, channels + low : channels + low + LANES])
                made = made.astype(jnp.bfloat16).astype(jnp.float32)
                if at < frames:
                    first = reach + at // CHUNKS
                    gated[first : first + group // CHUNKS] = made.reshape(group // CHUNKS, CHUNKS, LANES)
                else:
                    margin[...] = made
            for i in range(reach):
                before = pltpu.roll(gated[run_length + i], 1, 0)
                edge = margin[EDGE - reach + i : EDGE - reach + i + 1, :]
                gated[i] = jnp.where(sublane == 0, edge, before)
                after = pltpu.roll(gated[reach + i], CHUNKS - 1, 0)
                edge = margin[EDGE + i : EDGE + i + 1, :]
                gated[reach + run_length + i] = jnp.where(sublane == CHUNKS - 1, edge, after)

        def convolve(block):
            low = block * LANES
            run, held = 32, 8
            gated = (gated_a, gated_b)[block % 2]
            for start in range(0, run_length, run):
                sums = [None] * run
                for tap in range(0, tap_count, held):
                    taps = [taps_ref[j, :, low : low + LANES] for j in range(tap, min(tap + held, tap_count))]
                    for at in range(start + tap, start + tap + run + len(taps) - 1):
                        value = gated[at]
                        for j, weight_row in enumerate(taps):
                            k = at - tap - j - start
                            if 0 <= k < run:
                                term = value * weight_row
                                sums[k] = term if sums[k] is None else sums[k] + term
                for k in range(0, run, 2):
                    total = jnp.concatenate(sums[k : k + 2], axis=0)
                    first = (start + k) * CHUNKS
                    swished_ref[0, first : first + 2 * CHUNKS, low : low + LANES] = (
                        total * sigmoid(total)
                    ).astype(jnp.bfloat16)

        blocks = channels // LANES
        for block in range(blocks):
            gate(block)
            convolve(block)


def head_kernel(meta, swished_ref, stem_out_ref, code_ref, gain_ref, *rest):
    pieces = rest[:8]
    error_ref, back, head, acc_a, acc_b, norm_a, norm_b, logit_a, logit_b, sems = rest[8:]
    slot = pl.program_id(0)
    frames = swished_ref.shape[1]
    vocab = head.shape[1]
    groups = back.shape[1] // vocab
    back_rows = back.shape[0] // 8
    head_rows = head.shape[0] // 8
    group_rows = head_rows // groups

    @pl.when(jnp.logical_and(pl.program_id(0) == 0, meta[14] > 0))
    def _():
        copies = []
        for i, (ref, block) in enumerate(shards(meta, pieces)):
            copies.append(
                pltpu.make_async_copy(
                    ref.at[pl.ds(0, back_rows)],
                    back.at[pl.ds(pl.multiple_of(block * back_rows, 16), back_rows)],
                    sems.at[i, 0],
                )
            )
            for g in range(groups):
                copies.append(
                    pltpu.make_async_copy(
                        ref.at[pl.ds(back_rows, group_rows), pl.ds(g * vocab, vocab)],
                        head.at[pl.ds(pl.multiple_of(block * head_rows + g * group_rows, 16), group_rows)],
                        sems.at[i, 1 + g],
                    )
                )
        for copy in copies:
            copy.start()
        for copy in copies:
            copy.wait()

    @pl.when(meta[5 + slot] <= 0)
    def _():
        error_ref[...] = jnp.zeros_like(error_ref)

    @pl.when(meta[5 + slot] > 0)
    def _():
        part = acc_a.shape[0]
        lane = lax.broadcasted_iota(jnp.int32, (CHUNKS, LANES), 1)
        def norm(at, acc, normed):
            group = 16
            for row in range(0, part, group):
                values = acc[row : row + group, :] + stem_out_ref[0, at + row : at + row + group, :].astype(jnp.float32)
                normed[row : row + group, :] = norm_rows(values, gain_ref[1:2, :])

        def errors(at, logits, row):
            group = 32
            token = lax.broadcasted_iota(jnp.int32, (group, vocab), 1)
            for first in range(0, part, group):
                scores = logits[first : first + group, :]
                grown = jnp.exp(scores - jnp.max(scores, axis=-1, keepdims=True))
                posterior = grown * (1.0 / jnp.sum(grown, axis=-1, keepdims=True))
                steps = range((at + first) // CHUNKS, (at + first + group) // CHUNKS)
                code = jnp.concatenate([code_ref[0, :, m : m + 1] for m in steps], axis=0)
                differ = posterior - (token == code).astype(jnp.float32)
                error = jnp.sqrt(jnp.sum(differ * differ, axis=-1, keepdims=True))
                error = jnp.where(code >= 0, error, 0.0)
                for k, m in enumerate(steps):
                    row = jnp.where(lane == m, error[k * CHUNKS : (k + 1) * CHUNKS, :], row)
            return row

        halves = ((0, acc_a, norm_a, logit_a), (part, acc_b, norm_b, logit_b))
        for at, acc, _, _ in halves:
            acc[...] = jnp.dot(swished_ref[0, at : at + part, :], back[...], preferred_element_type=jnp.float32)
        for at, acc, normed, logits in halves:
            norm(at, acc, normed)
            logits[...] = jnp.dot(normed[...], head[...], preferred_element_type=jnp.float32)
        row = jnp.zeros((CHUNKS, LANES), jnp.float32)
        for at, _, _, logits in halves:
            row = errors(at, logits, row)
        error_ref[0] = row


def call(kernel, grid, in_specs, out_specs, out_shape, scratch, flops, moved, operands):
    return pl.pallas_call(
        kernel,
        grid_spec=pltpu.PrefetchScalarGridSpec(
            num_scalar_prefetch=1,
            grid=grid,
            in_specs=in_specs,
            out_specs=out_specs,
            scratch_shapes=scratch,
        ),
        out_shape=out_shape,
        compiler_params=pltpu.CompilerParams(
            dimension_semantics=("arbitrary",), vmem_limit_bytes=VMEM_BYTES
        ),
        cost_estimate=pl.CostEstimate(flops=flops // 16, bytes_accessed=moved // 16, transcendentals=0),
    )(*operands)


def whole(shape):
    return pl.BlockSpec(shape, lambda i, meta: (0,) * len(shape))


def by_slot(shape):
    return pl.BlockSpec((1,) + shape, lambda i, meta: (i,) + (0,) * len(shape))


INWARD = [(0, 1), (3, 2)]
ACROSS = [(1, 2), (2, 1)]
BEYOND = [(0, 2), (3, 1)]
OUTWARD = [(1, 0), (2, 3)]
OUT_BEYOND = [(2, 0), (1, 3)]


def along(x, pairs):
    return lax.ppermute(x, "seq", pairs)


def to_mate(x):
    pairs = [(a * 4 + z, (1 - a) * 4 + z) for a in (0, 1) for z in (1, 2)]
    return lax.ppermute(x, ("fsdp", "seq"), pairs)


def seed_swap(x, bit):
    return lax.ppermute(x, "seed", [(i, i ^ bit) for i in range(4)])


def hub_body(
    mel_frames,
    lengths,
    targets,
    frame_mask,
    stem_weight,
    conv_in_weight,
    conv_out_weight,
    depth_weight,
    head_weight,
    norm_gain,
):
    chip = lax.axis_index("seq")
    side = lax.axis_index("fsdp")
    seeds = lax.axis_size("seed")
    rows = targets.shape[1]
    width = stem_weight.shape[2]
    channels = depth_weight.shape[2]
    vocab = head_weight.shape[2]
    step = mel_frames.shape[1] // rows
    tile = rows // 2
    seed = lax.axis_index("seed")
    low = chip == 1
    is_hub = jnp.logical_or(low, chip == 2)

    first = conv_in_weight[0]
    blocks = mel_frames[0].reshape(rows, -1)
    deep_in = blocks.shape[1]
    share = rows // seeds
    stack = width // (-(-deep_in // LANES) * LANES)

    def widened(x, count):
        side = width // stack
        parts = jnp.pad(x, ((0, 0), (0, side - deep_in))).reshape(count, -1, side)
        return jnp.pad(jnp.concatenate(list(parts), axis=1), ((0, 0), (0, (stack - count) * side)))

    quarter = lax.dynamic_slice_in_dim(mel_frames[0], seed * share * step, share * step, 0).reshape(share, -1)
    margin = step * EDGE
    edge_out = jnp.where(low, mel_frames[0, -margin:], mel_frames[0, :margin]).reshape(EDGE, -1)
    far_first = along(first, BEYOND)
    near_first = along(jnp.concatenate([first, widened(quarter, stack)], axis=0), INWARD)
    hub_first = along(jnp.concatenate([first, widened(edge_out, 1)], axis=0), ACROSS)
    held = first.shape[0]
    edge = hub_first[held:, :deep_in]
    quarter_in = near_first[held:].reshape(share // stack, stack, -1).transpose(1, 0, 2).reshape(share, -1)
    quarter_in = quarter_in[:, :deep_in]

    pair = seed_swap(quarter_in, 1)
    odd = seed % 2 == 1
    pairs = jnp.concatenate([jnp.where(odd, pair, quarter_in), jnp.where(odd, quarter_in, pair)], axis=0)
    other = seed_swap(pairs, 2)
    upper = seed // 2 == 1
    outer = jnp.concatenate([jnp.where(upper, other, pairs), jnp.where(upper, pairs, other)], axis=0)

    groups = width // vocab
    head_rows = head_weight.shape[1]
    second = jnp.concatenate(
        [
            conv_out_weight[0],
            jnp.concatenate(jnp.split(head_weight[0], groups, axis=0), axis=1),
        ],
        axis=0,
    )
    slots = 4
    deep = tile + 2 * EDGE
    none = jnp.zeros_like(edge)
    frames = jnp.concatenate(
        [
            jnp.where(low, none, edge),
            jnp.where(low, outer, blocks),
            jnp.where(low, blocks, outer),
            jnp.where(low, edge, none),
            none[:1],
        ],
        axis=0,
    )
    pairs = jnp.concatenate([frames[:-1], frames[1:]], axis=1)
    main = pairs[EDGE : EDGE + slots * tile].reshape(slots, CHUNKS, tile // CHUNKS, -1)
    main = main.transpose(0, 2, 1, 3).reshape(slots, tile, -1)
    margins = jnp.stack(
        [
            jnp.concatenate([pairs[k * tile : k * tile + EDGE], pairs[(k + 1) * tile + EDGE : (k + 1) * tile + 2 * EDGE]])
            for k in range(slots)
        ]
    )

    length = lengths[0]
    positions = chip * rows + jnp.arange(rows, dtype=jnp.int32)
    counted = jnp.logical_and(frame_mask[0] > 0, positions < length)
    code = jnp.where(counted, targets[0], -1)
    starts = (chip - 1) * 2 * rows + tile * jnp.arange(slots, dtype=jnp.int32)
    alive = jnp.logical_and(is_hub, starts < length).astype(jnp.int32)
    hub = jnp.clip(chip, 1, 2)
    meta = jnp.concatenate(
        [
            starts,
            lengths,
            alive,
            jnp.stack([hub, 3 * (hub - 1), 3 - hub, 3 * (2 - hub), side, jnp.max(alive)]),
        ]
    ).astype(jnp.int32)

    gains = norm_gain[0]
    half = tile // 2
    stem_out, normed = call(
        stem_kernel,
        (slots,),
        [by_slot(main.shape[1:]), by_slot(margins.shape[1:]), whole(stem_weight.shape[1:]), whole(gains.shape)],
        [by_slot((tile, width)), by_slot((deep, width))],
        [
            jax.ShapeDtypeStruct((slots, tile, width), jnp.bfloat16),
            jax.ShapeDtypeStruct((slots, deep, width), jnp.bfloat16),
        ],
        [
            pltpu.VMEM((half, width), jnp.float32),
            pltpu.VMEM((half, width), jnp.float32),
            pltpu.VMEM((2 * EDGE, width), jnp.float32),
        ],
        2 * slots * deep * main.shape[2] * width,
        2 * slots * deep * (main.shape[2] + 2 * width),
        (meta, main, margins, stem_weight[0], gains),
    )
    pinned = pl.BlockSpec(memory_space=pltpu.HBM)

    outer_code = along(code, INWARD)
    codes = jnp.concatenate([jnp.where(low, outer_code, code), jnp.where(low, code, outer_code)])
    codes = codes.reshape(slots, CHUNKS, tile // CHUNKS)
    far_first, normed, codes = lax.optimization_barrier((far_first, normed, codes))
    mine = [first, near_first, hub_first, far_first]
    first_pieces = (*mine, *[to_mate(x) for x in mine])
    near_second, hub_second, far_second = [along(second, pairs_) for pairs_ in (INWARD, ACROSS, BEYOND)]
    taps = jnp.broadcast_to(
        depth_weight[0].astype(jnp.float32)[:, None, :], (depth_weight.shape[1], CHUNKS, channels)
    )
    extent = tile // CHUNKS + depth_weight.shape[1] - 1
    swished = call(
        conv_kernel,
        (slots,),
        [by_slot((deep, width)), whole(taps.shape)] + [pinned] * 8,
        by_slot((tile, channels)),
        jax.ShapeDtypeStruct((slots, tile, channels), jnp.bfloat16),
        [
            pltpu.VMEM((8 * held, width), jnp.bfloat16),
            pltpu.VMEM((deep, 2 * channels), jnp.float32),
            pltpu.VMEM((extent, CHUNKS, LANES), jnp.float32),
            pltpu.VMEM((extent, CHUNKS, LANES), jnp.float32),
            pltpu.VMEM((2 * EDGE, LANES), jnp.float32),
            pltpu.VMEM((deep, LANES), jnp.float32),
            pltpu.SemaphoreType.DMA((8,)),
        ],
        2 * slots * deep * width * 2 * channels,
        2 * slots * deep * width + 8 * first.size * 2,
        (meta, normed, taps, *first_pieces),
    )

    near_second, hub_second, far_second, swished = lax.optimization_barrier(
        (near_second, hub_second, far_second, swished)
    )
    mine = [second, near_second, hub_second, far_second]
    second_pieces = (*mine, to_mate(second), *[to_mate(x) for x in mine[1:]])
    errors = call(
        head_kernel,
        (slots,),
        [by_slot((tile, channels)), by_slot((tile, width)), by_slot(codes.shape[1:]), whole(gains.shape)]
        + [pinned] * 8,
        by_slot((CHUNKS, LANES)),
        jax.ShapeDtypeStruct((slots, CHUNKS, LANES), jnp.float32),
        [
            pltpu.VMEM((8 * conv_out_weight.shape[1], width), jnp.bfloat16),
            pltpu.VMEM((8 * head_rows, vocab), jnp.bfloat16),
            pltpu.VMEM((half, width), jnp.float32),
            pltpu.VMEM((half, width), jnp.float32),
            pltpu.VMEM((half, width), jnp.bfloat16),
            pltpu.VMEM((half, width), jnp.bfloat16),
            pltpu.VMEM((half, vocab), jnp.float32),
            pltpu.VMEM((half, vocab), jnp.float32),
            pltpu.SemaphoreType.DMA((8, 1 + groups)),
        ],
        2 * slots * tile * (channels + vocab) * width,
        2 * slots * tile * (channels + width),
        (meta, swished, stem_out, codes, gains, *second_pieces),
    )

    one, two, three = [seed_swap(errors, bit) for bit in (1, 2, 3)]
    total = ((errors + one) + (two + three)) / jnp.float32(seeds)
    total = total[:, :, : tile // CHUNKS].reshape(2, rows)
    part = jnp.sum(total).reshape(1)
    outer_half = jnp.where(low, total[0], total[1])
    own_half = jnp.where(low, total[1], total[0])
    from_hub = along(jnp.concatenate([outer_half, part]), OUTWARD)
    parts = [part[0], along(part, ACROSS)[0], along(part, OUT_BEYOND)[0], from_hub[rows]]
    frame_error = jnp.where(is_hub, own_half, from_hub[:rows])
    utt_score = ((parts[0] + parts[3]) + (parts[1] + parts[2])) / length.astype(jnp.float32)
    return (frame_error[None, :], utt_score.reshape(1))


def from_behind(x, axis, by):
    count = lax.axis_size(axis)
    pairs = [(i, i + by) for i in range(count) if 0 <= i + by < count]
    return lax.ppermute(x, axis, pairs)


def extended(x, sides, width):
    for axis, dim in sides:
        count, length = (lax.axis_size(axis), x.shape[dim])
        up = [(i, (i + 1) % count) for i in range(count - 1)]
        down = [(j, i) for i, j in up]
        last = lax.slice_in_dim(x, length - width, length, axis=dim)
        first = lax.slice_in_dim(x, 0, width, axis=dim)
        before = lax.ppermute(last, axis, up)
        after = lax.ppermute(first, axis, down)
        x = jnp.concatenate([before, x, after], axis=dim)
    return x


def layer_norm(values, gain_row):
    row_mean = jnp.mean(values, axis=-1, keepdims=True)
    centred = values - row_mean
    row_var = jnp.mean(centred * centred, axis=-1, keepdims=True)
    return (centred * lax.rsqrt(row_var + 1e-05) * gain_row).astype(jnp.bfloat16)


def block_product(left_rows, right_matrix):
    return jnp.dot(left_rows, right_matrix, preferred_element_type=jnp.float32)


def row_product(activations, shard_piece):
    return block_product(activations, shard_piece[0])


def body(
    mel_frames,
    lengths,
    targets,
    frame_mask,
    stem_weight,
    conv_in_weight,
    conv_out_weight,
    depth_weight,
    head_weight,
    norm_gain,
):
    frame_rows = targets.shape[1]
    blocks = mel_frames[0].reshape(frame_rows, -1)
    next_block = from_behind(blocks[:1], "seq", -1)
    following = jnp.concatenate([blocks[1:], next_block], 0)
    half_width = blocks.shape[1]
    stem_matrix = stem_weight[0]
    stem_out = (
        jnp.dot(blocks, stem_matrix[:half_width], preferred_element_type=jnp.float32)
        + jnp.dot(following, stem_matrix[half_width:], preferred_element_type=jnp.float32)
    ).astype(jnp.bfloat16)
    offset = lax.axis_index("seq") * frame_rows
    length = lengths[0]
    positions = offset + jnp.arange(frame_rows, dtype=jnp.int32)
    frame_live = positions < length
    gain_rows = norm_gain[0]
    normed_one = layer_norm(stem_out.astype(jnp.float32), gain_rows[0])
    tap_count = depth_weight.shape[1]
    channels = depth_weight.shape[2]
    halo_width = tap_count // 2
    conv_input = extended(normed_one, (("seq", 0),), halo_width)
    mixed_rows = row_product(
        conv_input, lax.all_gather(conv_in_weight, ("fsdp", "seq"), axis=1, tiled=True)
    )
    input_positions = offset - halo_width + jnp.arange(conv_input.shape[0], dtype=jnp.int32)
    input_live = jnp.logical_and(input_positions >= 0, input_positions < length)
    gated_rows = (
        mixed_rows[:, :channels]
        * jax.nn.sigmoid(mixed_rows[:, channels:])
        * input_live[:, None].astype(jnp.float32)
    ).astype(jnp.bfloat16)
    depthwise = jnp.zeros((frame_rows, channels), jnp.float32)
    for tap_index in range(tap_count):
        depthwise = depthwise + gated_rows[tap_index : tap_index + frame_rows].astype(
            jnp.float32
        ) * depth_weight[0, tap_index].astype(jnp.float32)
    swished = jax.nn.silu(depthwise).astype(jnp.bfloat16)
    conv_proj = row_product(
        swished, lax.all_gather(conv_out_weight, ("fsdp", "seq"), axis=1, tiled=True)
    )
    after_conv = stem_out.astype(jnp.float32) + conv_proj
    normed_two = layer_norm(after_conv, gain_rows[1])
    logits = row_product(
        normed_two, lax.all_gather(head_weight, ("fsdp", "seq"), axis=1, tiled=True)
    )
    posterior = jax.nn.softmax(logits, axis=-1)
    vocab_size = logits.shape[1]
    onehot = (jnp.arange(vocab_size, dtype=jnp.int32)[None, :] == targets[0][:, None]).astype(
        jnp.float32
    )
    differ = posterior - onehot
    frame_err = (
        jnp.sqrt(jnp.sum(differ * differ, axis=-1))
        * frame_live.astype(jnp.float32)
        * frame_mask[0].astype(jnp.float32)
    )
    seed_count = lax.axis_size("seed")
    frame_error = lax.psum(frame_err, "seed") / jnp.float32(seed_count)
    numerator = lax.psum(jnp.sum(frame_error), "seq")
    utt_score = numerator / length.astype(jnp.float32)
    return (frame_error[None, :], utt_score.reshape(1))


def solution(mesh):
    in_specs = (
        P("fsdp", "seq", None),
        P("fsdp"),
        P("fsdp", "seq"),
        P("fsdp", "seq"),
        P("seed", None, None),
        P("seed", ("fsdp", "seq"), None),
        P("seed", ("fsdp", "seq"), None),
        P("seed", None, None),
        P("seed", ("fsdp", "seq"), None),
        P("seed", None, None),
    )
    out_specs = (P("fsdp", "seq"), P("fsdp"))
    hubs = mesh.shape["seq"] == 4 and mesh.shape["fsdp"] == 2
    return jax.shard_map(
        hub_body if hubs else body, mesh=mesh, in_specs=in_specs, out_specs=out_specs, check_vma=False
    )
```

time: 154 us -> 174 us (1.13)
  local copies, waits for them, and re-layouts: 40.4 us -> 11.6 us
  waiting for transfers between devices: 44.2 us -> 71.8 us
  Pallas kernels: 3.61 us -> 19.6 us
  other arithmetic: 8.95 us -> 19 us
  starting transfers between devices: 50.1 us -> 44.9 us
    unnamed x77 -> x41, local copies, waits for them, and re-layouts: 29.3 us -> 1.95 us
    ppermute x13 -> x10, waiting for transfers between devices: 40 us -> 59 us  [along(): return lax.ppermute(x, 'seq', pairs)]
    pallas_call x5 -> x3, Pallas kernels: 3.61 us -> 19.6 us  [call(): pl.pallas_call(kernel, grid_spec=pltpu.PrefetchScalarGridSpec(num_scalar_...]
    unnamed x3 -> x5, other arithmetic: 1.35 us -> 12.9 us
    ppermute x13 -> x10, starting transfers between devices: 42.6 us -> 31.5 us  [along(): return lax.ppermute(x, 'seq', pairs)]
    ppermute x3 -> x5, waiting for transfers between devices: 4.16 us -> 12.8 us  [seed_swap(): return lax.ppermute(x, 'seed', [(i, i ^ bit) for i in range(4)])]
    ppermute x3 -> x5, starting transfers between devices: 3.55 us -> 6.69 us  [seed_swap(): return lax.ppermute(x, 'seed', [(i, i ^ bit) for i in range(4)])]
    ppermute x2 -> x8, starting transfers between devices: 3.97 us -> 6.72 us  [to_mate(): return lax.ppermute(x, ('fsdp', 'seq'), pairs)]
  transfers between devices with their start and end apart: 18 -> 23, of which waited for: 6 -> 8; matrix products, arithmetic and copies ran while one was open for 13% -> 15% of each run, Pallas kernels for 2% -> 8%
where the time goes in v5:
time: 174 us; the launch traced here: 173 us
  waiting for transfers between devices  71.8 us (41%)
  starting transfers between devices  44.9 us (26%)
  Pallas kernels  19.6 us (11%)
  other arithmetic  19 us (11%)
  local copies, waits for them, and re-layouts  11.6 us (7%)
  between operations  5.69 us (3%)
    ppermute x10, waiting for transfers between devices, along(): return lax.ppermute(x, 'seq', pairs)  59 us
    ppermute x10, starting transfers between devices, along(): return lax.ppermute(x, 'seq', pairs)  31.5 us
    pallas_call x3, Pallas kernels, call(): pl.pallas_call(kernel, grid_spec=pltpu.PrefetchScalarGridSpec(num_scalar_...  19.6 us
    unnamed x5, other arithmetic  12.9 us
    ppermute x5, waiting for transfers between devices, seed_swap(): return lax.ppermute(x, 'seed', [(i, i ^ bit) for i in range(4)])  12.8 us
    ppermute x8, starting transfers between devices, to_mate(): return lax.ppermute(x, ('fsdp', 'seq'), pairs)  6.72 us
    ppermute x5, starting transfers between devices, seed_swap(): return lax.ppermute(x, 'seed', [(i, i ^ bit) for i in range(4)])  6.69 us
  transfers between devices with their start and end apart: 23, of which 8 were waited for; matrix products, arithmetic and copies ran while one was open for 15% of the time, Pallas kernels for 8%

profile of v5, /device:TPU:0, one launch (start us, length us, event | category | flops | bytes accessed | tf_op | source)
XLA Modules:
  0.0 172.6 jit_solution(15714533929478197710)
XLA Ops:
  0.6 6.9 %collective-permute-start.3 = (bf16[192,1536]{1,0:T(8,128)(2,1)}, bf16[192,1536]{1,0:T(8,128)(2,1)}, u32[]{:S(2)}, u32[]{:S(2)}) collective-permute-start(bf16[192,1536]{1,0:T(8,128)(2,1)} %bitcast.48), channel_id=1, source_target_pairs={{0,2},{3,1},{4,6},{7,5},{8,10},{11,9},{12,14},{15,13},{16,18},{19,... | collective-permute-start | bytes 1769480 | tf_op jit(solution)/shard_map/ppermute | solution.py:254
  7.5 1.5 collective-permute-start.9
  9.0 1.0 constant_dynamic-slice_fusion
  10.0 0.2 copy.18
  10.2 0.2 reshape.66
  10.5 1.3 collective-permute-start.5
  12.2 0.9 fusion.1
  13.1 1.5 collective-permute-start.4
  15.3 1.8 %collective-permute-start.8 = (s32[1024]{0:T(1024)S(1)}, s32[1024]{0:T(1024)S(1)}, u32[]{:S(2)}, u32[]{:S(2)}) collective-permute-start(s32[1024]{0:T(1024)S(1)} %fusion.65), channel_id=1, source_target_pairs={{0,1},{3,2},{4,5},{7,6},{8,9},{11,10},{12,13},{15,14},{16,17},{19,... | collective-permute-start | bytes 12296 | tf_op jit(solution)/shard_map/ppermute | solution.py:254
  17.2 0.6 slice_bitcast_fusion.2
  17.8 0.6 fusion.66
  18.5 0.6 copy.20
  19.1 0.7 reshape_squeeze.3
  19.8 1.2 concatenate.56.meta
  21.1 15.4 %collective-permute-done.5.rest_1_ = bf16[256,1536]{1,0:T(8,128)(2,1)S(1)} collective-permute-done((bf16[256,1536]{1,0:T(8,128)(2,1)S(1)}, bf16[256,1536]{1,0:T(8,128)(2,1)S(1)}, u32[]{:S(2)}, u32[]{:S(2)}) %collective-permute-start.5) | collective-permute-done | bytes 786464 | tf_op jit(solution)/shard_map/ppermute | solution.py:254
  36.6 1.6 collective-permute-start.6
  38.3 4.1 %collective-permute-done.6 = bf16[256,320]{1,0:T(8,128)(2,1)S(1)} collective-permute-done((bf16[256,320]{1,0:T(8,128)(2,1)S(1)}, bf16[256,320]{1,0:T(8,128)(2,1)S(1)}, u32[]{:S(2)}, u32[]{:S(2)}) %collective-permute-start.6) | collective-permute-done | bytes 163872 | tf_op jit(solution)/shard_map/ppermute | solution.py:263
  42.4 1.6 collective-permute-start.7
  44.0 0.6 pad_add_fusion.code_ref
  44.6 0.7 collective-permute-start.11
  45.3 0.7 constant_dynamic-update-slice_fusion.4
  46.0 0.9 collective-permute-start.10
  46.9 4.3 %collective-permute-done.7 = bf16[512,320]{1,0:T(8,128)(2,1)S(1)} collective-permute-done((bf16[512,320]{1,0:T(8,128)(2,1)S(1)}, bf16[512,320]{1,0:T(8,128)(2,1)S(1)}, u32[]{:S(2)}, u32[]{:S(2)}) %collective-permute-start.7) | collective-permute-done | bytes 327712 | tf_op jit(solution)/shard_map/ppermute | solution.py:263
  51.2 0.2 broadcast_select_fusion.3
  51.4 0.3 constant_dynamic-update-slice_fusion.3
  51.7 0.3 constant_dynamic-update-slice_fusion.2
  52.0 0.7 constant_dynamic-update-slice_fusion.1
  52.8 0.4 slice.102
  53.2 10.9 %fusion.67 = (bf16[2080,640]{1,0:T(8,128)(2,1)S(1)}, bf16[2080,640]{1,0:T(8,128)(2,1)S(1)}) fusion(bf16[2080,320]{1,0:T(8,128)(2,1)S(1)} %slice.102, bf16[16,320]{1,0:T(8,128)(2,1)S(1)} %get-tuple-element.31, bf16[1024,320]{1,0:T(8,128)(2,1)S(1)} %get-tuple-element.33, bf16[1024,320]{1,0:T(8,128)(2,1)S(1)} %get-tuple-element.35, ...), kind=kLoop, calls=%fused_computation.119 | loop fusion | flops 13312000 | bytes 7987200
  64.2 0.2 slice.103
  64.5 3.0 %copy.23 = bf16[4,64,8,640]{3,2,1,0:T(8,128)(2,1)} copy(bf16[4,64,8,640]{3,1,2,0:T(8,128)(2,1)S(1)} %bitcast.47) | data formatting | bytes 5242880 | tf_op jit(solution)/shard_map/transpose | solution.py:344
  67.5 0.7 pad_maximum_fusion.3.margin_ref
  68.2 7.6 %shard_map.113 = (bf16[4,512,1536]{2,1,0:T(8,128)(2,1)}, bf16[4,544,1536]{2,1,0:T(8,128)(2,1)}) custom-call(s32[15]{0:T(128)} %concatenate.56.meta, bf16[4,512,640]{2,1,0:T(8,128)(2,1)} %bitcast.46, bf16[4,32,640]{2,1,0:T(8,128)(2,1)} %pad_maximum_fusion.3.margin_ref, bf16[640,1536]{1,0:T(8,128)(2,1)} %bitcast.53, f32[2,1536]{1,0:T(2,128)} %bitcast.58), custom_call_target="tpu_custom_call" | custom-call | flops 267386880 | bytes 1009664 | tf_op jit(solution)/shard_map/pallas_call | solution.py:221
  75.8 0.7 collective-permute-start.12
  76.6 11.4 %collective-permute-start = (bf16[160,1536]{1,0:T(8,128)(2,1)S(1)}, bf16[160,1536]{1,0:T(8,128)(2,1)S(1)}, u32[]{:S(2)}, u32[]{:S(2)}) collective-permute-start(bf16[160,1536]{1,0:T(8,128)(2,1)S(1)} %maximum_maximum_fusion.1.rest_0_), channel_id=1, source_target_pairs={{0,1},{3,2},{4,5},{7,6},{8,9},{11,10},{12,13},{15,14},{16,17},{19,... | collective-permute-start | bytes 1474568 | tf_op jit(solution)/shard_map/ppermute | solution.py:254
  88.1 0.7 collective-permute-start.1
  88.8 4.0 %collective-permute-start.2 = (bf16[160,1536]{1,0:T(8,128)(2,1)S(1)}, bf16[160,1536]{1,0:T(8,128)(2,1)S(1)}, u32[]{:S(2)}, u32[]{:S(2)}) collective-permute-start(bf16[160,1536]{1,0:T(8,128)(2,1)S(1)} %maximum_maximum_fusion.1.rest_0_), channel_id=1, source_target_pairs={{0,2},{3,1},{4,6},{7,5},{8,10},{11,9},{12,14},{15,13},{16,18},{19,... | collective-permute-start | bytes 1474568 | tf_op jit(solution)/shard_map/ppermute | solution.py:254
  92.8 0.9 collective-permute-start.13
  93.7 1.0 broadcast_in_dim.18.taps_ref
  94.8 5.8 %shard_map.114.swished_ref = bf16[4,512,768]{2,1,0:T(8,128)(2,1)} custom-call(s32[15]{0:T(128)} %concatenate.56.meta, bf16[4,544,1536]{2,1,0:T(8,128)(2,1)} %get-tuple-element.12.normed_ref, f32[31,8,768]{2,1,0:T(8,128)} %broadcast_in_dim.18.taps_ref, bf16[192,1536]{1,0:T(8,128)(2,1)} %bitcast.50, bf16[256,1536]{1,0:T(8,128)(2,1)} %copy-done.2, ...), custom_call_target="tpu_custom_call" | custom-call | flops 641728512 | bytes 712704 | tf_op jit(solution)/shard_map/pallas_call | solution.py:221
  100.7 9.0 %collective-permute-done.2.rest_3_ = bf16[160,1536]{1,0:T(8,128)(2,1)S(1)} collective-permute-done((bf16[160,1536]{1,0:T(8,128)(2,1)S(1)}, bf16[160,1536]{1,0:T(8,128)(2,1)S(1)}, u32[]{:S(2)}, u32[]{:S(2)}) %collective-permute-start.2) | collective-permute-done | bytes 491552 | tf_op jit(solution)/shard_map/ppermute | solution.py:254
  109.7 0.7 collective-permute-start.14
  110.4 0.7 collective-permute-start.15
  111.1 0.7 collective-permute-start.16
  111.9 0.7 copy-done.10
  112.6 0.2 copy-done.11
  112.8 0.2 copy-done.12
  112.9 0.2 copy-done.13
  113.1 6.1 %shard_map.115 = f32[4,8,128]{2,1,0:T(8,128)} custom-call(s32[15]{0:T(128)} %concatenate.56.meta, bf16[4,512,768]{2,1,0:T(8,128)(2,1)} %shard_map.114.swished_ref, bf16[4,512,1536]{2,1,0:T(8,128)(2,1)} %get-tuple-element.15.stem_out_ref, s32[4,8,64]{2,1,0:T(8,128)} %pad_add_fusion.code_ref, f32[2,1536]{1,0:T(2,128)} %bitcast.59, ...), custom_call_target="tpu_custom_call" | custom-call | flops 503316480 | bytes 589824 | tf_op jit(solution)/shard_map/pallas_call | solution.py:221
  119.2 1.6 collective-permute-start.17
  120.8 1.5 collective-permute-start.18
  122.3 0.5 collective-permute-start.19
  122.8 0.5 collective-permute-done.17
  123.3 1.5 collective-permute-done.18
  124.7 2.4 %collective-permute-done.19 = f32[4,8,128]{2,1,0:T(8,128)S(1)} collective-permute-done((f32[4,8,128]{2,1,0:T(8,128)}, f32[4,8,128]{2,1,0:T(8,128)S(1)}, u32[]{:S(2)}, u32[]{:S(2)}) %collective-permute-start.19) | collective-permute-done | bytes 16416 | tf_op jit(solution)/shard_map/ppermute | solution.py:263
  127.2 0.7 add_multiply_fusion
  127.9 0.6 slice_reduce_fusion
  128.6 0.6 pad_maximum_fusion.10
  129.2 1.3 collective-permute-start.20
  130.5 1.2 collective-permute-start.21
  131.8 1.3 collective-permute-start.22
  133.1 34.6 %collective-permute-done.22 = f32[1]{0:T(128)} collective-permute-done((f32[1]{0:T(128)}, f32[1]{0:T(128)}, u32[]{:S(2)}, u32[]{:S(2)}) %collective-permute-start.22) | collective-permute-done | bytes 36 | tf_op jit(solution)/shard_map/ppermute | solution.py:254
  169.0 0.5 slice.108
  170.9 0.6 slice_select_fusion.3
  (77 shorter events, 1.3 us)
Async XLA Ops:
  0.6 9.8 %copy-start = (bf16[1,192,1536]{2,1,0:T(8,128)(2,1)S(1)}, bf16[1,192,1536]{2,1,0:T(8,128)(2,1)}, u32[]{:S(2)}) copy-start(bf16[1,192,1536]{2,1,0:T(8,128)(2,1)} %param.15) | copy-start | bytes 1769476
  0.6 75.2 %collective-permute-start.3 = (bf16[192,1536]{1,0:T(8,128)(2,1)}, bf16[192,1536]{1,0:T(8,128)(2,1)}, u32[]{:S(2)}, u32[]{:S(2)}) collective-permute-start(bf16[192,1536]{1,0:T(8,128)(2,1)} %bitcast.48), channel_id=1, source_target_pairs={{0,2},{3,1},{4,6},{7,5},{8,10},{11,9},{12,14},{15,13},{16,18},{19,... | collective-permute-start | bytes 1769480 | tf_op jit(solution)/shard_map/ppermute | solution.py:254
  7.5 80.5 %collective-permute-start.9 = (bf16[192,1536]{1,0:T(8,128)(2,1)}, bf16[192,1536]{1,0:T(8,128)(2,1)}, u32[]{:S(2)}, u32[]{:S(2)}) collective-permute-start(bf16[192,1536]{1,0:T(8,128)(2,1)} %bitcast.49), channel_id=1, source_target_pairs={{1,5},{2,6},{5,1},{6,2},{9,13},{10,14},{13,9},{14,10},{17,21},{18,... | collective-permute-start | bytes 1769480 | tf_op jit(solution)/shard_map/ppermute | solution.py:259
  9.0 2.9 %copy-start.3 = (bf16[1,4096,80]{1,2,0:T(8,128)(2,1)S(1)}, bf16[1,4096,80]{1,2,0:T(8,128)(2,1)}, u32[]{:S(2)}) copy-start(bf16[1,4096,80]{1,2,0:T(8,128)(2,1)} %param.10) | copy-start | bytes 1966084
  10.4 4.8 %copy-start.18 = (s32[1,1024]{1,0:T(1,128)S(1)}, s32[1,1024]{1,0:T(1,128)}, u32[]{:S(2)}) copy-start(s32[1,1024]{1,0:T(1,128)} %param.13) | copy-start | bytes 12292
  10.4 4.9 %copy-start.19 = (s32[1,1024]{1,0:T(1,128)S(1)}, s32[1,1024]{1,0:T(1,128)}, u32[]{:S(2)}) copy-start(s32[1,1024]{1,0:T(1,128)} %param.12) | copy-start | bytes 12292
  10.5 6.7 %copy-start.16 = (bf16[1,192,512]{2,1,0:T(8,128)(2,1)S(1)}, bf16[1,192,512]{2,1,0:T(8,128)(2,1)}, u32[]{:S(2)}) copy-start(bf16[1,192,512]{2,1,0:T(8,128)(2,1)} %param.18) | copy-start | bytes 589828
  10.5 25.9 %collective-permute-start.5 = (bf16[256,1536]{1,0:T(8,128)(2,1)S(1)}, bf16[256,1536]{1,0:T(8,128)(2,1)S(1)}, u32[]{:S(2)}, u32[]{:S(2)}) collective-permute-start(bf16[256,1536]{1,0:T(8,128)(2,1)S(1)} %maximum_maximum_fusion), channel_id=1, source_target_pairs={{0,1},{3,2},{4,5},{7,6},{8,9},{11,10},{12,13},{15,14},{16,17},{19,... | collective-permute-start | bytes 2359304 | tf_op jit(solution)/shard_map/ppermute | solution.py:254
  13.1 31.5 %collective-permute-start.4 = (bf16[208,1536]{1,0:T(8,128)(2,1)}, bf16[208,1536]{1,0:T(8,128)(2,1)}, u32[]{:S(2)}, u32[]{:S(2)}) collective-permute-start(bf16[208,1536]{1,0:T(8,128)(2,1)} %fusion.1), channel_id=1, source_target_pairs={{1,2},{2,1},{5,6},{6,5},{9,10},{10,9},{13,14},{14,13},{17,18},{18,... | collective-permute-start | bytes 1916936 | tf_op jit(solution)/shard_map/ppermute | solution.py:254
  15.3 22.8 %collective-permute-start.8 = (s32[1024]{0:T(1024)S(1)}, s32[1024]{0:T(1024)S(1)}, u32[]{:S(2)}, u32[]{:S(2)}) collective-permute-start(s32[1024]{0:T(1024)S(1)} %fusion.65), channel_id=1, source_target_pairs={{0,1},{3,2},{4,5},{7,6},{8,9},{11,10},{12,13},{15,14},{16,17},{19,... | collective-permute-start | bytes 12296 | tf_op jit(solution)/shard_map/ppermute | solution.py:254
  36.4 15.0 %copy-start.2 = (bf16[256,1536]{1,0:T(8,128)(2,1)}, bf16[256,1536]{1,0:T(8,128)(2,1)S(1)}, u32[]{:S(2)}) copy-start(bf16[256,1536]{1,0:T(8,128)(2,1)S(1)} %collective-permute-done.5.rest_1_) | copy-start | bytes 2359300
  36.6 5.8 %collective-permute-start.6 = (bf16[256,320]{1,0:T(8,128)(2,1)S(1)}, bf16[256,320]{1,0:T(8,128)(2,1)S(1)}, u32[]{:S(2)}, u32[]{:S(2)}) collective-permute-start(bf16[256,320]{1,0:T(8,128)(2,1)S(1)} %bitcast.55), channel_id=1, source_target_pairs={{0,8},{8,0},{16,24},{24,16},{1,9},{9,1},{17,25},{25,17},{2,10},{10... | collective-permute-start | bytes 491528 | tf_op jit(solution)/shard_map/ppermute | solution.py:263
  42.4 8.8 %collective-permute-start.7 = (bf16[512,320]{1,0:T(8,128)(2,1)S(1)}, bf16[512,320]{1,0:T(8,128)(2,1)S(1)}, u32[]{:S(2)}, u32[]{:S(2)}) collective-permute-start(bf16[512,320]{1,0:T(8,128)(2,1)S(1)} %pad_maximum_fusion.2), channel_id=1, source_target_pairs={{0,16},{8,24},{16,0},{24,8},{1,17},{9,25},{17,1},{25,9},{2,18},{10... | collective-permute-start | bytes 983048 | tf_op jit(solution)/shard_map/ppermute | solution.py:263
  44.6 44.1 %collective-permute-start.11 = (bf16[208,1536]{1,0:T(8,128)(2,1)}, bf16[208,1536]{1,0:T(8,128)(2,1)S(1)}, u32[]{:S(2)}, u32[]{:S(2)}) collective-permute-start(bf16[208,1536]{1,0:T(8,128)(2,1)} %collective-permute-done.4.rest_2_), channel_id=1, source_target_pairs={{1,5},{2,6},{5,1},{6,2},{9,13},{10,14},{13,9},{14,10},{17,21},{18,... | collective-permute-start | bytes 1916936 | tf_op jit(solution)/shard_map/ppermute | solution.py:259
  46.0 46.7 %collective-permute-start.10 = (bf16[256,1536]{1,0:T(8,128)(2,1)S(1)}, bf16[256,1536]{1,0:T(8,128)(2,1)S(1)}, u32[]{:S(2)}, u32[]{:S(2)}) collective-permute-start(bf16[256,1536]{1,0:T(8,128)(2,1)S(1)} %collective-permute-done.5.rest_1_), channel_id=1, source_target_pairs={{1,5},{2,6},{5,1},{6,2},{9,13},{10,14},{13,9},{14,10},{17,21},{18,... | collective-permute-start | bytes 2359304 | tf_op jit(solution)/shard_map/ppermute | solution.py:259
  68.2 8.3 %copy-start.14 = (bf16[1,96,1536]{2,1,0:T(8,128)(2,1)S(1)}, bf16[1,96,1536]{2,1,0:T(8,128)(2,1)}, u32[]{:S(2)}) copy-start(bf16[1,96,1536]{2,1,0:T(8,128)(2,1)} %param.16) | copy-start | bytes 884740
  68.2 8.4 %copy-start.15 = (bf16[64,512]{1,0:T(8,128)(2,1)S(1)}, bf16[64,512]{1,0:T(8,128)(2,1)}, u32[]{:S(2)}) copy-start(bf16[64,512]{1,0:T(8,128)(2,1)} %get-tuple-element.52) | copy-start | bytes 196612
  68.2 24.6 %copy-start.17 = (bf16[1,31,768]{2,1,0:T(8,128)(2,1)S(1)}, bf16[1,31,768]{2,1,0:T(8,128)(2,1)}, u32[]{:S(2)}) copy-start(bf16[1,31,768]{2,1,0:T(8,128)(2,1)} %param.17) | copy-start | bytes 142852
  75.8 17.9 %collective-permute-start.12 = (bf16[192,1536]{1,0:T(8,128)(2,1)}, bf16[192,1536]{1,0:T(8,128)(2,1)S(1)}, u32[]{:S(2)}, u32[]{:S(2)}) collective-permute-start(bf16[192,1536]{1,0:T(8,128)(2,1)} %collective-permute-done.3.rest_3_), channel_id=1, source_target_pairs={{1,5},{2,6},{5,1},{6,2},{9,13},{10,14},{13,9},{14,10},{17,21},{18,... | collective-permute-start | bytes 1769480 | tf_op jit(solution)/shard_map/ppermute | solution.py:259
  76.6 24.0 %copy-start.1 = (bf16[160,1536]{1,0:T(8,128)(2,1)}, bf16[160,1536]{1,0:T(8,128)(2,1)S(1)}, u32[]{:S(2)}) copy-start(bf16[160,1536]{1,0:T(8,128)(2,1)S(1)} %maximum_maximum_fusion.1.rest_0_) | copy-start | bytes 1474564
  76.6 24.0 %collective-permute-start = (bf16[160,1536]{1,0:T(8,128)(2,1)S(1)}, bf16[160,1536]{1,0:T(8,128)(2,1)S(1)}, u32[]{:S(2)}, u32[]{:S(2)}) collective-permute-start(bf16[160,1536]{1,0:T(8,128)(2,1)S(1)} %maximum_maximum_fusion.1.rest_0_), channel_id=1, source_target_pairs={{0,1},{3,2},{4,5},{7,6},{8,9},{11,10},{12,13},{15,14},{16,17},{19,... | collective-permute-start | bytes 1474568 | tf_op jit(solution)/shard_map/ppermute | solution.py:254
  88.1 12.6 %collective-permute-start.1 = (bf16[160,1536]{1,0:T(8,128)(2,1)S(1)}, bf16[160,1536]{1,0:T(8,128)(2,1)S(1)}, u32[]{:S(2)}, u32[]{:S(2)}) collective-permute-start(bf16[160,1536]{1,0:T(8,128)(2,1)S(1)} %maximum_maximum_fusion.1.rest_0_), channel_id=1, source_target_pairs={{1,2},{2,1},{5,6},{6,5},{9,10},{10,9},{13,14},{14,13},{17,18},{18,... | collective-permute-start | bytes 1474568 | tf_op jit(solution)/shard_map/ppermute | solution.py:254
  88.8 6.0 %copy-start.5 = (bf16[208,1536]{1,0:T(8,128)(2,1)}, bf16[208,1536]{1,0:T(8,128)(2,1)S(1)}, u32[]{:S(2)}) copy-start(bf16[208,1536]{1,0:T(8,128)(2,1)S(1)} %collective-permute-done.11.rest_6_) | copy-start | bytes 1916932
  88.8 20.9 %collective-permute-start.2 = (bf16[160,1536]{1,0:T(8,128)(2,1)S(1)}, bf16[160,1536]{1,0:T(8,128)(2,1)S(1)}, u32[]{:S(2)}, u32[]{:S(2)}) collective-permute-start(bf16[160,1536]{1,0:T(8,128)(2,1)S(1)} %maximum_maximum_fusion.1.rest_0_), channel_id=1, source_target_pairs={{0,2},{3,1},{4,6},{7,5},{8,10},{11,9},{12,14},{15,13},{16,18},{19,... | collective-permute-start | bytes 1474568 | tf_op jit(solution)/shard_map/ppermute | solution.py:254
  92.8 1.9 %copy-start.4 = (bf16[256,1536]{1,0:T(8,128)(2,1)}, bf16[256,1536]{1,0:T(8,128)(2,1)S(1)}, u32[]{:S(2)}) copy-start(bf16[256,1536]{1,0:T(8,128)(2,1)S(1)} %collective-permute-done.10.rest_5_) | copy-start | bytes 2359300
  92.8 19.0 %collective-permute-start.13 = (bf16[160,1536]{1,0:T(8,128)(2,1)S(1)}, bf16[160,1536]{1,0:T(8,128)(2,1)S(1)}, u32[]{:S(2)}, u32[]{:S(2)}) collective-permute-start(bf16[160,1536]{1,0:T(8,128)(2,1)S(1)} %maximum_maximum_fusion.1.rest_0_), channel_id=1, source_target_pairs={{1,5},{2,6},{5,1},{6,2},{9,13},{10,14},{13,9},{14,10},{17,21},{18,... | collective-permute-start | bytes 1474568 | tf_op jit(solution)/shard_map/ppermute | solution.py:259
  93.7 1.1 copy-start.6
  100.7 11.2 %copy-start.7 = (bf16[160,1536]{1,0:T(8,128)(2,1)}, bf16[160,1536]{1,0:T(8,128)(2,1)S(1)}, u32[]{:S(2)}) copy-start(bf16[160,1536]{1,0:T(8,128)(2,1)S(1)} %collective-permute-done.rest_1_) | copy-start | bytes 1474564
  100.7 11.2 %copy-start.8 = (bf16[160,1536]{1,0:T(8,128)(2,1)}, bf16[160,1536]{1,0:T(8,128)(2,1)S(1)}, u32[]{:S(2)}) copy-start(bf16[160,1536]{1,0:T(8,128)(2,1)S(1)} %collective-permute-done.1.rest_2_) | copy-start | bytes 1474564
  109.7 2.2 %copy-start.9 = (bf16[160,1536]{1,0:T(8,128)(2,1)}, bf16[160,1536]{1,0:T(8,128)(2,1)S(1)}, u32[]{:S(2)}) copy-start(bf16[160,1536]{1,0:T(8,128)(2,1)S(1)} %collective-permute-done.2.rest_3_) | copy-start | bytes 1474564
  109.7 2.1 %collective-permute-start.14 = (bf16[160,1536]{1,0:T(8,128)(2,1)S(1)}, bf16[160,1536]{1,0:T(8,128)(2,1)S(1)}, u32[]{:S(2)}, u32[]{:S(2)}) collective-permute-start(bf16[160,1536]{1,0:T(8,128)(2,1)S(1)} %collective-permute-done.rest_1_), channel_id=1, source_target_pairs={{1,5},{2,6},{5,1},{6,2},{9,13},{10,14},{13,9},{14,10},{17,21},{18,... | collective-permute-start | bytes 1474568 | tf_op jit(solution)/shard_map/ppermute | solution.py:259
  110.4 1.4 collective-permute-start.15
  111.1 0.8 collective-permute-start.16
  111.8 0.8 copy-start.10
  111.8 0.9 copy-start.11
  111.9 1.1 copy-start.12
  111.9 1.2 copy-start.13
  119.2 4.0 %collective-permute-start.17 = (f32[4,8,128]{2,1,0:T(8,128)}, f32[4,8,128]{2,1,0:T(8,128)S(1)}, u32[]{:S(2)}, u32[]{:S(2)}) collective-permute-start(f32[4,8,128]{2,1,0:T(8,128)} %shard_map.115), channel_id=1, source_target_pairs={{0,8},{8,0},{16,24},{24,16},{1,9},{9,1},{17,25},{25,17},{2,10},{10... | collective-permute-start | bytes 49160 | tf_op jit(solution)/shard_map/ppermute | solution.py:263
  120.8 3.9 %collective-permute-start.18 = (f32[4,8,128]{2,1,0:T(8,128)}, f32[4,8,128]{2,1,0:T(8,128)S(1)}, u32[]{:S(2)}, u32[]{:S(2)}) collective-permute-start(f32[4,8,128]{2,1,0:T(8,128)} %shard_map.115), channel_id=1, source_target_pairs={{0,16},{8,24},{16,0},{24,8},{1,17},{9,25},{17,1},{25,9},{2,18},{10... | collective-permute-start | bytes 49160 | tf_op jit(solution)/shard_map/ppermute | solution.py:263
  122.3 4.8 %collective-permute-start.19 = (f32[4,8,128]{2,1,0:T(8,128)}, f32[4,8,128]{2,1,0:T(8,128)S(1)}, u32[]{:S(2)}, u32[]{:S(2)}) collective-permute-start(f32[4,8,128]{2,1,0:T(8,128)} %shard_map.115), channel_id=1, source_target_pairs={{0,24},{8,16},{16,8},{24,0},{1,25},{9,17},{17,9},{25,1},{2,26},{10... | collective-permute-start | bytes 49160 | tf_op jit(solution)/shard_map/ppermute | solution.py:263
  129.2 39.8 %collective-permute-start.20 = (f32[1025]{0:T(1024)S(1)}, f32[1025]{0:T(1024)S(1)}, u32[]{:S(2)}, u32[]{:S(2)}) collective-permute-start(f32[1025]{0:T(1024)S(1)} %pad_maximum_fusion.10), channel_id=1, source_target_pairs={{1,0},{2,3},{5,4},{6,7},{9,8},{10,11},{13,12},{14,15},{17,16},{18,... | collective-permute-start | bytes 12308 | tf_op jit(solution)/shard_map/ppermute | solution.py:254
  130.5 2.6 %collective-permute-start.21 = (f32[1]{0:T(128)}, f32[1]{0:T(128)}, u32[]{:S(2)}, u32[]{:S(2)}) collective-permute-start(f32[1]{0:T(128)} %bitcast.25), channel_id=1, source_target_pairs={{1,2},{2,1},{5,6},{6,5},{9,10},{10,9},{13,14},{14,13},{17,18},{18,... | collective-permute-start | bytes 20 | tf_op jit(solution)/shard_map/ppermute | solution.py:254
  131.8 36.0 %collective-permute-start.22 = (f32[1]{0:T(128)}, f32[1]{0:T(128)}, u32[]{:S(2)}, u32[]{:S(2)}) collective-permute-start(f32[1]{0:T(128)} %bitcast.25), channel_id=1, source_target_pairs={{2,0},{1,3},{6,4},{5,7},{10,8},{9,11},{14,12},{13,15},{18,16},{17,... | collective-permute-start | bytes 20 | tf_op jit(solution)/shard_map/ppermute | solution.py:254

commit v6 on v5

--- a/solution.py
+++ b/solution.py
@@ -8,7 +8,7 @@
 LANES = 128
 CHUNKS = 8
 EDGE = 16
-VMEM_BYTES = 56 * 1024 * 1024
+VMEM_BYTES = 24 * 1024 * 1024
 
 
 def norm_rows(values, gain_row):
@@ -48,12 +48,14 @@
 
 def shards(meta, pieces):
     side = meta[13]
-    return [(pieces[i], (side if i < 4 else 1 - side) * 4 + meta[9 + i % 4]) for i in range(8)]
+    length = pieces[0].shape[0]
+    places = [(pieces[i], 0) for i in range(5)] + [(pieces[5], i * length) for i in range(3)]
+    return [(*place, (side if i < 4 else 1 - side) * 4 + meta[9 + i % 4]) for i, place in enumerate(places)]
 
 
 def conv_kernel(meta, normed_ref, taps_ref, *rest):
-    pieces = rest[:8]
-    swished_ref, weight, mixed, gated_a, gated_b, margin, mask, sems = rest[8:]
+    pieces = rest[:6]
+    swished_ref, weight, mixed_a, mixed_b, gated, margin, mask, sems = rest[6:]
     slot = pl.program_id(0)
     rows = normed_ref.shape[1]
     frames = swished_ref.shape[1]
@@ -67,9 +69,9 @@
     def _():
         copies = [
             pltpu.make_async_copy(
-                ref.at[pl.ds(0, piece)], weight.at[pl.ds(pl.multiple_of(block * piece, 16), piece)], sems.at[i]
+                ref.at[pl.ds(at, piece)], weight.at[pl.ds(pl.multiple_of(block * piece, 16), piece)], sems.at[i]
             )
-            for i, (ref, block) in enumerate(shards(meta, pieces))
+            for i, (ref, at, block) in enumerate(shards(meta, pieces))
         ]
         for copy in copies:
             copy.start()
@@ -84,20 +86,21 @@
         at = meta[slot] + jnp.where(row < frames, inner, outer)
         mask[...] = jnp.logical_and(at >= 0, at < meta[4]).astype(jnp.float32)
         sublane = lax.broadcasted_iota(jnp.int32, (CHUNKS, LANES), 0)
-        half = rows // 2
-        for first in (0, half):
-            mixed[first : first + half, :] = jnp.dot(
-                normed_ref[0, first : first + half, :], weight[...], preferred_element_type=jnp.float32
+        buffers = (mixed_a, mixed_b)
+
+        def mix(block):
+            low = block * LANES
+            right = jnp.concatenate(
+                [weight[:, low : low + LANES], weight[:, channels + low : channels + low + LANES]], axis=1
             )
+            buffers[block % 2][...] = jnp.dot(normed_ref[0], right, preferred_element_type=jnp.float32)
 
         def gate(block):
-            low = block * LANES
-            gated = (gated_a, gated_b)[block % 2]
+            mixed = buffers[block % 2]
             group = 32
             for at in range(0, rows, group):
                 here = slice(at, at + group)
-                made = mixed[here, low : low + LANES] * mask[here, :]
-                made = made * sigmoid(mixed[here, channels + low : channels + low + LANES])
+                made = mixed[here, :LANES] * sigmoid(mixed[here, LANES:]) * mask[here, :]
                 made = made.astype(jnp.bfloat16).astype(jnp.float32)
                 if at < frames:
                     first = reach + at // CHUNKS
@@ -114,19 +117,15 @@
 
         def convolve(block):
             low = block * LANES
-            run, held = 32, 8
-            gated = (gated_a, gated_b)[block % 2]
+            run = 16
             for start in range(0, run_length, run):
                 sums = [None] * run
-                for tap in range(0, tap_count, held):
-                    taps = [taps_ref[j, :, low : low + LANES] for j in range(tap, min(tap + held, tap_count))]
-                    for at in range(start + tap, start + tap + run + len(taps) - 1):
-                        value = gated[at]
-                        for j, weight_row in enumerate(taps):
-                            k = at - tap - j - start
-                            if 0 <= k < run:
-                                term = value * weight_row
-                                sums[k] = term if sums[k] is None else sums[k] + term
+                for at in range(start, start + run + tap_count - 1):
+                    value = gated[at]
+                    for m in range(max(start, at - tap_count + 1), min(start + run, at + 1)):
+                        term = value * taps_ref[at - m, :, low : low + LANES]
+                        k = m - start
+                        sums[k] = term if sums[k] is None else sums[k] + term
                 for k in range(0, run, 2):
                     total = jnp.concatenate(sums[k : k + 2], axis=0)
                     first = (start + k) * CHUNKS
@@ -135,14 +134,17 @@
                     ).astype(jnp.bfloat16)
 
         blocks = channels // LANES
+        mix(0)
         for block in range(blocks):
+            if block + 1 < blocks:
+                mix(block + 1)
             gate(block)
             convolve(block)
 
 
 def head_kernel(meta, swished_ref, stem_out_ref, code_ref, gain_ref, *rest):
-    pieces = rest[:8]
-    error_ref, back, head, acc_a, acc_b, norm_a, norm_b, logit_a, logit_b, sems = rest[8:]
+    pieces = rest[:6]
+    error_ref, back, head, acc_a, acc_b, norm_a, norm_b, logit_a, logit_b, sems = rest[6:]
     slot = pl.program_id(0)
     frames = swished_ref.shape[1]
     vocab = head.shape[1]
@@ -154,10 +156,10 @@
     @pl.when(jnp.logical_and(pl.program_id(0) == 0, meta[14] > 0))
     def _():
         copies = []
-        for i, (ref, block) in enumerate(shards(meta, pieces)):
+        for i, (ref, at, block) in enumerate(shards(meta, pieces)):
             copies.append(
                 pltpu.make_async_copy(
-                    ref.at[pl.ds(0, back_rows)],
+                    ref.at[pl.ds(at, back_rows)],
                     back.at[pl.ds(pl.multiple_of(block * back_rows, 16), back_rows)],
                     sems.at[i, 0],
                 )
@@ -165,7 +167,7 @@
             for g in range(groups):
                 copies.append(
                     pltpu.make_async_copy(
-                        ref.at[pl.ds(back_rows, group_rows), pl.ds(g * vocab, vocab)],
+                        ref.at[pl.ds(at + back_rows, group_rows), pl.ds(g * vocab, vocab)],
                         head.at[pl.ds(pl.multiple_of(block * head_rows + g * group_rows, 16), group_rows)],
                         sems.at[i, 1 + g],
                     )
@@ -288,27 +290,22 @@
     low = chip == 1
     is_hub = jnp.logical_or(low, chip == 2)
 
+    length = lengths[0]
+    positions = chip * rows + jnp.arange(rows, dtype=jnp.int32)
+    counted = jnp.logical_and(frame_mask[0] > 0, positions < length)
+    code = jnp.where(counted, targets[0], -1)
     first = conv_in_weight[0]
     blocks = mel_frames[0].reshape(rows, -1)
-    deep_in = blocks.shape[1]
     share = rows // seeds
-    stack = width // (-(-deep_in // LANES) * LANES)
-
-    def widened(x, count):
-        side = width // stack
-        parts = jnp.pad(x, ((0, 0), (0, side - deep_in))).reshape(count, -1, side)
-        return jnp.pad(jnp.concatenate(list(parts), axis=1), ((0, 0), (0, (stack - count) * side)))
-
+    margin = step * EDGE
     quarter = lax.dynamic_slice_in_dim(mel_frames[0], seed * share * step, share * step, 0).reshape(share, -1)
-    margin = step * EDGE
     edge_out = jnp.where(low, mel_frames[0, -margin:], mel_frames[0, :margin]).reshape(EDGE, -1)
-    far_first = along(first, BEYOND)
-    near_first = along(jnp.concatenate([first, widened(quarter, stack)], axis=0), INWARD)
-    hub_first = along(jnp.concatenate([first, widened(edge_out, 1)], axis=0), ACROSS)
+    quarter_in = along(quarter, INWARD)
+    edge = along(edge_out, ACROSS)
+    outer_code = along(code, INWARD)
+    first_held, quarter_in, edge, outer_code = lax.optimization_barrier((first, quarter_in, edge, outer_code))
+    near_first, hub_first, far_first = [along(first_held, pairs_) for pairs_ in (INWARD, ACROSS, BEYOND)]
     held = first.shape[0]
-    edge = hub_first[held:, :deep_in]
-    quarter_in = near_first[held:].reshape(share // stack, stack, -1).transpose(1, 0, 2).reshape(share, -1)
-    quarter_in = quarter_in[:, :deep_in]
 
     pair = seed_swap(quarter_in, 1)
     odd = seed % 2 == 1
@@ -335,7 +332,7 @@
             jnp.where(low, outer, blocks),
             jnp.where(low, blocks, outer),
             jnp.where(low, edge, none),
-            none[:1],
+            none,
         ],
         axis=0,
     )
@@ -349,10 +346,6 @@
         ]
     )
 
-    length = lengths[0]
-    positions = chip * rows + jnp.arange(rows, dtype=jnp.int32)
-    counted = jnp.logical_and(frame_mask[0] > 0, positions < length)
-    code = jnp.where(counted, targets[0], -1)
     starts = (chip - 1) * 2 * rows + tile * jnp.arange(slots, dtype=jnp.int32)
     alive = jnp.logical_and(is_hub, starts < length).astype(jnp.int32)
     hub = jnp.clip(chip, 1, 2)
@@ -387,12 +380,11 @@
     )
     pinned = pl.BlockSpec(memory_space=pltpu.HBM)
 
-    outer_code = along(code, INWARD)
     codes = jnp.concatenate([jnp.where(low, outer_code, code), jnp.where(low, code, outer_code)])
     codes = codes.reshape(slots, CHUNKS, tile // CHUNKS)
     far_first, normed, codes = lax.optimization_barrier((far_first, normed, codes))
     mine = [first, near_first, hub_first, far_first]
-    first_pieces = (*mine, *[to_mate(x) for x in mine])
+    first_pieces = (*mine, to_mate(first), to_mate(jnp.concatenate(mine[1:], axis=0)))
     near_second, hub_second, far_second = [along(second, pairs_) for pairs_ in (INWARD, ACROSS, BEYOND)]
     taps = jnp.broadcast_to(
         depth_weight[0].astype(jnp.float32)[:, None, :], (depth_weight.shape[1], CHUNKS, channels)
@@ -401,13 +393,13 @@
     swished = call(
         conv_kernel,
         (slots,),
-        [by_slot((deep, width)), whole(taps.shape)] + [pinned] * 8,
+        [by_slot((deep, width)), whole(taps.shape)] + [pinned] * 6,
         by_slot((tile, channels)),
         jax.ShapeDtypeStruct((slots, tile, channels), jnp.bfloat16),
         [
             pltpu.VMEM((8 * held, width), jnp.bfloat16),
-            pltpu.VMEM((deep, 2 * channels), jnp.float32),
-            pltpu.VMEM((extent, CHUNKS, LANES), jnp.float32),
+            pltpu.VMEM((deep, 2 * LANES), jnp.float32),
+            pltpu.VMEM((deep, 2 * LANES), jnp.float32),
             pltpu.VMEM((extent, CHUNKS, LANES), jnp.float32),
             pltpu.VMEM((2 * EDGE, LANES), jnp.float32),
             pltpu.VMEM((deep, LANES), jnp.float32),
@@ -422,12 +414,12 @@
         (near_second, hub_second, far_second, swished)
     )
     mine = [second, near_second, hub_second, far_second]
-    second_pieces = (*mine, to_mate(second), *[to_mate(x) for x in mine[1:]])
+    second_pieces = (*mine, to_mate(second), to_mate(jnp.concatenate(mine[1:], axis=0)))
     errors = call(
         head_kernel,
         (slots,),
         [by_slot((tile, channels)), by_slot((tile, width)), by_slot(codes.shape[1:]), whole(gains.shape)]
-        + [pinned] * 8,
+        + [pinned] * 6,
         by_slot((CHUNKS, LANES)),
         jax.ShapeDtypeStruct((slots, CHUNKS, LANES), jnp.float32),
         [

time: 174 us -> 128 us (0.74)
  waiting for transfers between devices: 71.8 us -> 51.5 us
  Pallas kernels: 19.6 us -> 2.42 us
  other arithmetic: 19 us -> 9.09 us
  starting transfers between devices: 44.9 us -> 48.1 us
    ppermute x10 -> x12, waiting for transfers between devices: 59 us -> 41.3 us  [along(): return lax.ppermute(x, 'seq', pairs)]
    pallas_call x3, Pallas kernels: 19.6 us -> 2.42 us  [call(): pl.pallas_call(kernel, grid_spec=pltpu.PrefetchScalarGridSpec(num_scalar_...]
    unnamed x5 -> x4, other arithmetic: 12.9 us -> 0.61 us
    ppermute x10 -> x12, starting transfers between devices: 31.5 us -> 38.4 us  [along(): return lax.ppermute(x, 'seq', pairs)]
    ppermute x8 -> x4, starting transfers between devices: 6.72 us -> 3.05 us  [to_mate(): return lax.ppermute(x, ('fsdp', 'seq'), pairs)]
    ppermute x5, waiting for transfers between devices: 12.8 us -> 10.1 us  [seed_swap(): return lax.ppermute(x, 'seed', [(i, i ^ bit) for i in range(4)])]
    concatenate x2, local copies, waits for them, and re-layouts: 0.14 us -> 2.68 us  [hub_body(): jnp.concatenate([jnp.where(low, outer_code, code), jnp.where(low, code, o...]
  transfers between devices with their start and end apart: 23 -> 21, of which waited for: 8 -> 8; matrix products, arithmetic and copies ran while one was open for 15% -> 11% of each run, Pallas kernels for 8% -> 1%
where the time goes in v6:
time: 128 us; the launch traced here: 127 us
  waiting for transfers between devices  51.5 us (40%)
  starting transfers between devices  48.1 us (38%)
  local copies, waits for them, and re-layouts  10.5 us (8%)
  other arithmetic  9.09 us (7%)
  between operations  5.54 us (4%)
  Pallas kernels  2.42 us (2%)
    ppermute x12, waiting for transfers between devices, along(): return lax.ppermute(x, 'seq', pairs)  41.3 us
    ppermute x12, starting transfers between devices, along(): return lax.ppermute(x, 'seq', pairs)  38.4 us
    ppermute x5, waiting for transfers between devices, seed_swap(): return lax.ppermute(x, 'seed', [(i, i ^ bit) for i in range(4)])  10.1 us
    ppermute x5, starting transfers between devices, seed_swap(): return lax.ppermute(x, 'seed', [(i, i ^ bit) for i in range(4)])  6.69 us
    ppermute x4, starting transfers between devices, to_mate(): return lax.ppermute(x, ('fsdp', 'seq'), pairs)  3.05 us
    concatenate x2, local copies, waits for them, and re-layouts, hub_body(): jnp.concatenate([jnp.where(low, outer_code, code), jnp.where(low, code, o...  2.68 us
  transfers between devices with their start and end apart: 21, of which 8 were waited for; matrix products, arithmetic and copies ran while one was open for 11% of the time, Pallas kernels for 1%

profile of v6, /device:TPU:0, one launch (start us, length us, event | category | flops | bytes accessed | tf_op | source)
XLA Modules:
  0.0 127.1 jit_solution(5696627939491791421)
XLA Ops:
  0.6 1.0 constant_dynamic-slice_fusion
  1.6 0.2 copy.16
  1.8 0.2 reshape.51
  2.0 4.9 %collective-permute-start.3 = (bf16[256,320]{1,0:T(8,128)(2,1)S(1)}, bf16[256,320]{1,0:T(8,128)(2,1)S(1)}, u32[]{:S(2)}, u32[]{:S(2)}) collective-permute-start(bf16[256,320]{1,0:T(8,128)(2,1)S(1)} %reshape.51), channel_id=1, source_target_pairs={{0,1},{3,2},{4,5},{7,6},{8,9},{11,10},{12,13},{15,14},{16,17},{19,... | collective-permute-start | bytes 491528 | tf_op jit(solution)/shard_map/ppermute | solution.py:256
  7.0 0.8 slice_select_fusion
  7.8 0.1 copy.17
  7.9 0.1 select_n.119
  8.0 0.7 collective-permute-start.4
  9.3 0.7 compare_reduce_fusion
  10.0 0.7 fusion.14
  10.7 4.1 %collective-permute-start.5 = (s32[1024]{0:T(1024)S(1)}, s32[1024]{0:T(1024)S(1)}, u32[]{:S(2)}, u32[]{:S(2)}) collective-permute-start(s32[1024]{0:T(1024)S(1)} %fusion.14), channel_id=1, source_target_pairs={{0,1},{3,2},{4,5},{7,6},{8,9},{11,10},{12,13},{15,14},{16,17},{19,... | collective-permute-start | bytes 12296 | tf_op jit(solution)/shard_map/ppermute | solution.py:256
  14.9 0.6 fusion.15
  15.5 0.6 copy.18
  16.2 0.7 reshape_squeeze.3
  16.9 0.7 concatenate.50.meta
  17.7 2.6 %collective-permute-start.6 = (bf16[192,1536]{1,0:T(8,128)(2,1)S(1)}, bf16[192,1536]{1,0:T(8,128)(2,1)S(1)}, u32[]{:S(2)}, u32[]{:S(2)}) collective-permute-start(bf16[192,1536]{1,0:T(8,128)(2,1)S(1)} %bitcast.45), channel_id=1, source_target_pairs={{0,2},{3,1},{4,6},{7,5},{8,10},{11,9},{12,14},{15,13},{16,18},{19,... | collective-permute-start | bytes 1769480 | tf_op jit(solution)/shard_map/ppermute | solution.py:256
  20.3 0.7 collective-permute-start.10
  21.0 3.1 %collective-permute-start.9 = (bf16[192,1536]{1,0:T(8,128)(2,1)S(1)}, bf16[192,1536]{1,0:T(8,128)(2,1)S(1)}, u32[]{:S(2)}, u32[]{:S(2)}) collective-permute-start(bf16[192,1536]{1,0:T(8,128)(2,1)S(1)} %bitcast.47), channel_id=1, source_target_pairs={{0,1},{3,2},{4,5},{7,6},{8,9},{11,10},{12,13},{15,14},{16,17},{19,... | collective-permute-start | bytes 1769480 | tf_op jit(solution)/shard_map/ppermute | solution.py:256
  24.1 1.6 %collective-permute-start.7 = (bf16[256,320]{1,0:T(8,128)(2,1)S(1)}, bf16[256,320]{1,0:T(8,128)(2,1)S(1)}, u32[]{:S(2)}, u32[]{:S(2)}) collective-permute-start(bf16[256,320]{1,0:T(8,128)(2,1)S(1)} %collective-permute-done.3), channel_id=1, source_target_pairs={{0,8},{8,0},{16,24},{24,16},{1,9},{9,1},{17,25},{25,17},{2,10},{10... | collective-permute-start | bytes 491528 | tf_op jit(solution)/shard_map/ppermute | solution.py:265
  25.6 1.3 %broadcast_select_fusion.5 = (s32[1024]{0:T(1024)}, s32[1024]{0:T(1024)}) fusion(s32[1024]{0:T(1024)} %copy-done.8, s32[1024]{0:T(1024)} %copy-done.7, pred[]{:T(512)S(6)} %eq.14), kind=kLoop, calls=%fused_computation.66 | loop fusion | flops 2048 | bytes 16385 | tf_op jit(solution)/shard_map/jit(_where)/select_n | solution.py:383
  26.9 1.3 %concatenate.61 = s32[2,8,64]{2,1,0:T(8,128)} reshape(s32[1024]{0:T(1024)} %get-tuple-element.48) | data formatting | bytes 8192 | tf_op jit(solution)/shard_map/concatenate | solution.py:383
  28.3 1.3 %concatenate.62 = s32[2,8,64]{2,1,0:T(8,128)} reshape(s32[1024]{0:T(1024)} %get-tuple-element.49) | data formatting | bytes 8192 | tf_op jit(solution)/shard_map/concatenate | solution.py:383
  29.6 0.2 collective-permute-done.7
  29.9 1.6 %collective-permute-start.8 = (bf16[512,320]{1,0:T(8,128)(2,1)S(1)}, bf16[512,320]{1,0:T(8,128)(2,1)S(1)}, u32[]{:S(2)}, u32[]{:S(2)}) collective-permute-start(bf16[512,320]{1,0:T(8,128)(2,1)S(1)} %pad_maximum_fusion.3), channel_id=1, source_target_pairs={{0,16},{8,24},{16,0},{24,8},{1,17},{9,25},{17,1},{25,9},{2,18},{10... | collective-permute-start | bytes 983048 | tf_op jit(solution)/shard_map/ppermute | solution.py:265
  31.5 0.7 pad_add_fusion.code_ref
  32.2 6.2 %collective-permute-done.8 = bf16[512,320]{1,0:T(8,128)(2,1)S(1)} collective-permute-done((bf16[512,320]{1,0:T(8,128)(2,1)S(1)}, bf16[512,320]{1,0:T(8,128)(2,1)S(1)}, u32[]{:S(2)}, u32[]{:S(2)}) %collective-permute-start.8) | collective-permute-done | bytes 327712 | tf_op jit(solution)/shard_map/ppermute | solution.py:265
  38.4 0.2 broadcast_select_fusion.1
  38.5 0.3 select_dynamic-update-slice_fusion.1
  38.8 0.3 select_dynamic-update-slice_fusion
  39.2 0.5 fusion.16
  39.7 1.0 fusion
  40.7 1.5 %copy.21 = bf16[4,64,8,640]{3,2,1,0:T(8,128)(2,1)S(1)} copy(bf16[4,64,8,640]{3,1,2,0:T(8,128)(2,1)S(1)} %bitcast.52) | data formatting | bytes 5242880 | tf_op jit(solution)/shard_map/transpose | solution.py:341
  42.2 0.1 fusion.7
  42.3 0.1 fusion.5
  42.4 1.4 %copy-done = bf16[1,640,1536]{2,1,0:T(8,128)(2,1)S(1)} copy-done((bf16[1,640,1536]{2,1,0:T(8,128)(2,1)S(1)}, bf16[1,640,1536]{2,1,0:T(8,128)(2,1)}, u32[]{:S(2)}) %copy-start) | copy-done | bytes 1966104
  43.8 0.6 shard_map.113
  44.5 0.1 pad_maximum_fusion
  44.7 0.9 collective-permute-start.12
  45.6 0.7 collective-permute-start.11
  46.4 13.7 %collective-permute-start = (bf16[160,1536]{1,0:T(8,128)(2,1)S(1)}, bf16[160,1536]{1,0:T(8,128)(2,1)S(1)}, u32[]{:S(2)}, u32[]{:S(2)}) collective-permute-start(bf16[160,1536]{1,0:T(8,128)(2,1)S(1)} %maximum_maximum_fusion.rest_0_), channel_id=1, source_target_pairs={{0,1},{3,2},{4,5},{7,6},{8,9},{11,10},{12,13},{15,14},{16,17},{19,... | collective-permute-start | bytes 1474568 | tf_op jit(solution)/shard_map/ppermute | solution.py:256
  60.1 0.7 collective-permute-start.1
  60.8 4.2 %collective-permute-start.2 = (bf16[160,1536]{1,0:T(8,128)(2,1)S(1)}, bf16[160,1536]{1,0:T(8,128)(2,1)S(1)}, u32[]{:S(2)}, u32[]{:S(2)}) collective-permute-start(bf16[160,1536]{1,0:T(8,128)(2,1)S(1)} %maximum_maximum_fusion.rest_0_), channel_id=1, source_target_pairs={{0,2},{3,1},{4,6},{7,5},{8,10},{11,9},{12,14},{15,13},{16,18},{19,... | collective-permute-start | bytes 1474568 | tf_op jit(solution)/shard_map/ppermute | solution.py:256
  65.1 0.8 shard_map.114.swished_ref
  65.8 5.8 %collective-permute-done.rest_1_ = bf16[160,1536]{1,0:T(8,128)(2,1)S(1)} collective-permute-done((bf16[160,1536]{1,0:T(8,128)(2,1)S(1)}, bf16[160,1536]{1,0:T(8,128)(2,1)S(1)}, u32[]{:S(2)}, u32[]{:S(2)}) %collective-permute-start) | collective-permute-done | bytes 491552 | tf_op jit(solution)/shard_map/ppermute | solution.py:256
  71.7 9.6 %collective-permute-done.2.rest_3_ = bf16[160,1536]{1,0:T(8,128)(2,1)S(1)} collective-permute-done((bf16[160,1536]{1,0:T(8,128)(2,1)S(1)}, bf16[160,1536]{1,0:T(8,128)(2,1)S(1)}, u32[]{:S(2)}, u32[]{:S(2)}) %collective-permute-start.2) | collective-permute-done | bytes 491552 | tf_op jit(solution)/shard_map/ppermute | solution.py:256
  81.3 0.1 pad_maximum_fusion.1
  81.4 0.8 collective-permute-start.14
  82.1 0.7 collective-permute-start.13
  82.9 1.0 shard_map.115
  83.9 1.2 collective-permute-start.15
  85.1 1.5 %collective-permute-start.16 = (f32[4,8,128]{2,1,0:T(8,128)S(1)}, f32[4,8,128]{2,1,0:T(8,128)S(1)}, u32[]{:S(2)}, u32[]{:S(2)}) collective-permute-start(f32[4,8,128]{2,1,0:T(8,128)S(1)} %shard_map.115), channel_id=1, source_target_pairs={{0,16},{8,24},{16,0},{24,8},{1,17},{9,25},{17,1},{25,9},{2,18},{10... | collective-permute-start | bytes 49160 | tf_op jit(solution)/shard_map/ppermute | solution.py:265
  86.6 0.9 collective-permute-start.17
  87.5 0.2 collective-permute-done.15
  87.7 1.3 %collective-permute-done.16 = f32[4,8,128]{2,1,0:T(8,128)S(1)} collective-permute-done((f32[4,8,128]{2,1,0:T(8,128)S(1)}, f32[4,8,128]{2,1,0:T(8,128)S(1)}, u32[]{:S(2)}, u32[]{:S(2)}) %collective-permute-start.16) | collective-permute-done | bytes 16416 | tf_op jit(solution)/shard_map/ppermute | solution.py:265
  89.0 2.2 %collective-permute-done.17 = f32[4,8,128]{2,1,0:T(8,128)S(1)} collective-permute-done((f32[4,8,128]{2,1,0:T(8,128)S(1)}, f32[4,8,128]{2,1,0:T(8,128)S(1)}, u32[]{:S(2)}, u32[]{:S(2)}) %collective-permute-start.17) | collective-permute-done | bytes 16416 | tf_op jit(solution)/shard_map/ppermute | solution.py:265
  91.2 0.6 slice_reduce_fusion
  91.8 0.1 select_n.141
  91.9 0.6 pad_maximum_fusion.5
  92.6 1.3 %collective-permute-start.18 = (f32[1025]{0:T(1024)S(1)}, f32[1025]{0:T(1024)S(1)}, u32[]{:S(2)}, u32[]{:S(2)}) collective-permute-start(f32[1025]{0:T(1024)S(1)} %pad_maximum_fusion.5), channel_id=1, source_target_pairs={{1,0},{2,3},{5,4},{6,7},{9,8},{10,11},{13,12},{14,15},{17,16},{18,... | collective-permute-start | bytes 12308 | tf_op jit(solution)/shard_map/ppermute | solution.py:256
  93.9 1.2 collective-permute-start.19
  95.0 1.3 %collective-permute-start.20 = (f32[1]{0:T(128)}, f32[1]{0:T(128)}, u32[]{:S(2)}, u32[]{:S(2)}) collective-permute-start(f32[1]{0:T(128)} %bitcast.23), channel_id=1, source_target_pairs={{2,0},{1,3},{6,4},{5,7},{10,8},{9,11},{14,12},{13,15},{18,16},{17,... | collective-permute-start | bytes 20 | tf_op jit(solution)/shard_map/ppermute | solution.py:256
  96.4 25.9 %collective-permute-done.20 = f32[1]{0:T(128)} collective-permute-done((f32[1]{0:T(128)}, f32[1]{0:T(128)}, u32[]{:S(2)}, u32[]{:S(2)}) %collective-permute-start.20) | collective-permute-done | bytes 36 | tf_op jit(solution)/shard_map/ppermute | solution.py:256
  123.5 0.5 slice.103
  125.3 0.6 slice_select_fusion.3
  (45 shorter events, 0.4 us)
Async XLA Ops:
  0.6 14.9 %copy-start.3 = (bf16[1,4096,80]{1,2,0:T(8,128)(2,1)S(1)}, bf16[1,4096,80]{1,2,0:T(8,128)(2,1)}, u32[]{:S(2)}) copy-start(bf16[1,4096,80]{1,2,0:T(8,128)(2,1)} %param.10) | copy-start | bytes 1966084
  2.0 15.6 %collective-permute-start.3 = (bf16[256,320]{1,0:T(8,128)(2,1)S(1)}, bf16[256,320]{1,0:T(8,128)(2,1)S(1)}, u32[]{:S(2)}, u32[]{:S(2)}) collective-permute-start(bf16[256,320]{1,0:T(8,128)(2,1)S(1)} %reshape.51), channel_id=1, source_target_pairs={{0,1},{3,2},{4,5},{7,6},{8,9},{11,10},{12,13},{15,14},{16,17},{19,... | collective-permute-start | bytes 491528 | tf_op jit(solution)/shard_map/ppermute | solution.py:256
  8.0 9.6 %collective-permute-start.4 = (bf16[16,320]{1,0:T(8,128)(2,1)S(1)}, bf16[16,320]{1,0:T(8,128)(2,1)S(1)}, u32[]{:S(2)}, u32[]{:S(2)}) collective-permute-start(bf16[16,320]{1,0:T(8,128)(2,1)S(1)} %select_n.119), channel_id=1, source_target_pairs={{1,2},{2,1},{5,6},{6,5},{9,10},{10,9},{13,14},{14,13},{17,18},{18,... | collective-permute-start | bytes 30728 | tf_op jit(solution)/shard_map/ppermute | solution.py:256
  10.7 6.1 %copy-start.7 = (s32[1024]{0:T(1024)}, s32[1024]{0:T(1024)S(1)}, u32[]{:S(2)}) copy-start(s32[1024]{0:T(1024)S(1)} %fusion.14) | copy-start | bytes 12292
  10.7 6.9 %collective-permute-start.5 = (s32[1024]{0:T(1024)S(1)}, s32[1024]{0:T(1024)S(1)}, u32[]{:S(2)}, u32[]{:S(2)}) collective-permute-start(s32[1024]{0:T(1024)S(1)} %fusion.14), channel_id=1, source_target_pairs={{0,1},{3,2},{4,5},{7,6},{8,9},{11,10},{12,13},{15,14},{16,17},{19,... | collective-permute-start | bytes 12296 | tf_op jit(solution)/shard_map/ppermute | solution.py:256
  15.5 2.1 %copy-start.1 = (bf16[1,192,1536]{2,1,0:T(8,128)(2,1)S(1)}, bf16[1,192,1536]{2,1,0:T(8,128)(2,1)}, u32[]{:S(2)}) copy-start(bf16[1,192,1536]{2,1,0:T(8,128)(2,1)} %param.15) | copy-start | bytes 1769476
  17.6 2.7 %copy-start.8 = (s32[1024]{0:T(1024)}, s32[1024]{0:T(1024)S(1)}, u32[]{:S(2)}) copy-start(s32[1024]{0:T(1024)S(1)} %collective-permute-done.5) | copy-start | bytes 12292
  17.7 26.8 %collective-permute-start.6 = (bf16[192,1536]{1,0:T(8,128)(2,1)S(1)}, bf16[192,1536]{1,0:T(8,128)(2,1)S(1)}, u32[]{:S(2)}, u32[]{:S(2)}) collective-permute-start(bf16[192,1536]{1,0:T(8,128)(2,1)S(1)} %bitcast.45), channel_id=1, source_target_pairs={{0,2},{3,1},{4,6},{7,5},{8,10},{11,9},{12,14},{15,13},{16,18},{19,... | collective-permute-start | bytes 1769480 | tf_op jit(solution)/shard_map/ppermute | solution.py:256
  20.3 24.2 %collective-permute-start.10 = (bf16[192,1536]{1,0:T(8,128)(2,1)S(1)}, bf16[192,1536]{1,0:T(8,128)(2,1)S(1)}, u32[]{:S(2)}, u32[]{:S(2)}) collective-permute-start(bf16[192,1536]{1,0:T(8,128)(2,1)S(1)} %bitcast.46), channel_id=1, source_target_pairs={{1,2},{2,1},{5,6},{6,5},{9,10},{10,9},{13,14},{14,13},{17,18},{18,... | collective-permute-start | bytes 1769480 | tf_op jit(solution)/shard_map/ppermute | solution.py:256
  21.0 23.5 %collective-permute-start.9 = (bf16[192,1536]{1,0:T(8,128)(2,1)S(1)}, bf16[192,1536]{1,0:T(8,128)(2,1)S(1)}, u32[]{:S(2)}, u32[]{:S(2)}) collective-permute-start(bf16[192,1536]{1,0:T(8,128)(2,1)S(1)} %bitcast.47), channel_id=1, source_target_pairs={{0,1},{3,2},{4,5},{7,6},{8,9},{11,10},{12,13},{15,14},{16,17},{19,... | collective-permute-start | bytes 1769480 | tf_op jit(solution)/shard_map/ppermute | solution.py:256
  24.1 5.7 %collective-permute-start.7 = (bf16[256,320]{1,0:T(8,128)(2,1)S(1)}, bf16[256,320]{1,0:T(8,128)(2,1)S(1)}, u32[]{:S(2)}, u32[]{:S(2)}) collective-permute-start(bf16[256,320]{1,0:T(8,128)(2,1)S(1)} %collective-permute-done.3), channel_id=1, source_target_pairs={{0,8},{8,0},{16,24},{24,16},{1,9},{9,1},{17,25},{25,17},{2,10},{10... | collective-permute-start | bytes 491528 | tf_op jit(solution)/shard_map/ppermute | solution.py:265
  29.9 8.5 %collective-permute-start.8 = (bf16[512,320]{1,0:T(8,128)(2,1)S(1)}, bf16[512,320]{1,0:T(8,128)(2,1)S(1)}, u32[]{:S(2)}, u32[]{:S(2)}) collective-permute-start(bf16[512,320]{1,0:T(8,128)(2,1)S(1)} %pad_maximum_fusion.3), channel_id=1, source_target_pairs={{0,16},{8,24},{16,0},{24,8},{1,17},{9,25},{17,1},{25,9},{2,18},{10... | collective-permute-start | bytes 983048 | tf_op jit(solution)/shard_map/ppermute | solution.py:265
  42.3 1.5 %copy-start = (bf16[1,640,1536]{2,1,0:T(8,128)(2,1)S(1)}, bf16[1,640,1536]{2,1,0:T(8,128)(2,1)}, u32[]{:S(2)}) copy-start(bf16[1,640,1536]{2,1,0:T(8,128)(2,1)} %param.14) | copy-start | bytes 5898244
  42.3 1.5 %copy-start.2 = (f32[1,2,1536]{2,1,0:T(2,128)S(1)}, f32[1,2,1536]{2,1,0:T(2,128)}, u32[]{:S(2)}) copy-start(f32[1,2,1536]{2,1,0:T(2,128)} %param.19) | copy-start | bytes 36868
  44.5 1.8 %copy-start.5 = (bf16[1,192,512]{2,1,0:T(8,128)(2,1)S(1)}, bf16[1,192,512]{2,1,0:T(8,128)(2,1)}, u32[]{:S(2)}) copy-start(bf16[1,192,512]{2,1,0:T(8,128)(2,1)} %param.18) | copy-start | bytes 589828
  44.5 1.8 %copy-start.4 = (bf16[1,96,1536]{2,1,0:T(8,128)(2,1)S(1)}, bf16[1,96,1536]{2,1,0:T(8,128)(2,1)}, u32[]{:S(2)}) copy-start(bf16[1,96,1536]{2,1,0:T(8,128)(2,1)} %param.16) | copy-start | bytes 884740
  44.5 20.4 %copy-start.6 = (bf16[1,31,768]{2,1,0:T(8,128)(2,1)S(1)}, bf16[1,31,768]{2,1,0:T(8,128)(2,1)}, u32[]{:S(2)}) copy-start(bf16[1,31,768]{2,1,0:T(8,128)(2,1)} %param.17) | copy-start | bytes 142852
  44.7 20.3 %collective-permute-start.12 = (bf16[576,1536]{1,0:T(8,128)(2,1)S(1)}, bf16[576,1536]{1,0:T(8,128)(2,1)S(1)}, u32[]{:S(2)}, u32[]{:S(2)}) collective-permute-start(bf16[576,1536]{1,0:T(8,128)(2,1)S(1)} %pad_maximum_fusion), channel_id=1, source_target_pairs={{1,5},{2,6},{5,1},{6,2},{9,13},{10,14},{13,9},{14,10},{17,21},{18,... | collective-permute-start | bytes 5308424 | tf_op jit(solution)/shard_map/ppermute | solution.py:261
  45.6 19.4 %collective-permute-start.11 = (bf16[192,1536]{1,0:T(8,128)(2,1)S(1)}, bf16[192,1536]{1,0:T(8,128)(2,1)S(1)}, u32[]{:S(2)}, u32[]{:S(2)}) collective-permute-start(bf16[192,1536]{1,0:T(8,128)(2,1)S(1)} %bitcast.48), channel_id=1, source_target_pairs={{1,5},{2,6},{5,1},{6,2},{9,13},{10,14},{13,9},{14,10},{17,21},{18,... | collective-permute-start | bytes 1769480 | tf_op jit(solution)/shard_map/ppermute | solution.py:261
  46.4 25.3 %collective-permute-start = (bf16[160,1536]{1,0:T(8,128)(2,1)S(1)}, bf16[160,1536]{1,0:T(8,128)(2,1)S(1)}, u32[]{:S(2)}, u32[]{:S(2)}) collective-permute-start(bf16[160,1536]{1,0:T(8,128)(2,1)S(1)} %maximum_maximum_fusion.rest_0_), channel_id=1, source_target_pairs={{0,1},{3,2},{4,5},{7,6},{8,9},{11,10},{12,13},{15,14},{16,17},{19,... | collective-permute-start | bytes 1474568 | tf_op jit(solution)/shard_map/ppermute | solution.py:256
  60.1 11.6 %collective-permute-start.1 = (bf16[160,1536]{1,0:T(8,128)(2,1)S(1)}, bf16[160,1536]{1,0:T(8,128)(2,1)S(1)}, u32[]{:S(2)}, u32[]{:S(2)}) collective-permute-start(bf16[160,1536]{1,0:T(8,128)(2,1)S(1)} %maximum_maximum_fusion.rest_0_), channel_id=1, source_target_pairs={{1,2},{2,1},{5,6},{6,5},{9,10},{10,9},{13,14},{14,13},{17,18},{18,... | collective-permute-start | bytes 1474568 | tf_op jit(solution)/shard_map/ppermute | solution.py:256
  60.8 20.5 %collective-permute-start.2 = (bf16[160,1536]{1,0:T(8,128)(2,1)S(1)}, bf16[160,1536]{1,0:T(8,128)(2,1)S(1)}, u32[]{:S(2)}, u32[]{:S(2)}) collective-permute-start(bf16[160,1536]{1,0:T(8,128)(2,1)S(1)} %maximum_maximum_fusion.rest_0_), channel_id=1, source_target_pairs={{0,2},{3,1},{4,6},{7,5},{8,10},{11,9},{12,14},{15,13},{16,18},{19,... | collective-permute-start | bytes 1474568 | tf_op jit(solution)/shard_map/ppermute | solution.py:256
  81.4 1.5 %collective-permute-start.14 = (bf16[480,1536]{1,0:T(8,128)(2,1)S(1)}, bf16[480,1536]{1,0:T(8,128)(2,1)S(1)}, u32[]{:S(2)}, u32[]{:S(2)}) collective-permute-start(bf16[480,1536]{1,0:T(8,128)(2,1)S(1)} %pad_maximum_fusion.1), channel_id=1, source_target_pairs={{1,5},{2,6},{5,1},{6,2},{9,13},{10,14},{13,9},{14,10},{17,21},{18,... | collective-permute-start | bytes 4423688 | tf_op jit(solution)/shard_map/ppermute | solution.py:261
  82.1 0.7 collective-permute-start.13
  83.9 3.8 %collective-permute-start.15 = (f32[4,8,128]{2,1,0:T(8,128)S(1)}, f32[4,8,128]{2,1,0:T(8,128)S(1)}, u32[]{:S(2)}, u32[]{:S(2)}) collective-permute-start(f32[4,8,128]{2,1,0:T(8,128)S(1)} %shard_map.115), channel_id=1, source_target_pairs={{0,8},{8,0},{16,24},{24,16},{1,9},{9,1},{17,25},{25,17},{2,10},{10... | collective-permute-start | bytes 49160 | tf_op jit(solution)/shard_map/ppermute | solution.py:265
  85.1 3.9 %collective-permute-start.16 = (f32[4,8,128]{2,1,0:T(8,128)S(1)}, f32[4,8,128]{2,1,0:T(8,128)S(1)}, u32[]{:S(2)}, u32[]{:S(2)}) collective-permute-start(f32[4,8,128]{2,1,0:T(8,128)S(1)} %shard_map.115), channel_id=1, source_target_pairs={{0,16},{8,24},{16,0},{24,8},{1,17},{9,25},{17,1},{25,9},{2,18},{10... | collective-permute-start | bytes 49160 | tf_op jit(solution)/shard_map/ppermute | solution.py:265
  86.6 4.6 %collective-permute-start.17 = (f32[4,8,128]{2,1,0:T(8,128)S(1)}, f32[4,8,128]{2,1,0:T(8,128)S(1)}, u32[]{:S(2)}, u32[]{:S(2)}) collective-permute-start(f32[4,8,128]{2,1,0:T(8,128)S(1)} %shard_map.115), channel_id=1, source_target_pairs={{0,24},{8,16},{16,8},{24,0},{1,25},{9,17},{17,9},{25,1},{2,26},{10... | collective-permute-start | bytes 49160 | tf_op jit(solution)/shard_map/ppermute | solution.py:265
  92.6 30.9 %collective-permute-start.18 = (f32[1025]{0:T(1024)S(1)}, f32[1025]{0:T(1024)S(1)}, u32[]{:S(2)}, u32[]{:S(2)}) collective-permute-start(f32[1025]{0:T(1024)S(1)} %pad_maximum_fusion.5), channel_id=1, source_target_pairs={{1,0},{2,3},{5,4},{6,7},{9,8},{10,11},{13,12},{14,15},{17,16},{18,... | collective-permute-start | bytes 12308 | tf_op jit(solution)/shard_map/ppermute | solution.py:256
  93.9 2.5 %collective-permute-start.19 = (f32[1]{0:T(128)}, f32[1]{0:T(128)}, u32[]{:S(2)}, u32[]{:S(2)}) collective-permute-start(f32[1]{0:T(128)} %bitcast.23), channel_id=1, source_target_pairs={{1,2},{2,1},{5,6},{6,5},{9,10},{10,9},{13,14},{14,13},{17,18},{18,... | collective-permute-start | bytes 20 | tf_op jit(solution)/shard_map/ppermute | solution.py:256
  95.0 27.2 %collective-permute-start.20 = (f32[1]{0:T(128)}, f32[1]{0:T(128)}, u32[]{:S(2)}, u32[]{:S(2)}) collective-permute-start(f32[1]{0:T(128)} %bitcast.23), channel_id=1, source_target_pairs={{2,0},{1,3},{6,4},{5,7},{10,8},{9,11},{14,12},{13,15},{18,16},{17,... | collective-permute-start | bytes 20 | tf_op jit(solution)/shard_map/ppermute | solution.py:256

commit v7 on v6

--- a/solution.py
+++ b/solution.py
@@ -1,3 +1,5 @@
+import functools
+
 import jax
 import jax.numpy as jnp
 from jax import lax
@@ -23,9 +25,9 @@
 
 
 def stem_kernel(
-    meta, main_ref, margin_ref, stem_ref, gain_ref, stem_out_ref, normed_ref, acc_a, acc_b, acc_c
+    first_slot, meta, main_ref, margin_ref, stem_ref, gain_ref, stem_out_ref, normed_ref, acc_a, acc_b, acc_c
 ):
-    slot = pl.program_id(0)
+    slot = pl.program_id(0) + first_slot
     frames = main_ref.shape[1]
     part = acc_a.shape[0]
     group = 16
@@ -49,15 +51,16 @@
 def shards(meta, pieces):
     side = meta[13]
     length = pieces[0].shape[0]
-    places = [(pieces[i], 0) for i in range(5)] + [(pieces[5], i * length) for i in range(3)]
+    places = [(piece, 0) for piece in pieces[:-1]]
+    places += [(pieces[-1], i * length) for i in range(8 - len(places))]
     return [(*place, (side if i < 4 else 1 - side) * 4 + meta[9 + i % 4]) for i, place in enumerate(places)]
 
 
-def conv_kernel(meta, normed_ref, taps_ref, *rest):
+def conv_kernel(meta, own_ref, outer_ref, taps_ref, *rest):
     pieces = rest[:6]
     swished_ref, weight, mixed_a, mixed_b, gated, margin, mask, sems = rest[6:]
     slot = pl.program_id(0)
-    rows = normed_ref.shape[1]
+    rows = own_ref.shape[1]
     frames = swished_ref.shape[1]
     channels = swished_ref.shape[2]
     tap_count = taps_ref.shape[0]
@@ -78,8 +81,7 @@
         for copy in copies:
             copy.wait()
 
-    @pl.when(meta[5 + slot] > 0)
-    def _():
+    def run_tile(normed_ref):
         row = lax.broadcasted_iota(jnp.int32, (rows, LANES), 0)
         inner = (row % CHUNKS) * run_length + row // CHUNKS
         outer = jnp.where(row < frames + EDGE, row - frames - EDGE, row - EDGE)
@@ -141,10 +143,16 @@
             gate(block)
             convolve(block)
 
-
-def head_kernel(meta, swished_ref, stem_out_ref, code_ref, gain_ref, *rest):
-    pieces = rest[:6]
-    error_ref, back, head, acc_a, acc_b, norm_a, norm_b, logit_a, logit_b, sems = rest[6:]
+    for is_own, normed_ref in ((True, own_ref), (False, outer_ref)):
+
+        @pl.when(jnp.logical_and(meta[5 + slot] > 0, (slot < 2) == is_own))
+        def _(normed_ref=normed_ref):
+            run_tile(normed_ref)
+
+
+def head_kernel(meta, swished_ref, own_stem, outer_stem, own_code, outer_code, gain_ref, *rest):
+    pieces = rest[:5]
+    error_ref, back, head, acc_a, acc_b, norm_a, norm_b, logit_a, logit_b, sems = rest[5:]
     slot = pl.program_id(0)
     frames = swished_ref.shape[1]
     vocab = head.shape[1]
@@ -185,10 +193,14 @@
     def _():
         part = acc_a.shape[0]
         lane = lax.broadcasted_iota(jnp.int32, (CHUNKS, LANES), 1)
+        is_own = slot < 2
+        codes = jnp.where(is_own, own_code[0], outer_code[0])
         def norm(at, acc, normed):
             group = 16
             for row in range(0, part, group):
-                values = acc[row : row + group, :] + stem_out_ref[0, at + row : at + row + group, :].astype(jnp.float32)
+                here = slice(at + row, at + row + group)
+                stem_out = [ref[0, here, :].astype(jnp.float32) for ref in (own_stem, outer_stem)]
+                values = acc[row : row + group, :] + jnp.where(is_own, *stem_out)
                 normed[row : row + group, :] = norm_rows(values, gain_ref[1:2, :])
 
         def errors(at, logits, row):
@@ -199,7 +211,7 @@
                 grown = jnp.exp(scores - jnp.max(scores, axis=-1, keepdims=True))
                 posterior = grown * (1.0 / jnp.sum(grown, axis=-1, keepdims=True))
                 steps = range((at + first) // CHUNKS, (at + first + group) // CHUNKS)
-                code = jnp.concatenate([code_ref[0, :, m : m + 1] for m in steps], axis=0)
+                code = jnp.concatenate([codes[:, m : m + 1] for m in steps], axis=0)
                 differ = posterior - (token == code).astype(jnp.float32)
                 error = jnp.sqrt(jnp.sum(differ * differ, axis=-1, keepdims=True))
                 error = jnp.where(code >= 0, error, 0.0)
@@ -245,10 +257,20 @@
     return pl.BlockSpec((1,) + shape, lambda i, meta: (i,) + (0,) * len(shape))
 
 
+def own_slots(shape):
+    return pl.BlockSpec((1,) + shape, lambda i, meta: (jnp.minimum(i, 1),) + (0,) * len(shape))
+
+
+def outer_slots(shape):
+    return pl.BlockSpec((1,) + shape, lambda i, meta: (jnp.maximum(i - 2, 0),) + (0,) * len(shape))
+
+
 INWARD = [(0, 1), (3, 2)]
 ACROSS = [(1, 2), (2, 1)]
 BEYOND = [(0, 2), (3, 1)]
 OUTWARD = [(1, 0), (2, 3)]
+FORWARD = [(0, 1), (1, 2), (2, 3)]
+BACKWARD = [(1, 0), (2, 1), (3, 2)]
 OUT_BEYOND = [(2, 0), (1, 3)]
 
 
@@ -299,13 +321,15 @@
     share = rows // seeds
     margin = step * EDGE
     quarter = lax.dynamic_slice_in_dim(mel_frames[0], seed * share * step, share * step, 0).reshape(share, -1)
-    edge_out = jnp.where(low, mel_frames[0, -margin:], mel_frames[0, :margin]).reshape(EDGE, -1)
     quarter_in = along(quarter, INWARD)
-    edge = along(edge_out, ACROSS)
-    outer_code = along(code, INWARD)
-    first_held, quarter_in, edge, outer_code = lax.optimization_barrier((first, quarter_in, edge, outer_code))
+    before = along(mel_frames[0, -margin:].reshape(EDGE, -1), FORWARD)
+    after = along(mel_frames[0, :margin].reshape(EDGE, -1), BACKWARD)
+    first_held, quarter_in, before, after = lax.optimization_barrier((first, quarter_in, before, after))
     near_first, hub_first, far_first = [along(first_held, pairs_) for pairs_ in (INWARD, ACROSS, BEYOND)]
     held = first.shape[0]
+    code = code.reshape(2, CHUNKS, tile // CHUNKS)
+    code_held, quarter_in = lax.optimization_barrier((code, quarter_in))
+    outer_code = along(code_held, INWARD)
 
     pair = seed_swap(quarter_in, 1)
     odd = seed % 2 == 1
@@ -325,28 +349,20 @@
     )
     slots = 4
     deep = tile + 2 * EDGE
-    none = jnp.zeros_like(edge)
-    frames = jnp.concatenate(
-        [
-            jnp.where(low, none, edge),
-            jnp.where(low, outer, blocks),
-            jnp.where(low, blocks, outer),
-            jnp.where(low, edge, none),
-            none,
-        ],
-        axis=0,
-    )
-    pairs = jnp.concatenate([frames[:-1], frames[1:]], axis=1)
-    main = pairs[EDGE : EDGE + slots * tile].reshape(slots, CHUNKS, tile // CHUNKS, -1)
-    main = main.transpose(0, 2, 1, 3).reshape(slots, tile, -1)
-    margins = jnp.stack(
-        [
+
+    def paired(before, block, after):
+        frames = jnp.concatenate([before, block, after, after], axis=0)
+        pairs = jnp.concatenate([frames[:-1], frames[1:]], axis=1)
+        main = pairs[EDGE : EDGE + 2 * tile].reshape(2, CHUNKS, tile // CHUNKS, -1)
+        main = main.transpose(0, 2, 1, 3).reshape(2, tile, -1)
+        sides = [
             jnp.concatenate([pairs[k * tile : k * tile + EDGE], pairs[(k + 1) * tile + EDGE : (k + 1) * tile + 2 * EDGE]])
-            for k in range(slots)
+            for k in range(2)
         ]
-    )
-
-    starts = (chip - 1) * 2 * rows + tile * jnp.arange(slots, dtype=jnp.int32)
+        return main, jnp.stack(sides)
+
+    lone = jnp.where(low, 0, 3)
+    starts = jnp.stack([chip * rows, chip * rows + tile, lone * rows, lone * rows + tile]).astype(jnp.int32)
     alive = jnp.logical_and(is_hub, starts < length).astype(jnp.int32)
     hub = jnp.clip(chip, 1, 2)
     meta = jnp.concatenate(
@@ -360,31 +376,38 @@
 
     gains = norm_gain[0]
     half = tile // 2
-    stem_out, normed = call(
-        stem_kernel,
-        (slots,),
-        [by_slot(main.shape[1:]), by_slot(margins.shape[1:]), whole(stem_weight.shape[1:]), whole(gains.shape)],
-        [by_slot((tile, width)), by_slot((deep, width))],
-        [
-            jax.ShapeDtypeStruct((slots, tile, width), jnp.bfloat16),
-            jax.ShapeDtypeStruct((slots, deep, width), jnp.bfloat16),
-        ],
-        [
-            pltpu.VMEM((half, width), jnp.float32),
-            pltpu.VMEM((half, width), jnp.float32),
-            pltpu.VMEM((2 * EDGE, width), jnp.float32),
-        ],
-        2 * slots * deep * main.shape[2] * width,
-        2 * slots * deep * (main.shape[2] + 2 * width),
-        (meta, main, margins, stem_weight[0], gains),
-    )
+
+    def stems(first_slot, main, sides):
+        return call(
+            functools.partial(stem_kernel, first_slot),
+            (2,),
+            [by_slot(main.shape[1:]), by_slot(sides.shape[1:]), whole(stem_weight.shape[1:]), whole(gains.shape)],
+            [by_slot((tile, width)), by_slot((deep, width))],
+            [
+                jax.ShapeDtypeStruct((2, tile, width), jnp.bfloat16),
+                jax.ShapeDtypeStruct((2, deep, width), jnp.bfloat16),
+            ],
+            [
+                pltpu.VMEM((half, width), jnp.float32),
+                pltpu.VMEM((half, width), jnp.float32),
+                pltpu.VMEM((2 * EDGE, width), jnp.float32),
+            ],
+            slots * deep * main.shape[2] * width,
+            slots * deep * (main.shape[2] + 2 * width),
+            (meta, main, sides, stem_weight[0], gains),
+        )
+
+    own_stem, own_normed = stems(0, *paired(before, blocks, after))
+    none = jnp.zeros_like(before)
+    outer_pairs = paired(jnp.where(low, none, blocks[-EDGE:]), outer, jnp.where(low, blocks[:EDGE], none))
+    first_mate = to_mate(first)
+    outer_pairs, first_mate, own_normed = lax.optimization_barrier((outer_pairs, first_mate, own_normed))
+    outer_stem, outer_normed = stems(2, *outer_pairs)
     pinned = pl.BlockSpec(memory_space=pltpu.HBM)
 
-    codes = jnp.concatenate([jnp.where(low, outer_code, code), jnp.where(low, code, outer_code)])
-    codes = codes.reshape(slots, CHUNKS, tile // CHUNKS)
-    far_first, normed, codes = lax.optimization_barrier((far_first, normed, codes))
+    far_first, outer_normed = lax.optimization_barrier((far_first, outer_normed))
     mine = [first, near_first, hub_first, far_first]
-    first_pieces = (*mine, to_mate(first), to_mate(jnp.concatenate(mine[1:], axis=0)))
+    first_pieces = (*mine, first_mate, to_mate(jnp.concatenate(mine[1:], axis=0)))
     near_second, hub_second, far_second = [along(second, pairs_) for pairs_ in (INWARD, ACROSS, BEYOND)]
     taps = jnp.broadcast_to(
         depth_weight[0].astype(jnp.float32)[:, None, :], (depth_weight.shape[1], CHUNKS, channels)
@@ -393,7 +416,7 @@
     swished = call(
         conv_kernel,
         (slots,),
-        [by_slot((deep, width)), whole(taps.shape)] + [pinned] * 6,
+        [own_slots((deep, width)), outer_slots((deep, width)), whole(taps.shape)] + [pinned] * 6,
         by_slot((tile, channels)),
         jax.ShapeDtypeStruct((slots, tile, channels), jnp.bfloat16),
         [
@@ -407,19 +430,20 @@
         ],
         2 * slots * deep * width * 2 * channels,
         2 * slots * deep * width + 8 * first.size * 2,
-        (meta, normed, taps, *first_pieces),
+        (meta, own_normed, outer_normed, taps, *first_pieces),
     )
 
     near_second, hub_second, far_second, swished = lax.optimization_barrier(
         (near_second, hub_second, far_second, swished)
     )
     mine = [second, near_second, hub_second, far_second]
-    second_pieces = (*mine, to_mate(second), to_mate(jnp.concatenate(mine[1:], axis=0)))
+    second_pieces = (*mine, to_mate(jnp.concatenate(mine, axis=0)))
     errors = call(
         head_kernel,
         (slots,),
-        [by_slot((tile, channels)), by_slot((tile, width)), by_slot(codes.shape[1:]), whole(gains.shape)]
-        + [pinned] * 6,
+        [by_slot((tile, channels)), own_slots((tile, width)), outer_slots((tile, width))]
+        + [own_slots(code.shape[1:]), outer_slots(code.shape[1:]), whole(gains.shape)]
+        + [pinned] * 5,
         by_slot((CHUNKS, LANES)),
         jax.ShapeDtypeStruct((slots, CHUNKS, LANES), jnp.float32),
         [
@@ -435,15 +459,14 @@
         ],
         2 * slots * tile * (channels + vocab) * width,
         2 * slots * tile * (channels + width),
-        (meta, swished, stem_out, codes, gains, *second_pieces),
+        (meta, swished, own_stem, outer_stem, code, outer_code, gains, *second_pieces),
     )
 
     one, two, three = [seed_swap(errors, bit) for bit in (1, 2, 3)]
     total = ((errors + one) + (two + three)) / jnp.float32(seeds)
     total = total[:, :, : tile // CHUNKS].reshape(2, rows)
     part = jnp.sum(total).reshape(1)
-    outer_half = jnp.where(low, total[0], total[1])
-    own_half = jnp.where(low, total[1], total[0])
+    own_half, outer_half = total
     from_hub = along(jnp.concatenate([outer_half, part]), OUTWARD)
     parts = [part[0], along(part, ACROSS)[0], along(part, OUT_BEYOND)[0], from_hub[rows]]
     frame_error = jnp.where(is_hub, own_half, from_hub[:rows])

time: 128 us -> 133 us (1.039)
  starting transfers between devices: 48.1 us -> 52.8 us
  other arithmetic: 9.09 us -> 6.47 us
    ppermute x5, waiting for transfers between devices: 10.1 us -> 16.3 us  [seed_swap(): return lax.ppermute(x, 'seed', [(i, i ^ bit) for i in range(4)])]
    ppermute x12 -> x13, waiting for transfers between devices: 41.3 us -> 35.2 us  [along(): return lax.ppermute(x, 'seq', pairs)]
    ppermute x12 -> x13, starting transfers between devices: 38.4 us -> 43.8 us  [along(): return lax.ppermute(x, 'seq', pairs)]
    concatenate x3 -> x2, local copies, waits for them, and re-layouts: 2.69 us -> 0.04 us  [the longest x1 0.03 us: hub_body(): second_pieces = (*mine, to_mate(jnp.concatenate(mine, axis=0)))]
    select_n x4 -> x0, other arithmetic: 2.31 us -> none  [the longest x1 1.31 us: hub_body(): jnp.where(low, outer_code, code)]
    unnamed x19 -> x20, local copies, waits for them, and re-layouts: 2.08 us -> 3.52 us
    ppermute x4 -> x3, starting transfers between devices: 3.05 us -> 2.26 us  [to_mate(): return lax.ppermute(x, ('fsdp', 'seq'), pairs)]
    pallas_call x3 -> x4, Pallas kernels: 2.42 us -> 3.06 us  [call(): pl.pallas_call(kernel, grid_spec=pltpu.PrefetchScalarGridSpec(num_scalar_...]
  transfers between devices with their start and end apart: 21 -> 21, of which waited for: 8 -> 10; matrix products, arithmetic and copies ran while one was open for 11% -> 11% of each run, Pallas kernels for 1% -> 2%
where the time goes in v7:
time: 133 us; the launch traced here: 131 us
  starting transfers between devices  52.8 us (40%)
  waiting for transfers between devices  51.6 us (39%)
  local copies, waits for them, and re-layouts  11.3 us (8%)
  other arithmetic  6.47 us (5%)
  between operations  5.64 us (4%)
  Pallas kernels  3.06 us (2%)
    ppermute x13, starting transfers between devices, along(): return lax.ppermute(x, 'seq', pairs)  43.8 us
    ppermute x13, waiting for transfers between devices, along(): return lax.ppermute(x, 'seq', pairs)  35.2 us
    ppermute x5, waiting for transfers between devices, seed_swap(): return lax.ppermute(x, 'seed', [(i, i ^ bit) for i in range(4)])  16.3 us
    ppermute x5, starting transfers between devices, seed_swap(): return lax.ppermute(x, 'seed', [(i, i ^ bit) for i in range(4)])  6.69 us
    unnamed x20, local copies, waits for them, and re-layouts  3.52 us
    pallas_call x4, Pallas kernels, call(): pl.pallas_call(kernel, grid_spec=pltpu.PrefetchScalarGridSpec(num_scalar_...  3.06 us
  transfers between devices with their start and end apart: 21, of which 10 were waited for; matrix products, arithmetic and copies ran while one was open for 11% of the time, Pallas kernels for 2%

profile of v7, /device:TPU:0, one launch (start us, length us, event | category | flops | bytes accessed | tf_op | source)
XLA Modules:
  0.0 130.8 jit_solution(4877885755729647060)
XLA Ops:
  0.6 0.9 constant_dynamic-slice_fusion
  1.6 0.2 copy.19
  1.7 0.2 reshape.51
  2.0 5.1 %collective-permute-start.3 = (bf16[256,320]{1,0:T(8,128)(2,1)S(1)}, bf16[256,320]{1,0:T(8,128)(2,1)S(1)}, u32[]{:S(2)}, u32[]{:S(2)}) collective-permute-start(bf16[256,320]{1,0:T(8,128)(2,1)S(1)} %reshape.51), channel_id=1, source_target_pairs={{0,1},{3,2},{4,5},{7,6},{8,9},{11,10},{12,13},{15,14},{16,17},{19,... | collective-permute-start | bytes 491528 | tf_op jit(solution)/shard_map/ppermute | solution.py:278
  7.0 0.8 fusion.23
  7.9 0.1 copy.20
  8.0 0.1 reshape_squeeze.7
  8.0 1.3 collective-permute-start.5
  9.3 0.1 copy.18
  9.4 0.1 slice.71
  9.5 4.5 %collective-permute-start.4 = (bf16[16,320]{1,0:T(8,128)(2,1)S(1)}, bf16[16,320]{1,0:T(8,128)(2,1)S(1)}, u32[]{:S(2)}, u32[]{:S(2)}) collective-permute-start(bf16[16,320]{1,0:T(8,128)(2,1)S(1)} %slice.71), channel_id=1, source_target_pairs={{0,1},{1,2},{2,3},{4,5},{5,6},{6,7},{8,9},{9,10},{10,11},{12,13},{... | collective-permute-start | bytes 30728 | tf_op jit(solution)/shard_map/ppermute | solution.py:278
  14.1 0.7 collective-permute-start.8
  15.5 0.5 broadcast.28
  16.0 1.3 %reduce.6 = s32[1024]{0:T(1024)S(1)} reduce(s32[1,1024]{1,0:T(1,128)} %param.12, s32[]{:T(128)} %broadcast.28), dimensions={0}, to_apply=%param.12.reduce_sub_computation.3 | reduce | bytes 8196 | tf_op args[2]
  17.4 0.7 compare_reduce_fusion
  18.2 0.7 fusion.20
  19.0 1.6 %copy.22 = bf16[1,4096,80]{2,1,0:T(8,128)(2,1)S(1)} copy(bf16[1,4096,80]{1,2,0:T(8,128)(2,1)} %param.10) | data formatting | bytes 1310720 | tf_op args[0]
  20.6 1.6 %reshape_squeeze.8 = bf16[1024,320]{1,0:T(8,128)(2,1)} reshape(bf16[1,4096,80]{2,1,0:T(8,128)(2,1)S(1)} %copy.22) | data formatting | bytes 1310720 | tf_op jit(solution)/shard_map/reshape;squeeze | solution.py:320
  22.2 0.7 concatenate.47.meta
  22.9 3.6 %collective-permute-start.9 = (bf16[192,1536]{1,0:T(8,128)(2,1)S(1)}, bf16[192,1536]{1,0:T(8,128)(2,1)S(1)}, u32[]{:S(2)}, u32[]{:S(2)}) collective-permute-start(bf16[192,1536]{1,0:T(8,128)(2,1)S(1)} %bitcast.58), channel_id=1, source_target_pairs={{0,2},{3,1},{4,6},{7,5},{8,10},{11,9},{12,14},{15,13},{16,18},{19,... | collective-permute-start | bytes 1769480 | tf_op jit(solution)/shard_map/ppermute | solution.py:278
  26.5 1.3 %collective-permute-start.10 = (bf16[192,1536]{1,0:T(8,128)(2,1)S(1)}, bf16[192,1536]{1,0:T(8,128)(2,1)S(1)}, u32[]{:S(2)}, u32[]{:S(2)}) collective-permute-start(bf16[192,1536]{1,0:T(8,128)(2,1)S(1)} %bitcast.59), channel_id=1, source_target_pairs={{0,1},{3,2},{4,5},{7,6},{8,9},{11,10},{12,13},{15,14},{16,17},{19,... | collective-permute-start | bytes 1769480 | tf_op jit(solution)/shard_map/ppermute | solution.py:278
  27.8 0.7 collective-permute-start.11
  28.5 1.3 constant_dynamic-update-slice_fusion.5
  29.8 1.6 %collective-permute-start.6 = (bf16[256,320]{1,0:T(8,128)(2,1)S(1)}, bf16[256,320]{1,0:T(8,128)(2,1)S(1)}, u32[]{:S(2)}, u32[]{:S(2)}) collective-permute-start(bf16[256,320]{1,0:T(8,128)(2,1)S(1)} %collective-permute-done.3), channel_id=1, source_target_pairs={{0,8},{8,0},{16,24},{24,16},{1,9},{9,1},{17,25},{25,17},{2,10},{10... | collective-permute-start | bytes 491528 | tf_op jit(solution)/shard_map/ppermute | solution.py:287
  31.4 0.3 fusion.21
  31.7 0.4 fusion
  32.1 0.7 copy.26
  32.9 4.1 %collective-permute-done.6 = bf16[256,320]{1,0:T(8,128)(2,1)S(1)} collective-permute-done((bf16[256,320]{1,0:T(8,128)(2,1)S(1)}, bf16[256,320]{1,0:T(8,128)(2,1)S(1)}, u32[]{:S(2)}, u32[]{:S(2)}) %collective-permute-start.6) | collective-permute-done | bytes 163872 | tf_op jit(solution)/shard_map/ppermute | solution.py:287
  37.1 1.6 %collective-permute-start.7 = (bf16[512,320]{1,0:T(8,128)(2,1)S(1)}, bf16[512,320]{1,0:T(8,128)(2,1)S(1)}, u32[]{:S(2)}, u32[]{:S(2)}) collective-permute-start(bf16[512,320]{1,0:T(8,128)(2,1)S(1)} %pad_maximum_fusion.1), channel_id=1, source_target_pairs={{0,16},{8,24},{16,0},{24,8},{1,17},{9,25},{17,1},{25,9},{2,18},{10... | collective-permute-start | bytes 983048 | tf_op jit(solution)/shard_map/ppermute | solution.py:287
  38.8 0.6 shard_map.113
  39.5 8.1 %collective-permute-done.7 = bf16[512,320]{1,0:T(8,128)(2,1)S(1)} collective-permute-done((bf16[512,320]{1,0:T(8,128)(2,1)S(1)}, bf16[512,320]{1,0:T(8,128)(2,1)S(1)}, u32[]{:S(2)}, u32[]{:S(2)}) %collective-permute-start.7) | collective-permute-done | bytes 327712 | tf_op jit(solution)/shard_map/ppermute | solution.py:287
  47.5 0.2 select_dynamic-update-slice_fusion.1
  47.7 0.2 select_dynamic-update-slice_fusion
  47.9 0.3 fusion.22
  48.2 0.4 fusion.1
  48.6 0.7 copy.27
  49.6 0.6 shard_map.114
  50.2 2.1 %collective-permute-done.10.rest_1_ = bf16[192,1536]{1,0:T(8,128)(2,1)S(1)} collective-permute-done((bf16[192,1536]{1,0:T(8,128)(2,1)S(1)}, bf16[192,1536]{1,0:T(8,128)(2,1)S(1)}, u32[]{:S(2)}, u32[]{:S(2)}) %collective-permute-start.10) | collective-permute-done | bytes 589856 | tf_op jit(solution)/shard_map/ppermute | solution.py:278
  52.4 0.1 pad_maximum_fusion
  52.5 0.8 collective-permute-start.12
  53.3 6.8 %collective-permute-start = (bf16[160,1536]{1,0:T(8,128)(2,1)S(1)}, bf16[160,1536]{1,0:T(8,128)(2,1)S(1)}, u32[]{:S(2)}, u32[]{:S(2)}) collective-permute-start(bf16[160,1536]{1,0:T(8,128)(2,1)S(1)} %maximum_maximum_fusion.rest_0_), channel_id=1, source_target_pairs={{0,1},{3,2},{4,5},{7,6},{8,9},{11,10},{12,13},{15,14},{16,17},{19,... | collective-permute-start | bytes 1474568 | tf_op jit(solution)/shard_map/ppermute | solution.py:278
  60.2 0.7 collective-permute-start.1
  60.9 4.2 %collective-permute-start.2 = (bf16[160,1536]{1,0:T(8,128)(2,1)S(1)}, bf16[160,1536]{1,0:T(8,128)(2,1)S(1)}, u32[]{:S(2)}, u32[]{:S(2)}) collective-permute-start(bf16[160,1536]{1,0:T(8,128)(2,1)S(1)} %maximum_maximum_fusion.rest_0_), channel_id=1, source_target_pairs={{0,2},{3,1},{4,6},{7,5},{8,10},{11,9},{12,14},{15,13},{16,18},{19,... | collective-permute-start | bytes 1474568 | tf_op jit(solution)/shard_map/ppermute | solution.py:278
  65.2 0.8 shard_map.115.swished_ref
  66.0 5.7 %collective-permute-done.rest_1_ = bf16[160,1536]{1,0:T(8,128)(2,1)S(1)} collective-permute-done((bf16[160,1536]{1,0:T(8,128)(2,1)S(1)}, bf16[160,1536]{1,0:T(8,128)(2,1)S(1)}, u32[]{:S(2)}, u32[]{:S(2)}) %collective-permute-start) | collective-permute-done | bytes 491552 | tf_op jit(solution)/shard_map/ppermute | solution.py:278
  71.7 10.2 %collective-permute-done.2.rest_3_ = bf16[160,1536]{1,0:T(8,128)(2,1)S(1)} collective-permute-done((bf16[160,1536]{1,0:T(8,128)(2,1)S(1)}, bf16[160,1536]{1,0:T(8,128)(2,1)S(1)}, u32[]{:S(2)}, u32[]{:S(2)}) %collective-permute-start.2) | collective-permute-done | bytes 491552 | tf_op jit(solution)/shard_map/ppermute | solution.py:278
  82.0 0.8 collective-permute-start.14
  82.8 11.8 %collective-permute-start.13 = (s32[2,8,64]{2,1,0:T(8,128)S(1)}, s32[2,8,64]{2,1,0:T(8,128)S(1)}, u32[]{:S(2)}, u32[]{:S(2)}) collective-permute-start(s32[2,8,64]{2,1,0:T(8,128)S(1)} %fusion.19.own_code), channel_id=1, source_target_pairs={{0,1},{3,2},{4,5},{7,6},{8,9},{11,10},{12,13},{15,14},{16,17},{19,... | collective-permute-start | bytes 12296 | tf_op jit(solution)/shard_map/ppermute | solution.py:278
  94.6 1.1 collective-permute-done.13.outer_code
  95.7 1.0 shard_map.116
  96.8 1.6 %collective-permute-start.15 = (f32[4,8,128]{2,1,0:T(8,128)S(1)}, f32[4,8,128]{2,1,0:T(8,128)S(1)}, u32[]{:S(2)}, u32[]{:S(2)}) collective-permute-start(f32[4,8,128]{2,1,0:T(8,128)S(1)} %shard_map.116), channel_id=1, source_target_pairs={{0,8},{8,0},{16,24},{24,16},{1,9},{9,1},{17,25},{25,17},{2,10},{10... | collective-permute-start | bytes 49160 | tf_op jit(solution)/shard_map/ppermute | solution.py:287
  98.3 1.5 %collective-permute-start.16 = (f32[4,8,128]{2,1,0:T(8,128)S(1)}, f32[4,8,128]{2,1,0:T(8,128)S(1)}, u32[]{:S(2)}, u32[]{:S(2)}) collective-permute-start(f32[4,8,128]{2,1,0:T(8,128)S(1)} %shard_map.116), channel_id=1, source_target_pairs={{0,16},{8,24},{16,0},{24,8},{1,17},{9,25},{17,1},{25,9},{2,18},{10... | collective-permute-start | bytes 49160 | tf_op jit(solution)/shard_map/ppermute | solution.py:287
  99.9 0.5 collective-permute-start.17
  100.3 0.2 collective-permute-done.15
  100.6 1.7 %collective-permute-done.16 = f32[4,8,128]{2,1,0:T(8,128)S(1)} collective-permute-done((f32[4,8,128]{2,1,0:T(8,128)S(1)}, f32[4,8,128]{2,1,0:T(8,128)S(1)}, u32[]{:S(2)}, u32[]{:S(2)}) %collective-permute-start.16) | collective-permute-done | bytes 16416 | tf_op jit(solution)/shard_map/ppermute | solution.py:287
  102.3 2.3 %collective-permute-done.17 = f32[4,8,128]{2,1,0:T(8,128)S(1)} collective-permute-done((f32[4,8,128]{2,1,0:T(8,128)S(1)}, f32[4,8,128]{2,1,0:T(8,128)S(1)}, u32[]{:S(2)}, u32[]{:S(2)}) %collective-permute-start.17) | collective-permute-done | bytes 16416 | tf_op jit(solution)/shard_map/ppermute | solution.py:287
  104.5 0.6 slice_reduce_fusion
  105.2 0.6 pad_maximum_fusion.4
  105.9 1.3 collective-permute-start.18
  107.2 1.3 collective-permute-start.19
  108.4 1.3 collective-permute-start.20
  109.8 16.1 %collective-permute-done.20 = f32[1]{0:T(128)} collective-permute-done((f32[1]{0:T(128)}, f32[1]{0:T(128)}, u32[]{:S(2)}, u32[]{:S(2)}) %collective-permute-start.20) | collective-permute-done | bytes 36 | tf_op jit(solution)/shard_map/ppermute | solution.py:278
  127.2 0.5 slice.112
  129.1 0.6 slice_select_fusion
  (53 shorter events, 1.1 us)
Async XLA Ops:
  1.9 21.0 %copy-start.1 = (bf16[1,192,1536]{2,1,0:T(8,128)(2,1)S(1)}, bf16[1,192,1536]{2,1,0:T(8,128)(2,1)}, u32[]{:S(2)}) copy-start(bf16[1,192,1536]{2,1,0:T(8,128)(2,1)} %param.15) | copy-start | bytes 1769476
  2.0 20.9 %collective-permute-start.3 = (bf16[256,320]{1,0:T(8,128)(2,1)S(1)}, bf16[256,320]{1,0:T(8,128)(2,1)S(1)}, u32[]{:S(2)}, u32[]{:S(2)}) collective-permute-start(bf16[256,320]{1,0:T(8,128)(2,1)S(1)} %reshape.51), channel_id=1, source_target_pairs={{0,1},{3,2},{4,5},{7,6},{8,9},{11,10},{12,13},{15,14},{16,17},{19,... | collective-permute-start | bytes 491528 | tf_op jit(solution)/shard_map/ppermute | solution.py:278
  8.0 14.8 %collective-permute-start.5 = (bf16[16,320]{1,0:T(8,128)(2,1)S(1)}, bf16[16,320]{1,0:T(8,128)(2,1)S(1)}, u32[]{:S(2)}, u32[]{:S(2)}) collective-permute-start(bf16[16,320]{1,0:T(8,128)(2,1)S(1)} %reshape_squeeze.7), channel_id=1, source_target_pairs={{1,0},{2,1},{3,2},{5,4},{6,5},{7,6},{9,8},{10,9},{11,10},{13,12},{... | collective-permute-start | bytes 30728 | tf_op jit(solution)/shard_map/ppermute | solution.py:278
  9.5 13.3 %collective-permute-start.4 = (bf16[16,320]{1,0:T(8,128)(2,1)S(1)}, bf16[16,320]{1,0:T(8,128)(2,1)S(1)}, u32[]{:S(2)}, u32[]{:S(2)}) collective-permute-start(bf16[16,320]{1,0:T(8,128)(2,1)S(1)} %slice.71), channel_id=1, source_target_pairs={{0,1},{1,2},{2,3},{4,5},{5,6},{6,7},{8,9},{9,10},{10,11},{12,13},{... | collective-permute-start | bytes 30728 | tf_op jit(solution)/shard_map/ppermute | solution.py:278
  14.1 35.5 %collective-permute-start.8 = (bf16[192,1536]{1,0:T(8,128)(2,1)}, bf16[192,1536]{1,0:T(8,128)(2,1)S(1)}, u32[]{:S(2)}, u32[]{:S(2)}) collective-permute-start(bf16[192,1536]{1,0:T(8,128)(2,1)} %bitcast.57), channel_id=1, source_target_pairs={{1,5},{2,6},{5,1},{6,2},{9,13},{10,14},{13,9},{14,10},{17,21},{18,... | collective-permute-start | bytes 1769480 | tf_op jit(solution)/shard_map/ppermute | solution.py:283
  22.9 27.3 %collective-permute-start.9 = (bf16[192,1536]{1,0:T(8,128)(2,1)S(1)}, bf16[192,1536]{1,0:T(8,128)(2,1)S(1)}, u32[]{:S(2)}, u32[]{:S(2)}) collective-permute-start(bf16[192,1536]{1,0:T(8,128)(2,1)S(1)} %bitcast.58), channel_id=1, source_target_pairs={{0,2},{3,1},{4,6},{7,5},{8,10},{11,9},{12,14},{15,13},{16,18},{19,... | collective-permute-start | bytes 1769480 | tf_op jit(solution)/shard_map/ppermute | solution.py:278
  26.5 25.9 %collective-permute-start.10 = (bf16[192,1536]{1,0:T(8,128)(2,1)S(1)}, bf16[192,1536]{1,0:T(8,128)(2,1)S(1)}, u32[]{:S(2)}, u32[]{:S(2)}) collective-permute-start(bf16[192,1536]{1,0:T(8,128)(2,1)S(1)} %bitcast.59), channel_id=1, source_target_pairs={{0,1},{3,2},{4,5},{7,6},{8,9},{11,10},{12,13},{15,14},{16,17},{19,... | collective-permute-start | bytes 1769480 | tf_op jit(solution)/shard_map/ppermute | solution.py:278
  27.8 24.5 %collective-permute-start.11 = (bf16[192,1536]{1,0:T(8,128)(2,1)S(1)}, bf16[192,1536]{1,0:T(8,128)(2,1)S(1)}, u32[]{:S(2)}, u32[]{:S(2)}) collective-permute-start(bf16[192,1536]{1,0:T(8,128)(2,1)S(1)} %bitcast.60), channel_id=1, source_target_pairs={{1,2},{2,1},{5,6},{6,5},{9,10},{10,9},{13,14},{14,13},{17,18},{18,... | collective-permute-start | bytes 1769480 | tf_op jit(solution)/shard_map/ppermute | solution.py:278
  29.8 7.1 %collective-permute-start.6 = (bf16[256,320]{1,0:T(8,128)(2,1)S(1)}, bf16[256,320]{1,0:T(8,128)(2,1)S(1)}, u32[]{:S(2)}, u32[]{:S(2)}) collective-permute-start(bf16[256,320]{1,0:T(8,128)(2,1)S(1)} %collective-permute-done.3), channel_id=1, source_target_pairs={{0,8},{8,0},{16,24},{24,16},{1,9},{9,1},{17,25},{25,17},{2,10},{10... | collective-permute-start | bytes 491528 | tf_op jit(solution)/shard_map/ppermute | solution.py:287
  37.0 1.8 %copy-start = (bf16[1,640,1536]{2,1,0:T(8,128)(2,1)S(1)}, bf16[1,640,1536]{2,1,0:T(8,128)(2,1)}, u32[]{:S(2)}) copy-start(bf16[1,640,1536]{2,1,0:T(8,128)(2,1)} %param.14) | copy-start | bytes 5898244
  37.1 1.8 %copy-start.2 = (f32[1,2,1536]{2,1,0:T(2,128)S(1)}, f32[1,2,1536]{2,1,0:T(2,128)}, u32[]{:S(2)}) copy-start(f32[1,2,1536]{2,1,0:T(2,128)} %param.19) | copy-start | bytes 36868
  37.1 10.5 %collective-permute-start.7 = (bf16[512,320]{1,0:T(8,128)(2,1)S(1)}, bf16[512,320]{1,0:T(8,128)(2,1)S(1)}, u32[]{:S(2)}, u32[]{:S(2)}) collective-permute-start(bf16[512,320]{1,0:T(8,128)(2,1)S(1)} %pad_maximum_fusion.1), channel_id=1, source_target_pairs={{0,16},{8,24},{16,0},{24,8},{1,17},{9,25},{17,1},{25,9},{2,18},{10... | collective-permute-start | bytes 983048 | tf_op jit(solution)/shard_map/ppermute | solution.py:287
  50.2 3.1 %copy-start.4 = (bf16[1,192,512]{2,1,0:T(8,128)(2,1)S(1)}, bf16[1,192,512]{2,1,0:T(8,128)(2,1)}, u32[]{:S(2)}) copy-start(bf16[1,192,512]{2,1,0:T(8,128)(2,1)} %param.18) | copy-start | bytes 589828
  50.2 3.1 %copy-start.3 = (bf16[1,96,1536]{2,1,0:T(8,128)(2,1)S(1)}, bf16[1,96,1536]{2,1,0:T(8,128)(2,1)}, u32[]{:S(2)}) copy-start(bf16[1,96,1536]{2,1,0:T(8,128)(2,1)} %param.16) | copy-start | bytes 884740
  50.2 14.9 %copy-start.5 = (bf16[1,31,768]{2,1,0:T(8,128)(2,1)S(1)}, bf16[1,31,768]{2,1,0:T(8,128)(2,1)}, u32[]{:S(2)}) copy-start(bf16[1,31,768]{2,1,0:T(8,128)(2,1)} %param.17) | copy-start | bytes 142852
  52.5 12.6 %collective-permute-start.12 = (bf16[576,1536]{1,0:T(8,128)(2,1)S(1)}, bf16[576,1536]{1,0:T(8,128)(2,1)S(1)}, u32[]{:S(2)}, u32[]{:S(2)}) collective-permute-start(bf16[576,1536]{1,0:T(8,128)(2,1)S(1)} %pad_maximum_fusion), channel_id=1, source_target_pairs={{1,5},{2,6},{5,1},{6,2},{9,13},{10,14},{13,9},{14,10},{17,21},{18,... | collective-permute-start | bytes 5308424 | tf_op jit(solution)/shard_map/ppermute | solution.py:283
  53.3 18.3 %collective-permute-start = (bf16[160,1536]{1,0:T(8,128)(2,1)S(1)}, bf16[160,1536]{1,0:T(8,128)(2,1)S(1)}, u32[]{:S(2)}, u32[]{:S(2)}) collective-permute-start(bf16[160,1536]{1,0:T(8,128)(2,1)S(1)} %maximum_maximum_fusion.rest_0_), channel_id=1, source_target_pairs={{0,1},{3,2},{4,5},{7,6},{8,9},{11,10},{12,13},{15,14},{16,17},{19,... | collective-permute-start | bytes 1474568 | tf_op jit(solution)/shard_map/ppermute | solution.py:278
  60.2 11.5 %collective-permute-start.1 = (bf16[160,1536]{1,0:T(8,128)(2,1)S(1)}, bf16[160,1536]{1,0:T(8,128)(2,1)S(1)}, u32[]{:S(2)}, u32[]{:S(2)}) collective-permute-start(bf16[160,1536]{1,0:T(8,128)(2,1)S(1)} %maximum_maximum_fusion.rest_0_), channel_id=1, source_target_pairs={{1,2},{2,1},{5,6},{6,5},{9,10},{10,9},{13,14},{14,13},{17,18},{18,... | collective-permute-start | bytes 1474568 | tf_op jit(solution)/shard_map/ppermute | solution.py:278
  60.9 21.0 %collective-permute-start.2 = (bf16[160,1536]{1,0:T(8,128)(2,1)S(1)}, bf16[160,1536]{1,0:T(8,128)(2,1)S(1)}, u32[]{:S(2)}, u32[]{:S(2)}) collective-permute-start(bf16[160,1536]{1,0:T(8,128)(2,1)S(1)} %maximum_maximum_fusion.rest_0_), channel_id=1, source_target_pairs={{0,2},{3,1},{4,6},{7,5},{8,10},{11,9},{12,14},{15,13},{16,18},{19,... | collective-permute-start | bytes 1474568 | tf_op jit(solution)/shard_map/ppermute | solution.py:278
  82.0 13.8 %collective-permute-start.14 = (bf16[640,1536]{1,0:T(8,128)(2,1)S(1)}, bf16[640,1536]{1,0:T(8,128)(2,1)S(1)}, u32[]{:S(2)}, u32[]{:S(2)}) collective-permute-start(bf16[640,1536]{1,0:T(8,128)(2,1)S(1)} %constant_dynamic-update-slice_fusion.7), channel_id=1, source_target_pairs={{1,5},{2,6},{5,1},{6,2},{9,13},{10,14},{13,9},{14,10},{17,21},{18,... | collective-permute-start | bytes 5898248 | tf_op jit(solution)/shard_map/ppermute | solution.py:283
  82.8 13.0 %collective-permute-start.13 = (s32[2,8,64]{2,1,0:T(8,128)S(1)}, s32[2,8,64]{2,1,0:T(8,128)S(1)}, u32[]{:S(2)}, u32[]{:S(2)}) collective-permute-start(s32[2,8,64]{2,1,0:T(8,128)S(1)} %fusion.19.own_code), channel_id=1, source_target_pairs={{0,1},{3,2},{4,5},{7,6},{8,9},{11,10},{12,13},{15,14},{16,17},{19,... | collective-permute-start | bytes 12296 | tf_op jit(solution)/shard_map/ppermute | solution.py:278
  96.8 3.8 %collective-permute-start.15 = (f32[4,8,128]{2,1,0:T(8,128)S(1)}, f32[4,8,128]{2,1,0:T(8,128)S(1)}, u32[]{:S(2)}, u32[]{:S(2)}) collective-permute-start(f32[4,8,128]{2,1,0:T(8,128)S(1)} %shard_map.116), channel_id=1, source_target_pairs={{0,8},{8,0},{16,24},{24,16},{1,9},{9,1},{17,25},{25,17},{2,10},{10... | collective-permute-start | bytes 49160 | tf_op jit(solution)/shard_map/ppermute | solution.py:287
  98.3 3.9 %collective-permute-start.16 = (f32[4,8,128]{2,1,0:T(8,128)S(1)}, f32[4,8,128]{2,1,0:T(8,128)S(1)}, u32[]{:S(2)}, u32[]{:S(2)}) collective-permute-start(f32[4,8,128]{2,1,0:T(8,128)S(1)} %shard_map.116), channel_id=1, source_target_pairs={{0,16},{8,24},{16,0},{24,8},{1,17},{9,25},{17,1},{25,9},{2,18},{10... | collective-permute-start | bytes 49160 | tf_op jit(solution)/shard_map/ppermute | solution.py:287
  99.9 4.6 %collective-permute-start.17 = (f32[4,8,128]{2,1,0:T(8,128)S(1)}, f32[4,8,128]{2,1,0:T(8,128)S(1)}, u32[]{:S(2)}, u32[]{:S(2)}) collective-permute-start(f32[4,8,128]{2,1,0:T(8,128)S(1)} %shard_map.116), channel_id=1, source_target_pairs={{0,24},{8,16},{16,8},{24,0},{1,25},{9,17},{17,9},{25,1},{2,26},{10... | collective-permute-start | bytes 49160 | tf_op jit(solution)/shard_map/ppermute | solution.py:287
  105.9 21.3 %collective-permute-start.18 = (f32[1025]{0:T(1024)S(1)}, f32[1025]{0:T(1024)S(1)}, u32[]{:S(2)}, u32[]{:S(2)}) collective-permute-start(f32[1025]{0:T(1024)S(1)} %pad_maximum_fusion.4), channel_id=1, source_target_pairs={{1,0},{2,3},{5,4},{6,7},{9,8},{10,11},{13,12},{14,15},{17,16},{18,... | collective-permute-start | bytes 12308 | tf_op jit(solution)/shard_map/ppermute | solution.py:278
  107.2 2.6 %collective-permute-start.19 = (f32[1]{0:T(128)}, f32[1]{0:T(128)}, u32[]{:S(2)}, u32[]{:S(2)}) collective-permute-start(f32[1]{0:T(128)} %bitcast.29), channel_id=1, source_target_pairs={{1,2},{2,1},{5,6},{6,5},{9,10},{10,9},{13,14},{14,13},{17,18},{18,... | collective-permute-start | bytes 20 | tf_op jit(solution)/shard_map/ppermute | solution.py:278
  108.4 17.5 %collective-permute-start.20 = (f32[1]{0:T(128)}, f32[1]{0:T(128)}, u32[]{:S(2)}, u32[]{:S(2)}) collective-permute-start(f32[1]{0:T(128)} %bitcast.29), channel_id=1, source_target_pairs={{2,0},{1,3},{6,4},{5,7},{10,8},{9,11},{14,12},{13,15},{18,16},{17,... | collective-permute-start | bytes 20 | tf_op jit(solution)/shard_map/ppermute | solution.py:278

commit v8 on v6

--- a/solution.py
+++ b/solution.py
@@ -49,13 +49,14 @@
 def shards(meta, pieces):
     side = meta[13]
     length = pieces[0].shape[0]
-    places = [(pieces[i], 0) for i in range(5)] + [(pieces[5], i * length) for i in range(3)]
+    places = [(piece, 0) for piece in pieces[:-1]]
+    places += [(pieces[-1], i * length) for i in range(8 - len(places))]
     return [(*place, (side if i < 4 else 1 - side) * 4 + meta[9 + i % 4]) for i, place in enumerate(places)]
 
 
 def conv_kernel(meta, normed_ref, taps_ref, *rest):
-    pieces = rest[:6]
-    swished_ref, weight, mixed_a, mixed_b, gated, margin, mask, sems = rest[6:]
+    pieces = rest[:5]
+    swished_ref, weight, mixed_a, mixed_b, gated, margin, mask, sems = rest[5:]
     slot = pl.program_id(0)
     rows = normed_ref.shape[1]
     frames = swished_ref.shape[1]
@@ -290,24 +291,21 @@
     low = chip == 1
     is_hub = jnp.logical_or(low, chip == 2)
 
-    length = lengths[0]
-    positions = chip * rows + jnp.arange(rows, dtype=jnp.int32)
-    counted = jnp.logical_and(frame_mask[0] > 0, positions < length)
-    code = jnp.where(counted, targets[0], -1)
     first = conv_in_weight[0]
-    blocks = mel_frames[0].reshape(rows, -1)
     share = rows // seeds
     margin = step * EDGE
     quarter = lax.dynamic_slice_in_dim(mel_frames[0], seed * share * step, share * step, 0).reshape(share, -1)
     edge_out = jnp.where(low, mel_frames[0, -margin:], mel_frames[0, :margin]).reshape(EDGE, -1)
     quarter_in = along(quarter, INWARD)
     edge = along(edge_out, ACROSS)
-    outer_code = along(code, INWARD)
-    first_held, quarter_in, edge, outer_code = lax.optimization_barrier((first, quarter_in, edge, outer_code))
+    first_held, quarter_in, edge, mel_frames, lengths = lax.optimization_barrier(
+        (first, quarter_in, edge, mel_frames, lengths)
+    )
     near_first, hub_first, far_first = [along(first_held, pairs_) for pairs_ in (INWARD, ACROSS, BEYOND)]
     held = first.shape[0]
-
-    pair = seed_swap(quarter_in, 1)
+    blocks = mel_frames[0].reshape(rows, -1)
+
+    pair, targets, frame_mask = lax.optimization_barrier((seed_swap(quarter_in, 1), targets, frame_mask))
     odd = seed % 2 == 1
     pairs = jnp.concatenate([jnp.where(odd, pair, quarter_in), jnp.where(odd, quarter_in, pair)], axis=0)
     other = seed_swap(pairs, 2)
@@ -346,6 +344,11 @@
         ]
     )
 
+    length = lengths[0]
+    positions = chip * rows + jnp.arange(rows, dtype=jnp.int32)
+    counted = jnp.logical_and(frame_mask[0] > 0, positions < length)
+    code = jnp.where(counted, targets[0], -1).reshape(2, CHUNKS, tile // CHUNKS)
+
     starts = (chip - 1) * 2 * rows + tile * jnp.arange(slots, dtype=jnp.int32)
     alive = jnp.logical_and(is_hub, starts < length).astype(jnp.int32)
     hub = jnp.clip(chip, 1, 2)
@@ -358,6 +361,10 @@
         ]
     ).astype(jnp.int32)
 
+    taps = jnp.broadcast_to(
+        depth_weight[0].astype(jnp.float32)[:, None, :], (depth_weight.shape[1], CHUNKS, channels)
+    )
+    main, margins, code, second, taps = lax.optimization_barrier((main, margins, code, second, taps))
     gains = norm_gain[0]
     half = tile // 2
     stem_out, normed = call(
@@ -380,20 +387,15 @@
     )
     pinned = pl.BlockSpec(memory_space=pltpu.HBM)
 
-    codes = jnp.concatenate([jnp.where(low, outer_code, code), jnp.where(low, code, outer_code)])
-    codes = codes.reshape(slots, CHUNKS, tile // CHUNKS)
-    far_first, normed, codes = lax.optimization_barrier((far_first, normed, codes))
+    far_first, normed = lax.optimization_barrier((far_first, normed))
     mine = [first, near_first, hub_first, far_first]
-    first_pieces = (*mine, to_mate(first), to_mate(jnp.concatenate(mine[1:], axis=0)))
+    first_pieces = (*mine, to_mate(jnp.concatenate(mine, axis=0)))
     near_second, hub_second, far_second = [along(second, pairs_) for pairs_ in (INWARD, ACROSS, BEYOND)]
-    taps = jnp.broadcast_to(
-        depth_weight[0].astype(jnp.float32)[:, None, :], (depth_weight.shape[1], CHUNKS, channels)
-    )
     extent = tile // CHUNKS + depth_weight.shape[1] - 1
     swished = call(
         conv_kernel,
         (slots,),
-        [by_slot((deep, width)), whole(taps.shape)] + [pinned] * 6,
+        [by_slot((deep, width)), whole(taps.shape)] + [pinned] * 5,
         by_slot((tile, channels)),
         jax.ShapeDtypeStruct((slots, tile, channels), jnp.bfloat16),
         [
@@ -410,9 +412,11 @@
         (meta, normed, taps, *first_pieces),
     )
 
-    near_second, hub_second, far_second, swished = lax.optimization_barrier(
-        (near_second, hub_second, far_second, swished)
-    )
+    near_second, hub_second, far_second, code, swished = lax.optimization_barrier(
+        (near_second, hub_second, far_second, code, swished)
+    )
+    outer_code = along(code, INWARD)
+    codes = jnp.concatenate([jnp.where(low, outer_code, code), jnp.where(low, code, outer_code)])
     mine = [second, near_second, hub_second, far_second]
     second_pieces = (*mine, to_mate(second), to_mate(jnp.concatenate(mine[1:], axis=0)))
     errors = call(

time: 128 us -> 138 us (1.078)
  other arithmetic: 9.09 us -> 15.5 us
  local copies, waits for them, and re-layouts: 10.5 us -> 15.1 us
  waiting for transfers between devices: 51.5 us -> 47.2 us
  starting transfers between devices: 48.1 us -> 51.4 us
    ppermute x12, waiting for transfers between devices: 41.3 us -> 35.9 us  [along(): return lax.ppermute(x, 'seq', pairs)]
    ppermute x12, starting transfers between devices: 38.4 us -> 42.5 us  [along(): return lax.ppermute(x, 'seq', pairs)]
    unnamed x4, other arithmetic: 0.61 us -> 4.61 us
    concatenate x2 -> x0, local copies, waits for them, and re-layouts: 2.68 us -> none  [hub_body(): jnp.concatenate([jnp.where(low, outer_code, code), jnp.where(low, code, o...]
    another operation x1, local copies, waits for them, and re-layouts: 0.67 us -> 2.67 us  [hub_body(): blocks = mel_frames[0].reshape(rows, -1)]
    slice x1, local copies, waits for them, and re-layouts: 0.52 us -> 2.37 us  [hub_body(): pairs = jnp.concatenate([frames[:-1], frames[1:]], axis=1)]
    optimization_barrier x0 -> x2, local copies, waits for them, and re-layouts: none -> 1.82 us  [the longest x1 1.31 us: hub_body(): lax.optimization_barrier((first, quarter_in, edge, mel_frames, lengths))]
    convert_element_type x1, other arithmetic: 0.01 us -> 1.44 us  [hub_body(): depth_weight[0].astype(jnp.float32)[:, None, :]]
  transfers between devices with their start and end apart: 21 -> 20, of which waited for: 8 -> 9; matrix products, arithmetic and copies ran while one was open for 11% -> 18% of each run, Pallas kernels for 1% -> 1%
where the time goes in v8:
time: 138 us; the launch traced here: 137 us
  starting transfers between devices  51.4 us (37%)
  waiting for transfers between devices  47.2 us (34%)
  other arithmetic  15.5 us (11%)
  local copies, waits for them, and re-layouts  15.1 us (11%)
  between operations  5.49 us (4%)
  Pallas kernels  2.42 us (2%)
    ppermute x12, starting transfers between devices, along(): return lax.ppermute(x, 'seq', pairs)  42.5 us
    ppermute x12, waiting for transfers between devices, along(): return lax.ppermute(x, 'seq', pairs)  35.9 us
    ppermute x5, waiting for transfers between devices, seed_swap(): return lax.ppermute(x, 'seed', [(i, i ^ bit) for i in range(4)])  11.3 us
    ppermute x5, starting transfers between devices, seed_swap(): return lax.ppermute(x, 'seed', [(i, i ^ bit) for i in range(4)])  6.63 us
    unnamed x4, other arithmetic  4.61 us
  transfers between devices with their start and end apart: 20, of which 9 were waited for; matrix products, arithmetic and copies ran while one was open for 18% of the time, Pallas kernels for 1%

profile of v8, /device:TPU:0, one launch (start us, length us, event | category | flops | bytes accessed | tf_op | source)
XLA Modules:
  0.0 137.2 jit_solution(14950806369687873222)
XLA Ops:
  0.7 1.0 constant_dynamic-slice_fusion
  1.7 0.2 copy.16
  1.9 0.2 reshape.52
  2.1 4.9 %collective-permute-start = (bf16[256,320]{1,0:T(8,128)(2,1)S(1)}, bf16[256,320]{1,0:T(8,128)(2,1)S(1)}, u32[]{:S(2)}, u32[]{:S(2)}) collective-permute-start(bf16[256,320]{1,0:T(8,128)(2,1)S(1)} %reshape.52), channel_id=1, source_target_pairs={{0,1},{3,2},{4,5},{7,6},{8,9},{11,10},{12,13},{15,14},{16,17},{19,... | collective-permute-start | bytes 491528 | tf_op jit(solution)/shard_map/ppermute | solution.py:257
  7.0 0.8 slice_select_fusion
  8.0 0.7 collective-permute-start.1
  8.7 0.9 slice_bitcast_fusion.2
  9.6 1.4 %bitcast_convert_fusion = f32[31,768]{1,0:T(8,128)} fusion(bf16[1,31,768]{2,1,0:T(8,128)(2,1)} %param.17), kind=kLoop, calls=%fused_computation.36 | loop fusion | flops 23808 | bytes 142848 | tf_op jit(solution)/shard_map/convert_element_type | solution.py:365
  11.1 1.0 maximum_maximum_fusion.rest_0_
  12.7 0.6 fusion.15
  13.4 0.7 concatenate.45.meta
  14.1 0.7 copy-done.6
  14.8 4.1 %collective-permute-start.7 = (bf16[192,1536]{1,0:T(8,128)(2,1)S(1)}, bf16[192,1536]{1,0:T(8,128)(2,1)S(1)}, u32[]{:S(2)}, u32[]{:S(2)}) collective-permute-start(bf16[192,1536]{1,0:T(8,128)(2,1)S(1)} %bitcast.43), channel_id=1, source_target_pairs={{0,2},{3,1},{4,6},{7,5},{8,10},{11,9},{12,14},{15,13},{16,18},{19,... | collective-permute-start | bytes 1769480 | tf_op jit(solution)/shard_map/ppermute | solution.py:257
  19.0 1.4 %collective-permute-start.8 = (bf16[192,1536]{1,0:T(8,128)(2,1)S(1)}, bf16[192,1536]{1,0:T(8,128)(2,1)S(1)}, u32[]{:S(2)}, u32[]{:S(2)}) collective-permute-start(bf16[192,1536]{1,0:T(8,128)(2,1)S(1)} %bitcast.44), channel_id=1, source_target_pairs={{0,1},{3,2},{4,5},{7,6},{8,9},{11,10},{12,13},{15,14},{16,17},{19,... | collective-permute-start | bytes 1769480 | tf_op jit(solution)/shard_map/ppermute | solution.py:257
  20.4 0.7 collective-permute-start.9
  21.1 1.6 %collective-permute-start.2 = (bf16[256,320]{1,0:T(8,128)(2,1)}, bf16[256,320]{1,0:T(8,128)(2,1)}, u32[]{:S(2)}, u32[]{:S(2)}) collective-permute-start(bf16[256,320]{1,0:T(8,128)(2,1)} %copy-done.6), channel_id=1, source_target_pairs={{0,8},{8,0},{16,24},{24,16},{1,9},{9,1},{17,25},{25,17},{2,10},{10... | collective-permute-start | bytes 491528 | tf_op jit(solution)/shard_map/ppermute | solution.py:266
  22.6 1.3 copy.18
  23.9 2.7 %reshape_squeeze.3 = bf16[1024,320]{1,0:T(8,128)(2,1)} reshape(bf16[1,4096,80]{2,1,0:T(8,128)(2,1)} %copy.18) | data formatting | bytes 1310720 | tf_op jit(solution)/shard_map/reshape;squeeze | solution.py:306
  26.6 0.6 select_dynamic-update-slice_fusion.3
  27.2 0.3 collective-permute-done.2
  27.5 1.1 broadcast_select_fusion.3
  28.6 0.8 pad_maximum_fusion.3
  29.4 1.5 %collective-permute-start.3 = (bf16[512,320]{1,0:T(8,128)(2,1)}, bf16[512,320]{1,0:T(8,128)(2,1)}, u32[]{:S(2)}, u32[]{:S(2)}) collective-permute-start(bf16[512,320]{1,0:T(8,128)(2,1)} %pad_maximum_fusion.3), channel_id=1, source_target_pairs={{0,16},{8,24},{16,0},{24,8},{1,17},{9,25},{17,1},{25,9},{2,18},{10... | collective-permute-start | bytes 983048 | tf_op jit(solution)/shard_map/ppermute | solution.py:266
  30.9 0.5 broadcast.35
  31.4 0.7 reduce.6
  32.3 7.1 %collective-permute-done.3 = bf16[512,320]{1,0:T(8,128)(2,1)} collective-permute-done((bf16[512,320]{1,0:T(8,128)(2,1)}, bf16[512,320]{1,0:T(8,128)(2,1)}, u32[]{:S(2)}, u32[]{:S(2)}) %collective-permute-start.3) | collective-permute-done | bytes 327712 | tf_op jit(solution)/shard_map/ppermute | solution.py:266
  39.4 1.2 broadcast_select_fusion.1
  40.6 2.3 %select_dynamic-update-slice_fusion.1 = bf16[2096,320]{1,0:T(8,128)(2,1)} fusion(bf16[2096,320]{1,0:T(8,128)(2,1)} %select_dynamic-update-slice_fusion.3, bf16[1024,320]{1,0:T(8,128)(2,1)} %reshape_squeeze.3, pred[]{:T(512)S(6)} %eq.14, bf16[512,320]{1,0:T(8,128)(2,1)S(1)} %get-tuple-element.58, bf16[512,320]{1,0:T(8,128)(2,1)S(1)} %get-tuple-element.57), kind=kLoop, calls=%fused_computation.22 | loop fusion | flops 1638400 | bytes 2228225
  42.8 1.1 select_dynamic-update-slice_fusion
  44.0 0.6 select_dynamic-update-slice_fusion.2
  44.6 0.6 constant_dynamic-update-slice_fusion
  45.2 2.4 %fusion.16 = (bf16[2095,320]{1,0:T(8,128)(2,1)S(1)}, bf16[2095,320]{1,0:T(8,128)(2,1)S(1)}) fusion(bf16[2096,320]{1,0:T(8,128)(2,1)} %constant_dynamic-update-slice_fusion), kind=kLoop, calls=%fused_computation.71 | loop fusion | bytes 5363200 | tf_op jit(solution)/shard_map/slice | solution.py:337
  47.5 1.0 fusion
  48.5 1.5 %copy.21 = bf16[4,64,8,640]{3,2,1,0:T(8,128)(2,1)S(1)} copy(bf16[4,64,8,640]{3,1,2,0:T(8,128)(2,1)S(1)} %bitcast.51) | data formatting | bytes 5242880 | tf_op jit(solution)/shard_map/transpose | solution.py:339
  50.3 0.7 copy-done.5
  51.1 0.7 copy-done.1
  51.8 0.6 shard_map.113
  52.4 0.2 pad_maximum_fusion
  52.6 0.8 collective-permute-start.10
  53.4 12.2 %collective-permute-start.4 = (bf16[160,1536]{1,0:T(8,128)(2,1)S(1)}, bf16[160,1536]{1,0:T(8,128)(2,1)S(1)}, u32[]{:S(2)}, u32[]{:S(2)}) collective-permute-start(bf16[160,1536]{1,0:T(8,128)(2,1)S(1)} %maximum_maximum_fusion.rest_0_), channel_id=1, source_target_pairs={{0,1},{3,2},{4,5},{7,6},{8,9},{11,10},{12,13},{15,14},{16,17},{19,... | collective-permute-start | bytes 1474568 | tf_op jit(solution)/shard_map/ppermute | solution.py:257
  65.6 0.7 collective-permute-start.5
  66.3 4.2 %collective-permute-start.6 = (bf16[160,1536]{1,0:T(8,128)(2,1)S(1)}, bf16[160,1536]{1,0:T(8,128)(2,1)S(1)}, u32[]{:S(2)}, u32[]{:S(2)}) collective-permute-start(bf16[160,1536]{1,0:T(8,128)(2,1)S(1)} %maximum_maximum_fusion.rest_0_), channel_id=1, source_target_pairs={{0,2},{3,1},{4,6},{7,5},{8,10},{11,9},{12,14},{15,13},{16,18},{19,... | collective-permute-start | bytes 1474568 | tf_op jit(solution)/shard_map/ppermute | solution.py:257
  70.5 0.8 shard_map.114.swished_ref
  71.3 5.9 %collective-permute-done.4.rest_1_ = bf16[160,1536]{1,0:T(8,128)(2,1)S(1)} collective-permute-done((bf16[160,1536]{1,0:T(8,128)(2,1)S(1)}, bf16[160,1536]{1,0:T(8,128)(2,1)S(1)}, u32[]{:S(2)}, u32[]{:S(2)}) %collective-permute-start.4) | collective-permute-done | bytes 491552 | tf_op jit(solution)/shard_map/ppermute | solution.py:257
  77.1 10.2 %collective-permute-done.6.rest_3_ = bf16[160,1536]{1,0:T(8,128)(2,1)S(1)} collective-permute-done((bf16[160,1536]{1,0:T(8,128)(2,1)S(1)}, bf16[160,1536]{1,0:T(8,128)(2,1)S(1)}, u32[]{:S(2)}, u32[]{:S(2)}) %collective-permute-start.6) | collective-permute-done | bytes 491552 | tf_op jit(solution)/shard_map/ppermute | solution.py:257
  87.4 0.8 collective-permute-start.13
  88.1 0.7 collective-permute-start.12
  88.8 9.8 %collective-permute-start.11 = (s32[2,8,64]{2,1,0:T(8,128)S(1)}, s32[2,8,64]{2,1,0:T(8,128)S(1)}, u32[]{:S(2)}, u32[]{:S(2)}) collective-permute-start(s32[2,8,64]{2,1,0:T(8,128)S(1)} %fusion.14), channel_id=1, source_target_pairs={{0,1},{3,2},{4,5},{7,6},{8,9},{11,10},{12,13},{15,14},{16,17},{19,... | collective-permute-start | bytes 12296 | tf_op jit(solution)/shard_map/ppermute | solution.py:257
  98.7 1.3 collective-permute-done.11
  100.0 1.0 shard_map.115
  101.1 1.2 collective-permute-start.14
  102.3 1.5 %collective-permute-start.15 = (f32[4,8,128]{2,1,0:T(8,128)S(1)}, f32[4,8,128]{2,1,0:T(8,128)S(1)}, u32[]{:S(2)}, u32[]{:S(2)}) collective-permute-start(f32[4,8,128]{2,1,0:T(8,128)S(1)} %shard_map.115), channel_id=1, source_target_pairs={{0,16},{8,24},{16,0},{24,8},{1,17},{9,25},{17,1},{25,9},{2,18},{10... | collective-permute-start | bytes 49160 | tf_op jit(solution)/shard_map/ppermute | solution.py:266
  103.8 0.8 collective-permute-start.16
  104.6 0.2 collective-permute-done.14
  104.9 1.2 collective-permute-done.15
  106.0 2.4 %collective-permute-done.16 = f32[4,8,128]{2,1,0:T(8,128)S(1)} collective-permute-done((f32[4,8,128]{2,1,0:T(8,128)S(1)}, f32[4,8,128]{2,1,0:T(8,128)S(1)}, u32[]{:S(2)}, u32[]{:S(2)}) %collective-permute-start.16) | collective-permute-done | bytes 16416 | tf_op jit(solution)/shard_map/ppermute | solution.py:266
  108.5 0.6 slice_reduce_fusion
  109.2 0.6 pad_maximum_fusion.5
  109.8 1.3 collective-permute-start.17
  111.1 1.3 collective-permute-start.18
  112.4 1.3 collective-permute-start.19
  113.7 18.5 %collective-permute-done.19 = f32[1]{0:T(128)} collective-permute-done((f32[1]{0:T(128)}, f32[1]{0:T(128)}, u32[]{:S(2)}, u32[]{:S(2)}) %collective-permute-start.19) | collective-permute-done | bytes 36 | tf_op jit(solution)/shard_map/ppermute | solution.py:257
  133.6 0.5 slice.103
  135.4 0.6 slice_select_fusion.3
  (45 shorter events, 1.0 us)
Async XLA Ops:
  0.6 22.0 %copy-start.4 = (bf16[1,4096,80]{1,2,0:T(8,128)(2,1)S(1)}, bf16[1,4096,80]{1,2,0:T(8,128)(2,1)}, u32[]{:S(2)}) copy-start(bf16[1,4096,80]{1,2,0:T(8,128)(2,1)} %param.10) | copy-start | bytes 1966084
  0.6 14.2 %copy-start = (bf16[1,192,1536]{2,1,0:T(8,128)(2,1)S(1)}, bf16[1,192,1536]{2,1,0:T(8,128)(2,1)}, u32[]{:S(2)}) copy-start(bf16[1,192,1536]{2,1,0:T(8,128)(2,1)} %param.15) | copy-start | bytes 1769476
  2.1 12.0 %collective-permute-start = (bf16[256,320]{1,0:T(8,128)(2,1)S(1)}, bf16[256,320]{1,0:T(8,128)(2,1)S(1)}, u32[]{:S(2)}, u32[]{:S(2)}) collective-permute-start(bf16[256,320]{1,0:T(8,128)(2,1)S(1)} %reshape.52), channel_id=1, source_target_pairs={{0,1},{3,2},{4,5},{7,6},{8,9},{11,10},{12,13},{15,14},{16,17},{19,... | collective-permute-start | bytes 491528 | tf_op jit(solution)/shard_map/ppermute | solution.py:257
  8.0 6.1 %collective-permute-start.1 = (bf16[16,320]{1,0:T(8,128)(2,1)S(1)}, bf16[16,320]{1,0:T(8,128)(2,1)S(1)}, u32[]{:S(2)}, u32[]{:S(2)}) collective-permute-start(bf16[16,320]{1,0:T(8,128)(2,1)S(1)} %select_n.118), channel_id=1, source_target_pairs={{1,2},{2,1},{5,6},{6,5},{9,10},{10,9},{13,14},{14,13},{17,18},{18,... | collective-permute-start | bytes 30728 | tf_op jit(solution)/shard_map/ppermute | solution.py:257
  14.1 0.7 copy-start.6
  14.8 16.6 %copy-start.8 = (s32[1,1024]{1,0:T(1,128)S(1)}, s32[1,1024]{1,0:T(1,128)}, u32[]{:S(2)}) copy-start(s32[1,1024]{1,0:T(1,128)} %param.12) | copy-start | bytes 12292
  14.8 17.4 %copy-start.7 = (s32[1,1024]{1,0:T(1,128)S(1)}, s32[1,1024]{1,0:T(1,128)}, u32[]{:S(2)}) copy-start(s32[1,1024]{1,0:T(1,128)} %param.13) | copy-start | bytes 12292
  14.8 37.6 %collective-permute-start.7 = (bf16[192,1536]{1,0:T(8,128)(2,1)S(1)}, bf16[192,1536]{1,0:T(8,128)(2,1)S(1)}, u32[]{:S(2)}, u32[]{:S(2)}) collective-permute-start(bf16[192,1536]{1,0:T(8,128)(2,1)S(1)} %bitcast.43), channel_id=1, source_target_pairs={{0,2},{3,1},{4,6},{7,5},{8,10},{11,9},{12,14},{15,13},{16,18},{19,... | collective-permute-start | bytes 1769480 | tf_op jit(solution)/shard_map/ppermute | solution.py:257
  19.0 33.5 %collective-permute-start.8 = (bf16[192,1536]{1,0:T(8,128)(2,1)S(1)}, bf16[192,1536]{1,0:T(8,128)(2,1)S(1)}, u32[]{:S(2)}, u32[]{:S(2)}) collective-permute-start(bf16[192,1536]{1,0:T(8,128)(2,1)S(1)} %bitcast.44), channel_id=1, source_target_pairs={{0,1},{3,2},{4,5},{7,6},{8,9},{11,10},{12,13},{15,14},{16,17},{19,... | collective-permute-start | bytes 1769480 | tf_op jit(solution)/shard_map/ppermute | solution.py:257
  20.4 32.1 %collective-permute-start.9 = (bf16[192,1536]{1,0:T(8,128)(2,1)S(1)}, bf16[192,1536]{1,0:T(8,128)(2,1)S(1)}, u32[]{:S(2)}, u32[]{:S(2)}) collective-permute-start(bf16[192,1536]{1,0:T(8,128)(2,1)S(1)} %bitcast.45), channel_id=1, source_target_pairs={{1,2},{2,1},{5,6},{6,5},{9,10},{10,9},{13,14},{14,13},{17,18},{18,... | collective-permute-start | bytes 1769480 | tf_op jit(solution)/shard_map/ppermute | solution.py:257
  21.1 6.5 %collective-permute-start.2 = (bf16[256,320]{1,0:T(8,128)(2,1)}, bf16[256,320]{1,0:T(8,128)(2,1)}, u32[]{:S(2)}, u32[]{:S(2)}) collective-permute-start(bf16[256,320]{1,0:T(8,128)(2,1)} %copy-done.6), channel_id=1, source_target_pairs={{0,8},{8,0},{16,24},{24,16},{1,9},{9,1},{17,25},{25,17},{2,10},{10... | collective-permute-start | bytes 491528 | tf_op jit(solution)/shard_map/ppermute | solution.py:266
  29.4 10.0 %collective-permute-start.3 = (bf16[512,320]{1,0:T(8,128)(2,1)}, bf16[512,320]{1,0:T(8,128)(2,1)}, u32[]{:S(2)}, u32[]{:S(2)}) collective-permute-start(bf16[512,320]{1,0:T(8,128)(2,1)} %pad_maximum_fusion.3), channel_id=1, source_target_pairs={{0,16},{8,24},{16,0},{24,8},{1,17},{9,25},{17,1},{25,9},{2,18},{10... | collective-permute-start | bytes 983048 | tf_op jit(solution)/shard_map/ppermute | solution.py:266
  32.3 10.5 %copy-start.3 = (bf16[1024,320]{1,0:T(8,128)(2,1)S(1)}, bf16[1024,320]{1,0:T(8,128)(2,1)}, u32[]{:S(2)}) copy-start(bf16[1024,320]{1,0:T(8,128)(2,1)} %reshape_squeeze.3) | copy-start | bytes 1966084
  50.2 0.9 copy-start.5
  50.2 1.6 %copy-start.1 = (bf16[1,640,1536]{2,1,0:T(8,128)(2,1)S(1)}, bf16[1,640,1536]{2,1,0:T(8,128)(2,1)}, u32[]{:S(2)}) copy-start(bf16[1,640,1536]{2,1,0:T(8,128)(2,1)} %param.14) | copy-start | bytes 5898244
  50.2 1.6 %copy-start.2 = (f32[1,2,1536]{2,1,0:T(2,128)S(1)}, f32[1,2,1536]{2,1,0:T(2,128)}, u32[]{:S(2)}) copy-start(f32[1,2,1536]{2,1,0:T(2,128)} %param.19) | copy-start | bytes 36868
  52.6 17.9 %collective-permute-start.10 = (bf16[768,1536]{1,0:T(8,128)(2,1)S(1)}, bf16[768,1536]{1,0:T(8,128)(2,1)S(1)}, u32[]{:S(2)}, u32[]{:S(2)}) collective-permute-start(bf16[768,1536]{1,0:T(8,128)(2,1)S(1)} %pad_maximum_fusion), channel_id=1, source_target_pairs={{1,5},{2,6},{5,1},{6,2},{9,13},{10,14},{13,9},{14,10},{17,21},{18,... | collective-permute-start | bytes 7077896 | tf_op jit(solution)/shard_map/ppermute | solution.py:262
  53.4 23.7 %collective-permute-start.4 = (bf16[160,1536]{1,0:T(8,128)(2,1)S(1)}, bf16[160,1536]{1,0:T(8,128)(2,1)S(1)}, u32[]{:S(2)}, u32[]{:S(2)}) collective-permute-start(bf16[160,1536]{1,0:T(8,128)(2,1)S(1)} %maximum_maximum_fusion.rest_0_), channel_id=1, source_target_pairs={{0,1},{3,2},{4,5},{7,6},{8,9},{11,10},{12,13},{15,14},{16,17},{19,... | collective-permute-start | bytes 1474568 | tf_op jit(solution)/shard_map/ppermute | solution.py:257
  65.6 11.5 %collective-permute-start.5 = (bf16[160,1536]{1,0:T(8,128)(2,1)S(1)}, bf16[160,1536]{1,0:T(8,128)(2,1)S(1)}, u32[]{:S(2)}, u32[]{:S(2)}) collective-permute-start(bf16[160,1536]{1,0:T(8,128)(2,1)S(1)} %maximum_maximum_fusion.rest_0_), channel_id=1, source_target_pairs={{1,2},{2,1},{5,6},{6,5},{9,10},{10,9},{13,14},{14,13},{17,18},{18,... | collective-permute-start | bytes 1474568 | tf_op jit(solution)/shard_map/ppermute | solution.py:257
  66.3 21.0 %collective-permute-start.6 = (bf16[160,1536]{1,0:T(8,128)(2,1)S(1)}, bf16[160,1536]{1,0:T(8,128)(2,1)S(1)}, u32[]{:S(2)}, u32[]{:S(2)}) collective-permute-start(bf16[160,1536]{1,0:T(8,128)(2,1)S(1)} %maximum_maximum_fusion.rest_0_), channel_id=1, source_target_pairs={{0,2},{3,1},{4,6},{7,5},{8,10},{11,9},{12,14},{15,13},{16,18},{19,... | collective-permute-start | bytes 1474568 | tf_op jit(solution)/shard_map/ppermute | solution.py:257
  87.4 12.6 %collective-permute-start.13 = (bf16[480,1536]{1,0:T(8,128)(2,1)S(1)}, bf16[480,1536]{1,0:T(8,128)(2,1)S(1)}, u32[]{:S(2)}, u32[]{:S(2)}) collective-permute-start(bf16[480,1536]{1,0:T(8,128)(2,1)S(1)} %pad_maximum_fusion.1), channel_id=1, source_target_pairs={{1,5},{2,6},{5,1},{6,2},{9,13},{10,14},{13,9},{14,10},{17,21},{18,... | collective-permute-start | bytes 4423688 | tf_op jit(solution)/shard_map/ppermute | solution.py:262
  88.1 11.9 %collective-permute-start.12 = (bf16[160,1536]{1,0:T(8,128)(2,1)S(1)}, bf16[160,1536]{1,0:T(8,128)(2,1)S(1)}, u32[]{:S(2)}, u32[]{:S(2)}) collective-permute-start(bf16[160,1536]{1,0:T(8,128)(2,1)S(1)} %maximum_maximum_fusion.rest_0_), channel_id=1, source_target_pairs={{1,5},{2,6},{5,1},{6,2},{9,13},{10,14},{13,9},{14,10},{17,21},{18,... | collective-permute-start | bytes 1474568 | tf_op jit(solution)/shard_map/ppermute | solution.py:262
  88.8 11.2 %collective-permute-start.11 = (s32[2,8,64]{2,1,0:T(8,128)S(1)}, s32[2,8,64]{2,1,0:T(8,128)S(1)}, u32[]{:S(2)}, u32[]{:S(2)}) collective-permute-start(s32[2,8,64]{2,1,0:T(8,128)S(1)} %fusion.14), channel_id=1, source_target_pairs={{0,1},{3,2},{4,5},{7,6},{8,9},{11,10},{12,13},{15,14},{16,17},{19,... | collective-permute-start | bytes 12296 | tf_op jit(solution)/shard_map/ppermute | solution.py:257
  101.1 3.8 %collective-permute-start.14 = (f32[4,8,128]{2,1,0:T(8,128)S(1)}, f32[4,8,128]{2,1,0:T(8,128)S(1)}, u32[]{:S(2)}, u32[]{:S(2)}) collective-permute-start(f32[4,8,128]{2,1,0:T(8,128)S(1)} %shard_map.115), channel_id=1, source_target_pairs={{0,8},{8,0},{16,24},{24,16},{1,9},{9,1},{17,25},{25,17},{2,10},{10... | collective-permute-start | bytes 49160 | tf_op jit(solution)/shard_map/ppermute | solution.py:266
  102.3 3.7 %collective-permute-start.15 = (f32[4,8,128]{2,1,0:T(8,128)S(1)}, f32[4,8,128]{2,1,0:T(8,128)S(1)}, u32[]{:S(2)}, u32[]{:S(2)}) collective-permute-start(f32[4,8,128]{2,1,0:T(8,128)S(1)} %shard_map.115), channel_id=1, source_target_pairs={{0,16},{8,24},{16,0},{24,8},{1,17},{9,25},{17,1},{25,9},{2,18},{10... | collective-permute-start | bytes 49160 | tf_op jit(solution)/shard_map/ppermute | solution.py:266
  103.8 4.6 %collective-permute-start.16 = (f32[4,8,128]{2,1,0:T(8,128)S(1)}, f32[4,8,128]{2,1,0:T(8,128)S(1)}, u32[]{:S(2)}, u32[]{:S(2)}) collective-permute-start(f32[4,8,128]{2,1,0:T(8,128)S(1)} %shard_map.115), channel_id=1, source_target_pairs={{0,24},{8,16},{16,8},{24,0},{1,25},{9,17},{17,9},{25,1},{2,26},{10... | collective-permute-start | bytes 49160 | tf_op jit(solution)/shard_map/ppermute | solution.py:266
  109.8 23.8 %collective-permute-start.17 = (f32[1025]{0:T(1024)S(1)}, f32[1025]{0:T(1024)S(1)}, u32[]{:S(2)}, u32[]{:S(2)}) collective-permute-start(f32[1025]{0:T(1024)S(1)} %pad_maximum_fusion.5), channel_id=1, source_target_pairs={{1,0},{2,3},{5,4},{6,7},{9,8},{10,11},{13,12},{14,15},{17,16},{18,... | collective-permute-start | bytes 12308 | tf_op jit(solution)/shard_map/ppermute | solution.py:257
  111.1 2.6 %collective-permute-start.18 = (f32[1]{0:T(128)}, f32[1]{0:T(128)}, u32[]{:S(2)}, u32[]{:S(2)}) collective-permute-start(f32[1]{0:T(128)} %bitcast.22), channel_id=1, source_target_pairs={{1,2},{2,1},{5,6},{6,5},{9,10},{10,9},{13,14},{14,13},{17,18},{18,... | collective-permute-start | bytes 20 | tf_op jit(solution)/shard_map/ppermute | solution.py:257
  112.4 19.9 %collective-permute-start.19 = (f32[1]{0:T(128)}, f32[1]{0:T(128)}, u32[]{:S(2)}, u32[]{:S(2)}) collective-permute-start(f32[1]{0:T(128)} %bitcast.22), channel_id=1, source_target_pairs={{2,0},{1,3},{6,4},{5,7},{10,8},{9,11},{14,12},{13,15},{18,16},{17,... | collective-permute-start | bytes 20 | tf_op jit(solution)/shard_map/ppermute | solution.py:257

commit v9 on v8

--- a/solution.py
+++ b/solution.py
@@ -298,9 +298,7 @@
     edge_out = jnp.where(low, mel_frames[0, -margin:], mel_frames[0, :margin]).reshape(EDGE, -1)
     quarter_in = along(quarter, INWARD)
     edge = along(edge_out, ACROSS)
-    first_held, quarter_in, edge, mel_frames, lengths = lax.optimization_barrier(
-        (first, quarter_in, edge, mel_frames, lengths)
-    )
+    first_held, quarter_in, edge = lax.optimization_barrier((first, quarter_in, edge))
     near_first, hub_first, far_first = [along(first_held, pairs_) for pairs_ in (INWARD, ACROSS, BEYOND)]
     held = first.shape[0]
     blocks = mel_frames[0].reshape(rows, -1)
@@ -364,7 +362,7 @@
     taps = jnp.broadcast_to(
         depth_weight[0].astype(jnp.float32)[:, None, :], (depth_weight.shape[1], CHUNKS, channels)
     )
-    main, margins, code, second, taps = lax.optimization_barrier((main, margins, code, second, taps))
+    main, margins, code = lax.optimization_barrier((main, margins, code))
     gains = norm_gain[0]
     half = tile // 2
     stem_out, normed = call(

time: 138 us -> 135 us (0.978)
  waiting for transfers between devices: 47.2 us -> 45.3 us
    another operation x1, local copies, waits for them, and re-layouts: 2.67 us -> 0.68 us  [hub_body(): blocks = mel_frames[0].reshape(rows, -1)]
    ppermute x5, waiting for transfers between devices: 11.3 us -> 9.45 us  [seed_swap(): return lax.ppermute(x, 'seed', [(i, i ^ bit) for i in range(4)])]
    convert_element_type x1, other arithmetic: 1.44 us -> 0.01 us  [hub_body(): depth_weight[0].astype(jnp.float32)[:, None, :]]
    unnamed x18 -> x15, local copies, waits for them, and re-layouts: 2.1 us -> 2.98 us
where the time goes in v9:
time: 135 us; the launch traced here: 134 us
  starting transfers between devices  51.9 us (38%)
  waiting for transfers between devices  45.3 us (34%)
  other arithmetic  15 us (11%)
  local copies, waits for them, and re-layouts  14.2 us (11%)
  between operations  5.51 us (4%)
  Pallas kernels  2.42 us (2%)
    ppermute x12, starting transfers between devices, along(): return lax.ppermute(x, 'seq', pairs)  43 us
    ppermute x12, waiting for transfers between devices, along(): return lax.ppermute(x, 'seq', pairs)  35.9 us
    ppermute x5, waiting for transfers between devices, seed_swap(): return lax.ppermute(x, 'seed', [(i, i ^ bit) for i in range(4)])  9.45 us
    ppermute x5, starting transfers between devices, seed_swap(): return lax.ppermute(x, 'seed', [(i, i ^ bit) for i in range(4)])  6.63 us
    unnamed x4, other arithmetic  3.45 us
    unnamed x15, local copies, waits for them, and re-layouts  2.98 us
  transfers between devices with their start and end apart: 20, of which 9 were waited for; matrix products, arithmetic and copies ran while one was open for 18% of the time, Pallas kernels for 1%

profile of v9, /device:TPU:0, one launch (start us, length us, event | category | flops | bytes accessed | tf_op | source)
XLA Modules:
  0.0 134.5 jit_solution(2125779457151686210)
XLA Ops:
  0.6 0.9 constant_dynamic-slice_fusion
  1.6 0.2 copy.16
  1.8 0.2 reshape.52
  2.0 4.9 %collective-permute-start.3 = (bf16[256,320]{1,0:T(8,128)(2,1)S(1)}, bf16[256,320]{1,0:T(8,128)(2,1)S(1)}, u32[]{:S(2)}, u32[]{:S(2)}) collective-permute-start(bf16[256,320]{1,0:T(8,128)(2,1)S(1)} %reshape.52), channel_id=1, source_target_pairs={{0,1},{3,2},{4,5},{7,6},{8,9},{11,10},{12,13},{15,14},{16,17},{19,... | collective-permute-start | bytes 491528 | tf_op jit(solution)/shard_map/ppermute | solution.py:257
  6.9 0.8 slice_select_fusion
  7.9 0.7 collective-permute-start.4
  9.3 0.6 fusion.15
  9.9 1.5 %copy.18 = bf16[1,4096,80]{2,1,0:T(8,128)(2,1)S(1)} copy(bf16[1,4096,80]{1,2,0:T(8,128)(2,1)} %param.10) | data formatting | bytes 1310720 | tf_op args[0]
  11.5 0.7 reshape_squeeze.3
  12.2 0.7 concatenate.45.meta
  13.0 4.0 %collective-permute-start.7 = (bf16[192,1536]{1,0:T(8,128)(2,1)S(1)}, bf16[192,1536]{1,0:T(8,128)(2,1)S(1)}, u32[]{:S(2)}, u32[]{:S(2)}) collective-permute-start(bf16[192,1536]{1,0:T(8,128)(2,1)S(1)} %bitcast.43), channel_id=1, source_target_pairs={{0,2},{3,1},{4,6},{7,5},{8,10},{11,9},{12,14},{15,13},{16,18},{19,... | collective-permute-start | bytes 1769480 | tf_op jit(solution)/shard_map/ppermute | solution.py:257
  17.0 1.4 %collective-permute-start.8 = (bf16[192,1536]{1,0:T(8,128)(2,1)S(1)}, bf16[192,1536]{1,0:T(8,128)(2,1)S(1)}, u32[]{:S(2)}, u32[]{:S(2)}) collective-permute-start(bf16[192,1536]{1,0:T(8,128)(2,1)S(1)} %bitcast.44), channel_id=1, source_target_pairs={{0,1},{3,2},{4,5},{7,6},{8,9},{11,10},{12,13},{15,14},{16,17},{19,... | collective-permute-start | bytes 1769480 | tf_op jit(solution)/shard_map/ppermute | solution.py:257
  18.4 0.7 collective-permute-start.9
  19.1 1.6 %collective-permute-start.5 = (bf16[256,320]{1,0:T(8,128)(2,1)S(1)}, bf16[256,320]{1,0:T(8,128)(2,1)S(1)}, u32[]{:S(2)}, u32[]{:S(2)}) collective-permute-start(bf16[256,320]{1,0:T(8,128)(2,1)S(1)} %collective-permute-done.3), channel_id=1, source_target_pairs={{0,8},{8,0},{16,24},{24,16},{1,9},{9,1},{17,25},{25,17},{2,10},{10... | collective-permute-start | bytes 491528 | tf_op jit(solution)/shard_map/ppermute | solution.py:266
  20.7 0.6 select_dynamic-update-slice_fusion.3
  21.3 4.0 %collective-permute-done.5 = bf16[256,320]{1,0:T(8,128)(2,1)S(1)} collective-permute-done((bf16[256,320]{1,0:T(8,128)(2,1)S(1)}, bf16[256,320]{1,0:T(8,128)(2,1)S(1)}, u32[]{:S(2)}, u32[]{:S(2)}) %collective-permute-start.5) | collective-permute-done | bytes 163872 | tf_op jit(solution)/shard_map/ppermute | solution.py:266
  25.3 1.0 broadcast_select_fusion.3
  26.2 0.8 pad_maximum_fusion.3
  27.1 1.5 %collective-permute-start.6 = (bf16[512,320]{1,0:T(8,128)(2,1)}, bf16[512,320]{1,0:T(8,128)(2,1)}, u32[]{:S(2)}, u32[]{:S(2)}) collective-permute-start(bf16[512,320]{1,0:T(8,128)(2,1)} %pad_maximum_fusion.3), channel_id=1, source_target_pairs={{0,16},{8,24},{16,0},{24,8},{1,17},{9,25},{17,1},{25,9},{2,18},{10... | collective-permute-start | bytes 983048 | tf_op jit(solution)/shard_map/ppermute | solution.py:266
  28.6 0.5 broadcast.35
  29.1 1.8 %reduce.6 = s32[1024]{0:T(1024)} reduce(s32[1,1024]{1,0:T(1,128)} %param.12, s32[]{:T(128)} %broadcast.35), dimensions={0}, to_apply=%get-tuple-element.24.reduce_sub_computation.3 | reduce | bytes 8196 | tf_op jit(solution)/shard_map/optimization_barrier | solution.py:306
  30.9 1.3 %squeeze.17 = s32[2,8,64]{2,1,0:T(8,128)} reshape(s32[1024]{0:T(1024)} %reduce.6) | data formatting | bytes 8192 | tf_op jit(solution)/shard_map/squeeze | solution.py:348
  32.2 1.2 compare_reduce_fusion
  33.5 1.3 gt.12
  34.7 0.7 fusion.14
  35.4 1.3 collective-permute-done.6
  36.7 1.2 broadcast_select_fusion.1
  37.9 1.1 select_dynamic-update-slice_fusion.1
  39.0 1.2 select_dynamic-update-slice_fusion
  40.2 0.6 select_dynamic-update-slice_fusion.2
  40.8 0.6 constant_dynamic-update-slice_fusion
  41.3 2.4 %fusion.16 = (bf16[2095,320]{1,0:T(8,128)(2,1)S(1)}, bf16[2095,320]{1,0:T(8,128)(2,1)S(1)}) fusion(bf16[2096,320]{1,0:T(8,128)(2,1)} %constant_dynamic-update-slice_fusion), kind=kLoop, calls=%fused_computation.71 | loop fusion | bytes 5363200 | tf_op jit(solution)/shard_map/slice | solution.py:335
  43.8 1.0 fusion
  44.8 1.5 %copy.21 = bf16[4,64,8,640]{3,2,1,0:T(8,128)(2,1)S(1)} copy(bf16[4,64,8,640]{3,1,2,0:T(8,128)(2,1)S(1)} %bitcast.51) | data formatting | bytes 5242880 | tf_op jit(solution)/shard_map/transpose | solution.py:337
  46.3 0.1 fusion.7
  46.6 1.4 %copy-done.1 = bf16[1,640,1536]{2,1,0:T(8,128)(2,1)S(1)} copy-done((bf16[1,640,1536]{2,1,0:T(8,128)(2,1)S(1)}, bf16[1,640,1536]{2,1,0:T(8,128)(2,1)}, u32[]{:S(2)}) %copy-start.1) | copy-done | bytes 1966104
  48.0 0.6 shard_map.113
  48.7 0.2 pad_maximum_fusion
  48.8 0.8 collective-permute-start.10
  49.7 13.3 %collective-permute-start = (bf16[160,1536]{1,0:T(8,128)(2,1)S(1)}, bf16[160,1536]{1,0:T(8,128)(2,1)S(1)}, u32[]{:S(2)}, u32[]{:S(2)}) collective-permute-start(bf16[160,1536]{1,0:T(8,128)(2,1)S(1)} %maximum_maximum_fusion.rest_0_), channel_id=1, source_target_pairs={{0,1},{3,2},{4,5},{7,6},{8,9},{11,10},{12,13},{15,14},{16,17},{19,... | collective-permute-start | bytes 1474568 | tf_op jit(solution)/shard_map/ppermute | solution.py:257
  63.1 0.7 collective-permute-start.1
  63.8 4.2 %collective-permute-start.2 = (bf16[160,1536]{1,0:T(8,128)(2,1)S(1)}, bf16[160,1536]{1,0:T(8,128)(2,1)S(1)}, u32[]{:S(2)}, u32[]{:S(2)}) collective-permute-start(bf16[160,1536]{1,0:T(8,128)(2,1)S(1)} %maximum_maximum_fusion.rest_0_), channel_id=1, source_target_pairs={{0,2},{3,1},{4,6},{7,5},{8,10},{11,9},{12,14},{15,13},{16,18},{19,... | collective-permute-start | bytes 1474568 | tf_op jit(solution)/shard_map/ppermute | solution.py:257
  68.0 0.8 shard_map.114.swished_ref
  68.8 5.8 %collective-permute-done.rest_1_ = bf16[160,1536]{1,0:T(8,128)(2,1)S(1)} collective-permute-done((bf16[160,1536]{1,0:T(8,128)(2,1)S(1)}, bf16[160,1536]{1,0:T(8,128)(2,1)S(1)}, u32[]{:S(2)}, u32[]{:S(2)}) %collective-permute-start) | collective-permute-done | bytes 491552 | tf_op jit(solution)/shard_map/ppermute | solution.py:257
  74.5 10.2 %collective-permute-done.2.rest_3_ = bf16[160,1536]{1,0:T(8,128)(2,1)S(1)} collective-permute-done((bf16[160,1536]{1,0:T(8,128)(2,1)S(1)}, bf16[160,1536]{1,0:T(8,128)(2,1)S(1)}, u32[]{:S(2)}, u32[]{:S(2)}) %collective-permute-start.2) | collective-permute-done | bytes 491552 | tf_op jit(solution)/shard_map/ppermute | solution.py:257
  84.8 0.8 collective-permute-start.13
  85.6 0.7 collective-permute-start.12
  86.3 9.4 %collective-permute-start.11 = (s32[2,8,64]{2,1,0:T(8,128)S(1)}, s32[2,8,64]{2,1,0:T(8,128)S(1)}, u32[]{:S(2)}, u32[]{:S(2)}) collective-permute-start(s32[2,8,64]{2,1,0:T(8,128)S(1)} %fusion.14), channel_id=1, source_target_pairs={{0,1},{3,2},{4,5},{7,6},{8,9},{11,10},{12,13},{15,14},{16,17},{19,... | collective-permute-start | bytes 12296 | tf_op jit(solution)/shard_map/ppermute | solution.py:257
  95.7 1.3 %collective-permute-done.11 = s32[2,8,64]{2,1,0:T(8,128)S(1)} collective-permute-done((s32[2,8,64]{2,1,0:T(8,128)S(1)}, s32[2,8,64]{2,1,0:T(8,128)S(1)}, u32[]{:S(2)}, u32[]{:S(2)}) %collective-permute-start.11) | collective-permute-done | bytes 4128 | tf_op jit(solution)/shard_map/ppermute | solution.py:257
  97.1 1.0 shard_map.115
  98.1 1.6 %collective-permute-start.14 = (f32[4,8,128]{2,1,0:T(8,128)S(1)}, f32[4,8,128]{2,1,0:T(8,128)S(1)}, u32[]{:S(2)}, u32[]{:S(2)}) collective-permute-start(f32[4,8,128]{2,1,0:T(8,128)S(1)} %shard_map.115), channel_id=1, source_target_pairs={{0,8},{8,0},{16,24},{24,16},{1,9},{9,1},{17,25},{25,17},{2,10},{10... | collective-permute-start | bytes 49160 | tf_op jit(solution)/shard_map/ppermute | solution.py:266
  99.7 1.5 %collective-permute-start.15 = (f32[4,8,128]{2,1,0:T(8,128)S(1)}, f32[4,8,128]{2,1,0:T(8,128)S(1)}, u32[]{:S(2)}, u32[]{:S(2)}) collective-permute-start(f32[4,8,128]{2,1,0:T(8,128)S(1)} %shard_map.115), channel_id=1, source_target_pairs={{0,16},{8,24},{16,0},{24,8},{1,17},{9,25},{17,1},{25,9},{2,18},{10... | collective-permute-start | bytes 49160 | tf_op jit(solution)/shard_map/ppermute | solution.py:266
  101.2 0.5 collective-permute-start.16
  101.7 0.2 collective-permute-done.14
  101.9 1.5 %collective-permute-done.15 = f32[4,8,128]{2,1,0:T(8,128)S(1)} collective-permute-done((f32[4,8,128]{2,1,0:T(8,128)S(1)}, f32[4,8,128]{2,1,0:T(8,128)S(1)}, u32[]{:S(2)}, u32[]{:S(2)}) %collective-permute-start.15) | collective-permute-done | bytes 16416 | tf_op jit(solution)/shard_map/ppermute | solution.py:266
  103.4 2.4 %collective-permute-done.16 = f32[4,8,128]{2,1,0:T(8,128)S(1)} collective-permute-done((f32[4,8,128]{2,1,0:T(8,128)S(1)}, f32[4,8,128]{2,1,0:T(8,128)S(1)}, u32[]{:S(2)}, u32[]{:S(2)}) %collective-permute-start.16) | collective-permute-done | bytes 16416 | tf_op jit(solution)/shard_map/ppermute | solution.py:266
  105.9 0.6 slice_reduce_fusion
  106.5 0.6 pad_maximum_fusion.5
  107.2 1.3 collective-permute-start.17
  108.5 1.2 collective-permute-start.18
  109.7 1.3 collective-permute-start.19
  111.0 18.6 %collective-permute-done.19 = f32[1]{0:T(128)} collective-permute-done((f32[1]{0:T(128)}, f32[1]{0:T(128)}, u32[]{:S(2)}, u32[]{:S(2)}) %collective-permute-start.19) | collective-permute-done | bytes 36 | tf_op jit(solution)/shard_map/ppermute | solution.py:257
  130.9 0.5 slice.103
  132.7 0.6 slice_select_fusion.3
  (41 shorter events, 0.7 us)
Async XLA Ops:
  1.6 11.4 %copy-start = (bf16[1,192,1536]{2,1,0:T(8,128)(2,1)S(1)}, bf16[1,192,1536]{2,1,0:T(8,128)(2,1)}, u32[]{:S(2)}) copy-start(bf16[1,192,1536]{2,1,0:T(8,128)(2,1)} %param.15) | copy-start | bytes 1769476
  2.0 11.0 %collective-permute-start.3 = (bf16[256,320]{1,0:T(8,128)(2,1)S(1)}, bf16[256,320]{1,0:T(8,128)(2,1)S(1)}, u32[]{:S(2)}, u32[]{:S(2)}) collective-permute-start(bf16[256,320]{1,0:T(8,128)(2,1)S(1)} %reshape.52), channel_id=1, source_target_pairs={{0,1},{3,2},{4,5},{7,6},{8,9},{11,10},{12,13},{15,14},{16,17},{19,... | collective-permute-start | bytes 491528 | tf_op jit(solution)/shard_map/ppermute | solution.py:257
  7.9 5.0 %collective-permute-start.4 = (bf16[16,320]{1,0:T(8,128)(2,1)S(1)}, bf16[16,320]{1,0:T(8,128)(2,1)S(1)}, u32[]{:S(2)}, u32[]{:S(2)}) collective-permute-start(bf16[16,320]{1,0:T(8,128)(2,1)S(1)} %select_n.119), channel_id=1, source_target_pairs={{1,2},{2,1},{5,6},{6,5},{9,10},{10,9},{13,14},{14,13},{17,18},{18,... | collective-permute-start | bytes 30728 | tf_op jit(solution)/shard_map/ppermute | solution.py:257
  12.9 8.3 %copy-start.5 = (bf16[256,320]{1,0:T(8,128)(2,1)}, bf16[256,320]{1,0:T(8,128)(2,1)S(1)}, u32[]{:S(2)}) copy-start(bf16[256,320]{1,0:T(8,128)(2,1)S(1)} %collective-permute-done.3) | copy-start | bytes 491524
  13.0 35.6 %collective-permute-start.7 = (bf16[192,1536]{1,0:T(8,128)(2,1)S(1)}, bf16[192,1536]{1,0:T(8,128)(2,1)S(1)}, u32[]{:S(2)}, u32[]{:S(2)}) collective-permute-start(bf16[192,1536]{1,0:T(8,128)(2,1)S(1)} %bitcast.43), channel_id=1, source_target_pairs={{0,2},{3,1},{4,6},{7,5},{8,10},{11,9},{12,14},{15,13},{16,18},{19,... | collective-permute-start | bytes 1769480 | tf_op jit(solution)/shard_map/ppermute | solution.py:257
  17.0 31.7 %collective-permute-start.8 = (bf16[192,1536]{1,0:T(8,128)(2,1)S(1)}, bf16[192,1536]{1,0:T(8,128)(2,1)S(1)}, u32[]{:S(2)}, u32[]{:S(2)}) collective-permute-start(bf16[192,1536]{1,0:T(8,128)(2,1)S(1)} %bitcast.44), channel_id=1, source_target_pairs={{0,1},{3,2},{4,5},{7,6},{8,9},{11,10},{12,13},{15,14},{16,17},{19,... | collective-permute-start | bytes 1769480 | tf_op jit(solution)/shard_map/ppermute | solution.py:257
  18.4 30.2 %collective-permute-start.9 = (bf16[192,1536]{1,0:T(8,128)(2,1)S(1)}, bf16[192,1536]{1,0:T(8,128)(2,1)S(1)}, u32[]{:S(2)}, u32[]{:S(2)}) collective-permute-start(bf16[192,1536]{1,0:T(8,128)(2,1)S(1)} %bitcast.45), channel_id=1, source_target_pairs={{1,2},{2,1},{5,6},{6,5},{9,10},{10,9},{13,14},{14,13},{17,18},{18,... | collective-permute-start | bytes 1769480 | tf_op jit(solution)/shard_map/ppermute | solution.py:257
  19.1 6.1 %collective-permute-start.5 = (bf16[256,320]{1,0:T(8,128)(2,1)S(1)}, bf16[256,320]{1,0:T(8,128)(2,1)S(1)}, u32[]{:S(2)}, u32[]{:S(2)}) collective-permute-start(bf16[256,320]{1,0:T(8,128)(2,1)S(1)} %collective-permute-done.3), channel_id=1, source_target_pairs={{0,8},{8,0},{16,24},{24,16},{1,9},{9,1},{17,25},{25,17},{2,10},{10... | collective-permute-start | bytes 491528 | tf_op jit(solution)/shard_map/ppermute | solution.py:266
  27.1 9.7 %collective-permute-start.6 = (bf16[512,320]{1,0:T(8,128)(2,1)}, bf16[512,320]{1,0:T(8,128)(2,1)}, u32[]{:S(2)}, u32[]{:S(2)}) collective-permute-start(bf16[512,320]{1,0:T(8,128)(2,1)} %pad_maximum_fusion.3), channel_id=1, source_target_pairs={{0,16},{8,24},{16,0},{24,8},{1,17},{9,25},{17,1},{25,9},{2,18},{10... | collective-permute-start | bytes 983048 | tf_op jit(solution)/shard_map/ppermute | solution.py:266
  46.4 1.5 %copy-start.1 = (bf16[1,640,1536]{2,1,0:T(8,128)(2,1)S(1)}, bf16[1,640,1536]{2,1,0:T(8,128)(2,1)}, u32[]{:S(2)}) copy-start(bf16[1,640,1536]{2,1,0:T(8,128)(2,1)} %param.14) | copy-start | bytes 5898244
  46.4 1.5 %copy-start.2 = (f32[1,2,1536]{2,1,0:T(2,128)S(1)}, f32[1,2,1536]{2,1,0:T(2,128)}, u32[]{:S(2)}) copy-start(f32[1,2,1536]{2,1,0:T(2,128)} %param.19) | copy-start | bytes 36868
  48.6 1.0 copy-start.4
  48.6 1.1 copy-start.3
  48.6 19.3 %copy-start.6 = (bf16[1,31,768]{2,1,0:T(8,128)(2,1)S(1)}, bf16[1,31,768]{2,1,0:T(8,128)(2,1)}, u32[]{:S(2)}) copy-start(bf16[1,31,768]{2,1,0:T(8,128)(2,1)} %param.17) | copy-start | bytes 142852
  48.8 19.1 %collective-permute-start.10 = (bf16[768,1536]{1,0:T(8,128)(2,1)S(1)}, bf16[768,1536]{1,0:T(8,128)(2,1)S(1)}, u32[]{:S(2)}, u32[]{:S(2)}) collective-permute-start(bf16[768,1536]{1,0:T(8,128)(2,1)S(1)} %pad_maximum_fusion), channel_id=1, source_target_pairs={{1,5},{2,6},{5,1},{6,2},{9,13},{10,14},{13,9},{14,10},{17,21},{18,... | collective-permute-start | bytes 7077896 | tf_op jit(solution)/shard_map/ppermute | solution.py:262
  49.7 24.8 %collective-permute-start = (bf16[160,1536]{1,0:T(8,128)(2,1)S(1)}, bf16[160,1536]{1,0:T(8,128)(2,1)S(1)}, u32[]{:S(2)}, u32[]{:S(2)}) collective-permute-start(bf16[160,1536]{1,0:T(8,128)(2,1)S(1)} %maximum_maximum_fusion.rest_0_), channel_id=1, source_target_pairs={{0,1},{3,2},{4,5},{7,6},{8,9},{11,10},{12,13},{15,14},{16,17},{19,... | collective-permute-start | bytes 1474568 | tf_op jit(solution)/shard_map/ppermute | solution.py:257
  63.1 11.5 %collective-permute-start.1 = (bf16[160,1536]{1,0:T(8,128)(2,1)S(1)}, bf16[160,1536]{1,0:T(8,128)(2,1)S(1)}, u32[]{:S(2)}, u32[]{:S(2)}) collective-permute-start(bf16[160,1536]{1,0:T(8,128)(2,1)S(1)} %maximum_maximum_fusion.rest_0_), channel_id=1, source_target_pairs={{1,2},{2,1},{5,6},{6,5},{9,10},{10,9},{13,14},{14,13},{17,18},{18,... | collective-permute-start | bytes 1474568 | tf_op jit(solution)/shard_map/ppermute | solution.py:257
  63.8 21.0 %collective-permute-start.2 = (bf16[160,1536]{1,0:T(8,128)(2,1)S(1)}, bf16[160,1536]{1,0:T(8,128)(2,1)S(1)}, u32[]{:S(2)}, u32[]{:S(2)}) collective-permute-start(bf16[160,1536]{1,0:T(8,128)(2,1)S(1)} %maximum_maximum_fusion.rest_0_), channel_id=1, source_target_pairs={{0,2},{3,1},{4,6},{7,5},{8,10},{11,9},{12,14},{15,13},{16,18},{19,... | collective-permute-start | bytes 1474568 | tf_op jit(solution)/shard_map/ppermute | solution.py:257
  84.8 12.3 %collective-permute-start.13 = (bf16[480,1536]{1,0:T(8,128)(2,1)S(1)}, bf16[480,1536]{1,0:T(8,128)(2,1)S(1)}, u32[]{:S(2)}, u32[]{:S(2)}) collective-permute-start(bf16[480,1536]{1,0:T(8,128)(2,1)S(1)} %pad_maximum_fusion.1), channel_id=1, source_target_pairs={{1,5},{2,6},{5,1},{6,2},{9,13},{10,14},{13,9},{14,10},{17,21},{18,... | collective-permute-start | bytes 4423688 | tf_op jit(solution)/shard_map/ppermute | solution.py:262
  85.6 11.5 %collective-permute-start.12 = (bf16[160,1536]{1,0:T(8,128)(2,1)S(1)}, bf16[160,1536]{1,0:T(8,128)(2,1)S(1)}, u32[]{:S(2)}, u32[]{:S(2)}) collective-permute-start(bf16[160,1536]{1,0:T(8,128)(2,1)S(1)} %maximum_maximum_fusion.rest_0_), channel_id=1, source_target_pairs={{1,5},{2,6},{5,1},{6,2},{9,13},{10,14},{13,9},{14,10},{17,21},{18,... | collective-permute-start | bytes 1474568 | tf_op jit(solution)/shard_map/ppermute | solution.py:262
  86.3 10.8 %collective-permute-start.11 = (s32[2,8,64]{2,1,0:T(8,128)S(1)}, s32[2,8,64]{2,1,0:T(8,128)S(1)}, u32[]{:S(2)}, u32[]{:S(2)}) collective-permute-start(s32[2,8,64]{2,1,0:T(8,128)S(1)} %fusion.14), channel_id=1, source_target_pairs={{0,1},{3,2},{4,5},{7,6},{8,9},{11,10},{12,13},{15,14},{16,17},{19,... | collective-permute-start | bytes 12296 | tf_op jit(solution)/shard_map/ppermute | solution.py:257
  98.1 3.8 %collective-permute-start.14 = (f32[4,8,128]{2,1,0:T(8,128)S(1)}, f32[4,8,128]{2,1,0:T(8,128)S(1)}, u32[]{:S(2)}, u32[]{:S(2)}) collective-permute-start(f32[4,8,128]{2,1,0:T(8,128)S(1)} %shard_map.115), channel_id=1, source_target_pairs={{0,8},{8,0},{16,24},{24,16},{1,9},{9,1},{17,25},{25,17},{2,10},{10... | collective-permute-start | bytes 49160 | tf_op jit(solution)/shard_map/ppermute | solution.py:266
  99.7 3.7 %collective-permute-start.15 = (f32[4,8,128]{2,1,0:T(8,128)S(1)}, f32[4,8,128]{2,1,0:T(8,128)S(1)}, u32[]{:S(2)}, u32[]{:S(2)}) collective-permute-start(f32[4,8,128]{2,1,0:T(8,128)S(1)} %shard_map.115), channel_id=1, source_target_pairs={{0,16},{8,24},{16,0},{24,8},{1,17},{9,25},{17,1},{25,9},{2,18},{10... | collective-permute-start | bytes 49160 | tf_op jit(solution)/shard_map/ppermute | solution.py:266
  101.2 4.6 %collective-permute-start.16 = (f32[4,8,128]{2,1,0:T(8,128)S(1)}, f32[4,8,128]{2,1,0:T(8,128)S(1)}, u32[]{:S(2)}, u32[]{:S(2)}) collective-permute-start(f32[4,8,128]{2,1,0:T(8,128)S(1)} %shard_map.115), channel_id=1, source_target_pairs={{0,24},{8,16},{16,8},{24,0},{1,25},{9,17},{17,9},{25,1},{2,26},{10... | collective-permute-start | bytes 49160 | tf_op jit(solution)/shard_map/ppermute | solution.py:266
  107.2 23.7 %collective-permute-start.17 = (f32[1025]{0:T(1024)S(1)}, f32[1025]{0:T(1024)S(1)}, u32[]{:S(2)}, u32[]{:S(2)}) collective-permute-start(f32[1025]{0:T(1024)S(1)} %pad_maximum_fusion.5), channel_id=1, source_target_pairs={{1,0},{2,3},{5,4},{6,7},{9,8},{10,11},{13,12},{14,15},{17,16},{18,... | collective-permute-start | bytes 12308 | tf_op jit(solution)/shard_map/ppermute | solution.py:257
  108.5 2.5 %collective-permute-start.18 = (f32[1]{0:T(128)}, f32[1]{0:T(128)}, u32[]{:S(2)}, u32[]{:S(2)}) collective-permute-start(f32[1]{0:T(128)} %bitcast.22), channel_id=1, source_target_pairs={{1,2},{2,1},{5,6},{6,5},{9,10},{10,9},{13,14},{14,13},{17,18},{18,... | collective-permute-start | bytes 20 | tf_op jit(solution)/shard_map/ppermute | solution.py:257
  109.7 19.9 %collective-permute-start.19 = (f32[1]{0:T(128)}, f32[1]{0:T(128)}, u32[]{:S(2)}, u32[]{:S(2)}) collective-permute-start(f32[1]{0:T(128)} %bitcast.22), channel_id=1, source_target_pairs={{2,0},{1,3},{6,4},{5,7},{10,8},{9,11},{14,12},{13,15},{18,16},{17,... | collective-permute-start | bytes 20 | tf_op jit(solution)/shard_map/ppermute | solution.py:257

commit v10 on v6

--- a/solution.py
+++ b/solution.py
@@ -49,13 +49,14 @@
 def shards(meta, pieces):
     side = meta[13]
     length = pieces[0].shape[0]
-    places = [(pieces[i], 0) for i in range(5)] + [(pieces[5], i * length) for i in range(3)]
+    places = [(piece, 0) for piece in pieces[:-1]]
+    places += [(pieces[-1], i * length) for i in range(8 - len(places))]
     return [(*place, (side if i < 4 else 1 - side) * 4 + meta[9 + i % 4]) for i, place in enumerate(places)]
 
 
 def conv_kernel(meta, normed_ref, taps_ref, *rest):
-    pieces = rest[:6]
-    swished_ref, weight, mixed_a, mixed_b, gated, margin, mask, sems = rest[6:]
+    pieces = rest[:5]
+    swished_ref, weight, mixed_a, mixed_b, gated, margin, mask, sems = rest[5:]
     slot = pl.program_id(0)
     rows = normed_ref.shape[1]
     frames = swished_ref.shape[1]
@@ -384,7 +385,7 @@
     codes = codes.reshape(slots, CHUNKS, tile // CHUNKS)
     far_first, normed, codes = lax.optimization_barrier((far_first, normed, codes))
     mine = [first, near_first, hub_first, far_first]
-    first_pieces = (*mine, to_mate(first), to_mate(jnp.concatenate(mine[1:], axis=0)))
+    first_pieces = (*mine, to_mate(jnp.concatenate(mine, axis=0)))
     near_second, hub_second, far_second = [along(second, pairs_) for pairs_ in (INWARD, ACROSS, BEYOND)]
     taps = jnp.broadcast_to(
         depth_weight[0].astype(jnp.float32)[:, None, :], (depth_weight.shape[1], CHUNKS, channels)
@@ -393,7 +394,7 @@
     swished = call(
         conv_kernel,
         (slots,),
-        [by_slot((deep, width)), whole(taps.shape)] + [pinned] * 6,
+        [by_slot((deep, width)), whole(taps.shape)] + [pinned] * 5,
         by_slot((tile, channels)),
         jax.ShapeDtypeStruct((slots, tile, channels), jnp.bfloat16),
         [

time: 128 us -> 126 us (0.984)
  starting transfers between devices: 48.1 us -> 44.7 us
    ppermute x12, starting transfers between devices: 38.4 us -> 35.7 us  [along(): return lax.ppermute(x, 'seq', pairs)]
    unnamed x19 -> x17, local copies, waits for them, and re-layouts: 2.08 us -> 2.99 us
    ppermute x4 -> x3, starting transfers between devices: 3.05 us -> 2.26 us  [to_mate(): return lax.ppermute(x, ('fsdp', 'seq'), pairs)]
  transfers between devices with their start and end apart: 21 -> 20, of which waited for: 8 -> 8; matrix products, arithmetic and copies ran while one was open for 11% -> 12% of each run, Pallas kernels for 1% -> 1%
where the time goes in v10:
time: 126 us; the launch traced here: 125 us
  waiting for transfers between devices  52.3 us (42%)
  starting transfers between devices  44.7 us (35%)
  local copies, waits for them, and re-layouts  11.3 us (9%)
  other arithmetic  9.1 us (7%)
  between operations  5.62 us (4%)
  Pallas kernels  2.42 us (2%)
    ppermute x12, waiting for transfers between devices, along(): return lax.ppermute(x, 'seq', pairs)  41.5 us
    ppermute x12, starting transfers between devices, along(): return lax.ppermute(x, 'seq', pairs)  35.7 us
    ppermute x5, waiting for transfers between devices, seed_swap(): return lax.ppermute(x, 'seed', [(i, i ^ bit) for i in range(4)])  10.8 us
    ppermute x5, starting transfers between devices, seed_swap(): return lax.ppermute(x, 'seed', [(i, i ^ bit) for i in range(4)])  6.69 us
    unnamed x17, local copies, waits for them, and re-layouts  2.99 us
    concatenate x2, local copies, waits for them, and re-layouts, hub_body(): jnp.concatenate([jnp.where(low, outer_code, code), jnp.where(low, code, o...  2.68 us
  transfers between devices with their start and end apart: 20, of which 8 were waited for; matrix products, arithmetic and copies ran while one was open for 12% of the time, Pallas kernels for 1%

profile of v10, /device:TPU:0, one launch (start us, length us, event | category | flops | bytes accessed | tf_op | source)
XLA Modules:
  0.0 125.4 jit_solution(6442526781770559987)
XLA Ops:
  0.6 0.9 constant_dynamic-slice_fusion
  1.6 0.2 copy.16
  1.8 0.2 reshape.51
  2.0 4.9 %collective-permute-start.3 = (bf16[256,320]{1,0:T(8,128)(2,1)S(1)}, bf16[256,320]{1,0:T(8,128)(2,1)S(1)}, u32[]{:S(2)}, u32[]{:S(2)}) collective-permute-start(bf16[256,320]{1,0:T(8,128)(2,1)S(1)} %reshape.51), channel_id=1, source_target_pairs={{0,1},{3,2},{4,5},{7,6},{8,9},{11,10},{12,13},{15,14},{16,17},{19,... | collective-permute-start | bytes 491528 | tf_op jit(solution)/shard_map/ppermute | solution.py:257
  6.9 0.8 slice_select_fusion
  7.8 0.1 copy.17
  7.8 0.1 select_n.119
  7.9 0.7 collective-permute-start.4
  9.3 0.7 compare_reduce_fusion
  10.0 0.7 fusion.14
  10.7 4.1 %collective-permute-start.5 = (s32[1024]{0:T(1024)S(1)}, s32[1024]{0:T(1024)S(1)}, u32[]{:S(2)}, u32[]{:S(2)}) collective-permute-start(s32[1024]{0:T(1024)S(1)} %fusion.14), channel_id=1, source_target_pairs={{0,1},{3,2},{4,5},{7,6},{8,9},{11,10},{12,13},{15,14},{16,17},{19,... | collective-permute-start | bytes 12296 | tf_op jit(solution)/shard_map/ppermute | solution.py:257
  14.8 0.6 fusion.15
  15.4 1.5 %copy.18 = bf16[1,4096,80]{2,1,0:T(8,128)(2,1)S(1)} copy(bf16[1,4096,80]{1,2,0:T(8,128)(2,1)} %param.10) | data formatting | bytes 1310720 | tf_op args[0]
  17.0 0.7 reshape_squeeze.3
  17.7 0.7 concatenate.50.meta
  18.5 1.7 %collective-permute-start.6 = (bf16[192,1536]{1,0:T(8,128)(2,1)S(1)}, bf16[192,1536]{1,0:T(8,128)(2,1)S(1)}, u32[]{:S(2)}, u32[]{:S(2)}) collective-permute-start(bf16[192,1536]{1,0:T(8,128)(2,1)S(1)} %bitcast.44), channel_id=1, source_target_pairs={{0,2},{3,1},{4,6},{7,5},{8,10},{11,9},{12,14},{15,13},{16,18},{19,... | collective-permute-start | bytes 1769480 | tf_op jit(solution)/shard_map/ppermute | solution.py:257
  20.2 0.7 collective-permute-start.10
  20.9 3.1 %collective-permute-start.9 = (bf16[192,1536]{1,0:T(8,128)(2,1)S(1)}, bf16[192,1536]{1,0:T(8,128)(2,1)S(1)}, u32[]{:S(2)}, u32[]{:S(2)}) collective-permute-start(bf16[192,1536]{1,0:T(8,128)(2,1)S(1)} %bitcast.46), channel_id=1, source_target_pairs={{0,1},{3,2},{4,5},{7,6},{8,9},{11,10},{12,13},{15,14},{16,17},{19,... | collective-permute-start | bytes 1769480 | tf_op jit(solution)/shard_map/ppermute | solution.py:257
  24.0 1.6 %collective-permute-start.7 = (bf16[256,320]{1,0:T(8,128)(2,1)S(1)}, bf16[256,320]{1,0:T(8,128)(2,1)S(1)}, u32[]{:S(2)}, u32[]{:S(2)}) collective-permute-start(bf16[256,320]{1,0:T(8,128)(2,1)S(1)} %collective-permute-done.3), channel_id=1, source_target_pairs={{0,8},{8,0},{16,24},{24,16},{1,9},{9,1},{17,25},{25,17},{2,10},{10... | collective-permute-start | bytes 491528 | tf_op jit(solution)/shard_map/ppermute | solution.py:266
  25.6 1.3 %broadcast_select_fusion.5 = (s32[1024]{0:T(1024)}, s32[1024]{0:T(1024)}) fusion(s32[1024]{0:T(1024)} %copy-done.7, s32[1024]{0:T(1024)} %copy-done.6, pred[]{:T(512)S(6)} %eq.14), kind=kLoop, calls=%fused_computation.66 | loop fusion | flops 2048 | bytes 16385 | tf_op jit(solution)/shard_map/jit(_where)/select_n | solution.py:384
  26.9 1.3 %concatenate.61 = s32[2,8,64]{2,1,0:T(8,128)} reshape(s32[1024]{0:T(1024)} %get-tuple-element.48) | data formatting | bytes 8192 | tf_op jit(solution)/shard_map/concatenate | solution.py:384
  28.2 1.3 %concatenate.62 = s32[2,8,64]{2,1,0:T(8,128)} reshape(s32[1024]{0:T(1024)} %get-tuple-element.49) | data formatting | bytes 8192 | tf_op jit(solution)/shard_map/concatenate | solution.py:384
  29.5 0.2 collective-permute-done.7
  29.8 1.6 %collective-permute-start.8 = (bf16[512,320]{1,0:T(8,128)(2,1)S(1)}, bf16[512,320]{1,0:T(8,128)(2,1)S(1)}, u32[]{:S(2)}, u32[]{:S(2)}) collective-permute-start(bf16[512,320]{1,0:T(8,128)(2,1)S(1)} %pad_maximum_fusion.3), channel_id=1, source_target_pairs={{0,16},{8,24},{16,0},{24,8},{1,17},{9,25},{17,1},{25,9},{2,18},{10... | collective-permute-start | bytes 983048 | tf_op jit(solution)/shard_map/ppermute | solution.py:266
  31.4 0.7 pad_add_fusion.code_ref
  32.2 6.8 %collective-permute-done.8 = bf16[512,320]{1,0:T(8,128)(2,1)S(1)} collective-permute-done((bf16[512,320]{1,0:T(8,128)(2,1)S(1)}, bf16[512,320]{1,0:T(8,128)(2,1)S(1)}, u32[]{:S(2)}, u32[]{:S(2)}) %collective-permute-start.8) | collective-permute-done | bytes 327712 | tf_op jit(solution)/shard_map/ppermute | solution.py:266
  39.0 0.2 broadcast_select_fusion.1
  39.1 0.3 select_dynamic-update-slice_fusion.1
  39.4 0.3 select_dynamic-update-slice_fusion
  39.7 0.5 fusion.16
  40.2 1.0 fusion
  41.2 1.5 %copy.21 = bf16[4,64,8,640]{3,2,1,0:T(8,128)(2,1)S(1)} copy(bf16[4,64,8,640]{3,1,2,0:T(8,128)(2,1)S(1)} %bitcast.52) | data formatting | bytes 5242880 | tf_op jit(solution)/shard_map/transpose | solution.py:342
  42.8 0.1 fusion.7
  42.9 0.1 fusion.5
  43.0 1.4 %copy-done.1 = bf16[1,640,1536]{2,1,0:T(8,128)(2,1)S(1)} copy-done((bf16[1,640,1536]{2,1,0:T(8,128)(2,1)S(1)}, bf16[1,640,1536]{2,1,0:T(8,128)(2,1)}, u32[]{:S(2)}) %copy-start.1) | copy-done | bytes 1966104
  44.4 0.6 shard_map.113
  45.1 0.2 pad_maximum_fusion
  45.3 0.8 collective-permute-start.11
  46.2 11.9 %collective-permute-start = (bf16[160,1536]{1,0:T(8,128)(2,1)S(1)}, bf16[160,1536]{1,0:T(8,128)(2,1)S(1)}, u32[]{:S(2)}, u32[]{:S(2)}) collective-permute-start(bf16[160,1536]{1,0:T(8,128)(2,1)S(1)} %maximum_maximum_fusion.rest_0_), channel_id=1, source_target_pairs={{0,1},{3,2},{4,5},{7,6},{8,9},{11,10},{12,13},{15,14},{16,17},{19,... | collective-permute-start | bytes 1474568 | tf_op jit(solution)/shard_map/ppermute | solution.py:257
  58.1 0.7 collective-permute-start.1
  58.8 4.2 %collective-permute-start.2 = (bf16[160,1536]{1,0:T(8,128)(2,1)S(1)}, bf16[160,1536]{1,0:T(8,128)(2,1)S(1)}, u32[]{:S(2)}, u32[]{:S(2)}) collective-permute-start(bf16[160,1536]{1,0:T(8,128)(2,1)S(1)} %maximum_maximum_fusion.rest_0_), channel_id=1, source_target_pairs={{0,2},{3,1},{4,6},{7,5},{8,10},{11,9},{12,14},{15,13},{16,18},{19,... | collective-permute-start | bytes 1474568 | tf_op jit(solution)/shard_map/ppermute | solution.py:257
  63.1 0.8 shard_map.114.swished_ref
  63.8 5.8 %collective-permute-done.rest_1_ = bf16[160,1536]{1,0:T(8,128)(2,1)S(1)} collective-permute-done((bf16[160,1536]{1,0:T(8,128)(2,1)S(1)}, bf16[160,1536]{1,0:T(8,128)(2,1)S(1)}, u32[]{:S(2)}, u32[]{:S(2)}) %collective-permute-start) | collective-permute-done | bytes 491552 | tf_op jit(solution)/shard_map/ppermute | solution.py:257
  69.6 10.2 %collective-permute-done.2.rest_3_ = bf16[160,1536]{1,0:T(8,128)(2,1)S(1)} collective-permute-done((bf16[160,1536]{1,0:T(8,128)(2,1)S(1)}, bf16[160,1536]{1,0:T(8,128)(2,1)S(1)}, u32[]{:S(2)}, u32[]{:S(2)}) %collective-permute-start.2) | collective-permute-done | bytes 491552 | tf_op jit(solution)/shard_map/ppermute | solution.py:257
  79.8 0.1 pad_maximum_fusion.1
  79.9 0.8 collective-permute-start.13
  80.6 0.7 collective-permute-start.12
  81.4 1.0 shard_map.115
  82.4 1.2 collective-permute-start.14
  83.6 1.5 %collective-permute-start.15 = (f32[4,8,128]{2,1,0:T(8,128)S(1)}, f32[4,8,128]{2,1,0:T(8,128)S(1)}, u32[]{:S(2)}, u32[]{:S(2)}) collective-permute-start(f32[4,8,128]{2,1,0:T(8,128)S(1)} %shard_map.115), channel_id=1, source_target_pairs={{0,16},{8,24},{16,0},{24,8},{1,17},{9,25},{17,1},{25,9},{2,18},{10... | collective-permute-start | bytes 49160 | tf_op jit(solution)/shard_map/ppermute | solution.py:266
  85.1 0.8 collective-permute-start.16
  85.9 0.2 collective-permute-done.14
  86.2 1.1 collective-permute-done.15
  87.3 2.4 %collective-permute-done.16 = f32[4,8,128]{2,1,0:T(8,128)S(1)} collective-permute-done((f32[4,8,128]{2,1,0:T(8,128)S(1)}, f32[4,8,128]{2,1,0:T(8,128)S(1)}, u32[]{:S(2)}, u32[]{:S(2)}) %collective-permute-start.16) | collective-permute-done | bytes 16416 | tf_op jit(solution)/shard_map/ppermute | solution.py:266
  89.8 0.6 slice_reduce_fusion
  90.4 0.1 select_n.141
  90.4 0.6 pad_maximum_fusion.5
  91.1 1.3 %collective-permute-start.17 = (f32[1025]{0:T(1024)S(1)}, f32[1025]{0:T(1024)S(1)}, u32[]{:S(2)}, u32[]{:S(2)}) collective-permute-start(f32[1025]{0:T(1024)S(1)} %pad_maximum_fusion.5), channel_id=1, source_target_pairs={{1,0},{2,3},{5,4},{6,7},{9,8},{10,11},{13,12},{14,15},{17,16},{18,... | collective-permute-start | bytes 12308 | tf_op jit(solution)/shard_map/ppermute | solution.py:257
  92.4 1.2 collective-permute-start.18
  93.6 1.3 %collective-permute-start.19 = (f32[1]{0:T(128)}, f32[1]{0:T(128)}, u32[]{:S(2)}, u32[]{:S(2)}) collective-permute-start(f32[1]{0:T(128)} %bitcast.23), channel_id=1, source_target_pairs={{2,0},{1,3},{6,4},{5,7},{10,8},{9,11},{14,12},{13,15},{18,16},{17,... | collective-permute-start | bytes 20 | tf_op jit(solution)/shard_map/ppermute | solution.py:257
  94.9 0.1 select_n.139
  95.0 25.6 %collective-permute-done.19 = f32[1]{0:T(128)} collective-permute-done((f32[1]{0:T(128)}, f32[1]{0:T(128)}, u32[]{:S(2)}, u32[]{:S(2)}) %collective-permute-start.19) | collective-permute-done | bytes 36 | tf_op jit(solution)/shard_map/ppermute | solution.py:257
  121.8 0.5 slice.103
  123.7 0.6 slice_select_fusion.3
  (41 shorter events, 0.4 us)
Async XLA Ops:
  1.6 16.9 %copy-start = (bf16[1,192,1536]{2,1,0:T(8,128)(2,1)S(1)}, bf16[1,192,1536]{2,1,0:T(8,128)(2,1)}, u32[]{:S(2)}) copy-start(bf16[1,192,1536]{2,1,0:T(8,128)(2,1)} %param.15) | copy-start | bytes 1769476
  2.0 16.5 %collective-permute-start.3 = (bf16[256,320]{1,0:T(8,128)(2,1)S(1)}, bf16[256,320]{1,0:T(8,128)(2,1)S(1)}, u32[]{:S(2)}, u32[]{:S(2)}) collective-permute-start(bf16[256,320]{1,0:T(8,128)(2,1)S(1)} %reshape.51), channel_id=1, source_target_pairs={{0,1},{3,2},{4,5},{7,6},{8,9},{11,10},{12,13},{15,14},{16,17},{19,... | collective-permute-start | bytes 491528 | tf_op jit(solution)/shard_map/ppermute | solution.py:257
  7.9 10.5 %collective-permute-start.4 = (bf16[16,320]{1,0:T(8,128)(2,1)S(1)}, bf16[16,320]{1,0:T(8,128)(2,1)S(1)}, u32[]{:S(2)}, u32[]{:S(2)}) collective-permute-start(bf16[16,320]{1,0:T(8,128)(2,1)S(1)} %select_n.119), channel_id=1, source_target_pairs={{1,2},{2,1},{5,6},{6,5},{9,10},{10,9},{13,14},{14,13},{17,18},{18,... | collective-permute-start | bytes 30728 | tf_op jit(solution)/shard_map/ppermute | solution.py:257
  10.7 9.5 %copy-start.6 = (s32[1024]{0:T(1024)}, s32[1024]{0:T(1024)S(1)}, u32[]{:S(2)}) copy-start(s32[1024]{0:T(1024)S(1)} %fusion.14) | copy-start | bytes 12292
  10.7 7.8 %collective-permute-start.5 = (s32[1024]{0:T(1024)S(1)}, s32[1024]{0:T(1024)S(1)}, u32[]{:S(2)}, u32[]{:S(2)}) collective-permute-start(s32[1024]{0:T(1024)S(1)} %fusion.14), channel_id=1, source_target_pairs={{0,1},{3,2},{4,5},{7,6},{8,9},{11,10},{12,13},{15,14},{16,17},{19,... | collective-permute-start | bytes 12296 | tf_op jit(solution)/shard_map/ppermute | solution.py:257
  18.5 1.8 %copy-start.7 = (s32[1024]{0:T(1024)}, s32[1024]{0:T(1024)S(1)}, u32[]{:S(2)}) copy-start(s32[1024]{0:T(1024)S(1)} %collective-permute-done.5) | copy-start | bytes 12292
  18.5 26.6 %collective-permute-start.6 = (bf16[192,1536]{1,0:T(8,128)(2,1)S(1)}, bf16[192,1536]{1,0:T(8,128)(2,1)S(1)}, u32[]{:S(2)}, u32[]{:S(2)}) collective-permute-start(bf16[192,1536]{1,0:T(8,128)(2,1)S(1)} %bitcast.44), channel_id=1, source_target_pairs={{0,2},{3,1},{4,6},{7,5},{8,10},{11,9},{12,14},{15,13},{16,18},{19,... | collective-permute-start | bytes 1769480 | tf_op jit(solution)/shard_map/ppermute | solution.py:257
  20.2 24.9 %collective-permute-start.10 = (bf16[192,1536]{1,0:T(8,128)(2,1)S(1)}, bf16[192,1536]{1,0:T(8,128)(2,1)S(1)}, u32[]{:S(2)}, u32[]{:S(2)}) collective-permute-start(bf16[192,1536]{1,0:T(8,128)(2,1)S(1)} %bitcast.45), channel_id=1, source_target_pairs={{1,2},{2,1},{5,6},{6,5},{9,10},{10,9},{13,14},{14,13},{17,18},{18,... | collective-permute-start | bytes 1769480 | tf_op jit(solution)/shard_map/ppermute | solution.py:257
  20.9 24.2 %collective-permute-start.9 = (bf16[192,1536]{1,0:T(8,128)(2,1)S(1)}, bf16[192,1536]{1,0:T(8,128)(2,1)S(1)}, u32[]{:S(2)}, u32[]{:S(2)}) collective-permute-start(bf16[192,1536]{1,0:T(8,128)(2,1)S(1)} %bitcast.46), channel_id=1, source_target_pairs={{0,1},{3,2},{4,5},{7,6},{8,9},{11,10},{12,13},{15,14},{16,17},{19,... | collective-permute-start | bytes 1769480 | tf_op jit(solution)/shard_map/ppermute | solution.py:257
  24.0 5.7 %collective-permute-start.7 = (bf16[256,320]{1,0:T(8,128)(2,1)S(1)}, bf16[256,320]{1,0:T(8,128)(2,1)S(1)}, u32[]{:S(2)}, u32[]{:S(2)}) collective-permute-start(bf16[256,320]{1,0:T(8,128)(2,1)S(1)} %collective-permute-done.3), channel_id=1, source_target_pairs={{0,8},{8,0},{16,24},{24,16},{1,9},{9,1},{17,25},{25,17},{2,10},{10... | collective-permute-start | bytes 491528 | tf_op jit(solution)/shard_map/ppermute | solution.py:266
  29.8 9.1 %collective-permute-start.8 = (bf16[512,320]{1,0:T(8,128)(2,1)S(1)}, bf16[512,320]{1,0:T(8,128)(2,1)S(1)}, u32[]{:S(2)}, u32[]{:S(2)}) collective-permute-start(bf16[512,320]{1,0:T(8,128)(2,1)S(1)} %pad_maximum_fusion.3), channel_id=1, source_target_pairs={{0,16},{8,24},{16,0},{24,8},{1,17},{9,25},{17,1},{25,9},{2,18},{10... | collective-permute-start | bytes 983048 | tf_op jit(solution)/shard_map/ppermute | solution.py:266
  42.9 1.5 %copy-start.1 = (bf16[1,640,1536]{2,1,0:T(8,128)(2,1)S(1)}, bf16[1,640,1536]{2,1,0:T(8,128)(2,1)}, u32[]{:S(2)}) copy-start(bf16[1,640,1536]{2,1,0:T(8,128)(2,1)} %param.14) | copy-start | bytes 5898244
  42.9 1.5 %copy-start.2 = (f32[1,2,1536]{2,1,0:T(2,128)S(1)}, f32[1,2,1536]{2,1,0:T(2,128)}, u32[]{:S(2)}) copy-start(f32[1,2,1536]{2,1,0:T(2,128)} %param.19) | copy-start | bytes 36868
  45.1 1.0 copy-start.4
  45.1 1.1 copy-start.3
  45.1 17.9 %copy-start.5 = (bf16[1,31,768]{2,1,0:T(8,128)(2,1)S(1)}, bf16[1,31,768]{2,1,0:T(8,128)(2,1)}, u32[]{:S(2)}) copy-start(bf16[1,31,768]{2,1,0:T(8,128)(2,1)} %param.17) | copy-start | bytes 142852
  45.3 17.7 %collective-permute-start.11 = (bf16[768,1536]{1,0:T(8,128)(2,1)S(1)}, bf16[768,1536]{1,0:T(8,128)(2,1)S(1)}, u32[]{:S(2)}, u32[]{:S(2)}) collective-permute-start(bf16[768,1536]{1,0:T(8,128)(2,1)S(1)} %pad_maximum_fusion), channel_id=1, source_target_pairs={{1,5},{2,6},{5,1},{6,2},{9,13},{10,14},{13,9},{14,10},{17,21},{18,... | collective-permute-start | bytes 7077896 | tf_op jit(solution)/shard_map/ppermute | solution.py:262
  46.2 23.4 %collective-permute-start = (bf16[160,1536]{1,0:T(8,128)(2,1)S(1)}, bf16[160,1536]{1,0:T(8,128)(2,1)S(1)}, u32[]{:S(2)}, u32[]{:S(2)}) collective-permute-start(bf16[160,1536]{1,0:T(8,128)(2,1)S(1)} %maximum_maximum_fusion.rest_0_), channel_id=1, source_target_pairs={{0,1},{3,2},{4,5},{7,6},{8,9},{11,10},{12,13},{15,14},{16,17},{19,... | collective-permute-start | bytes 1474568 | tf_op jit(solution)/shard_map/ppermute | solution.py:257
  58.1 11.5 %collective-permute-start.1 = (bf16[160,1536]{1,0:T(8,128)(2,1)S(1)}, bf16[160,1536]{1,0:T(8,128)(2,1)S(1)}, u32[]{:S(2)}, u32[]{:S(2)}) collective-permute-start(bf16[160,1536]{1,0:T(8,128)(2,1)S(1)} %maximum_maximum_fusion.rest_0_), channel_id=1, source_target_pairs={{1,2},{2,1},{5,6},{6,5},{9,10},{10,9},{13,14},{14,13},{17,18},{18,... | collective-permute-start | bytes 1474568 | tf_op jit(solution)/shard_map/ppermute | solution.py:257
  58.8 21.0 %collective-permute-start.2 = (bf16[160,1536]{1,0:T(8,128)(2,1)S(1)}, bf16[160,1536]{1,0:T(8,128)(2,1)S(1)}, u32[]{:S(2)}, u32[]{:S(2)}) collective-permute-start(bf16[160,1536]{1,0:T(8,128)(2,1)S(1)} %maximum_maximum_fusion.rest_0_), channel_id=1, source_target_pairs={{0,2},{3,1},{4,6},{7,5},{8,10},{11,9},{12,14},{15,13},{16,18},{19,... | collective-permute-start | bytes 1474568 | tf_op jit(solution)/shard_map/ppermute | solution.py:257
  79.9 1.5 %collective-permute-start.13 = (bf16[480,1536]{1,0:T(8,128)(2,1)S(1)}, bf16[480,1536]{1,0:T(8,128)(2,1)S(1)}, u32[]{:S(2)}, u32[]{:S(2)}) collective-permute-start(bf16[480,1536]{1,0:T(8,128)(2,1)S(1)} %pad_maximum_fusion.1), channel_id=1, source_target_pairs={{1,5},{2,6},{5,1},{6,2},{9,13},{10,14},{13,9},{14,10},{17,21},{18,... | collective-permute-start | bytes 4423688 | tf_op jit(solution)/shard_map/ppermute | solution.py:262
  80.6 0.7 collective-permute-start.12
  82.4 3.8 %collective-permute-start.14 = (f32[4,8,128]{2,1,0:T(8,128)S(1)}, f32[4,8,128]{2,1,0:T(8,128)S(1)}, u32[]{:S(2)}, u32[]{:S(2)}) collective-permute-start(f32[4,8,128]{2,1,0:T(8,128)S(1)} %shard_map.115), channel_id=1, source_target_pairs={{0,8},{8,0},{16,24},{24,16},{1,9},{9,1},{17,25},{25,17},{2,10},{10... | collective-permute-start | bytes 49160 | tf_op jit(solution)/shard_map/ppermute | solution.py:266
  83.6 3.7 %collective-permute-start.15 = (f32[4,8,128]{2,1,0:T(8,128)S(1)}, f32[4,8,128]{2,1,0:T(8,128)S(1)}, u32[]{:S(2)}, u32[]{:S(2)}) collective-permute-start(f32[4,8,128]{2,1,0:T(8,128)S(1)} %shard_map.115), channel_id=1, source_target_pairs={{0,16},{8,24},{16,0},{24,8},{1,17},{9,25},{17,1},{25,9},{2,18},{10... | collective-permute-start | bytes 49160 | tf_op jit(solution)/shard_map/ppermute | solution.py:266
  85.1 4.6 %collective-permute-start.16 = (f32[4,8,128]{2,1,0:T(8,128)S(1)}, f32[4,8,128]{2,1,0:T(8,128)S(1)}, u32[]{:S(2)}, u32[]{:S(2)}) collective-permute-start(f32[4,8,128]{2,1,0:T(8,128)S(1)} %shard_map.115), channel_id=1, source_target_pairs={{0,24},{8,16},{16,8},{24,0},{1,25},{9,17},{17,9},{25,1},{2,26},{10... | collective-permute-start | bytes 49160 | tf_op jit(solution)/shard_map/ppermute | solution.py:266
  91.1 30.7 %collective-permute-start.17 = (f32[1025]{0:T(1024)S(1)}, f32[1025]{0:T(1024)S(1)}, u32[]{:S(2)}, u32[]{:S(2)}) collective-permute-start(f32[1025]{0:T(1024)S(1)} %pad_maximum_fusion.5), channel_id=1, source_target_pairs={{1,0},{2,3},{5,4},{6,7},{9,8},{10,11},{13,12},{14,15},{17,16},{18,... | collective-permute-start | bytes 12308 | tf_op jit(solution)/shard_map/ppermute | solution.py:257
  92.4 2.6 %collective-permute-start.18 = (f32[1]{0:T(128)}, f32[1]{0:T(128)}, u32[]{:S(2)}, u32[]{:S(2)}) collective-permute-start(f32[1]{0:T(128)} %bitcast.23), channel_id=1, source_target_pairs={{1,2},{2,1},{5,6},{6,5},{9,10},{10,9},{13,14},{14,13},{17,18},{18,... | collective-permute-start | bytes 20 | tf_op jit(solution)/shard_map/ppermute | solution.py:257
  93.6 26.9 %collective-permute-start.19 = (f32[1]{0:T(128)}, f32[1]{0:T(128)}, u32[]{:S(2)}, u32[]{:S(2)}) collective-permute-start(f32[1]{0:T(128)} %bitcast.23), channel_id=1, source_target_pairs={{2,0},{1,3},{6,4},{5,7},{10,8},{9,11},{14,12},{13,15},{18,16},{17,... | collective-permute-start | bytes 20 | tf_op jit(solution)/shard_map/ppermute | solution.py:257

commit v11 on v10

--- a/solution.py
+++ b/solution.py
@@ -308,12 +308,19 @@
     near_first, hub_first, far_first = [along(first_held, pairs_) for pairs_ in (INWARD, ACROSS, BEYOND)]
     held = first.shape[0]
 
-    pair = seed_swap(quarter_in, 1)
-    odd = seed % 2 == 1
-    pairs = jnp.concatenate([jnp.where(odd, pair, quarter_in), jnp.where(odd, quarter_in, pair)], axis=0)
-    other = seed_swap(pairs, 2)
-    upper = seed // 2 == 1
-    outer = jnp.concatenate([jnp.where(upper, other, pairs), jnp.where(upper, pairs, other)], axis=0)
+    odd, upper = seed % 2 == 1, seed // 2 == 1
+    beside, above, across = [seed_swap(quarter_in, bit) for bit in (1, 2, 3)]
+    even_piece, odd_piece = jnp.where(odd, beside, quarter_in), jnp.where(odd, quarter_in, beside)
+    even_other, odd_other = jnp.where(odd, across, above), jnp.where(odd, above, across)
+    outer = jnp.concatenate(
+        [
+            jnp.where(upper, even_other, even_piece),
+            jnp.where(upper, odd_other, odd_piece),
+            jnp.where(upper, even_piece, even_other),
+            jnp.where(upper, odd_piece, odd_other),
+        ],
+        axis=0,
+    )
 
     groups = width // vocab
     head_rows = head_weight.shape[1]

time: 126 us -> 122 us (0.968); the launches traced: 125 us -> 120 us
  starting transfers between devices: 44.7 us -> 38 us
    ppermute x12, starting transfers between devices: 35.7 us -> 28.6 us  [along(): return lax.ppermute(x, 'seq', pairs)]
    ppermute x12, waiting for transfers between devices: 41.5 us -> 45.4 us  [along(): return lax.ppermute(x, 'seq', pairs)]
    ppermute x5 -> x6, waiting for transfers between devices: 10.8 us -> 7.43 us  [seed_swap(): return lax.ppermute(x, 'seed', [(i, i ^ bit) for i in range(4)])]
    unnamed x4, other arithmetic: 0.59 us -> 3.47 us
    concatenate x2, local copies, waits for them, and re-layouts: 2.68 us -> 0.14 us  [hub_body(): jnp.concatenate([jnp.where(low, outer_code, code), jnp.where(low, code, o...]
    slice x1, local copies, waits for them, and re-layouts: 0.52 us -> 2.37 us  [hub_body(): pairs = jnp.concatenate([frames[:-1], frames[1:]], axis=1)]
    select_n x1, other arithmetic: 1.29 us -> 0.01 us  [hub_body(): jnp.where(low, outer_code, code)]
    ppermute x5 -> x6, starting transfers between devices: 6.69 us -> 7.11 us  [seed_swap(): return lax.ppermute(x, 'seed', [(i, i ^ bit) for i in range(4)])]
  transfers between devices with their start and end apart: 20 -> 21, of which waited for: 8 -> 10; matrix products, arithmetic and copies ran while one was open for 12% -> 13% of each run, Pallas kernels for 1% -> 1%
where the time goes in v11:
time: 122 us; the launch traced here: 120 us
  waiting for transfers between devices  52.8 us (43%)
  starting transfers between devices  38 us (31%)
  local copies, waits for them, and re-layouts  11.2 us (9%)
  other arithmetic  9.84 us (8%)
  between operations  5.57 us (5%)
  Pallas kernels  2.42 us (2%)
    ppermute x12, waiting for transfers between devices, along(): return lax.ppermute(x, 'seq', pairs)  45.4 us
    ppermute x12, starting transfers between devices, along(): return lax.ppermute(x, 'seq', pairs)  28.6 us
    ppermute x6, waiting for transfers between devices, seed_swap(): return lax.ppermute(x, 'seed', [(i, i ^ bit) for i in range(4)])  7.43 us
    ppermute x6, starting transfers between devices, seed_swap(): return lax.ppermute(x, 'seed', [(i, i ^ bit) for i in range(4)])  7.11 us
    unnamed x4, other arithmetic  3.47 us
    unnamed x13, local copies, waits for them, and re-layouts  2.98 us
  transfers between devices with their start and end apart: 21, of which 10 were waited for; matrix products, arithmetic and copies ran while one was open for 13% of the time, Pallas kernels for 1%

profile of v11, /device:TPU:0, one launch (start us, length us, event | category | flops | bytes accessed | tf_op | source)
XLA Modules:
  0.0 119.8 jit_solution(10247150203778097801)
XLA Ops:
  0.6 0.9 constant_dynamic-slice_fusion
  1.6 0.2 copy.16
  1.7 0.2 reshape.51
  2.0 5.1 %collective-permute-start.3 = (bf16[256,320]{1,0:T(8,128)(2,1)S(1)}, bf16[256,320]{1,0:T(8,128)(2,1)S(1)}, u32[]{:S(2)}, u32[]{:S(2)}) collective-permute-start(bf16[256,320]{1,0:T(8,128)(2,1)S(1)} %reshape.51), channel_id=1, source_target_pairs={{0,1},{3,2},{4,5},{7,6},{8,9},{11,10},{12,13},{15,14},{16,17},{19,... | collective-permute-start | bytes 491528 | tf_op jit(solution)/shard_map/ppermute | solution.py:257
  7.0 0.8 slice_select_fusion
  7.9 0.1 copy.17
  8.0 0.1 select_n.133
  8.1 0.7 collective-permute-start.4
  9.4 0.7 compare_reduce_fusion
  10.1 0.7 fusion.14
  10.8 4.1 %collective-permute-start.5 = (s32[1024]{0:T(1024)S(1)}, s32[1024]{0:T(1024)S(1)}, u32[]{:S(2)}, u32[]{:S(2)}) collective-permute-start(s32[1024]{0:T(1024)S(1)} %fusion.14), channel_id=1, source_target_pairs={{0,1},{3,2},{4,5},{7,6},{8,9},{11,10},{12,13},{15,14},{16,17},{19,... | collective-permute-start | bytes 12296 | tf_op jit(solution)/shard_map/ppermute | solution.py:257
  14.9 0.6 fusion.15
  15.5 1.5 %copy.18 = bf16[1,4096,80]{2,1,0:T(8,128)(2,1)S(1)} copy(bf16[1,4096,80]{1,2,0:T(8,128)(2,1)} %param.10) | data formatting | bytes 1310720 | tf_op args[0]
  17.1 0.7 reshape_squeeze.3
  17.8 0.7 concatenate.47.meta
  18.6 2.5 %collective-permute-start.7 = (bf16[256,320]{1,0:T(8,128)(2,1)S(1)}, bf16[256,320]{1,0:T(8,128)(2,1)S(1)}, u32[]{:S(2)}, u32[]{:S(2)}) collective-permute-start(bf16[256,320]{1,0:T(8,128)(2,1)S(1)} %collective-permute-done.3), channel_id=1, source_target_pairs={{0,24},{8,16},{16,8},{24,0},{1,25},{9,17},{17,9},{25,1},{2,26},{10... | collective-permute-start | bytes 491528 | tf_op jit(solution)/shard_map/ppermute | solution.py:266
  21.1 0.5 collective-permute-start.8
  21.6 0.5 collective-permute-start.9
  22.1 1.6 %collective-permute-start.6 = (bf16[192,1536]{1,0:T(8,128)(2,1)S(1)}, bf16[192,1536]{1,0:T(8,128)(2,1)S(1)}, u32[]{:S(2)}, u32[]{:S(2)}) collective-permute-start(bf16[192,1536]{1,0:T(8,128)(2,1)S(1)} %bitcast.44), channel_id=1, source_target_pairs={{0,2},{3,1},{4,6},{7,5},{8,10},{11,9},{12,14},{15,13},{16,18},{19,... | collective-permute-start | bytes 1769480 | tf_op jit(solution)/shard_map/ppermute | solution.py:257
  23.8 1.4 %collective-permute-start.10 = (bf16[192,1536]{1,0:T(8,128)(2,1)S(1)}, bf16[192,1536]{1,0:T(8,128)(2,1)S(1)}, u32[]{:S(2)}, u32[]{:S(2)}) collective-permute-start(bf16[192,1536]{1,0:T(8,128)(2,1)S(1)} %bitcast.45), channel_id=1, source_target_pairs={{0,1},{3,2},{4,5},{7,6},{8,9},{11,10},{12,13},{15,14},{16,17},{19,... | collective-permute-start | bytes 1769480 | tf_op jit(solution)/shard_map/ppermute | solution.py:257
  25.2 0.6 select_dynamic-update-slice_fusion.3
  26.0 1.4 %collective-permute-done.7 = bf16[256,320]{1,0:T(8,128)(2,1)S(1)} collective-permute-done((bf16[256,320]{1,0:T(8,128)(2,1)S(1)}, bf16[256,320]{1,0:T(8,128)(2,1)S(1)}, u32[]{:S(2)}, u32[]{:S(2)}) %collective-permute-start.7) | collective-permute-done | bytes 163872 | tf_op jit(solution)/shard_map/ppermute | solution.py:266
  27.4 0.7 collective-permute-start.11
  28.1 1.8 %collective-permute-done.8 = bf16[256,320]{1,0:T(8,128)(2,1)S(1)} collective-permute-done((bf16[256,320]{1,0:T(8,128)(2,1)S(1)}, bf16[256,320]{1,0:T(8,128)(2,1)S(1)}, u32[]{:S(2)}, u32[]{:S(2)}) %collective-permute-start.8) | collective-permute-done | bytes 163872 | tf_op jit(solution)/shard_map/ppermute | solution.py:266
  29.8 0.1 collective-permute-done.9
  29.9 0.1 broadcast_select_fusion.7
  30.1 1.1 select_dynamic-update-slice_fusion.1
  31.2 1.1 select_dynamic-update-slice_fusion
  32.3 0.6 select_dynamic-update-slice_fusion.2
  32.9 0.6 constant_dynamic-update-slice_fusion
  33.5 2.4 %fusion.16 = (bf16[2095,320]{1,0:T(8,128)(2,1)S(1)}, bf16[2095,320]{1,0:T(8,128)(2,1)S(1)}) fusion(bf16[2096,320]{1,0:T(8,128)(2,1)} %constant_dynamic-update-slice_fusion), kind=kLoop, calls=%fused_computation.74 | loop fusion | bytes 5363200 | tf_op jit(solution)/shard_map/slice | solution.py:347
  35.9 1.0 fusion
  36.9 1.5 %copy.21 = bf16[4,64,8,640]{3,2,1,0:T(8,128)(2,1)S(1)} copy(bf16[4,64,8,640]{3,1,2,0:T(8,128)(2,1)S(1)} %bitcast.52) | data formatting | bytes 5242880 | tf_op jit(solution)/shard_map/transpose | solution.py:349
  38.4 0.1 fusion.7
  38.5 0.1 fusion.5
  38.7 1.4 %copy-done.1 = bf16[1,640,1536]{2,1,0:T(8,128)(2,1)S(1)} copy-done((bf16[1,640,1536]{2,1,0:T(8,128)(2,1)S(1)}, bf16[1,640,1536]{2,1,0:T(8,128)(2,1)}, u32[]{:S(2)}) %copy-start.1) | copy-done | bytes 1966104
  40.1 0.6 shard_map.113
  40.7 6.8 %collective-permute-done.10.rest_1_ = bf16[192,1536]{1,0:T(8,128)(2,1)S(1)} collective-permute-done((bf16[192,1536]{1,0:T(8,128)(2,1)S(1)}, bf16[192,1536]{1,0:T(8,128)(2,1)S(1)}, u32[]{:S(2)}, u32[]{:S(2)}) %collective-permute-start.10) | collective-permute-done | bytes 589856 | tf_op jit(solution)/shard_map/ppermute | solution.py:257
  47.6 0.2 pad_maximum_fusion
  47.7 0.8 collective-permute-start.12
  48.6 6.4 %collective-permute-start = (bf16[160,1536]{1,0:T(8,128)(2,1)S(1)}, bf16[160,1536]{1,0:T(8,128)(2,1)S(1)}, u32[]{:S(2)}, u32[]{:S(2)}) collective-permute-start(bf16[160,1536]{1,0:T(8,128)(2,1)S(1)} %maximum_maximum_fusion.rest_0_), channel_id=1, source_target_pairs={{0,1},{3,2},{4,5},{7,6},{8,9},{11,10},{12,13},{15,14},{16,17},{19,... | collective-permute-start | bytes 1474568 | tf_op jit(solution)/shard_map/ppermute | solution.py:257
  55.0 0.7 collective-permute-start.1
  55.7 4.2 %collective-permute-start.2 = (bf16[160,1536]{1,0:T(8,128)(2,1)S(1)}, bf16[160,1536]{1,0:T(8,128)(2,1)S(1)}, u32[]{:S(2)}, u32[]{:S(2)}) collective-permute-start(bf16[160,1536]{1,0:T(8,128)(2,1)S(1)} %maximum_maximum_fusion.rest_0_), channel_id=1, source_target_pairs={{0,2},{3,1},{4,6},{7,5},{8,10},{11,9},{12,14},{15,13},{16,18},{19,... | collective-permute-start | bytes 1474568 | tf_op jit(solution)/shard_map/ppermute | solution.py:257
  60.0 0.8 shard_map.114.swished_ref
  60.7 5.8 %collective-permute-done.rest_1_ = bf16[160,1536]{1,0:T(8,128)(2,1)S(1)} collective-permute-done((bf16[160,1536]{1,0:T(8,128)(2,1)S(1)}, bf16[160,1536]{1,0:T(8,128)(2,1)S(1)}, u32[]{:S(2)}, u32[]{:S(2)}) %collective-permute-start) | collective-permute-done | bytes 491552 | tf_op jit(solution)/shard_map/ppermute | solution.py:257
  66.5 10.2 %collective-permute-done.2.rest_3_ = bf16[160,1536]{1,0:T(8,128)(2,1)S(1)} collective-permute-done((bf16[160,1536]{1,0:T(8,128)(2,1)S(1)}, bf16[160,1536]{1,0:T(8,128)(2,1)S(1)}, u32[]{:S(2)}, u32[]{:S(2)}) %collective-permute-start.2) | collective-permute-done | bytes 491552 | tf_op jit(solution)/shard_map/ppermute | solution.py:257
  76.7 0.1 pad_maximum_fusion.1
  76.8 0.8 collective-permute-start.14
  77.5 0.7 collective-permute-start.13
  78.3 1.0 shard_map.115
  79.3 1.6 %collective-permute-start.15 = (f32[4,8,128]{2,1,0:T(8,128)S(1)}, f32[4,8,128]{2,1,0:T(8,128)S(1)}, u32[]{:S(2)}, u32[]{:S(2)}) collective-permute-start(f32[4,8,128]{2,1,0:T(8,128)S(1)} %shard_map.115), channel_id=1, source_target_pairs={{0,8},{8,0},{16,24},{24,16},{1,9},{9,1},{17,25},{25,17},{2,10},{10... | collective-permute-start | bytes 49160 | tf_op jit(solution)/shard_map/ppermute | solution.py:266
  80.9 1.5 %collective-permute-start.16 = (f32[4,8,128]{2,1,0:T(8,128)S(1)}, f32[4,8,128]{2,1,0:T(8,128)S(1)}, u32[]{:S(2)}, u32[]{:S(2)}) collective-permute-start(f32[4,8,128]{2,1,0:T(8,128)S(1)} %shard_map.115), channel_id=1, source_target_pairs={{0,16},{8,24},{16,0},{24,8},{1,17},{9,25},{17,1},{25,9},{2,18},{10... | collective-permute-start | bytes 49160 | tf_op jit(solution)/shard_map/ppermute | solution.py:266
  82.4 0.5 collective-permute-start.17
  82.9 0.2 collective-permute-done.15
  83.1 1.5 %collective-permute-done.16 = f32[4,8,128]{2,1,0:T(8,128)S(1)} collective-permute-done((f32[4,8,128]{2,1,0:T(8,128)S(1)}, f32[4,8,128]{2,1,0:T(8,128)S(1)}, u32[]{:S(2)}, u32[]{:S(2)}) %collective-permute-start.16) | collective-permute-done | bytes 16416 | tf_op jit(solution)/shard_map/ppermute | solution.py:266
  84.6 2.4 %collective-permute-done.17 = f32[4,8,128]{2,1,0:T(8,128)S(1)} collective-permute-done((f32[4,8,128]{2,1,0:T(8,128)S(1)}, f32[4,8,128]{2,1,0:T(8,128)S(1)}, u32[]{:S(2)}, u32[]{:S(2)}) %collective-permute-start.17) | collective-permute-done | bytes 16416 | tf_op jit(solution)/shard_map/ppermute | solution.py:266
  87.0 0.6 slice_reduce_fusion
  87.7 0.6 pad_maximum_fusion.4
  88.4 1.3 %collective-permute-start.18 = (f32[1025]{0:T(1024)S(1)}, f32[1025]{0:T(1024)S(1)}, u32[]{:S(2)}, u32[]{:S(2)}) collective-permute-start(f32[1025]{0:T(1024)S(1)} %pad_maximum_fusion.4), channel_id=1, source_target_pairs={{1,0},{2,3},{5,4},{6,7},{9,8},{10,11},{13,12},{14,15},{17,16},{18,... | collective-permute-start | bytes 12308 | tf_op jit(solution)/shard_map/ppermute | solution.py:257
  89.7 1.3 %collective-permute-start.19 = (f32[1]{0:T(128)}, f32[1]{0:T(128)}, u32[]{:S(2)}, u32[]{:S(2)}) collective-permute-start(f32[1]{0:T(128)} %bitcast.23), channel_id=1, source_target_pairs={{1,2},{2,1},{5,6},{6,5},{9,10},{10,9},{13,14},{14,13},{17,18},{18,... | collective-permute-start | bytes 20 | tf_op jit(solution)/shard_map/ppermute | solution.py:257
  90.9 1.3 %collective-permute-start.20 = (f32[1]{0:T(128)}, f32[1]{0:T(128)}, u32[]{:S(2)}, u32[]{:S(2)}) collective-permute-start(f32[1]{0:T(128)} %bitcast.23), channel_id=1, source_target_pairs={{2,0},{1,3},{6,4},{5,7},{10,8},{9,11},{14,12},{13,15},{18,16},{17,... | collective-permute-start | bytes 20 | tf_op jit(solution)/shard_map/ppermute | solution.py:257
  92.3 22.6 %collective-permute-done.20 = f32[1]{0:T(128)} collective-permute-done((f32[1]{0:T(128)}, f32[1]{0:T(128)}, u32[]{:S(2)}, u32[]{:S(2)}) %collective-permute-start.20) | collective-permute-done | bytes 36 | tf_op jit(solution)/shard_map/ppermute | solution.py:257
  116.2 0.5 slice.103
  118.1 0.6 slice_select_fusion.3
  (37 shorter events, 0.5 us)
Async XLA Ops:
  1.9 20.2 %copy-start = (bf16[1,192,1536]{2,1,0:T(8,128)(2,1)S(1)}, bf16[1,192,1536]{2,1,0:T(8,128)(2,1)}, u32[]{:S(2)}) copy-start(bf16[1,192,1536]{2,1,0:T(8,128)(2,1)} %param.15) | copy-start | bytes 1769476
  2.0 16.6 %collective-permute-start.3 = (bf16[256,320]{1,0:T(8,128)(2,1)S(1)}, bf16[256,320]{1,0:T(8,128)(2,1)S(1)}, u32[]{:S(2)}, u32[]{:S(2)}) collective-permute-start(bf16[256,320]{1,0:T(8,128)(2,1)S(1)} %reshape.51), channel_id=1, source_target_pairs={{0,1},{3,2},{4,5},{7,6},{8,9},{11,10},{12,13},{15,14},{16,17},{19,... | collective-permute-start | bytes 491528 | tf_op jit(solution)/shard_map/ppermute | solution.py:257
  8.1 10.5 %collective-permute-start.4 = (bf16[16,320]{1,0:T(8,128)(2,1)S(1)}, bf16[16,320]{1,0:T(8,128)(2,1)S(1)}, u32[]{:S(2)}, u32[]{:S(2)}) collective-permute-start(bf16[16,320]{1,0:T(8,128)(2,1)S(1)} %select_n.133), channel_id=1, source_target_pairs={{1,2},{2,1},{5,6},{6,5},{9,10},{10,9},{13,14},{14,13},{17,18},{18,... | collective-permute-start | bytes 30728 | tf_op jit(solution)/shard_map/ppermute | solution.py:257
  10.8 7.8 %collective-permute-start.5 = (s32[1024]{0:T(1024)S(1)}, s32[1024]{0:T(1024)S(1)}, u32[]{:S(2)}, u32[]{:S(2)}) collective-permute-start(s32[1024]{0:T(1024)S(1)} %fusion.14), channel_id=1, source_target_pairs={{0,1},{3,2},{4,5},{7,6},{8,9},{11,10},{12,13},{15,14},{16,17},{19,... | collective-permute-start | bytes 12296 | tf_op jit(solution)/shard_map/ppermute | solution.py:257
  18.6 8.8 %collective-permute-start.7 = (bf16[256,320]{1,0:T(8,128)(2,1)S(1)}, bf16[256,320]{1,0:T(8,128)(2,1)S(1)}, u32[]{:S(2)}, u32[]{:S(2)}) collective-permute-start(bf16[256,320]{1,0:T(8,128)(2,1)S(1)} %collective-permute-done.3), channel_id=1, source_target_pairs={{0,24},{8,16},{16,8},{24,0},{1,25},{9,17},{17,9},{25,1},{2,26},{10... | collective-permute-start | bytes 491528 | tf_op jit(solution)/shard_map/ppermute | solution.py:266
  21.1 8.7 %collective-permute-start.8 = (bf16[256,320]{1,0:T(8,128)(2,1)S(1)}, bf16[256,320]{1,0:T(8,128)(2,1)S(1)}, u32[]{:S(2)}, u32[]{:S(2)}) collective-permute-start(bf16[256,320]{1,0:T(8,128)(2,1)S(1)} %collective-permute-done.3), channel_id=1, source_target_pairs={{0,16},{8,24},{16,0},{24,8},{1,17},{9,25},{17,1},{25,9},{2,18},{10... | collective-permute-start | bytes 491528 | tf_op jit(solution)/shard_map/ppermute | solution.py:266
  21.6 8.3 %collective-permute-start.9 = (bf16[256,320]{1,0:T(8,128)(2,1)S(1)}, bf16[256,320]{1,0:T(8,128)(2,1)S(1)}, u32[]{:S(2)}, u32[]{:S(2)}) collective-permute-start(bf16[256,320]{1,0:T(8,128)(2,1)S(1)} %collective-permute-done.3), channel_id=1, source_target_pairs={{0,8},{8,0},{16,24},{24,16},{1,9},{9,1},{17,25},{25,17},{2,10},{10... | collective-permute-start | bytes 491528 | tf_op jit(solution)/shard_map/ppermute | solution.py:266
  22.1 18.6 %collective-permute-start.6 = (bf16[192,1536]{1,0:T(8,128)(2,1)S(1)}, bf16[192,1536]{1,0:T(8,128)(2,1)S(1)}, u32[]{:S(2)}, u32[]{:S(2)}) collective-permute-start(bf16[192,1536]{1,0:T(8,128)(2,1)S(1)} %bitcast.44), channel_id=1, source_target_pairs={{0,2},{3,1},{4,6},{7,5},{8,10},{11,9},{12,14},{15,13},{16,18},{19,... | collective-permute-start | bytes 1769480 | tf_op jit(solution)/shard_map/ppermute | solution.py:257
  23.8 23.8 %collective-permute-start.10 = (bf16[192,1536]{1,0:T(8,128)(2,1)S(1)}, bf16[192,1536]{1,0:T(8,128)(2,1)S(1)}, u32[]{:S(2)}, u32[]{:S(2)}) collective-permute-start(bf16[192,1536]{1,0:T(8,128)(2,1)S(1)} %bitcast.45), channel_id=1, source_target_pairs={{0,1},{3,2},{4,5},{7,6},{8,9},{11,10},{12,13},{15,14},{16,17},{19,... | collective-permute-start | bytes 1769480 | tf_op jit(solution)/shard_map/ppermute | solution.py:257
  27.4 20.2 %collective-permute-start.11 = (bf16[192,1536]{1,0:T(8,128)(2,1)S(1)}, bf16[192,1536]{1,0:T(8,128)(2,1)S(1)}, u32[]{:S(2)}, u32[]{:S(2)}) collective-permute-start(bf16[192,1536]{1,0:T(8,128)(2,1)S(1)} %bitcast.46), channel_id=1, source_target_pairs={{1,2},{2,1},{5,6},{6,5},{9,10},{10,9},{13,14},{14,13},{17,18},{18,... | collective-permute-start | bytes 1769480 | tf_op jit(solution)/shard_map/ppermute | solution.py:257
  38.5 1.5 %copy-start.1 = (bf16[1,640,1536]{2,1,0:T(8,128)(2,1)S(1)}, bf16[1,640,1536]{2,1,0:T(8,128)(2,1)}, u32[]{:S(2)}) copy-start(bf16[1,640,1536]{2,1,0:T(8,128)(2,1)} %param.14) | copy-start | bytes 5898244
  38.5 1.5 %copy-start.2 = (f32[1,2,1536]{2,1,0:T(2,128)S(1)}, f32[1,2,1536]{2,1,0:T(2,128)}, u32[]{:S(2)}) copy-start(f32[1,2,1536]{2,1,0:T(2,128)} %param.19) | copy-start | bytes 36868
  40.7 7.8 %copy-start.4 = (bf16[1,192,512]{2,1,0:T(8,128)(2,1)S(1)}, bf16[1,192,512]{2,1,0:T(8,128)(2,1)}, u32[]{:S(2)}) copy-start(bf16[1,192,512]{2,1,0:T(8,128)(2,1)} %param.18) | copy-start | bytes 589828
  40.7 7.9 %copy-start.3 = (bf16[1,96,1536]{2,1,0:T(8,128)(2,1)S(1)}, bf16[1,96,1536]{2,1,0:T(8,128)(2,1)}, u32[]{:S(2)}) copy-start(bf16[1,96,1536]{2,1,0:T(8,128)(2,1)} %param.16) | copy-start | bytes 884740
  40.7 19.1 %copy-start.5 = (bf16[1,31,768]{2,1,0:T(8,128)(2,1)S(1)}, bf16[1,31,768]{2,1,0:T(8,128)(2,1)}, u32[]{:S(2)}) copy-start(bf16[1,31,768]{2,1,0:T(8,128)(2,1)} %param.17) | copy-start | bytes 142852
  47.7 12.2 %collective-permute-start.12 = (bf16[768,1536]{1,0:T(8,128)(2,1)S(1)}, bf16[768,1536]{1,0:T(8,128)(2,1)S(1)}, u32[]{:S(2)}, u32[]{:S(2)}) collective-permute-start(bf16[768,1536]{1,0:T(8,128)(2,1)S(1)} %pad_maximum_fusion), channel_id=1, source_target_pairs={{1,5},{2,6},{5,1},{6,2},{9,13},{10,14},{13,9},{14,10},{17,21},{18,... | collective-permute-start | bytes 7077896 | tf_op jit(solution)/shard_map/ppermute | solution.py:262
  48.6 17.9 %collective-permute-start = (bf16[160,1536]{1,0:T(8,128)(2,1)S(1)}, bf16[160,1536]{1,0:T(8,128)(2,1)S(1)}, u32[]{:S(2)}, u32[]{:S(2)}) collective-permute-start(bf16[160,1536]{1,0:T(8,128)(2,1)S(1)} %maximum_maximum_fusion.rest_0_), channel_id=1, source_target_pairs={{0,1},{3,2},{4,5},{7,6},{8,9},{11,10},{12,13},{15,14},{16,17},{19,... | collective-permute-start | bytes 1474568 | tf_op jit(solution)/shard_map/ppermute | solution.py:257
  55.0 11.5 %collective-permute-start.1 = (bf16[160,1536]{1,0:T(8,128)(2,1)S(1)}, bf16[160,1536]{1,0:T(8,128)(2,1)S(1)}, u32[]{:S(2)}, u32[]{:S(2)}) collective-permute-start(bf16[160,1536]{1,0:T(8,128)(2,1)S(1)} %maximum_maximum_fusion.rest_0_), channel_id=1, source_target_pairs={{1,2},{2,1},{5,6},{6,5},{9,10},{10,9},{13,14},{14,13},{17,18},{18,... | collective-permute-start | bytes 1474568 | tf_op jit(solution)/shard_map/ppermute | solution.py:257
  55.7 21.0 %collective-permute-start.2 = (bf16[160,1536]{1,0:T(8,128)(2,1)S(1)}, bf16[160,1536]{1,0:T(8,128)(2,1)S(1)}, u32[]{:S(2)}, u32[]{:S(2)}) collective-permute-start(bf16[160,1536]{1,0:T(8,128)(2,1)S(1)} %maximum_maximum_fusion.rest_0_), channel_id=1, source_target_pairs={{0,2},{3,1},{4,6},{7,5},{8,10},{11,9},{12,14},{15,13},{16,18},{19,... | collective-permute-start | bytes 1474568 | tf_op jit(solution)/shard_map/ppermute | solution.py:257
  76.8 1.5 %collective-permute-start.14 = (bf16[480,1536]{1,0:T(8,128)(2,1)S(1)}, bf16[480,1536]{1,0:T(8,128)(2,1)S(1)}, u32[]{:S(2)}, u32[]{:S(2)}) collective-permute-start(bf16[480,1536]{1,0:T(8,128)(2,1)S(1)} %pad_maximum_fusion.1), channel_id=1, source_target_pairs={{1,5},{2,6},{5,1},{6,2},{9,13},{10,14},{13,9},{14,10},{17,21},{18,... | collective-permute-start | bytes 4423688 | tf_op jit(solution)/shard_map/ppermute | solution.py:262
  77.5 0.7 collective-permute-start.13
  79.3 3.8 %collective-permute-start.15 = (f32[4,8,128]{2,1,0:T(8,128)S(1)}, f32[4,8,128]{2,1,0:T(8,128)S(1)}, u32[]{:S(2)}, u32[]{:S(2)}) collective-permute-start(f32[4,8,128]{2,1,0:T(8,128)S(1)} %shard_map.115), channel_id=1, source_target_pairs={{0,8},{8,0},{16,24},{24,16},{1,9},{9,1},{17,25},{25,17},{2,10},{10... | collective-permute-start | bytes 49160 | tf_op jit(solution)/shard_map/ppermute | solution.py:266
  80.9 3.7 %collective-permute-start.16 = (f32[4,8,128]{2,1,0:T(8,128)S(1)}, f32[4,8,128]{2,1,0:T(8,128)S(1)}, u32[]{:S(2)}, u32[]{:S(2)}) collective-permute-start(f32[4,8,128]{2,1,0:T(8,128)S(1)} %shard_map.115), channel_id=1, source_target_pairs={{0,16},{8,24},{16,0},{24,8},{1,17},{9,25},{17,1},{25,9},{2,18},{10... | collective-permute-start | bytes 49160 | tf_op jit(solution)/shard_map/ppermute | solution.py:266
  82.4 4.6 %collective-permute-start.17 = (f32[4,8,128]{2,1,0:T(8,128)S(1)}, f32[4,8,128]{2,1,0:T(8,128)S(1)}, u32[]{:S(2)}, u32[]{:S(2)}) collective-permute-start(f32[4,8,128]{2,1,0:T(8,128)S(1)} %shard_map.115), channel_id=1, source_target_pairs={{0,24},{8,16},{16,8},{24,0},{1,25},{9,17},{17,9},{25,1},{2,26},{10... | collective-permute-start | bytes 49160 | tf_op jit(solution)/shard_map/ppermute | solution.py:266
  88.4 27.8 %collective-permute-start.18 = (f32[1025]{0:T(1024)S(1)}, f32[1025]{0:T(1024)S(1)}, u32[]{:S(2)}, u32[]{:S(2)}) collective-permute-start(f32[1025]{0:T(1024)S(1)} %pad_maximum_fusion.4), channel_id=1, source_target_pairs={{1,0},{2,3},{5,4},{6,7},{9,8},{10,11},{13,12},{14,15},{17,16},{18,... | collective-permute-start | bytes 12308 | tf_op jit(solution)/shard_map/ppermute | solution.py:257
  89.7 2.6 %collective-permute-start.19 = (f32[1]{0:T(128)}, f32[1]{0:T(128)}, u32[]{:S(2)}, u32[]{:S(2)}) collective-permute-start(f32[1]{0:T(128)} %bitcast.23), channel_id=1, source_target_pairs={{1,2},{2,1},{5,6},{6,5},{9,10},{10,9},{13,14},{14,13},{17,18},{18,... | collective-permute-start | bytes 20 | tf_op jit(solution)/shard_map/ppermute | solution.py:257
  90.9 24.0 %collective-permute-start.20 = (f32[1]{0:T(128)}, f32[1]{0:T(128)}, u32[]{:S(2)}, u32[]{:S(2)}) collective-permute-start(f32[1]{0:T(128)} %bitcast.23), channel_id=1, source_target_pairs={{2,0},{1,3},{6,4},{5,7},{10,8},{9,11},{14,12},{13,15},{18,16},{17,... | collective-permute-start | bytes 20 | tf_op jit(solution)/shard_map/ppermute | solution.py:257
